TPU v7x, 32 devices: a whole 2x2x4 slice. The times are simulated.
32 devices in a mesh: len: 8 (over z, y), pipe: 4 (over x, core).
Axes of the slice: x: 2, y: 2, z: 4, core: 2. Of those that a mesh axis runs over, the one named last changes fastest.
Arguments:
- inputs: bfloat16 [32, 2048, 256], P(('len', 'pipe')), may hold values from -6 to 6
- cotangent: bfloat16 [32, 2048, 256], P(('len', 'pipe')), may hold values from -6 to 6
- point_weight: bfloat16 [256, 256], replicated, may hold values from -0.375 to 0.375
- point_bias: float32 [256], replicated, may hold values from -3 to 3
- spec_real: bfloat16 [128, 256, 256], P('len'), may hold values from -0.25 to 0.25
- spec_imag: bfloat16 [128, 256, 256], P('len'), may hold values from -0.25 to 0.25
- junc_weight: bfloat16 [256, 256], replicated, may hold values from -0.375 to 0.375
- junc_bias: float32 [256], replicated, may hold values from -3 to 3
- inlet_ids: int32 [32], replicated, may hold values from 0 to 31
- outlet_ids: int32 [32], replicated, may hold values from 0 to 31
Outputs:
- outputs: bfloat16 [32, 2048, 256], P(('len', 'pipe'))
- grad_inputs: bfloat16 [32, 2048, 256], P(('len', 'pipe'))
- grad_real: float32 [128, 256, 256], P('len')
- grad_imag: float32 [128, 256, 256], P('len')
All inputs are finite; a program needn't handle non-finite values.
Results may differ from a plain program's by a relative error of at most 0.015.
Values may be sent and summed in bfloat16 or wider, within the bound.
No kernel may reach another device: no remote copies, remote signals or barrier semaphores. Data moves between devices by JAX's collectives and lax.ppermute only.
A program may use at most 64 MiB of HBM per device.

v0:
```python
import math

import jax
import jax.numpy as jnp
from jax import lax
from jax.sharding import PartitionSpec as P

COUPLING = 0.125


def tables(cell_count, mode_count):
    position = lax.broadcasted_iota(jnp.int32, (mode_count, cell_count), 1)
    frequency = lax.broadcasted_iota(jnp.int32, (mode_count, cell_count), 0)
    product_index = frequency * position % cell_count
    angles = product_index.astype(jnp.float32) * (2.0 * math.pi / cell_count)
    norm_scale = 1.0 / math.sqrt(cell_count)
    cosine = jnp.cos(angles) * norm_scale
    sine_table = jnp.sin(angles) * norm_scale
    doubled = jnp.where(frequency == 0, 1.0, 2.0)
    forward = (
        jnp.stack([cosine, -sine_table], axis=1)
        .reshape(2 * mode_count, cell_count)
        .astype(jnp.bfloat16)
    )
    inverse = jnp.transpose(
        jnp.stack([doubled * cosine, -doubled * sine_table], axis=1).reshape(
            2 * mode_count, cell_count
        )
    ).astype(jnp.bfloat16)
    return (forward, inverse)


def spectral_blocks(spec_real, spec_imag):
    upper = jnp.concatenate([spec_real, spec_imag], axis=2)
    lower = jnp.concatenate([-spec_imag, spec_real], axis=2)
    return jnp.concatenate([upper, lower], axis=1)


def activate(values):
    return jax.nn.gelu(values, approximate=True)


def silu_slope(values):
    sigmoid_part = jax.nn.sigmoid(values)
    return sigmoid_part * (1.0 + values * (1.0 - sigmoid_part))


def to_modes(field):
    return lax.all_to_all(field, "len", split_axis=1, concat_axis=0, tiled=True)


def from_modes(field):
    return lax.all_to_all(field, "len", split_axis=0, concat_axis=1, tiled=True)


def junction_pass(partial_value, rowwise, carried):
    summed_rows = lax.psum(partial_value, ("len", "pipe"))
    return rowwise(summed_rows, carried)


def body(
    inputs,
    cotangent,
    point_weight,
    point_bias,
    spec_real,
    spec_imag,
    junc_weight,
    junc_bias,
    inlet_ids,
    outlet_ids,
):
    per_dev, cell_count, channels = inputs.shape
    len_count = lax.axis_size("len")
    mode_count = spec_real.shape[0] * len_count
    junc_count = inlet_ids.shape[0]
    forward, inverse = tables(cell_count, mode_count)
    blocks = spectral_blocks(spec_real, spec_imag)
    start = (lax.axis_index("len") * lax.axis_size("pipe") + lax.axis_index("pipe")) * per_dev
    my_inlets = lax.dynamic_slice_in_dim(inlet_ids, start, per_dev)
    my_outlets = lax.dynamic_slice_in_dim(outlet_ids, start, per_dev)
    junction_iota = lax.broadcasted_iota(jnp.int32, (per_dev, junc_count), 1)
    in_hot = (my_inlets[:, None] == junction_iota).astype(jnp.bfloat16)
    out_hot = (my_outlets[:, None] == junction_iota).astype(jnp.bfloat16)
    spectra = jnp.einsum("kl,plc->pkc", forward, inputs, preferred_element_type=jnp.float32).astype(
        jnp.bfloat16
    )
    mode_rows = to_modes(spectra.reshape(per_dev, mode_count, 2, channels))
    mode_rows = mode_rows.reshape(mode_rows.shape[0], -1, 2 * channels)
    mixed = jnp.einsum(
        "pmk,mkn->pmn", mode_rows, blocks, preferred_element_type=jnp.float32
    ).astype(jnp.bfloat16)
    returned_modes = from_modes(mixed.reshape(mixed.shape[0], -1, 2, channels)).reshape(
        per_dev, 2 * mode_count, channels
    )

    def forward_rows(summed_rows, carried):
        junc_act = (
            jnp.dot(
                summed_rows.astype(jnp.bfloat16), junc_weight, preferred_element_type=jnp.float32
            )
            + junc_bias
        )
        return (jax.nn.silu(junc_act).astype(jnp.bfloat16), junc_act)

    def backward_rows(summed_rows, carried):
        act_grad = (summed_rows * silu_slope(carried)).astype(jnp.bfloat16)
        return (
            jnp.dot(act_grad, junc_weight.T, preferred_element_type=jnp.float32).astype(
                jnp.bfloat16
            ),
            carried,
        )

    partial_value = jnp.dot(
        in_hot.T, inputs[:, 0, :], preferred_element_type=jnp.float32
    ) + jnp.dot(out_hot.T, inputs[:, -1, :], preferred_element_type=jnp.float32)
    junc_rows, junc_act = junction_pass(partial_value, forward_rows, None)
    cond = COUPLING * (
        jnp.dot(in_hot, junc_rows, preferred_element_type=jnp.float32)
        + jnp.dot(out_hot, junc_rows, preferred_element_type=jnp.float32)
    )
    spectral = jnp.einsum(
        "lk,pkc->plc", inverse, returned_modes, preferred_element_type=jnp.float32
    )
    pre = (spectral + cond[:, None, :]).astype(jnp.bfloat16)
    pointwise = jnp.dot(
        inputs.reshape(-1, channels), point_weight, preferred_element_type=jnp.float32
    ).reshape(inputs.shape)
    summed = pointwise + point_bias + pre.astype(jnp.float32)
    result, pullback = jax.vjp(activate, summed)
    outputs = result.astype(jnp.bfloat16)
    grad_total = pullback(cotangent.astype(jnp.float32))[0].astype(jnp.bfloat16)
    grad_spec = jnp.einsum(
        "lk,plc->pkc", inverse, grad_total, preferred_element_type=jnp.float32
    ).astype(jnp.bfloat16)
    grad_modes = to_modes(grad_spec.reshape(per_dev, mode_count, 2, channels))
    grad_modes = grad_modes.reshape(grad_modes.shape[0], -1, 2 * channels)
    grad_mixed = jnp.einsum(
        "pmn,mkn->pmk", grad_modes, blocks, preferred_element_type=jnp.float32
    ).astype(jnp.bfloat16)
    weight_terms = jnp.einsum(
        "pmk,pmn->mkn", mode_rows, grad_modes, preferred_element_type=jnp.float32
    )
    real_terms = weight_terms[:, :channels, :channels] + weight_terms[:, channels:, channels:]
    imag_terms = weight_terms[:, :channels, channels:] - weight_terms[:, channels:, :channels]
    grad_real, grad_imag = (
        lax.psum(real_terms.astype(jnp.bfloat16), "pipe").astype(jnp.float32),
        lax.psum(imag_terms.astype(jnp.bfloat16), "pipe").astype(jnp.float32),
    )
    grad_back = from_modes(grad_mixed.reshape(grad_mixed.shape[0], -1, 2, channels)).reshape(
        per_dev, 2 * mode_count, channels
    )
    grad_cells = jnp.einsum("kl,pkc->plc", forward, grad_back, preferred_element_type=jnp.float32)
    grad_cond = jnp.sum(grad_total, axis=1, dtype=jnp.float32)
    in_wide = in_hot.astype(jnp.float32)
    out_wide = out_hot.astype(jnp.float32)
    partial_grad = COUPLING * (
        jnp.dot(in_wide.T, grad_cond, precision=lax.Precision.HIGHEST)
        + jnp.dot(out_wide.T, grad_cond, precision=lax.Precision.HIGHEST)
    )
    sums_grad, unused = junction_pass(partial_grad, backward_rows, junc_act)
    end_first = jnp.dot(in_hot, sums_grad, preferred_element_type=jnp.float32)
    end_last = jnp.dot(out_hot, sums_grad, preferred_element_type=jnp.float32)
    grad_cells = grad_cells.at[:, 0, :].add(end_first).at[:, -1, :].add(end_last)
    spread = grad_cells.astype(jnp.bfloat16)
    grad_local = jnp.dot(
        grad_total.reshape(-1, channels), point_weight.T, preferred_element_type=jnp.float32
    ).reshape(inputs.shape)
    grad_inputs = (grad_local + spread.astype(jnp.float32)).astype(jnp.bfloat16)
    return (outputs, grad_inputs, grad_real, grad_imag)


def solution(mesh):
    placed = (
        P(("len", "pipe"), None, None),
        P(("len", "pipe"), None, None),
        P(),
        P(),
        P("len", None, None),
        P("len", None, None),
        P(),
        P(),
        P(),
        P(),
    )
    return jax.shard_map(
        body,
        mesh=mesh,
        in_specs=placed,
        out_specs=(
            P(("len", "pipe"), None, None),
            P(("len", "pipe"), None, None),
            P("len", None, None),
            P("len", None, None),
        ),
        check_vma=False,
    )
```

profile of v0, /device:TPU:0, one launch (start us, length us, event | category | flops | bytes accessed | tf_op | source)
XLA Modules:
  0.0 250.1 jit_solution(3287028381111833984)
XLA Ops:
  7.2 4.3 %negate_convert_fusion = (bf16[128,1,2048]{2,0,1:T(8,128)(2,1)S(1)}, bf16[128,1,2048]{2,0,1:T(8,128)(2,1)S(1)}) fusion(), kind=kLoop, calls=%fused_computation.58 | loop fusion | flops 4980736 | bytes 1048576 | tf_op jit(solution)/shard_map/convert.18
  11.6 1.1 copy.44
  14.4 7.3 %all-to-all-start = ((bf16[1,128,2,256]{3,2,0,1:T(2,128)(2,1)}), bf16[1,128,2,256]{3,2,0,1:T(2,128)(2,1)S(1)}, u32[]{:S(2)}, u32[]{:S(2)}) async-start(bf16[1,128,2,256]{3,2,0,1:T(2,128)(2,1)} %bitcast.5), calls=%async_computation | async-start | bytes 262144 | tf_op jit(solution)/shard_map/all_to_all | solution.py:49
  22.9 1.2 fusion.53
  24.2 40.9 %psum.28 = bf16[32,256]{1,0:T(8,128)(2,1)S(1)} all-reduce(f32[32,256]{1,0:T(8,128)S(1)} %multiply_add_fusion), channel_id=1, replica_groups=mesh['len'=8,'pipe'=4] {'len','pipe'}, use_global_device_ids=true, to_apply=%region_0.1 | all-reduce | flops 8192 | bytes 49152 | tf_op jit(solution)/shard_map/psum | solution.py:57
  65.1 4.4 %multiply_convert_fusion.1 = (bf16[128,1,2048]{2,0,1:T(8,128)(2,1)S(1)}, bf16[128,1,2048]{2,0,1:T(8,128)(2,1)S(1)}) fusion(f32[128]{0:T(128)S(1)} %negate_multiply_fusion, f32[128]{0:T(128)S(1)} %fusion.55), kind=kLoop, calls=%fused_computation.56 | loop fusion | flops 4718592 | bytes 1049600 | tf_op jit(solution)/shard_map/convert.16
  71.1 3.3 %neg.22 = bf16[16,256,256]{2,1,0:T(8,128)(2,1)} negate(bf16[16,256,256]{2,1,0:T(8,128)(2,1)} %param.19) | non-fusion elementwise | flops 1048576 | bytes 4194304 | tf_op jit(solution)/shard_map/neg | solution.py:35
  75.2 4.1 %fusion.22 = bf16[16,512,8]{1,2,0:T(8,128)(2,1)S(1)} fusion(bf16[16,256,256]{2,1,0:T(8,128)(2,1)} %param.18, bf16[16,256,256]{2,1,0:T(8,128)(2,1)} %neg.22, bf16[16,256,256]{2,1,0:T(8,128)(2,1)} %param.19, bf16[8,16,512]{2,1,0:T(8,128)(2,1)S(1)} %reshape.366), kind=kOutput, calls=%fused_computation.37 | convolution fusion | flops 100728832 | bytes 6553600 | tf_op jit(solution)/shard_map/pmk,mkn->pmn/dot_general | solution.py:90
  80.1 5.3 %all-to-all-start.1 = ((bf16[8,16,2,256]{3,2,1,0:T(2,128)(2,1)}), bf16[8,16,2,256]{3,2,1,0:T(2,128)(2,1)}, u32[]{:S(2)}, u32[]{:S(2)}) async-start(bf16[8,16,2,256]{3,2,1,0:T(2,128)(2,1)} %copy.47), calls=%async_computation.1 | async-start | bytes 262144 | tf_op jit(solution)/shard_map/all_to_all | solution.py:53
  85.4 1.2 convert_add_fusion
  86.6 1.1 copy.48
  88.2 4.7 %all-to-all-done.1 = bf16[8,16,2,256]{3,2,1,0:T(2,128)(2,1)} async-done(((bf16[8,16,2,256]{3,2,1,0:T(2,128)(2,1)}), bf16[8,16,2,256]{3,2,1,0:T(2,128)(2,1)}, u32[]{:S(2)}, u32[]{:S(2)}) %all-to-all-start.1) | async-done | bytes 131104 | tf_op jit(solution)/shard_map/all_to_all | solution.py:53
  92.9 1.0 reshape.368
  95.1 3.7 %convert_reduce_fusion = (f32[256]{0:T(256)S(1)}, bf16[1,2048,256]{2,1,0:T(8,128)(2,1)S(1)}, bf16[1,2048,256]{2,1,0:T(8,128)(2,1)}) fusion(bf16[1,2048,256]{2,1,0:T(8,128)(2,1)S(1)} %copy-done.7, f32[1,2048,256]{2,1,0:T(8,128)S(1)} %fusion.9, f32[256]{0:T(256)} %param.17, bf16[256,256]{1,0:T(8,128)(2,1)S(1)} %copy-done, bf16[1,2048,256]{2,1,0:T(8,128)(2,1)S(1)} %copy-done.6), kind=kOutput, calls=%fused_computation.32 | convolution fusion | flops 282590976 | bytes 6424576 | tf_op jit(solution)/shard_map/dot_general | solution.py:127
  98.7 1.0 copy-done.1
  100.9 3.4 %all-to-all-start.2 = ((bf16[1,128,2,256]{3,2,0,1:T(2,128)(2,1)}), bf16[1,128,2,256]{3,2,0,1:T(2,128)(2,1)S(1)}, u32[]{:S(2)}, u32[]{:S(2)}) async-start(bf16[1,128,2,256]{3,2,0,1:T(2,128)(2,1)} %bitcast.24), calls=%async_computation.2 | async-start | bytes 262144 | tf_op jit(solution)/shard_map/all_to_all | solution.py:49
  104.4 40.3 %psum.29 = f32[32,256]{1,0:T(8,128)S(1)} all-reduce(f32[32,256]{1,0:T(8,128)S(1)} %multiply_multiply_fusion.2), channel_id=1, replica_groups=mesh['len'=8,'pipe'=4] {'len','pipe'}, use_global_device_ids=true, to_apply=%region_2.3 | all-reduce | flops 8192 | bytes 65536 | tf_op jit(solution)/shard_map/psum | solution.py:57
  144.8 2.4 fusion.39
  147.2 3.0 %fusion = (bf16[16,256,256]{2,1,0:T(8,128)(2,1)}, bf16[16,256,256]{2,1,0:T(8,128)(2,1)}) fusion(f32[16,512,512]{2,1,0:T(8,128)S(1)} %fusion.39), kind=kLoop, calls=%fused_computation.2 | loop fusion | flops 4194304 | bytes 20971520 | tf_op jit(solution)/shard_map/convert_element_type | solution.py:149
  150.2 1.6 copy-done.4
  151.8 4.6 %fusion.23 = bf16[16,512,8]{1,2,0:T(8,128)(2,1)S(1)} fusion(bf16[16,256,256]{2,1,0:T(8,128)(2,1)} %param.18, bf16[16,256,256]{2,1,0:T(8,128)(2,1)} %neg.22, bf16[16,256,256]{2,1,0:T(8,128)(2,1)S(1)} %copy-done.4, bf16[8,16,512]{2,1,0:T(8,128)(2,1)S(1)} %reshape.376), kind=kOutput, calls=%fused_computation.38 | convolution fusion | flops 100728832 | bytes 6553600 | tf_op jit(solution)/shard_map/pmn,mkn->pmk/dot_general | solution.py:139
  157.2 5.3 %all-to-all-start.3 = ((bf16[8,16,2,256]{3,2,1,0:T(2,128)(2,1)}), bf16[8,16,2,256]{3,2,1,0:T(2,128)(2,1)S(1)}, u32[]{:S(2)}, u32[]{:S(2)}) async-start(bf16[8,16,2,256]{3,2,1,0:T(2,128)(2,1)} %copy.52), calls=%async_computation.3 | async-start | bytes 262144 | tf_op jit(solution)/shard_map/all_to_all | solution.py:53
  162.5 1.1 convolution_convert_fusion.2
  164.2 5.6 %all-to-all-done.3 = bf16[8,16,2,256]{3,2,1,0:T(2,128)(2,1)S(1)} async-done(((bf16[8,16,2,256]{3,2,1,0:T(2,128)(2,1)}), bf16[8,16,2,256]{3,2,1,0:T(2,128)(2,1)S(1)}, u32[]{:S(2)}, u32[]{:S(2)}) %all-to-all-start.3) | async-done | bytes 131104 | tf_op jit(solution)/shard_map/all_to_all | solution.py:53
  170.3 1.8 copy.53
  172.3 1.3 scatter-add.6
  173.6 1.4 fusion.26
  175.0 1.3 scatter-add.9
  176.3 3.1 %fusion.6 = bf16[1,2048,256]{2,1,0:T(8,128)(2,1)} fusion(bf16[256,256]{1,0:T(8,128)(2,1)S(1)} %copy-done, bf16[1,2048,256]{2,1,0:T(8,128)(2,1)S(1)} %copy-done.2, f32[1,2048,256]{2,1,0:T(8,128)} %scatter-add.9), kind=kOutput, calls=%fused_computation.16 | convolution fusion | flops 270532608 | bytes 4325376 | tf_op jit(solution)/shard_map/dot_general | solution.py:167
  179.4 57.1 %all-reduce.3.cloned.1.call-done = (bf16[16,256,256]{2,1,0:T(8,128)(2,1)}, bf16[16,256,256]{2,1,0:T(8,128)(2,1)}) async-done(((bf16[16,256,256]{2,1,0:T(8,128)(2,1)}, bf16[16,256,256]{2,1,0:T(8,128)(2,1)}), (bf16[16,256,256]{2,1,0:T(8,128)(2,1)}, bf16[16,256,256]{2,1,0:T(8,128)(2,1)})) %all-reduce.3.cloned.1.call-update) | async-done | bytes 4194320 | tf_op jit(solution)/shard_map/psum | solution.py:148
  236.5 4.2 %convert_element_type.168 = f32[16,256,256]{2,1,0:T(8,128)} convert(bf16[16,256,256]{2,1,0:T(8,128)(2,1)} %get-tuple-element.28) | non-fusion elementwise | flops 1048576 | bytes 6291456 | tf_op jit(solution)/shard_map/convert_element_type | solution.py:148
  240.7 2.5 convert_element_type.170
  (57 shorter events, 11.3 us)
Async XLA Ops:
  7.2 87.3 %copy-start = (bf16[256,256]{1,0:T(8,128)(2,1)S(1)}, bf16[256,256]{1,0:T(8,128)(2,1)}, u32[]{:S(2)}) copy-start(bf16[256,256]{1,0:T(8,128)(2,1)} %param.16) | copy-start | bytes 393220
  11.6 1.6 copy-start.5
  12.7 9.0 %copy-start.10 = (s32[32]{0:T(128)S(1)}, s32[32]{0:T(128)}, u32[]{:S(2)}) copy-start(s32[32]{0:T(128)} %param.23) | copy-start | bytes 388
  12.7 9.6 %copy-start.11 = (s32[32]{0:T(128)S(1)}, s32[32]{0:T(128)}, u32[]{:S(2)}) copy-start(s32[32]{0:T(128)} %param.22) | copy-start | bytes 388
  13.7 55.9 %copy-start.8 = (bf16[256,256]{1,0:T(8,128)(2,1)S(1)}, bf16[256,256]{1,0:T(8,128)(2,1)}, u32[]{:S(2)}) copy-start(bf16[256,256]{1,0:T(8,128)(2,1)} %param.20) | copy-start | bytes 393220
  13.7 55.9 %copy-start.9 = (f32[256]{0:T(256)S(1)}, f32[256]{0:T(256)}, u32[]{:S(2)}) copy-start(f32[256]{0:T(256)} %param.21) | copy-start | bytes 3076
  14.4 60.7 %all-to-all-start = ((bf16[1,128,2,256]{3,2,0,1:T(2,128)(2,1)}), bf16[1,128,2,256]{3,2,0,1:T(2,128)(2,1)S(1)}, u32[]{:S(2)}, u32[]{:S(2)}) async-start(bf16[1,128,2,256]{3,2,0,1:T(2,128)(2,1)} %bitcast.5), calls=%async_computation | async-start | bytes 262144 | tf_op jit(solution)/shard_map/all_to_all | solution.py:49
  80.1 12.8 %all-to-all-start.1 = ((bf16[8,16,2,256]{3,2,1,0:T(2,128)(2,1)}), bf16[8,16,2,256]{3,2,1,0:T(2,128)(2,1)}, u32[]{:S(2)}, u32[]{:S(2)}) async-start(bf16[8,16,2,256]{3,2,1,0:T(2,128)(2,1)} %copy.47), calls=%async_computation.1 | async-start | bytes 262144 | tf_op jit(solution)/shard_map/all_to_all | solution.py:53
  88.2 6.3 %copy-start.6 = (bf16[1,2048,256]{2,1,0:T(8,128)(2,1)S(1)}, bf16[1,2048,256]{2,1,0:T(8,128)(2,1)}, u32[]{:S(2)}) copy-start(bf16[1,2048,256]{2,1,0:T(8,128)(2,1)} %param.14) | copy-start | bytes 3145732
  93.8 1.2 copy-start.7
  98.7 1.0 copy-start.1
  100.9 43.8 %all-to-all-start.2 = ((bf16[1,128,2,256]{3,2,0,1:T(2,128)(2,1)}), bf16[1,128,2,256]{3,2,0,1:T(2,128)(2,1)S(1)}, u32[]{:S(2)}, u32[]{:S(2)}) async-start(bf16[1,128,2,256]{3,2,0,1:T(2,128)(2,1)} %bitcast.24), calls=%async_computation.2 | async-start | bytes 262144 | tf_op jit(solution)/shard_map/all_to_all | solution.py:49
  104.3 132.3 %all-reduce.3.cloned.1.call-start = ((), (), s32[]{:S(2)}) async-start(), calls=%async_computation.4 | async-start | bytes 8388608 | tf_op jit(solution)/shard_map/psum | solution.py:148
  150.2 1.6 copy-start.4
  151.8 10.6 %copy-start.12 = (f32[32,256]{1,0:T(8,128)S(1)}, f32[32,256]{1,0:T(8,128)}, u32[]{:S(2)}) copy-start(f32[32,256]{1,0:T(8,128)} %get-tuple-element.38) | copy-start | bytes 98308
  157.2 12.6 %all-to-all-start.3 = ((bf16[8,16,2,256]{3,2,1,0:T(2,128)(2,1)}), bf16[8,16,2,256]{3,2,1,0:T(2,128)(2,1)S(1)}, u32[]{:S(2)}, u32[]{:S(2)}) async-start(bf16[8,16,2,256]{3,2,1,0:T(2,128)(2,1)} %copy.52), calls=%async_computation.3 | async-start | bytes 262144 | tf_op jit(solution)/shard_map/all_to_all | solution.py:53
  170.3 6.0 %copy-start.2 = (bf16[1,2048,256]{2,1,0:T(8,128)(2,1)S(1)}, bf16[1,2048,256]{2,1,0:T(8,128)(2,1)}, u32[]{:S(2)}) copy-start(bf16[1,2048,256]{2,1,0:T(8,128)(2,1)} %copy-done.1) | copy-start | bytes 3145732
  236.5 4.2 %copy-start.3 = (bf16[16,256,256]{2,1,0:T(8,128)(2,1)S(1)}, bf16[16,256,256]{2,1,0:T(8,128)(2,1)}, u32[]{:S(2)}) copy-start(bf16[16,256,256]{2,1,0:T(8,128)(2,1)} %get-tuple-element.29) | copy-start | bytes 6291460
Sparse Core Ops, SparseCore 0:
  150.4 86.1 all-reduce.2
where the time goes:
time: 251 us; the launch traced here: 250 us
  blocking collectives  81.2 us (32%)
  waiting for transfers between devices  67.4 us (27%)
  matrix products  25.1 us (10%)
  other arithmetic  24.5 us (10%)
  starting transfers between devices  21.3 us (8%)
  local copies, waits for them, and re-layouts  16.2 us (6%)
  between operations  14.4 us (6%)
    psum x2, blocking collectives, junction_pass(): summed_rows = lax.psum(partial_value, ('len', 'pipe'))  81.2 us
    psum x1, waiting for transfers between devices, body(): lax.psum(real_terms.astype(jnp.bfloat16), 'pipe').astype(jnp.float32)  57.1 us
    all_to_all x2, starting transfers between devices, to_modes(): return lax.all_to_all(field, 'len', split_axis=1, concat_axis=0, tiled=True)  10.7 us
    all_to_all x2, starting transfers between devices, from_modes(): return lax.all_to_all(field, 'len', split_axis=0, concat_axis=1, tiled=True)  10.6 us
    all_to_all x2, waiting for transfers between devices, from_modes(): return lax.all_to_all(field, 'len', split_axis=0, concat_axis=1, tiled=True)  10.2 us
    another operation x4, other arithmetic  9.89 us
  transfers between devices with their start and end apart: 5, of which 3 were waited for; matrix products, arithmetic and copies ran while one was open for 13% of the time, Pallas kernels for 0%

commit v1 on v0

v1 whole, which is shorter than its diff:
```python
import functools
import math

import jax
import jax.numpy as jnp
import ml_dtypes
import numpy as np
from jax import lax
from jax.experimental import pallas as pl
from jax.experimental.pallas import tpu as pltpu
from jax.sharding import PartitionSpec as P

COUPLING = 0.125
TILE = 256
LANES = 128
GELU_S = math.sqrt(2.0 / math.pi)
GELU_C = 0.044715
VMEM = pl.BlockSpec(memory_space=pltpu.VMEM)
SMEM = pl.BlockSpec(memory_space=pltpu.SMEM)


def forward_table(cell_count, mode_count, groups):
    product_index = np.arange(mode_count)[:, None] * np.arange(cell_count)[None, :] % cell_count
    angles = product_index.astype(np.float32) * np.float32(2.0 * math.pi / cell_count)
    norm_scale = np.float32(1.0 / math.sqrt(cell_count))
    cosine = (np.cos(angles) * norm_scale).reshape(groups, -1, cell_count)
    sine = (np.sin(angles) * norm_scale).reshape(groups, -1, cell_count)
    table = np.concatenate([cosine, -sine], axis=1).reshape(2 * mode_count, cell_count)
    return table.astype(ml_dtypes.bfloat16)


def dot(left, right, left_dim=1, right_dim=0):
    return lax.dot_general(
        left,
        right,
        (((left_dim,), (right_dim,)), ((), ())),
        preferred_element_type=jnp.float32,
    )


def put(ref, at, value):
    for lane in range(ref.shape[0]):
        ref[lane, at, :] = value[:, lane * LANES : (lane + 1) * LANES]


def take(ref, at):
    return jnp.concatenate([ref[lane, at, :] for lane in range(ref.shape[0])], axis=1)


def spectrum_kernel(groups, x_ref, f_ref, msg_ref):
    span = f_ref.shape[0] // groups
    cells = x_ref.shape[0]
    spectra = dot(f_ref[...], x_ref[...]).astype(jnp.bfloat16)
    ends = jnp.concatenate([x_ref[0:1, :], x_ref[cells - 1 : cells, :]], axis=0)
    for owner in range(groups):
        msg_ref[owner, 0:span, :] = spectra[owner * span : (owner + 1) * span]
        msg_ref[owner, span : span + 2, :] = ends


def mix_kernel(backward, r_ref, real_ref, imag_ref, out_ref, x_ref, y_ref):
    groups = r_ref.shape[0]
    modes = real_ref.shape[0]
    span = 2 * modes
    for source in range(groups):
        put(x_ref, pl.ds(source * span, span), r_ref[source, 0:span, :].astype(jnp.float32))
    for mode in range(modes):
        first = pl.ds(mode, groups, stride=span)
        second = pl.ds(modes + mode, groups, stride=span)
        rows = jnp.concatenate([take(x_ref, first), take(x_ref, second)], axis=0).astype(jnp.bfloat16)
        dim = 1 if backward else 0
        by_real = dot(rows, real_ref[mode], 1, dim)
        by_imag = dot(rows, imag_ref[mode], 1, dim)
        if backward:
            put(y_ref, first, by_real[:groups] + by_imag[groups:])
            put(y_ref, second, by_real[groups:] - by_imag[:groups])
        else:
            put(y_ref, first, by_real[:groups] - by_imag[groups:])
            put(y_ref, second, by_imag[:groups] + by_real[groups:])
    for source in range(groups):
        out_ref[source] = take(y_ref, pl.ds(source * span, span)).astype(jnp.bfloat16)


def junction_forward_kernel(pipes, *refs):
    msgs, (inlet_ref, outlet_ref, where_ref, weight_ref, bias_ref, cond_ref, slope_ref) = (
        refs[:pipes],
        refs[pipes:],
    )
    groups, rows = msgs[0].shape[0], msgs[0].shape[1]
    channels = msgs[0].shape[2]
    me, column = where_ref[0], where_ref[1]
    own_in, own_out = inlet_ref[me], outlet_ref[me]
    is_first = lax.broadcasted_iota(jnp.int32, (2, channels), 0) == 0

    def matches(pipe, junction):
        first = (inlet_ref[pipe] == junction).astype(jnp.float32)
        last = (outlet_ref[pipe] == junction).astype(jnp.float32)
        return jnp.where(is_first, first, last)

    totals = (jnp.zeros((2, channels), jnp.float32),) * 2
    for step in range(pipes):
        source = lax.rem(column + step, pipes)

        def add(group, carried, step=step, source=source):
            pipe = group * pipes + source
            ends = msgs[step][group, rows - 2 : rows, :].astype(jnp.float32)
            return (
                carried[0] + ends * matches(pipe, own_in),
                carried[1] + ends * matches(pipe, own_out),
            )

        totals = lax.fori_loop(0, groups, add, totals, unroll=min(groups, 8))
    sums = jnp.concatenate(
        [
            jnp.sum(totals[0], axis=0, keepdims=True),
            jnp.sum(totals[1], axis=0, keepdims=True),
            jnp.zeros((6, channels), jnp.float32),
        ],
        axis=0,
    )
    act = dot(sums.astype(jnp.bfloat16), weight_ref[...]) + bias_ref[...]
    sigmoid_part = jax.nn.sigmoid(act)
    junc_rows = (act * sigmoid_part).astype(jnp.bfloat16).astype(jnp.float32)
    cond_ref[...] = COUPLING * (junc_rows[0:1] + junc_rows[1:2])
    slope_ref[...] = sigmoid_part * (1.0 + act * (1.0 - sigmoid_part))


def junction_backward_kernel(pipes, *refs):
    msgs, (inlet_ref, outlet_ref, where_ref, weight_ref, slope_ref, rows_ref) = (
        refs[:pipes],
        refs[pipes:],
    )
    groups, rows = msgs[0].shape[0], msgs[0].shape[1]
    channels = msgs[0].shape[2]
    me, column = where_ref[0], where_ref[1]
    own_in, own_out = inlet_ref[me], outlet_ref[me]

    def matches(pipe, junction):
        return (inlet_ref[pipe] == junction).astype(jnp.float32) + (
            outlet_ref[pipe] == junction
        ).astype(jnp.float32)

    totals = (jnp.zeros((2, channels), jnp.float32),) * 2
    for step in range(pipes):
        source = lax.rem(column + step, pipes)

        def add(group, carried, step=step, source=source):
            pipe = group * pipes + source
            parts = msgs[step][group, rows - 2 : rows, :].astype(jnp.float32)
            return (
                carried[0] + parts * matches(pipe, own_in),
                carried[1] + parts * matches(pipe, own_out),
            )

        totals = lax.fori_loop(0, groups, add, totals, unroll=min(groups, 8))
    junc_grad = COUPLING * jnp.concatenate(
        [
            jnp.sum(totals[0], axis=0, keepdims=True),
            jnp.sum(totals[1], axis=0, keepdims=True),
            jnp.zeros((6, channels), jnp.float32),
        ],
        axis=0,
    )
    act_grad = (junc_grad * slope_ref[...]).astype(jnp.bfloat16)
    sums_grad = dot(act_grad, weight_ref[...], 1, 1).astype(jnp.bfloat16)
    rows_ref[...] = sums_grad.astype(jnp.float32)


def layer_kernel(
    groups,
    x_ref,
    cot_ref,
    weight_ref,
    bias_ref,
    modes_ref,
    cond_ref,
    f_ref,
    ft_ref,
    out_ref,
    total_ref,
    msg_ref,
    acc_ref,
):
    cells, channels = x_ref.shape
    all_rows = f_ref.shape[0]
    span = all_rows // groups
    row = lax.broadcasted_iota(jnp.int32, (all_rows, channels), 0)
    doubled = jnp.where((row == 0) | (row == span // 2), 1.0, 2.0).astype(jnp.float32)
    modes = (modes_ref[...].astype(jnp.float32) * doubled).astype(jnp.bfloat16)
    weight = weight_ref[...]
    cond = cond_ref[...]
    bias = bias_ref[...]
    for tile in range(cells // TILE):
        at = pl.ds(tile * TILE, TILE)
        spectral = dot(ft_ref[at, :], modes)
        pre = (spectral + cond).astype(jnp.bfloat16).astype(jnp.float32)
        summed = dot(x_ref[at, :], weight) + bias + pre
        square = summed * summed
        half = 0.5 + 0.5 * jnp.tanh(summed * (GELU_S + (GELU_S * GELU_C) * square))
        result = summed * half
        out_ref[at, :] = result.astype(jnp.bfloat16)
        slope = half + result * (1.0 - half) * (2.0 * GELU_S + (6.0 * GELU_S * GELU_C) * square)
        total = (cot_ref[at, :].astype(jnp.float32) * slope).astype(jnp.bfloat16)
        total_ref[at, :] = total
        part = dot(f_ref[:, at], total)
        if tile == 0:
            acc_ref[...] = part
        else:
            acc_ref[...] += part
    grad_cond = acc_ref[0:1, :] * (1.0 / f_ref[0:1, 0:1].astype(jnp.float32))
    high = grad_cond.astype(jnp.bfloat16)
    low = (grad_cond - high.astype(jnp.float32)).astype(jnp.bfloat16)
    extra = jnp.concatenate([high, low], axis=0)
    grad_spec = (acc_ref[...] * doubled).astype(jnp.bfloat16)
    for owner in range(groups):
        msg_ref[owner, 0:span, :] = grad_spec[owner * span : (owner + 1) * span]
        msg_ref[owner, span : span + 2, :] = extra


def local_grad_kernel(total_ref, weight_ref, out_ref):
    out_ref[...] = dot(total_ref[...], weight_ref[...], 1, 1)


def input_grad_kernel(modes_ref, ft_ref, local_ref, rows_ref, out_ref):
    cells, channels = out_ref.shape
    modes = modes_ref[...]
    row = lax.broadcasted_iota(jnp.int32, (TILE, channels), 0)
    tiles = cells // TILE
    for tile in range(tiles):
        at = pl.ds(tile * TILE, TILE)
        grad_cells = dot(ft_ref[at, :], modes)
        if tile == 0:
            grad_cells = grad_cells + jnp.where(row == 0, rows_ref[0:1, :], 0.0)
        if tile == tiles - 1:
            grad_cells = grad_cells + jnp.where(row == TILE - 1, rows_ref[1:2, :], 0.0)
        spread = grad_cells.astype(jnp.bfloat16).astype(jnp.float32)
        out_ref[at, :] = (local_ref[at, :] + spread).astype(jnp.bfloat16)


def weight_grad_kernel(pipes, per_step, modes, *refs):
    fields, grads = refs[:pipes], refs[pipes : 2 * pipes]
    real_ref, imag_ref, x_ref, g_ref = refs[2 * pipes :]
    groups = fields[0].shape[0]
    span = 2 * modes

    @pl.when(pl.program_id(0) == 0)
    def _():
        for step in range(pipes):
            for source in range(groups):
                at = pl.ds((step * groups + source) * span, span)
                put(x_ref, at, fields[step][source, 0:span, :].astype(jnp.float32))
                put(g_ref, at, grads[step][source, 0:span, :].astype(jnp.float32))

    count = pipes * groups
    for offset in range(per_step):
        mode = pl.program_id(0) * per_step + offset
        first = pl.ds(mode, count, stride=span)
        second = pl.ds(modes + mode, count, stride=span)
        a, b = take(x_ref, first), take(x_ref, second)
        u, v = take(g_ref, first), take(g_ref, second)
        left = jnp.concatenate([a, b], axis=0).astype(jnp.bfloat16)
        real_ref[offset] = dot(left, jnp.concatenate([u, v], axis=0).astype(jnp.bfloat16), 0, 0)
        imag_ref[offset] = dot(left, jnp.concatenate([v, -u], axis=0).astype(jnp.bfloat16), 0, 0)


def rows_of(count, channels):
    return pltpu.VMEM((channels // LANES, count, LANES), jnp.float32)


def call(kernel, outs, specs, scratch=(), out_specs=None, name=None):
    return pl.pallas_call(
        kernel,
        out_shape=outs,
        in_specs=specs,
        out_specs=out_specs if out_specs is not None else [VMEM] * len(outs),
        scratch_shapes=list(scratch),
        compiler_params=pltpu.CompilerParams(vmem_limit_bytes=16 * 1024 * 1024),
        name=name,
    )


def body(
    inputs,
    cotangent,
    point_weight,
    point_bias,
    spec_real,
    spec_imag,
    junc_weight,
    junc_bias,
    inlet_ids,
    outlet_ids,
):
    per_dev, cell_count, channels = inputs.shape
    assert per_dev == 1
    groups, pipes = lax.axis_size("len"), lax.axis_size("pipe")
    modes = spec_real.shape[0]
    span = 2 * modes
    table = forward_table(cell_count, modes * groups, groups)
    f_table = jnp.asarray(table)
    ft_table = jnp.asarray(np.ascontiguousarray(table.T))
    column = lax.axis_index("pipe")
    where = jnp.stack([lax.axis_index("len") * pipes + column, column]).astype(jnp.int32)
    field = inputs.reshape(cell_count, channels)
    cot = cotangent.reshape(cell_count, channels)
    bias_row = point_bias.reshape(1, channels)
    junc_bias_row = junc_bias.reshape(1, channels)
    shape = jax.ShapeDtypeStruct
    message = shape((groups, span + 2, channels), jnp.bfloat16)
    chunk = shape((groups, span, channels), jnp.bfloat16)

    def exchange(value):
        return lax.all_to_all(value, "len", split_axis=0, concat_axis=0, tiled=True)

    def gather(value):
        return [value] + [
            lax.ppermute(value, "pipe", [(i, (i - step) % pipes) for i in range(pipes)])
            for step in range(1, pipes)
        ]

    def mix(backward, value):
        return call(
            functools.partial(mix_kernel, backward),
            [chunk],
            [VMEM] * 3,
            [rows_of(groups * span, channels)] * 2,
            name="mix_grad" if backward else "mix",
        )(value, spec_real, spec_imag)[0]

    (sent,) = call(
        functools.partial(spectrum_kernel, groups), [message], [VMEM] * 2, name="spectrum"
    )(field, f_table)
    received = exchange(sent)
    fields = gather(received)
    returned = exchange(mix(False, received)).reshape(groups * span, channels)
    cond, slope = call(
        functools.partial(junction_forward_kernel, pipes),
        [shape((1, channels), jnp.float32), shape((8, channels), jnp.float32)],
        [VMEM] * pipes + [SMEM] * 3 + [VMEM] * 2,
        name="junction",
    )(*fields, inlet_ids, outlet_ids, where, junc_weight, junc_bias_row)
    outputs, total, sent = call(
        functools.partial(layer_kernel, groups),
        [shape(field.shape, jnp.bfloat16), shape(field.shape, jnp.bfloat16), message],
        [VMEM] * 8,
        [pltpu.VMEM((groups * span, channels), jnp.float32)],
        name="layer",
    )(field, cot, point_weight, bias_row, returned, cond, f_table, ft_table)
    received = exchange(sent)
    grads = gather(received)
    returned = exchange(mix(True, received)).reshape(groups * span, channels)
    (local,) = call(
        local_grad_kernel, [shape(field.shape, jnp.float32)], [VMEM] * 2, name="local_grad"
    )(total, point_weight)
    (rows,) = call(
        functools.partial(junction_backward_kernel, pipes),
        [shape((8, channels), jnp.float32)],
        [VMEM] * pipes + [SMEM] * 3 + [VMEM] * 2,
        name="junction_grad",
    )(*grads, inlet_ids, outlet_ids, where, junc_weight, slope)
    per_step = math.gcd(modes, 4)
    big = shape((modes, channels, channels), jnp.float32)
    whole = pl.BlockSpec(message.shape, lambda i: (0, 0, 0))
    part = pl.BlockSpec((per_step, channels, channels), lambda i: (i, 0, 0))
    grad_real, grad_imag = pl.pallas_call(
        functools.partial(weight_grad_kernel, pipes, per_step, modes),
        grid=(modes // per_step,),
        out_shape=[big, big],
        in_specs=[whole] * (2 * pipes),
        out_specs=[part, part],
        scratch_shapes=[rows_of(pipes * groups * span, channels)] * 2,
        compiler_params=pltpu.CompilerParams(vmem_limit_bytes=24 * 1024 * 1024),
        name="weight_grad",
    )(*fields, *grads)
    (grad_inputs,) = call(
        input_grad_kernel, [shape(field.shape, jnp.bfloat16)], [VMEM] * 4, name="input_grad"
    )(returned, ft_table, local, rows)
    return (
        outputs.reshape(inputs.shape),
        grad_inputs.reshape(inputs.shape),
        grad_real,
        grad_imag,
    )


def solution(mesh):
    placed = (
        P(("len", "pipe"), None, None),
        P(("len", "pipe"), None, None),
        P(),
        P(),
        P("len", None, None),
        P("len", None, None),
        P(),
        P(),
        P(),
        P(),
    )
    return jax.shard_map(
        body,
        mesh=mesh,
        in_specs=placed,
        out_specs=(
            P(("len", "pipe"), None, None),
            P(("len", "pipe"), None, None),
            P("len", None, None),
            P("len", None, None),
        ),
        check_vma=False,
    )
```

time: 251 us -> 86.7 us (0.35)
  the two profiles are of different devices: /device:TPU:0 before, /device:TPU:1 now
where the time goes in v1:
time: 86.7 us; the launch traced here: 86 us
  blocking collectives  25.2 us (29%)
  Pallas kernels  18.8 us (22%)
  starting transfers between devices  14.4 us (17%)
  local copies, waits for them, and re-layouts  13.7 us (16%)
  waiting for transfers between devices  13.1 us (15%)
    all_to_all x2, blocking collectives, exchange(): return lax.all_to_all(value, 'len', split_axis=0, concat_axis=0, tiled=True)  25.2 us
    unnamed x44, local copies, waits for them, and re-layouts  13.7 us
    ppermute x6, waiting for transfers between devices, gather(): lax.ppermute(value, 'pipe', [(i, (i - step) % pipes) for i in range(pipes)])  13.1 us
    all_to_all x2, starting transfers between devices, exchange(): return lax.all_to_all(value, 'len', split_axis=0, concat_axis=0, tiled=True)  8 us
    ppermute x6, starting transfers between devices, gather(): lax.ppermute(value, 'pipe', [(i, (i - step) % pipes) for i in range(pipes)])  6.36 us
    pallas_call x1, Pallas kernels, body(): pl.pallas_call(functools.partial(weight_grad_kernel, pipes, per_step, mod...  5.58 us
    pallas_call x1, Pallas kernels, body(): call(functools.partial(layer_kernel, groups), [shape(field.shape, jnp.bfl...  4.39 us
    pallas_call x2, Pallas kernels, mix(): call(functools.partial(mix_kernel, backward), [chunk], [VMEM] * 3, [rows_...  3.33 us
  transfers between devices with their start and end apart: 8, of which 5 were waited for; matrix products, arithmetic and copies ran while one was open for 0% of the time, Pallas kernels for 10%

profile of v1, /device:TPU:1, one launch (start us, length us, event | category | flops | bytes accessed | tf_op | source)
XLA Modules:
  0.0 86.0 jit_solution(18367996351338512146)
XLA Ops:
  0.7 1.4 %copy-done.3 = bf16[1,2048,256]{2,1,0:T(8,128)(2,1)S(1)} copy-done((bf16[1,2048,256]{2,1,0:T(8,128)(2,1)S(1)}, bf16[1,2048,256]{2,1,0:T(8,128)(2,1)}, u32[]{:S(2)}) %copy-start.3) | copy-done | bytes 1048600
  2.0 1.2 %copy-done.5 = bf16[256,2048]{1,0:T(8,128)(2,1)S(1)} copy-done((bf16[256,2048]{1,0:T(8,128)(2,1)S(1)}, bf16[256,2048]{1,0:T(8,128)(2,1)}, u32[]{:S(2)}) %copy-start.5) | copy-done | bytes 1048600
  3.7 12.6 %all_to_all.20.r_ref.refs_0_ = bf16[8,34,256]{2,1,0:T(8,128)(2,1)S(1)} all-to-all(bf16[8,34,256]{2,1,0:T(8,128)(2,1)S(1)} %spectrum.1), channel_id=1, replica_groups=mesh['len'=8,'pipe'=4] {'len'}, dimensions={0} | all-to-all | bytes 278528 | tf_op jit(solution)/shard_map/all_to_all | solution.py:312
  16.3 1.6 %copy-done.1 = bf16[16,256,256]{2,1,0:T(8,128)(2,1)S(1)} copy-done((bf16[16,256,256]{2,1,0:T(8,128)(2,1)S(1)}, bf16[16,256,256]{2,1,0:T(8,128)(2,1)}, u32[]{:S(2)}) %copy-start.1) | copy-done | bytes 2097176
  17.9 1.4 %mix.1 = bf16[8,32,256]{2,1,0:T(8,128)(2,1)} custom-call(bf16[8,34,256]{2,1,0:T(8,128)(2,1)S(1)} %all_to_all.20.r_ref.refs_0_, bf16[16,256,256]{2,1,0:T(8,128)(2,1)S(1)} %copy-done, bf16[16,256,256]{2,1,0:T(8,128)(2,1)S(1)} %copy-done.1), custom_call_target="tpu_custom_call" | custom-call | tf_op jit(solution)/shard_map/mix/pallas_call | solution.py:321
  19.3 4.0 %all-to-all-start.1 = ((bf16[8,32,256]{2,1,0:T(8,128)(2,1)}), bf16[8,32,256]{2,1,0:T(8,128)(2,1)}, u32[]{:S(2)}, u32[]{:S(2)}) async-start(bf16[8,32,256]{2,1,0:T(8,128)(2,1)} %mix.1), calls=%async_computation.1 | async-start | bytes 262144 | tf_op jit(solution)/shard_map/all_to_all | solution.py:312
  23.3 3.2 %collective-permute-start.2 = (bf16[8,34,256]{2,1,0:T(8,128)(2,1)S(1)}, bf16[8,34,256]{2,1,0:T(8,128)(2,1)S(1)}, u32[]{:S(2)}, u32[]{:S(2)}) collective-permute-start(bf16[8,34,256]{2,1,0:T(8,128)(2,1)S(1)} %all_to_all.20.r_ref.refs_0_), channel_id=1, source_target_pairs={{0,1},{1,2},{2,3},{3,0},{4,5},{5,6},{6,7},{7,4},{8,9},{9,10},{10,1... | collective-permute-start | bytes 417800 | tf_op jit(solution)/shard_map/ppermute | solution.py:316
  27.1 2.9 %collective-permute-done.2.refs_3_ = bf16[8,34,256]{2,1,0:T(8,128)(2,1)S(1)} collective-permute-done((bf16[8,34,256]{2,1,0:T(8,128)(2,1)S(1)}, bf16[8,34,256]{2,1,0:T(8,128)(2,1)S(1)}, u32[]{:S(2)}, u32[]{:S(2)}) %collective-permute-start.2) | collective-permute-done | bytes 139296 | tf_op jit(solution)/shard_map/ppermute | solution.py:316
  30.0 4.3 %collective-permute-done.1.refs_2_ = bf16[8,34,256]{2,1,0:T(8,128)(2,1)} collective-permute-done((bf16[8,34,256]{2,1,0:T(8,128)(2,1)S(1)}, bf16[8,34,256]{2,1,0:T(8,128)(2,1)}, u32[]{:S(2)}, u32[]{:S(2)}) %collective-permute-start.1) | collective-permute-done | bytes 139296 | tf_op jit(solution)/shard_map/ppermute | solution.py:316
  34.3 0.6 collective-permute-done.refs_1_
  34.9 0.9 %copy-done.16 = bf16[256,256]{1,0:T(8,128)(2,1)S(1)} copy-done((bf16[256,256]{1,0:T(8,128)(2,1)S(1)}, bf16[256,256]{1,0:T(8,128)(2,1)}, u32[]{:S(2)}) %copy-start.16) | copy-done | bytes 131096
  35.8 1.4 %junction.1 = (f32[1,256]{1,0:T(1,128)S(1)}, f32[8,256]{1,0:T(8,128)S(1)}) custom-call(bf16[8,34,256]{2,1,0:T(8,128)(2,1)S(1)} %all_to_all.20.r_ref.refs_0_, bf16[8,34,256]{2,1,0:T(8,128)(2,1)} %collective-permute-done.refs_1_, bf16[8,34,256]{2,1,0:T(8,128)(2,1)} %collective-permute-done.1.refs_2_, bf16[8,34,256]{2,1,0:T(8,128)(2,1)S(1)} %collective-permute-done.2.refs_3_, ...), custom_call_target="tpu_custom_call" | custom-call | tf_op jit(solution)/shard_map/junction/pallas_call | solution.py:335
  37.2 1.2 %copy-done.6 = bf16[256,2048]{1,0:T(8,128)(2,1)S(1)} copy-done((bf16[256,2048]{1,0:T(8,128)(2,1)S(1)}, bf16[256,2048]{1,0:T(8,128)(2,1)}, u32[]{:S(2)}) %copy-start.6) | copy-done | bytes 1048600
  38.4 1.2 %copy-done.7 = bf16[2048,256]{1,0:T(8,128)(2,1)S(1)} copy-done((bf16[2048,256]{1,0:T(8,128)(2,1)S(1)}, bf16[2048,256]{1,0:T(8,128)(2,1)}, u32[]{:S(2)}) %copy-start.7) | copy-done | bytes 1048600
  39.6 1.2 %copy-done.11 = bf16[1,2048,256]{2,1,0:T(8,128)(2,1)S(1)} copy-done((bf16[1,2048,256]{2,1,0:T(8,128)(2,1)S(1)}, bf16[1,2048,256]{2,1,0:T(8,128)(2,1)}, u32[]{:S(2)}) %copy-start.11) | copy-done | bytes 1048600
  40.9 0.9 %copy-done.14 = bf16[256,256]{1,0:T(8,128)(2,1)S(1)} copy-done((bf16[256,256]{1,0:T(8,128)(2,1)S(1)}, bf16[256,256]{1,0:T(8,128)(2,1)}, u32[]{:S(2)}) %copy-start.14) | copy-done | bytes 131096
  41.8 4.4 %layer.1 = (bf16[2048,256]{1,0:T(8,128)(2,1)}, bf16[2048,256]{1,0:T(8,128)(2,1)S(1)}, bf16[8,34,256]{2,1,0:T(8,128)(2,1)S(1)}) custom-call(bf16[2048,256]{1,0:T(8,128)(2,1)S(1)} %bitcast.11, bf16[2048,256]{1,0:T(8,128)(2,1)S(1)} %bitcast.12, bf16[256,256]{1,0:T(8,128)(2,1)S(1)} %copy-done.14, f32[1,256]{1,0:T(1,128)S(1)} %bitcast.14, ...), custom_call_target="tpu_custom_call" | custom-call | tf_op jit(solution)/shard_map/layer/pallas_call | solution.py:341
  46.2 1.0 %copy-done.9 = bf16[2048,256]{1,0:T(8,128)(2,1)} copy-done((bf16[2048,256]{1,0:T(8,128)(2,1)}, bf16[2048,256]{1,0:T(8,128)(2,1)S(1)}, u32[]{:S(2)}) %copy-start.9) | copy-done | bytes 1048600
  47.1 12.5 %all_to_all.21.r_ref.refs_0_.refs_4_ = bf16[8,34,256]{2,1,0:T(8,128)(2,1)S(1)} all-to-all(bf16[8,34,256]{2,1,0:T(8,128)(2,1)S(1)} %get-tuple-element.13), channel_id=1, replica_groups=mesh['len'=8,'pipe'=4] {'len'}, dimensions={0} | all-to-all | bytes 278528 | tf_op jit(solution)/shard_map/all_to_all | solution.py:312
  59.7 2.0 %mix_grad.1 = bf16[8,32,256]{2,1,0:T(8,128)(2,1)} custom-call(bf16[8,34,256]{2,1,0:T(8,128)(2,1)S(1)} %all_to_all.21.r_ref.refs_0_.refs_4_, bf16[16,256,256]{2,1,0:T(8,128)(2,1)S(1)} %copy-done, bf16[16,256,256]{2,1,0:T(8,128)(2,1)S(1)} %copy-done.2), custom_call_target="tpu_custom_call" | custom-call | tf_op jit(solution)/shard_map/mix_grad/pallas_call | solution.py:321
  61.6 4.0 %all-to-all-start.3 = ((bf16[8,32,256]{2,1,0:T(8,128)(2,1)}), bf16[8,32,256]{2,1,0:T(8,128)(2,1)}, u32[]{:S(2)}, u32[]{:S(2)}) async-start(bf16[8,32,256]{2,1,0:T(8,128)(2,1)} %mix_grad.1), calls=%async_computation.3 | async-start | bytes 262144 | tf_op jit(solution)/shard_map/all_to_all | solution.py:312
  65.6 1.0 %collective-permute-start.5 = (bf16[8,34,256]{2,1,0:T(8,128)(2,1)S(1)}, bf16[8,34,256]{2,1,0:T(8,128)(2,1)S(1)}, u32[]{:S(2)}, u32[]{:S(2)}) collective-permute-start(bf16[8,34,256]{2,1,0:T(8,128)(2,1)S(1)} %all_to_all.21.r_ref.refs_0_.refs_4_), channel_id=1, source_target_pairs={{0,1},{1,2},{2,3},{3,0},{4,5},{5,6},{6,7},{7,4},{8,9},{9,10},{10,1... | collective-permute-start | bytes 417800 | tf_op jit(solution)/shard_map/ppermute | solution.py:316
  66.6 1.7 %collective-permute-start.4 = (bf16[8,34,256]{2,1,0:T(8,128)(2,1)S(1)}, bf16[8,34,256]{2,1,0:T(8,128)(2,1)S(1)}, u32[]{:S(2)}, u32[]{:S(2)}) collective-permute-start(bf16[8,34,256]{2,1,0:T(8,128)(2,1)S(1)} %all_to_all.21.r_ref.refs_0_.refs_4_), channel_id=1, source_target_pairs={{0,2},{1,3},{2,0},{3,1},{4,6},{5,7},{6,4},{7,5},{8,10},{9,11},{10,... | collective-permute-start | bytes 417800 | tf_op jit(solution)/shard_map/ppermute | solution.py:316
  68.3 1.2 %copy-done.10 = bf16[2048,256]{1,0:T(8,128)(2,1)S(1)} copy-done((bf16[2048,256]{1,0:T(8,128)(2,1)S(1)}, bf16[2048,256]{1,0:T(8,128)(2,1)}, u32[]{:S(2)}) %copy-start.10) | copy-done | bytes 1048600
  69.5 0.9 %copy-done.15 = bf16[256,256]{1,0:T(8,128)(2,1)S(1)} copy-done((bf16[256,256]{1,0:T(8,128)(2,1)S(1)}, bf16[256,256]{1,0:T(8,128)(2,1)}, u32[]{:S(2)}) %copy-start.15) | copy-done | bytes 131096
  70.4 0.5 local_grad.1.local_ref
  70.9 4.7 %collective-permute-done.4.refs_2_.refs_6_ = bf16[8,34,256]{2,1,0:T(8,128)(2,1)S(1)} collective-permute-done((bf16[8,34,256]{2,1,0:T(8,128)(2,1)S(1)}, bf16[8,34,256]{2,1,0:T(8,128)(2,1)S(1)}, u32[]{:S(2)}, u32[]{:S(2)}) %collective-permute-start.4) | collective-permute-done | bytes 139296 | tf_op jit(solution)/shard_map/ppermute | solution.py:316
  75.7 0.6 collective-permute-done.3.refs_1_.refs_5_
  76.3 0.9 %copy-done.13 = bf16[8,34,256]{2,1,0:T(8,128)(2,1)S(1)} copy-done((bf16[8,34,256]{2,1,0:T(8,128)(2,1)S(1)}, bf16[8,34,256]{2,1,0:T(8,128)(2,1)}, u32[]{:S(2)}) %copy-start.13) | copy-done | bytes 139288
  77.2 5.6 %weight_grad.1 = (f32[16,256,256]{2,1,0:T(8,128)}, f32[16,256,256]{2,1,0:T(8,128)}) custom-call(bf16[8,34,256]{2,1,0:T(8,128)(2,1)S(1)} %all_to_all.20.r_ref.refs_0_, bf16[8,34,256]{2,1,0:T(8,128)(2,1)} %collective-permute-done.refs_1_, bf16[8,34,256]{2,1,0:T(8,128)(2,1)} %collective-permute-done.1.refs_2_, bf16[8,34,256]{2,1,0:T(8,128)(2,1)S(1)} %copy-done.13, ...), custom_call_target="tpu_custom_call" | custom-call | tf_op jit(solution)/shard_map/weight_grad/pallas_call | solution.py:364
  82.8 0.9 %junction_grad.1.rows_ref = f32[8,256]{1,0:T(8,128)S(1)} custom-call(bf16[8,34,256]{2,1,0:T(8,128)(2,1)S(1)} %all_to_all.21.r_ref.refs_0_.refs_4_, bf16[8,34,256]{2,1,0:T(8,128)(2,1)S(1)} %collective-permute-done.3.refs_1_.refs_5_, bf16[8,34,256]{2,1,0:T(8,128)(2,1)S(1)} %collective-permute-done.4.refs_2_.refs_6_, ...), custom_call_target="tpu_custom_call" | custom-call | tf_op jit(solution)/shard_map/junction_grad/pallas_call | solution.py:354
  83.7 2.3 %input_grad.1 = bf16[2048,256]{1,0:T(8,128)(2,1)} custom-call(bf16[256,256]{1,0:T(8,128)(2,1)} %bitcast.8.modes_ref, bf16[2048,256]{1,0:T(8,128)(2,1)S(1)} %copy-done.8, f32[2048,256]{1,0:T(8,128)S(1)} %local_grad.1.local_ref, f32[8,256]{1,0:T(8,128)S(1)} %junction_grad.1.rows_ref), custom_call_target="tpu_custom_call" | custom-call | tf_op jit(solution)/shard_map/input_grad/pallas_call | solution.py:374
  (40 shorter events, 1.1 us)
Async XLA Ops:
  0.6 15.7 %copy-start = (bf16[16,256,256]{2,1,0:T(8,128)(2,1)S(1)}, bf16[16,256,256]{2,1,0:T(8,128)(2,1)}, u32[]{:S(2)}) copy-start(bf16[16,256,256]{2,1,0:T(8,128)(2,1)} %real_ref.3) | copy-start | bytes 6291460
  0.6 1.4 %copy-start.3 = (bf16[1,2048,256]{2,1,0:T(8,128)(2,1)S(1)}, bf16[1,2048,256]{2,1,0:T(8,128)(2,1)}, u32[]{:S(2)}) copy-start(bf16[1,2048,256]{2,1,0:T(8,128)(2,1)} %param.12) | copy-start | bytes 3145732
  2.0 1.2 %copy-start.5 = (bf16[256,2048]{1,0:T(8,128)(2,1)S(1)}, bf16[256,2048]{1,0:T(8,128)(2,1)}, u32[]{:S(2)}) copy-start(bf16[256,2048]{1,0:T(8,128)(2,1)} %constant.15.clone.f_ref) | copy-start | bytes 3145732
  16.3 1.6 %copy-start.1 = (bf16[16,256,256]{2,1,0:T(8,128)(2,1)S(1)}, bf16[16,256,256]{2,1,0:T(8,128)(2,1)}, u32[]{:S(2)}) copy-start(bf16[16,256,256]{2,1,0:T(8,128)(2,1)} %imag_ref.3) | copy-start | bytes 6291460
  17.9 17.0 %copy-start.18 = (s32[32]{0:T(128)S(1)}, s32[32]{0:T(128)}, u32[]{:S(2)}) copy-start(s32[32]{0:T(128)} %refs_4_.3) | copy-start | bytes 388
  17.9 17.0 %copy-start.19 = (s32[32]{0:T(128)S(1)}, s32[32]{0:T(128)}, u32[]{:S(2)}) copy-start(s32[32]{0:T(128)} %refs_5_.3) | copy-start | bytes 388
  17.9 17.0 %copy-start.20 = (f32[256]{0:T(256)S(1)}, f32[256]{0:T(256)}, u32[]{:S(2)}) copy-start(f32[256]{0:T(256)} %param.19) | copy-start | bytes 3076
  17.9 19.3 %copy-start.4 = (bf16[1,2048,256]{2,1,0:T(8,128)(2,1)S(1)}, bf16[1,2048,256]{2,1,0:T(8,128)(2,1)}, u32[]{:S(2)}) copy-start(bf16[1,2048,256]{2,1,0:T(8,128)(2,1)} %param.12) | copy-start | bytes 3145732
  17.9 19.3 %copy-start.21 = (f32[256]{0:T(256)S(1)}, f32[256]{0:T(256)}, u32[]{:S(2)}) copy-start(f32[256]{0:T(256)} %param.15) | copy-start | bytes 3076
  19.3 17.9 %all-to-all-start.1 = ((bf16[8,32,256]{2,1,0:T(8,128)(2,1)}), bf16[8,32,256]{2,1,0:T(8,128)(2,1)}, u32[]{:S(2)}, u32[]{:S(2)}) async-start(bf16[8,32,256]{2,1,0:T(8,128)(2,1)} %mix.1), calls=%async_computation.1 | async-start | bytes 262144 | tf_op jit(solution)/shard_map/all_to_all | solution.py:312
  23.3 6.6 %collective-permute-start.2 = (bf16[8,34,256]{2,1,0:T(8,128)(2,1)S(1)}, bf16[8,34,256]{2,1,0:T(8,128)(2,1)S(1)}, u32[]{:S(2)}, u32[]{:S(2)}) collective-permute-start(bf16[8,34,256]{2,1,0:T(8,128)(2,1)S(1)} %all_to_all.20.r_ref.refs_0_), channel_id=1, source_target_pairs={{0,1},{1,2},{2,3},{3,0},{4,5},{5,6},{6,7},{7,4},{8,9},{9,10},{10,1... | collective-permute-start | bytes 417800 | tf_op jit(solution)/shard_map/ppermute | solution.py:316
  26.5 7.7 %collective-permute-start.1 = (bf16[8,34,256]{2,1,0:T(8,128)(2,1)S(1)}, bf16[8,34,256]{2,1,0:T(8,128)(2,1)}, u32[]{:S(2)}, u32[]{:S(2)}) collective-permute-start(bf16[8,34,256]{2,1,0:T(8,128)(2,1)S(1)} %all_to_all.20.r_ref.refs_0_), channel_id=1, source_target_pairs={{0,2},{1,3},{2,0},{3,1},{4,6},{5,7},{6,4},{7,5},{8,10},{9,11},{10,... | collective-permute-start | bytes 417800 | tf_op jit(solution)/shard_map/ppermute | solution.py:316
  26.8 8.1 %collective-permute-start = (bf16[8,34,256]{2,1,0:T(8,128)(2,1)S(1)}, bf16[8,34,256]{2,1,0:T(8,128)(2,1)}, u32[]{:S(2)}, u32[]{:S(2)}) collective-permute-start(bf16[8,34,256]{2,1,0:T(8,128)(2,1)S(1)} %all_to_all.20.r_ref.refs_0_), channel_id=1, source_target_pairs={{0,3},{1,0},{2,1},{3,2},{4,7},{5,4},{6,5},{7,6},{8,11},{9,8},{10,9... | collective-permute-start | bytes 417800 | tf_op jit(solution)/shard_map/ppermute | solution.py:316
  30.0 16.2 %copy-start.12 = (bf16[8,34,256]{2,1,0:T(8,128)(2,1)}, bf16[8,34,256]{2,1,0:T(8,128)(2,1)S(1)}, u32[]{:S(2)}) copy-start(bf16[8,34,256]{2,1,0:T(8,128)(2,1)S(1)} %collective-permute-done.2.refs_3_) | copy-start | bytes 417796
  34.9 0.9 %copy-start.16 = (bf16[256,256]{1,0:T(8,128)(2,1)S(1)}, bf16[256,256]{1,0:T(8,128)(2,1)}, u32[]{:S(2)}) copy-start(bf16[256,256]{1,0:T(8,128)(2,1)} %refs_7_.3) | copy-start | bytes 393220
  37.2 1.2 %copy-start.6 = (bf16[256,2048]{1,0:T(8,128)(2,1)S(1)}, bf16[256,2048]{1,0:T(8,128)(2,1)}, u32[]{:S(2)}) copy-start(bf16[256,2048]{1,0:T(8,128)(2,1)} %constant.15.clone.f_ref) | copy-start | bytes 3145732
  38.4 1.2 %copy-start.7 = (bf16[2048,256]{1,0:T(8,128)(2,1)S(1)}, bf16[2048,256]{1,0:T(8,128)(2,1)}, u32[]{:S(2)}) copy-start(bf16[2048,256]{1,0:T(8,128)(2,1)} %constant.16.clone.ft_ref) | copy-start | bytes 3145732
  39.6 1.2 %copy-start.11 = (bf16[1,2048,256]{2,1,0:T(8,128)(2,1)S(1)}, bf16[1,2048,256]{2,1,0:T(8,128)(2,1)}, u32[]{:S(2)}) copy-start(bf16[1,2048,256]{2,1,0:T(8,128)(2,1)} %param.13) | copy-start | bytes 3145732
  40.9 0.9 %copy-start.14 = (bf16[256,256]{1,0:T(8,128)(2,1)S(1)}, bf16[256,256]{1,0:T(8,128)(2,1)}, u32[]{:S(2)}) copy-start(bf16[256,256]{1,0:T(8,128)(2,1)} %weight_ref.3) | copy-start | bytes 393220
  41.8 17.9 %copy-start.2 = (bf16[16,256,256]{2,1,0:T(8,128)(2,1)S(1)}, bf16[16,256,256]{2,1,0:T(8,128)(2,1)}, u32[]{:S(2)}) copy-start(bf16[16,256,256]{2,1,0:T(8,128)(2,1)} %imag_ref.3) | copy-start | bytes 6291460
  46.2 1.0 %copy-start.9 = (bf16[2048,256]{1,0:T(8,128)(2,1)}, bf16[2048,256]{1,0:T(8,128)(2,1)S(1)}, u32[]{:S(2)}) copy-start(bf16[2048,256]{1,0:T(8,128)(2,1)S(1)} %get-tuple-element.14.total_ref) | copy-start | bytes 3145732
  61.6 22.0 %all-to-all-start.3 = ((bf16[8,32,256]{2,1,0:T(8,128)(2,1)}), bf16[8,32,256]{2,1,0:T(8,128)(2,1)}, u32[]{:S(2)}, u32[]{:S(2)}) async-start(bf16[8,32,256]{2,1,0:T(8,128)(2,1)} %mix_grad.1), calls=%async_computation.3 | async-start | bytes 262144 | tf_op jit(solution)/shard_map/all_to_all | solution.py:312
  65.6 5.3 %collective-permute-start.5 = (bf16[8,34,256]{2,1,0:T(8,128)(2,1)S(1)}, bf16[8,34,256]{2,1,0:T(8,128)(2,1)S(1)}, u32[]{:S(2)}, u32[]{:S(2)}) collective-permute-start(bf16[8,34,256]{2,1,0:T(8,128)(2,1)S(1)} %all_to_all.21.r_ref.refs_0_.refs_4_), channel_id=1, source_target_pairs={{0,1},{1,2},{2,3},{3,0},{4,5},{5,6},{6,7},{7,4},{8,9},{9,10},{10,1... | collective-permute-start | bytes 417800 | tf_op jit(solution)/shard_map/ppermute | solution.py:316
  66.6 9.0 %collective-permute-start.4 = (bf16[8,34,256]{2,1,0:T(8,128)(2,1)S(1)}, bf16[8,34,256]{2,1,0:T(8,128)(2,1)S(1)}, u32[]{:S(2)}, u32[]{:S(2)}) collective-permute-start(bf16[8,34,256]{2,1,0:T(8,128)(2,1)S(1)} %all_to_all.21.r_ref.refs_0_.refs_4_), channel_id=1, source_target_pairs={{0,2},{1,3},{2,0},{3,1},{4,6},{5,7},{6,4},{7,5},{8,10},{9,11},{10,... | collective-permute-start | bytes 417800 | tf_op jit(solution)/shard_map/ppermute | solution.py:316
  68.3 8.0 %collective-permute-start.3 = (bf16[8,34,256]{2,1,0:T(8,128)(2,1)S(1)}, bf16[8,34,256]{2,1,0:T(8,128)(2,1)S(1)}, u32[]{:S(2)}, u32[]{:S(2)}) collective-permute-start(bf16[8,34,256]{2,1,0:T(8,128)(2,1)S(1)} %all_to_all.21.r_ref.refs_0_.refs_4_), channel_id=1, source_target_pairs={{0,3},{1,0},{2,1},{3,2},{4,7},{5,4},{6,5},{7,6},{8,11},{9,8},{10,9... | collective-permute-start | bytes 417800 | tf_op jit(solution)/shard_map/ppermute | solution.py:316
  68.3 1.2 %copy-start.10 = (bf16[2048,256]{1,0:T(8,128)(2,1)S(1)}, bf16[2048,256]{1,0:T(8,128)(2,1)}, u32[]{:S(2)}) copy-start(bf16[2048,256]{1,0:T(8,128)(2,1)} %copy-done.9) | copy-start | bytes 3145732
  69.5 0.9 %copy-start.15 = (bf16[256,256]{1,0:T(8,128)(2,1)S(1)}, bf16[256,256]{1,0:T(8,128)(2,1)}, u32[]{:S(2)}) copy-start(bf16[256,256]{1,0:T(8,128)(2,1)} %weight_ref.3) | copy-start | bytes 393220
  70.4 12.3 %copy-start.17 = (bf16[256,256]{1,0:T(8,128)(2,1)S(1)}, bf16[256,256]{1,0:T(8,128)(2,1)}, u32[]{:S(2)}) copy-start(bf16[256,256]{1,0:T(8,128)(2,1)} %refs_7_.3) | copy-start | bytes 393220
  70.4 13.2 %copy-start.8 = (bf16[2048,256]{1,0:T(8,128)(2,1)S(1)}, bf16[2048,256]{1,0:T(8,128)(2,1)}, u32[]{:S(2)}) copy-start(bf16[2048,256]{1,0:T(8,128)(2,1)} %constant.16.clone.ft_ref) | copy-start | bytes 3145732
  76.3 0.9 %copy-start.13 = (bf16[8,34,256]{2,1,0:T(8,128)(2,1)S(1)}, bf16[8,34,256]{2,1,0:T(8,128)(2,1)}, u32[]{:S(2)}) copy-start(bf16[8,34,256]{2,1,0:T(8,128)(2,1)} %copy-done.12) | copy-start | bytes 417796

commit v2 on v1

v2 whole, which is shorter than its diff:
```python
import functools
import math

import jax
import jax.numpy as jnp
import ml_dtypes
import numpy as np
from jax import lax
from jax.experimental import pallas as pl
from jax.experimental.pallas import tpu as pltpu
from jax.sharding import PartitionSpec as P

COUPLING = 0.125
TILE = 256
LANES = 128
PAIRWISE = 8
GELU_S = math.sqrt(2.0 / math.pi)
GELU_C = 0.044715
VMEM = pl.BlockSpec(memory_space=pltpu.VMEM)
SMEM = pl.BlockSpec(memory_space=pltpu.SMEM)
HBM = pl.BlockSpec(memory_space=pltpu.HBM)
MIB = 1024 * 1024


def forward_table(cell_count, mode_count, groups):
    product_index = np.arange(mode_count)[:, None] * np.arange(cell_count)[None, :] % cell_count
    angles = product_index.astype(np.float32) * np.float32(2.0 * math.pi / cell_count)
    norm_scale = np.float32(1.0 / math.sqrt(cell_count))
    cosine = (np.cos(angles) * norm_scale).reshape(groups, -1, cell_count)
    sine = (np.sin(angles) * norm_scale).reshape(groups, -1, cell_count)
    table = np.concatenate([cosine, -sine], axis=1).reshape(2 * mode_count, cell_count)
    return table.astype(ml_dtypes.bfloat16)


def dot(left, right, left_dim=1, right_dim=0):
    return lax.dot_general(
        left,
        right,
        (((left_dim,), (right_dim,)), ((), ())),
        preferred_element_type=jnp.float32,
    )


def put(ref, at, value):
    for lane in range(ref.shape[0]):
        ref[lane, at, :] = value[:, lane * LANES : (lane + 1) * LANES]


def take(ref, at):
    return jnp.concatenate([ref[lane, at, :] for lane in range(ref.shape[0])], axis=1)


def chunk(refs, at):
    return refs[at] if len(refs) > 1 else refs[0].at[at]


def rows_at(refs, me, at, span):
    if len(refs) == 1:
        return pl.ds(at * span, span)
    return pl.ds(pl.multiple_of(lax.bitwise_xor(me, at) * span, span), span)


def spectrum_kernel(groups, parts, x_ref, f_ref, *refs):
    out_refs, (x_tiles, f_tiles, rows_ref, x_sems, f_sems) = refs[:parts], refs[parts:]
    me = lax.axis_index("len")
    tiles, all_rows, tile = f_ref.shape
    span = all_rows // groups
    copies = []
    for at in range(tiles):
        copies.append(
            (
                pltpu.make_async_copy(
                    x_ref.at[pl.ds(at * tile, tile)], x_tiles.at[at], x_sems.at[at]
                ),
                pltpu.make_async_copy(f_ref.at[at], f_tiles.at[at], f_sems.at[at]),
            )
        )
    for pair in copies:
        pair[0].start()
        pair[1].start()
    total = None
    for at, pair in enumerate(copies):
        pair[0].wait()
        pair[1].wait()
        part = dot(f_tiles[at], x_tiles[at])
        total = part if total is None else total + part
    rows_ref[...] = total.astype(jnp.bfloat16)
    ends = jnp.concatenate([x_tiles[0, 0:1, :], x_tiles[tiles - 1, tile - 1 : tile, :]], axis=0)
    for at in range(groups):
        out = chunk(out_refs, at)
        out[0:span, :] = rows_ref[rows_at(out_refs, me, at, span), :]
        out[span : span + 2, :] = ends


def pack_kernel(parts, *refs):
    for at in range(refs[parts].shape[0]):
        refs[parts][at] = chunk(refs[:parts], at)[...]


def mix_kernel(backward, parts, groups, *refs):
    ins, (real_ref, imag_ref) = refs[:parts], refs[parts : parts + 2]
    outs, (x_ref, y_ref) = refs[parts + 2 : 2 * parts + 2], refs[2 * parts + 2 :]
    modes = real_ref.shape[0]
    span = 2 * modes
    for source in range(groups):
        rows = chunk(ins, source)[0:span, :].astype(jnp.float32)
        put(x_ref, pl.ds(source * span, span), rows)
    for mode in range(modes):
        first = pl.ds(mode, groups, stride=span)
        second = pl.ds(modes + mode, groups, stride=span)
        rows = jnp.concatenate([take(x_ref, first), take(x_ref, second)], axis=0).astype(
            jnp.bfloat16
        )
        dim = 1 if backward else 0
        by_real = dot(rows, real_ref[mode], 1, dim)
        by_imag = dot(rows, imag_ref[mode], 1, dim)
        if backward:
            put(y_ref, first, by_real[:groups] + by_imag[groups:])
            put(y_ref, second, by_real[groups:] - by_imag[:groups])
        else:
            put(y_ref, first, by_real[:groups] - by_imag[groups:])
            put(y_ref, second, by_imag[:groups] + by_real[groups:])
    for source in range(groups):
        rows = take(y_ref, pl.ds(source * span, span))
        chunk(outs, source)[...] = rows.astype(jnp.bfloat16)


def pipe_index(groups, pipes, group, step):
    source = lax.bitwise_xor(lax.axis_index("pipe"), step)
    if groups <= PAIRWISE:
        group = lax.bitwise_xor(lax.axis_index("len"), group)
    return group * pipes + source


def own_pipe(pipes):
    return lax.axis_index("len") * pipes + lax.axis_index("pipe")


def two_rows(totals, channels):
    return jnp.concatenate(
        [
            jnp.sum(totals[0], axis=0, keepdims=True),
            jnp.sum(totals[1], axis=0, keepdims=True),
            jnp.zeros((6, channels), jnp.float32),
        ],
        axis=0,
    )


def junction_sums(pipes, msgs, inlet_ref, outlet_ref, both):
    groups, rows, channels = msgs[0].shape
    me = own_pipe(pipes)
    own_in, own_out = inlet_ref[me], outlet_ref[me]
    is_first = lax.broadcasted_iota(jnp.int32, (2, channels), 0) == 0

    def matches(pipe, junction):
        first = (inlet_ref[pipe] == junction).astype(jnp.float32)
        last = (outlet_ref[pipe] == junction).astype(jnp.float32)
        return first + last if both else jnp.where(is_first, first, last)

    totals = (jnp.zeros((2, channels), jnp.float32),) * 2
    for step in range(pipes):

        def add(group, carried, step=step):
            pipe = pipe_index(groups, pipes, group, step)
            ends = msgs[step][group, rows - 2 : rows, :].astype(jnp.float32)
            return (
                carried[0] + ends * matches(pipe, own_in),
                carried[1] + ends * matches(pipe, own_out),
            )

        totals = lax.fori_loop(0, groups, add, totals, unroll=min(groups, 8))
    return two_rows(totals, channels)


def junction_forward_kernel(pipes, *refs):
    msgs, (inlet_ref, outlet_ref, weight_ref, bias_ref, cond_ref, slope_ref) = (
        refs[:pipes],
        refs[pipes:],
    )
    sums = junction_sums(pipes, msgs, inlet_ref, outlet_ref, False)
    act = dot(sums.astype(jnp.bfloat16), weight_ref[...]) + bias_ref[...]
    sigmoid_part = jax.nn.sigmoid(act)
    junc_rows = (act * sigmoid_part).astype(jnp.bfloat16).astype(jnp.float32)
    cond_ref[...] = COUPLING * (junc_rows[0:1] + junc_rows[1:2])
    slope_ref[...] = sigmoid_part * (1.0 + act * (1.0 - sigmoid_part))


def junction_backward_kernel(pipes, *refs):
    msgs, (inlet_ref, outlet_ref, weight_ref, slope_ref, rows_ref) = refs[:pipes], refs[pipes:]
    junc_grad = COUPLING * junction_sums(pipes, msgs, inlet_ref, outlet_ref, True)
    act_grad = (junc_grad * slope_ref[...]).astype(jnp.bfloat16)
    sums_grad = dot(act_grad, weight_ref[...], 1, 1).astype(jnp.bfloat16)
    rows_ref[...] = sums_grad.astype(jnp.float32)


def layer_kernel(
    groups, parts, x_ref, cot_ref, weight_ref, bias_ref, cond_ref, f_ref, ft_ref, *refs
):
    mode_refs, (out_ref, total_ref) = refs[:parts], refs[parts : parts + 2]
    msg_refs, (modes_ref, acc_ref, rows_ref) = refs[parts + 2 : 2 * parts + 2], refs[2 * parts + 2 :]
    me = lax.axis_index("len")
    cells, channels = x_ref.shape
    tiles, all_rows, tile = f_ref.shape
    span = all_rows // groups
    row = lax.broadcasted_iota(jnp.int32, (all_rows, channels), 0)
    doubled = jnp.where((row == 0) | (row == span // 2), 1.0, 2.0).astype(jnp.float32)
    for at in range(groups):
        modes_ref[rows_at(mode_refs, me, at, span), :] = chunk(mode_refs, at)[...]
    modes = (modes_ref[...].astype(jnp.float32) * doubled).astype(jnp.bfloat16)
    weight = weight_ref[...]
    cond = cond_ref[...]
    bias = bias_ref[...]
    for step in range(tiles):
        at = pl.ds(step * tile, tile)
        spectral = dot(ft_ref[at, :], modes)
        pre = (spectral + cond).astype(jnp.bfloat16).astype(jnp.float32)
        summed = dot(x_ref[at, :], weight) + bias + pre
        square = summed * summed
        half = 0.5 + 0.5 * jnp.tanh(summed * (GELU_S + (GELU_S * GELU_C) * square))
        result = summed * half
        out_ref[at, :] = result.astype(jnp.bfloat16)
        slope = half + result * (1.0 - half) * (2.0 * GELU_S + (6.0 * GELU_S * GELU_C) * square)
        total = (cot_ref[at, :].astype(jnp.float32) * slope).astype(jnp.bfloat16)
        total_ref[at, :] = total
        part = dot(f_ref[step], total)
        if step == 0:
            acc_ref[...] = part
        else:
            acc_ref[...] += part
    grad_cond = acc_ref[0:1, :] * (1.0 / f_ref[0, 0:1, 0:1].astype(jnp.float32))
    high = grad_cond.astype(jnp.bfloat16)
    low = (grad_cond - high.astype(jnp.float32)).astype(jnp.bfloat16)
    extra = jnp.concatenate([high, low], axis=0)
    rows_ref[...] = (acc_ref[...] * doubled).astype(jnp.bfloat16)
    for at in range(groups):
        out = chunk(msg_refs, at)
        out[0:span, :] = rows_ref[rows_at(msg_refs, me, at, span), :]
        out[span : span + 2, :] = extra


def local_grad_kernel(total_ref, weight_ref, out_ref, grad_ref, copied_ref, sem):
    copy = pltpu.make_async_copy(out_ref, copied_ref, sem)
    copy.start()
    grad_ref[...] = dot(total_ref[...], weight_ref[...], 1, 1)
    copy.wait()


def input_grad_kernel(groups, parts, ft_ref, local_ref, rows_ref, *refs):
    mode_refs, (out_ref, modes_ref, tiles_ref, sems) = refs[:parts], refs[parts:]
    me = lax.axis_index("len")
    span = ft_ref.shape[1] // groups
    for at in range(groups):
        modes_ref[rows_at(mode_refs, me, at, span), :] = chunk(mode_refs, at)[...]
    modes = modes_ref[...]
    tiles, tile, channels = tiles_ref.shape
    row = lax.broadcasted_iota(jnp.int32, (tile, channels), 0)
    copies = []
    for step in range(tiles):
        at = pl.ds(step * tile, tile)
        grad_cells = dot(ft_ref[at, :], modes)
        if step == 0:
            grad_cells = grad_cells + jnp.where(row == 0, rows_ref[0:1, :], 0.0)
        if step == tiles - 1:
            grad_cells = grad_cells + jnp.where(row == tile - 1, rows_ref[1:2, :], 0.0)
        spread = grad_cells.astype(jnp.bfloat16).astype(jnp.float32)
        tiles_ref[step] = (local_ref[at, :] + spread).astype(jnp.bfloat16)
        copies.append(pltpu.make_async_copy(tiles_ref.at[step], out_ref.at[at], sems.at[step]))
        copies[-1].start()
    for copy in copies:
        copy.wait()


def weight_grad_kernel(pipes, modes, *refs):
    fields, grads = refs[:pipes], refs[pipes : 2 * pipes]
    real_out, imag_out, x_ref, g_ref, real_ref, imag_ref, real_sems, imag_sems = refs[2 * pipes :]
    groups = fields[0].shape[0]
    span = 2 * modes
    for step in range(pipes):
        for source in range(groups):
            at = pl.ds((step * groups + source) * span, span)
            put(x_ref, at, fields[step][source, 0:span, :].astype(jnp.float32))
            put(g_ref, at, grads[step][source, 0:span, :].astype(jnp.float32))
    count = pipes * groups
    copies = []
    for mode in range(modes):
        first = pl.ds(mode, count, stride=span)
        second = pl.ds(modes + mode, count, stride=span)
        a, b = take(x_ref, first), take(x_ref, second)
        u, v = take(g_ref, first), take(g_ref, second)
        left = jnp.concatenate([a, b], axis=0).astype(jnp.bfloat16)
        real_ref[mode] = dot(left, jnp.concatenate([u, v], axis=0).astype(jnp.bfloat16), 0, 0)
        imag_ref[mode] = dot(left, jnp.concatenate([v, -u], axis=0).astype(jnp.bfloat16), 0, 0)
        copies.append(pltpu.make_async_copy(real_ref.at[mode], real_out.at[mode], real_sems.at[mode]))
        copies.append(pltpu.make_async_copy(imag_ref.at[mode], imag_out.at[mode], imag_sems.at[mode]))
        copies[-2].start()
        copies[-1].start()
    for copy in copies:
        copy.wait()


def rows_of(count, channels):
    return pltpu.VMEM((channels // LANES, count, LANES), jnp.float32)


def call(kernel, outs, specs, scratch=(), out_specs=None, name=None, limit=8):
    return pl.pallas_call(
        kernel,
        out_shape=outs,
        in_specs=specs,
        out_specs=out_specs if out_specs is not None else [VMEM] * len(outs),
        scratch_shapes=list(scratch),
        compiler_params=pltpu.CompilerParams(vmem_limit_bytes=limit * MIB),
        name=name,
    )


def body(
    inputs,
    cotangent,
    point_weight,
    point_bias,
    spec_real,
    spec_imag,
    junc_weight,
    junc_bias,
    inlet_ids,
    outlet_ids,
):
    per_dev, cell_count, channels = inputs.shape
    assert per_dev == 1
    groups, pipes = lax.axis_size("len"), lax.axis_size("pipe")
    assert pipes == 4
    modes = spec_real.shape[0]
    span = 2 * modes
    all_rows = span * groups
    tiles = cell_count // TILE
    table = forward_table(cell_count, modes * groups, groups)
    tiled = table.reshape(all_rows, tiles, TILE).transpose(1, 0, 2)
    f_table = jnp.asarray(np.ascontiguousarray(tiled))
    ft_table = jnp.asarray(np.ascontiguousarray(table.T))
    field = inputs.reshape(cell_count, channels)
    cot = cotangent.reshape(cell_count, channels)
    bias_row = point_bias.reshape(1, channels)
    junc_bias_row = junc_bias.reshape(1, channels)
    shape = jax.ShapeDtypeStruct
    bf16, f32 = jnp.bfloat16, jnp.float32
    pairwise = groups <= PAIRWISE
    parts = groups if pairwise else 1

    def chunks(rows):
        if pairwise:
            return [shape((rows, channels), bf16)] * groups
        return [shape((groups, rows, channels), bf16)]

    def exchange(values):
        if not pairwise:
            return [lax.all_to_all(values[0], "len", split_axis=0, concat_axis=0, tiled=True)]
        moved = {
            step: lax.ppermute(values[step], "len", [(i, i ^ step) for i in range(groups)])
            for step in reversed(range(1, groups))
        }
        return [values[0]] + [moved[step] for step in range(1, groups)]

    def swap(value, step):
        return lax.ppermute(value, "pipe", [(i, i ^ step) for i in range(pipes)])

    def gather(values):
        if pairwise:
            whole = shape((groups, span + 2, channels), bf16)
            (own,) = call(
                functools.partial(pack_kernel, parts), [whole], [VMEM] * parts, name="pack"
            )(*values)
        else:
            own = values[0]
        across = swap(own, 2)
        return [own, swap(own, 1), across, swap(across, 1)]

    def mix(backward, values):
        return call(
            functools.partial(mix_kernel, backward, parts, groups),
            chunks(span),
            [VMEM] * (parts + 2),
            [rows_of(all_rows, channels)] * 2,
            name="mix_grad" if backward else "mix",
        )(*values, spec_real, spec_imag)

    sent = call(
        functools.partial(spectrum_kernel, groups, parts),
        chunks(span + 2),
        [HBM] * 2,
        [
            pltpu.VMEM((tiles, TILE, channels), bf16),
            pltpu.VMEM((tiles, all_rows, TILE), bf16),
            pltpu.VMEM((all_rows, channels), bf16),
            pltpu.SemaphoreType.DMA((tiles,)),
            pltpu.SemaphoreType.DMA((tiles,)),
        ],
        name="spectrum",
    )(field, f_table)
    received = exchange(sent)
    returned = exchange(mix(False, received))
    fields = gather(received)
    cond, slope = call(
        functools.partial(junction_forward_kernel, pipes),
        [shape((1, channels), f32), shape((8, channels), f32)],
        [VMEM] * pipes + [SMEM] * 2 + [VMEM] * 2,
        name="junction",
    )(*fields, inlet_ids, outlet_ids, junc_weight, junc_bias_row)
    early, total, *sent = call(
        functools.partial(layer_kernel, groups, parts),
        [shape(field.shape, bf16), shape(field.shape, bf16)] + chunks(span + 2),
        [VMEM] * (7 + parts),
        [
            pltpu.VMEM((all_rows, channels), bf16),
            pltpu.VMEM((all_rows, channels), f32),
            pltpu.VMEM((all_rows, channels), bf16),
        ],
        name="layer",
    )(field, cot, point_weight, bias_row, cond, f_table, ft_table, *returned)
    received = exchange(sent)
    returned = exchange(mix(True, received))
    grads = gather(received)
    local, outputs = call(
        local_grad_kernel,
        [shape(field.shape, f32), shape(field.shape, bf16)],
        [VMEM] * 3,
        [pltpu.SemaphoreType.DMA],
        out_specs=[VMEM, HBM],
        name="local_grad",
    )(total, point_weight, early)
    (rows,) = call(
        functools.partial(junction_backward_kernel, pipes),
        [shape((8, channels), f32)],
        [VMEM] * pipes + [SMEM] * 2 + [VMEM] * 2,
        name="junction_grad",
    )(*grads, inlet_ids, outlet_ids, junc_weight, slope)
    big = shape((modes, channels, channels), f32)
    grad_real, grad_imag = call(
        functools.partial(weight_grad_kernel, pipes, modes),
        [big, big],
        [VMEM] * (2 * pipes),
        [rows_of(pipes * all_rows, channels)] * 2
        + [pltpu.VMEM(big.shape, f32)] * 2
        + [pltpu.SemaphoreType.DMA((modes,))] * 2,
        out_specs=[HBM, HBM],
        name="weight_grad",
        limit=16,
    )(*fields, *grads)
    (grad_inputs,) = call(
        functools.partial(input_grad_kernel, groups, parts),
        [shape(field.shape, bf16)],
        [VMEM] * (3 + parts),
        [
            pltpu.VMEM((all_rows, channels), bf16),
            pltpu.VMEM((tiles, TILE, channels), bf16),
            pltpu.SemaphoreType.DMA((tiles,)),
        ],
        out_specs=[HBM],
        name="input_grad",
    )(ft_table, local, rows, *returned)
    return (
        outputs.reshape(inputs.shape),
        grad_inputs.reshape(inputs.shape),
        grad_real,
        grad_imag,
    )


def solution(mesh):
    placed = (
        P(("len", "pipe"), None, None),
        P(("len", "pipe"), None, None),
        P(),
        P(),
        P("len", None, None),
        P("len", None, None),
        P(),
        P(),
        P(),
        P(),
    )
    return jax.shard_map(
        body,
        mesh=mesh,
        in_specs=placed,
        out_specs=(
            P(("len", "pipe"), None, None),
            P(("len", "pipe"), None, None),
            P("len", None, None),
            P("len", None, None),
        ),
        check_vma=False,
    )
```

time: 86.7 us -> 93 us (1.073)
  the two profiles are of different devices: /device:TPU:1 before, /device:TPU:0 now
where the time goes in v2:
time: 93 us; the launch traced here: 92.9 us
  starting transfers between devices  48.2 us (52%)
  waiting for transfers between devices  22.9 us (25%)
  Pallas kernels  16.7 us (18%)
  local copies, waits for them, and re-layouts  4.23 us (5%)
    ppermute x28, starting transfers between devices, exchange(): lax.ppermute(values[step], 'len', [(i, i ^ step) for i in range(groups)])  45.1 us
    ppermute x28, waiting for transfers between devices, exchange(): lax.ppermute(values[step], 'len', [(i, i ^ step) for i in range(groups)])  15.2 us
    ppermute x6, waiting for transfers between devices, swap(): return lax.ppermute(value, 'pipe', [(i, i ^ step) for i in range(pipes)])  7.66 us
    unnamed x28, local copies, waits for them, and re-layouts  4.23 us
    pallas_call x1, Pallas kernels, body(): call(functools.partial(weight_grad_kernel, pipes, modes), [big, big], [VM...  3.99 us
    pallas_call x1, Pallas kernels, body(): call(functools.partial(spectrum_kernel, groups, parts), chunks(span + 2),...  3.85 us
    ppermute x6, starting transfers between devices, swap(): return lax.ppermute(value, 'pipe', [(i, i ^ step) for i in range(pipes)])  3.12 us
    pallas_call x1, Pallas kernels, body(): call(functools.partial(layer_kernel, groups, parts), [shape(field.shape,...  2.61 us
  transfers between devices with their start and end apart: 34, of which 12 were waited for; matrix products, arithmetic and copies ran while one was open for 0% of the time, Pallas kernels for 10%

profile of v2, /device:TPU:0, one launch (start us, length us, event | category | flops | bytes accessed | tf_op | source)
XLA Modules:
  0.0 92.9 jit_solution(1182660121647031536)
XLA Ops:
  0.7 1.4 %copy-done.3 = bf16[1,2048,256]{2,1,0:T(8,128)(2,1)S(1)} copy-done((bf16[1,2048,256]{2,1,0:T(8,128)(2,1)S(1)}, bf16[1,2048,256]{2,1,0:T(8,128)(2,1)}, u32[]{:S(2)}) %copy-start.3) | copy-done | bytes 1048600
  2.0 1.2 %copy-done.5 = bf16[8,256,256]{2,1,0:T(8,128)(2,1)S(1)} copy-done((bf16[8,256,256]{2,1,0:T(8,128)(2,1)S(1)}, bf16[8,256,256]{2,1,0:T(8,128)(2,1)}, u32[]{:S(2)}) %copy-start.5) | copy-done | bytes 1048600
  3.2 3.9 %spectrum.1 = (bf16[34,256]{1,0:T(8,128)(2,1)S(1)}, bf16[34,256]{1,0:T(8,128)(2,1)S(1)}, bf16[34,256]{1,0:T(8,128)(2,1)S(1)}, bf16[34,256]{1,0:T(8,128)(2,1)S(1)...) custom-call(bf16[2048,256]{1,0:T(8,128)(2,1)S(1)} %bitcast.6, ...), custom_call_target="tpu_custom_call" | custom-call | tf_op jit(solution)/shard_map/spectrum/pallas_call | solution.py:388
  7.1 3.0 %collective-permute-start = (bf16[34,256]{1,0:T(8,128)(2,1)S(1)}, bf16[34,256]{1,0:T(8,128)(2,1)S(1)}, u32[]{:S(2)}, u32[]{:S(2)}) collective-permute-start(bf16[34,256]{1,0:T(8,128)(2,1)S(1)} %get-tuple-element.45), channel_id=1, source_target_pairs={{0,4},{4,0},{8,12},{12,8},{16,20},{20,16},{24,28},{28,24},{1,5},{5... | collective-permute-start | bytes 52232 | tf_op jit(solution)/shard_map/ppermute | solution.py:360
  10.1 1.6 %collective-permute-start.1 = (bf16[34,256]{1,0:T(8,128)(2,1)S(1)}, bf16[34,256]{1,0:T(8,128)(2,1)S(1)}, u32[]{:S(2)}, u32[]{:S(2)}) collective-permute-start(bf16[34,256]{1,0:T(8,128)(2,1)S(1)} %get-tuple-element.46), channel_id=1, source_target_pairs={{0,8},{4,12},{8,0},{12,4},{16,24},{20,28},{24,16},{28,20},{1,9},{5... | collective-permute-start | bytes 52232 | tf_op jit(solution)/shard_map/ppermute | solution.py:360
  11.7 3.0 %collective-permute-start.3 = (bf16[34,256]{1,0:T(8,128)(2,1)S(1)}, bf16[34,256]{1,0:T(8,128)(2,1)S(1)}, u32[]{:S(2)}, u32[]{:S(2)}) collective-permute-start(bf16[34,256]{1,0:T(8,128)(2,1)S(1)} %get-tuple-element.48), channel_id=1, source_target_pairs={{0,16},{4,20},{8,24},{12,28},{16,0},{20,4},{24,8},{28,12},{1,17},{... | collective-permute-start | bytes 52232 | tf_op jit(solution)/shard_map/ppermute | solution.py:360
  14.7 1.3 %collective-permute-start.4 = (bf16[34,256]{1,0:T(8,128)(2,1)S(1)}, bf16[34,256]{1,0:T(8,128)(2,1)S(1)}, u32[]{:S(2)}, u32[]{:S(2)}) collective-permute-start(bf16[34,256]{1,0:T(8,128)(2,1)S(1)} %get-tuple-element.49), channel_id=1, source_target_pairs={{0,20},{4,16},{8,28},{12,24},{16,4},{20,0},{24,12},{28,8},{1,21},{... | collective-permute-start | bytes 52232 | tf_op jit(solution)/shard_map/ppermute | solution.py:360
  16.0 3.6 %collective-permute-start.5 = (bf16[34,256]{1,0:T(8,128)(2,1)S(1)}, bf16[34,256]{1,0:T(8,128)(2,1)S(1)}, u32[]{:S(2)}, u32[]{:S(2)}) collective-permute-start(bf16[34,256]{1,0:T(8,128)(2,1)S(1)} %get-tuple-element.50), channel_id=1, source_target_pairs={{0,24},{4,28},{8,16},{12,20},{16,8},{20,12},{24,0},{28,4},{1,25},{... | collective-permute-start | bytes 52232 | tf_op jit(solution)/shard_map/ppermute | solution.py:360
  20.3 1.2 %collective-permute-done.5.refs_6_ = bf16[34,256]{1,0:T(8,128)(2,1)S(1)} collective-permute-done((bf16[34,256]{1,0:T(8,128)(2,1)S(1)}, bf16[34,256]{1,0:T(8,128)(2,1)S(1)}, u32[]{:S(2)}, u32[]{:S(2)}) %collective-permute-start.5) | collective-permute-done | bytes 17440 | tf_op jit(solution)/shard_map/ppermute | solution.py:360
  21.6 4.5 %collective-permute-done.6.refs_7_ = bf16[34,256]{1,0:T(8,128)(2,1)S(1)} collective-permute-done((bf16[34,256]{1,0:T(8,128)(2,1)S(1)}, bf16[34,256]{1,0:T(8,128)(2,1)S(1)}, u32[]{:S(2)}, u32[]{:S(2)}) %collective-permute-start.6) | collective-permute-done | bytes 17440 | tf_op jit(solution)/shard_map/ppermute | solution.py:360
  26.1 1.6 %collective-permute-start.8 = (bf16[8,34,256]{2,1,0:T(8,128)(2,1)S(1)}, bf16[8,34,256]{2,1,0:T(8,128)(2,1)S(1)}, u32[]{:S(2)}, u32[]{:S(2)}) collective-permute-start(bf16[8,34,256]{2,1,0:T(8,128)(2,1)S(1)} %pack.2.refs_0_), channel_id=1, source_target_pairs={{0,2},{1,3},{2,0},{3,1},{4,6},{5,7},{6,4},{7,5},{8,10},{9,11},{10,... | collective-permute-start | bytes 417800 | tf_op jit(solution)/shard_map/ppermute | solution.py:366
  27.7 3.8 %collective-permute-done.8.refs_2_ = bf16[8,34,256]{2,1,0:T(8,128)(2,1)S(1)} collective-permute-done((bf16[8,34,256]{2,1,0:T(8,128)(2,1)S(1)}, bf16[8,34,256]{2,1,0:T(8,128)(2,1)S(1)}, u32[]{:S(2)}, u32[]{:S(2)}) %collective-permute-start.8) | collective-permute-done | bytes 139296 | tf_op jit(solution)/shard_map/ppermute | solution.py:366
  31.5 1.6 %copy-done.1 = bf16[16,256,256]{2,1,0:T(8,128)(2,1)S(1)} copy-done((bf16[16,256,256]{2,1,0:T(8,128)(2,1)S(1)}, bf16[16,256,256]{2,1,0:T(8,128)(2,1)}, u32[]{:S(2)}) %copy-start.1) | copy-done | bytes 2097176
  34.5 3.0 %collective-permute-start.12 = (bf16[32,256]{1,0:T(8,128)(2,1)S(1)}, bf16[32,256]{1,0:T(8,128)(2,1)S(1)}, u32[]{:S(2)}, u32[]{:S(2)}) collective-permute-start(bf16[32,256]{1,0:T(8,128)(2,1)S(1)} %get-tuple-element.56), channel_id=1, source_target_pairs={{0,12},{4,8},{8,4},{12,0},{16,28},{20,24},{24,20},{28,16},{1,13},{... | collective-permute-start | bytes 49160 | tf_op jit(solution)/shard_map/ppermute | solution.py:360
  38.2 2.4 %collective-permute-start.14 = (bf16[32,256]{1,0:T(8,128)(2,1)S(1)}, bf16[32,256]{1,0:T(8,128)(2,1)S(1)}, u32[]{:S(2)}, u32[]{:S(2)}) collective-permute-start(bf16[32,256]{1,0:T(8,128)(2,1)S(1)} %get-tuple-element.58), channel_id=1, source_target_pairs={{0,20},{4,16},{8,28},{12,24},{16,4},{20,0},{24,12},{28,8},{1,21},{... | collective-permute-start | bytes 49160 | tf_op jit(solution)/shard_map/ppermute | solution.py:360
  41.6 3.8 %collective-permute-start.16 = (bf16[32,256]{1,0:T(8,128)(2,1)S(1)}, bf16[32,256]{1,0:T(8,128)(2,1)S(1)}, u32[]{:S(2)}, u32[]{:S(2)}) collective-permute-start(bf16[32,256]{1,0:T(8,128)(2,1)S(1)} %get-tuple-element.60), channel_id=1, source_target_pairs={{0,28},{4,24},{8,20},{12,16},{16,12},{20,8},{24,4},{28,0},{1,29},{... | collective-permute-start | bytes 49160 | tf_op jit(solution)/shard_map/ppermute | solution.py:360
  46.4 1.6 %collective-permute-done.16.refs_7_ = bf16[32,256]{1,0:T(8,128)(2,1)S(1)} collective-permute-done((bf16[32,256]{1,0:T(8,128)(2,1)S(1)}, bf16[32,256]{1,0:T(8,128)(2,1)S(1)}, u32[]{:S(2)}, u32[]{:S(2)}) %collective-permute-start.16) | collective-permute-done | bytes 16416 | tf_op jit(solution)/shard_map/ppermute | solution.py:360
  48.0 2.6 %layer.1 = (bf16[2048,256]{1,0:T(8,128)(2,1)S(1)}, bf16[2048,256]{1,0:T(8,128)(2,1)S(1)}, bf16[34,256]{1,0:T(8,128)(2,1)S(1)}, bf16[34,256]{1,0:T(8,128)(2,1)S(1...) custom-call(bf16[2048,256]{1,0:T(8,128)(2,1)S(1)} %bitcast.7, ...), custom_call_target="tpu_custom_call" | custom-call | tf_op jit(solution)/shard_map/layer/pallas_call | solution.py:410
  51.5 2.7 %collective-permute-start.19 = (bf16[34,256]{1,0:T(8,128)(2,1)S(1)}, bf16[34,256]{1,0:T(8,128)(2,1)S(1)}, u32[]{:S(2)}, u32[]{:S(2)}) collective-permute-start(bf16[34,256]{1,0:T(8,128)(2,1)S(1)} %get-tuple-element.68), channel_id=1, source_target_pairs={{0,12},{4,8},{8,4},{12,0},{16,28},{20,24},{24,20},{28,16},{1,13},{... | collective-permute-start | bytes 52232 | tf_op jit(solution)/shard_map/ppermute | solution.py:360
  54.2 1.5 %collective-permute-start.20 = (bf16[34,256]{1,0:T(8,128)(2,1)S(1)}, bf16[34,256]{1,0:T(8,128)(2,1)S(1)}, u32[]{:S(2)}, u32[]{:S(2)}) collective-permute-start(bf16[34,256]{1,0:T(8,128)(2,1)S(1)} %get-tuple-element.69), channel_id=1, source_target_pairs={{0,16},{4,20},{8,24},{12,28},{16,0},{20,4},{24,8},{28,12},{1,17},{... | collective-permute-start | bytes 52232 | tf_op jit(solution)/shard_map/ppermute | solution.py:360
  55.7 1.7 %collective-permute-start.21 = (bf16[34,256]{1,0:T(8,128)(2,1)S(1)}, bf16[34,256]{1,0:T(8,128)(2,1)S(1)}, u32[]{:S(2)}, u32[]{:S(2)}) collective-permute-start(bf16[34,256]{1,0:T(8,128)(2,1)S(1)} %get-tuple-element.70), channel_id=1, source_target_pairs={{0,20},{4,16},{8,28},{12,24},{16,4},{20,0},{24,12},{28,8},{1,21},{... | collective-permute-start | bytes 52232 | tf_op jit(solution)/shard_map/ppermute | solution.py:360
  57.4 3.6 %collective-permute-start.22 = (bf16[34,256]{1,0:T(8,128)(2,1)S(1)}, bf16[34,256]{1,0:T(8,128)(2,1)S(1)}, u32[]{:S(2)}, u32[]{:S(2)}) collective-permute-start(bf16[34,256]{1,0:T(8,128)(2,1)S(1)} %get-tuple-element.71), channel_id=1, source_target_pairs={{0,24},{4,28},{8,16},{12,20},{16,8},{20,12},{24,0},{28,4},{1,25},{... | collective-permute-start | bytes 52232 | tf_op jit(solution)/shard_map/ppermute | solution.py:360
  61.9 1.1 %collective-permute-done.22.refs_6_ = bf16[34,256]{1,0:T(8,128)(2,1)S(1)} collective-permute-done((bf16[34,256]{1,0:T(8,128)(2,1)S(1)}, bf16[34,256]{1,0:T(8,128)(2,1)S(1)}, u32[]{:S(2)}, u32[]{:S(2)}) %collective-permute-start.22) | collective-permute-done | bytes 17440 | tf_op jit(solution)/shard_map/ppermute | solution.py:360
  63.0 4.5 %collective-permute-done.23.refs_7_ = bf16[34,256]{1,0:T(8,128)(2,1)S(1)} collective-permute-done((bf16[34,256]{1,0:T(8,128)(2,1)S(1)}, bf16[34,256]{1,0:T(8,128)(2,1)S(1)}, u32[]{:S(2)}, u32[]{:S(2)}) %collective-permute-start.23) | collective-permute-done | bytes 17440 | tf_op jit(solution)/shard_map/ppermute | solution.py:360
  67.5 1.6 %collective-permute-start.25 = (bf16[8,34,256]{2,1,0:T(8,128)(2,1)S(1)}, bf16[8,34,256]{2,1,0:T(8,128)(2,1)S(1)}, u32[]{:S(2)}, u32[]{:S(2)}) collective-permute-start(bf16[8,34,256]{2,1,0:T(8,128)(2,1)S(1)} %pack.3.refs_0_.refs_4_), channel_id=1, source_target_pairs={{0,2},{1,3},{2,0},{3,1},{4,6},{5,7},{6,4},{7,5},{8,10},{9,11},{10,... | collective-permute-start | bytes 417800 | tf_op jit(solution)/shard_map/ppermute | solution.py:366
  69.0 3.8 %collective-permute-done.25.refs_2_.refs_6_ = bf16[8,34,256]{2,1,0:T(8,128)(2,1)S(1)} collective-permute-done((bf16[8,34,256]{2,1,0:T(8,128)(2,1)S(1)}, bf16[8,34,256]{2,1,0:T(8,128)(2,1)S(1)}, u32[]{:S(2)}, u32[]{:S(2)}) %collective-permute-start.25) | collective-permute-done | bytes 139296 | tf_op jit(solution)/shard_map/ppermute | solution.py:366
  72.9 1.3 %mix_grad.1 = (bf16[32,256]{1,0:T(8,128)(2,1)S(1)}, bf16[32,256]{1,0:T(8,128)(2,1)S(1)}, bf16[32,256]{1,0:T(8,128)(2,1)S(1)}, bf16[32,256]{1,0:T(8,128)(2,1)S(1)...) custom-call(bf16[34,256]{1,0:T(8,128)(2,1)S(1)} %get-tuple-element.6, ...), custom_call_target="tpu_custom_call" | custom-call | tf_op jit(solution)/shard_map/mix_grad/pallas_call | solution.py:380
  74.7 3.0 %collective-permute-start.29 = (bf16[32,256]{1,0:T(8,128)(2,1)S(1)}, bf16[32,256]{1,0:T(8,128)(2,1)S(1)}, u32[]{:S(2)}, u32[]{:S(2)}) collective-permute-start(bf16[32,256]{1,0:T(8,128)(2,1)S(1)} %get-tuple-element.77), channel_id=1, source_target_pairs={{0,12},{4,8},{8,4},{12,0},{16,28},{20,24},{24,20},{28,16},{1,13},{... | collective-permute-start | bytes 49160 | tf_op jit(solution)/shard_map/ppermute | solution.py:360
  78.5 2.4 %collective-permute-start.31 = (bf16[32,256]{1,0:T(8,128)(2,1)S(1)}, bf16[32,256]{1,0:T(8,128)(2,1)S(1)}, u32[]{:S(2)}, u32[]{:S(2)}) collective-permute-start(bf16[32,256]{1,0:T(8,128)(2,1)S(1)} %get-tuple-element.79), channel_id=1, source_target_pairs={{0,20},{4,16},{8,28},{12,24},{16,4},{20,0},{24,12},{28,8},{1,21},{... | collective-permute-start | bytes 49160 | tf_op jit(solution)/shard_map/ppermute | solution.py:360
  81.8 3.8 %collective-permute-start.33 = (bf16[32,256]{1,0:T(8,128)(2,1)S(1)}, bf16[32,256]{1,0:T(8,128)(2,1)S(1)}, u32[]{:S(2)}, u32[]{:S(2)}) collective-permute-start(bf16[32,256]{1,0:T(8,128)(2,1)S(1)} %get-tuple-element.81), channel_id=1, source_target_pairs={{0,28},{4,24},{8,20},{12,16},{16,12},{20,8},{24,4},{28,0},{1,29},{... | collective-permute-start | bytes 49160 | tf_op jit(solution)/shard_map/ppermute | solution.py:360
  86.6 4.0 %weight_grad.1 = (f32[16,256,256]{2,1,0:T(8,128)}, f32[16,256,256]{2,1,0:T(8,128)}) custom-call(bf16[8,34,256]{2,1,0:T(8,128)(2,1)S(1)} %pack.2.refs_0_, bf16[8,34,256]{2,1,0:T(8,128)(2,1)S(1)} %collective-permute-done.7.refs_1_, bf16[8,34,256]{2,1,0:T(8,128)(2,1)S(1)} %collective-permute-done.8.refs_2_, ...), custom_call_target="tpu_custom_call" | custom-call | tf_op jit(solution)/shard_map/weight_grad/pallas_call | solution.py:439
  91.6 1.3 %input_grad.1 = bf16[2048,256]{1,0:T(8,128)(2,1)} custom-call(bf16[2048,256]{1,0:T(8,128)(2,1)S(1)} %copy-done.6, f32[2048,256]{1,0:T(8,128)S(1)} %get-tuple-element.64.local_ref, f32[8,256]{1,0:T(8,128)S(1)} %junction_grad.1.rows_ref, bf16[32,256]{1,0:T(8,128)(2,1)S(1)} %get-tuple-element.74.refs_0_, bf16[32,256]{1,0:T(8,128)(2,1)S(1)} %collective-permute-done.27.refs_1_, ...), custom_call_target="tpu_custom_call" | custom-call | tf_op jit(solution)/shard_map/input_grad/pallas_call | solution.py:450
  (75 shorter events, 10.7 us)
Async XLA Ops:
  7.1 8.9 %collective-permute-start = (bf16[34,256]{1,0:T(8,128)(2,1)S(1)}, bf16[34,256]{1,0:T(8,128)(2,1)S(1)}, u32[]{:S(2)}, u32[]{:S(2)}) collective-permute-start(bf16[34,256]{1,0:T(8,128)(2,1)S(1)} %get-tuple-element.45), channel_id=1, source_target_pairs={{0,4},{4,0},{8,12},{12,8},{16,20},{20,16},{24,28},{28,24},{1,5},{5... | collective-permute-start | bytes 52232 | tf_op jit(solution)/shard_map/ppermute | solution.py:360
  10.1 9.5 %collective-permute-start.1 = (bf16[34,256]{1,0:T(8,128)(2,1)S(1)}, bf16[34,256]{1,0:T(8,128)(2,1)S(1)}, u32[]{:S(2)}, u32[]{:S(2)}) collective-permute-start(bf16[34,256]{1,0:T(8,128)(2,1)S(1)} %get-tuple-element.46), channel_id=1, source_target_pairs={{0,8},{4,12},{8,0},{12,4},{16,24},{20,28},{24,16},{28,20},{1,9},{5... | collective-permute-start | bytes 52232 | tf_op jit(solution)/shard_map/ppermute | solution.py:360
  11.7 7.9 %collective-permute-start.2 = (bf16[34,256]{1,0:T(8,128)(2,1)S(1)}, bf16[34,256]{1,0:T(8,128)(2,1)S(1)}, u32[]{:S(2)}, u32[]{:S(2)}) collective-permute-start(bf16[34,256]{1,0:T(8,128)(2,1)S(1)} %get-tuple-element.47), channel_id=1, source_target_pairs={{0,12},{4,8},{8,4},{12,0},{16,28},{20,24},{24,20},{28,16},{1,13},{... | collective-permute-start | bytes 52232 | tf_op jit(solution)/shard_map/ppermute | solution.py:360
  11.7 7.9 %collective-permute-start.3 = (bf16[34,256]{1,0:T(8,128)(2,1)S(1)}, bf16[34,256]{1,0:T(8,128)(2,1)S(1)}, u32[]{:S(2)}, u32[]{:S(2)}) collective-permute-start(bf16[34,256]{1,0:T(8,128)(2,1)S(1)} %get-tuple-element.48), channel_id=1, source_target_pairs={{0,16},{4,20},{8,24},{12,28},{16,0},{20,4},{24,8},{28,12},{1,17},{... | collective-permute-start | bytes 52232 | tf_op jit(solution)/shard_map/ppermute | solution.py:360
  14.7 5.6 %collective-permute-start.4 = (bf16[34,256]{1,0:T(8,128)(2,1)S(1)}, bf16[34,256]{1,0:T(8,128)(2,1)S(1)}, u32[]{:S(2)}, u32[]{:S(2)}) collective-permute-start(bf16[34,256]{1,0:T(8,128)(2,1)S(1)} %get-tuple-element.49), channel_id=1, source_target_pairs={{0,20},{4,16},{8,28},{12,24},{16,4},{20,0},{24,12},{28,8},{1,21},{... | collective-permute-start | bytes 52232 | tf_op jit(solution)/shard_map/ppermute | solution.py:360
  16.0 5.6 %collective-permute-start.5 = (bf16[34,256]{1,0:T(8,128)(2,1)S(1)}, bf16[34,256]{1,0:T(8,128)(2,1)S(1)}, u32[]{:S(2)}, u32[]{:S(2)}) collective-permute-start(bf16[34,256]{1,0:T(8,128)(2,1)S(1)} %get-tuple-element.50), channel_id=1, source_target_pairs={{0,24},{4,28},{8,16},{12,20},{16,8},{20,12},{24,0},{28,4},{1,25},{... | collective-permute-start | bytes 52232 | tf_op jit(solution)/shard_map/ppermute | solution.py:360
  19.6 6.5 %collective-permute-start.6 = (bf16[34,256]{1,0:T(8,128)(2,1)S(1)}, bf16[34,256]{1,0:T(8,128)(2,1)S(1)}, u32[]{:S(2)}, u32[]{:S(2)}) collective-permute-start(bf16[34,256]{1,0:T(8,128)(2,1)S(1)} %get-tuple-element.51), channel_id=1, source_target_pairs={{0,28},{4,24},{8,20},{12,16},{16,12},{20,8},{24,4},{28,0},{1,29},{... | collective-permute-start | bytes 52232 | tf_op jit(solution)/shard_map/ppermute | solution.py:360
  26.1 5.4 %collective-permute-start.8 = (bf16[8,34,256]{2,1,0:T(8,128)(2,1)S(1)}, bf16[8,34,256]{2,1,0:T(8,128)(2,1)S(1)}, u32[]{:S(2)}, u32[]{:S(2)}) collective-permute-start(bf16[8,34,256]{2,1,0:T(8,128)(2,1)S(1)} %pack.2.refs_0_), channel_id=1, source_target_pairs={{0,2},{1,3},{2,0},{3,1},{4,6},{5,7},{6,4},{7,5},{8,10},{9,11},{10,... | collective-permute-start | bytes 417800 | tf_op jit(solution)/shard_map/ppermute | solution.py:366
  27.7 12.9 %collective-permute-start.7 = (bf16[8,34,256]{2,1,0:T(8,128)(2,1)S(1)}, bf16[8,34,256]{2,1,0:T(8,128)(2,1)S(1)}, u32[]{:S(2)}, u32[]{:S(2)}) collective-permute-start(bf16[8,34,256]{2,1,0:T(8,128)(2,1)S(1)} %pack.2.refs_0_), channel_id=1, source_target_pairs={{0,1},{1,0},{2,3},{3,2},{4,5},{5,4},{6,7},{7,6},{8,9},{9,8},{10,11... | collective-permute-start | bytes 417800 | tf_op jit(solution)/shard_map/ppermute | solution.py:366
  31.5 10.0 %collective-permute-start.9 = (bf16[8,34,256]{2,1,0:T(8,128)(2,1)S(1)}, bf16[8,34,256]{2,1,0:T(8,128)(2,1)S(1)}, u32[]{:S(2)}, u32[]{:S(2)}) collective-permute-start(bf16[8,34,256]{2,1,0:T(8,128)(2,1)S(1)} %collective-permute-done.8.refs_2_), channel_id=1, source_target_pairs={{0,1},{1,0},{2,3},{3,2},{4,5},{5,4},{6,7},{7,6},{8,9},{9,8},{10,11... | collective-permute-start | bytes 417800 | tf_op jit(solution)/shard_map/ppermute | solution.py:366
  33.9 3.8 %collective-permute-start.10 = (bf16[32,256]{1,0:T(8,128)(2,1)S(1)}, bf16[32,256]{1,0:T(8,128)(2,1)S(1)}, u32[]{:S(2)}, u32[]{:S(2)}) collective-permute-start(bf16[32,256]{1,0:T(8,128)(2,1)S(1)} %get-tuple-element.54), channel_id=1, source_target_pairs={{0,4},{4,0},{8,12},{12,8},{16,20},{20,16},{24,28},{28,24},{1,5},{5... | collective-permute-start | bytes 49160 | tf_op jit(solution)/shard_map/ppermute | solution.py:360
  34.5 11.8 %collective-permute-start.12 = (bf16[32,256]{1,0:T(8,128)(2,1)S(1)}, bf16[32,256]{1,0:T(8,128)(2,1)S(1)}, u32[]{:S(2)}, u32[]{:S(2)}) collective-permute-start(bf16[32,256]{1,0:T(8,128)(2,1)S(1)} %get-tuple-element.56), channel_id=1, source_target_pairs={{0,12},{4,8},{8,4},{12,0},{16,28},{20,24},{24,20},{28,16},{1,13},{... | collective-permute-start | bytes 49160 | tf_op jit(solution)/shard_map/ppermute | solution.py:360
  37.7 8.6 %collective-permute-start.13 = (bf16[32,256]{1,0:T(8,128)(2,1)S(1)}, bf16[32,256]{1,0:T(8,128)(2,1)S(1)}, u32[]{:S(2)}, u32[]{:S(2)}) collective-permute-start(bf16[32,256]{1,0:T(8,128)(2,1)S(1)} %get-tuple-element.57), channel_id=1, source_target_pairs={{0,16},{4,20},{8,24},{12,28},{16,0},{20,4},{24,8},{28,12},{1,17},{... | collective-permute-start | bytes 49160 | tf_op jit(solution)/shard_map/ppermute | solution.py:360
  38.2 8.1 %collective-permute-start.14 = (bf16[32,256]{1,0:T(8,128)(2,1)S(1)}, bf16[32,256]{1,0:T(8,128)(2,1)S(1)}, u32[]{:S(2)}, u32[]{:S(2)}) collective-permute-start(bf16[32,256]{1,0:T(8,128)(2,1)S(1)} %get-tuple-element.58), channel_id=1, source_target_pairs={{0,20},{4,16},{8,28},{12,24},{16,4},{20,0},{24,12},{28,8},{1,21},{... | collective-permute-start | bytes 49160 | tf_op jit(solution)/shard_map/ppermute | solution.py:360
  40.6 5.8 %collective-permute-start.15 = (bf16[32,256]{1,0:T(8,128)(2,1)S(1)}, bf16[32,256]{1,0:T(8,128)(2,1)S(1)}, u32[]{:S(2)}, u32[]{:S(2)}) collective-permute-start(bf16[32,256]{1,0:T(8,128)(2,1)S(1)} %get-tuple-element.59), channel_id=1, source_target_pairs={{0,24},{4,28},{8,16},{12,20},{16,8},{20,12},{24,0},{28,4},{1,25},{... | collective-permute-start | bytes 49160 | tf_op jit(solution)/shard_map/ppermute | solution.py:360
  41.6 6.4 %collective-permute-start.16 = (bf16[32,256]{1,0:T(8,128)(2,1)S(1)}, bf16[32,256]{1,0:T(8,128)(2,1)S(1)}, u32[]{:S(2)}, u32[]{:S(2)}) collective-permute-start(bf16[32,256]{1,0:T(8,128)(2,1)S(1)} %get-tuple-element.60), channel_id=1, source_target_pairs={{0,28},{4,24},{8,20},{12,16},{16,12},{20,8},{24,4},{28,0},{1,29},{... | collective-permute-start | bytes 49160 | tf_op jit(solution)/shard_map/ppermute | solution.py:360
  50.7 6.7 %collective-permute-start.17 = (bf16[34,256]{1,0:T(8,128)(2,1)S(1)}, bf16[34,256]{1,0:T(8,128)(2,1)S(1)}, u32[]{:S(2)}, u32[]{:S(2)}) collective-permute-start(bf16[34,256]{1,0:T(8,128)(2,1)S(1)} %get-tuple-element.66), channel_id=1, source_target_pairs={{0,4},{4,0},{8,12},{12,8},{16,20},{20,16},{24,28},{28,24},{1,5},{5... | collective-permute-start | bytes 52232 | tf_op jit(solution)/shard_map/ppermute | solution.py:360
  51.5 9.5 %collective-permute-start.18 = (bf16[34,256]{1,0:T(8,128)(2,1)S(1)}, bf16[34,256]{1,0:T(8,128)(2,1)S(1)}, u32[]{:S(2)}, u32[]{:S(2)}) collective-permute-start(bf16[34,256]{1,0:T(8,128)(2,1)S(1)} %get-tuple-element.67), channel_id=1, source_target_pairs={{0,8},{4,12},{8,0},{12,4},{16,24},{20,28},{24,16},{28,20},{1,9},{5... | collective-permute-start | bytes 52232 | tf_op jit(solution)/shard_map/ppermute | solution.py:360
  51.5 10.4 %collective-permute-start.19 = (bf16[34,256]{1,0:T(8,128)(2,1)S(1)}, bf16[34,256]{1,0:T(8,128)(2,1)S(1)}, u32[]{:S(2)}, u32[]{:S(2)}) collective-permute-start(bf16[34,256]{1,0:T(8,128)(2,1)S(1)} %get-tuple-element.68), channel_id=1, source_target_pairs={{0,12},{4,8},{8,4},{12,0},{16,28},{20,24},{24,20},{28,16},{1,13},{... | collective-permute-start | bytes 52232 | tf_op jit(solution)/shard_map/ppermute | solution.py:360
  54.2 7.7 %collective-permute-start.20 = (bf16[34,256]{1,0:T(8,128)(2,1)S(1)}, bf16[34,256]{1,0:T(8,128)(2,1)S(1)}, u32[]{:S(2)}, u32[]{:S(2)}) collective-permute-start(bf16[34,256]{1,0:T(8,128)(2,1)S(1)} %get-tuple-element.69), channel_id=1, source_target_pairs={{0,16},{4,20},{8,24},{12,28},{16,0},{20,4},{24,8},{28,12},{1,17},{... | collective-permute-start | bytes 52232 | tf_op jit(solution)/shard_map/ppermute | solution.py:360
  55.7 6.2 %collective-permute-start.21 = (bf16[34,256]{1,0:T(8,128)(2,1)S(1)}, bf16[34,256]{1,0:T(8,128)(2,1)S(1)}, u32[]{:S(2)}, u32[]{:S(2)}) collective-permute-start(bf16[34,256]{1,0:T(8,128)(2,1)S(1)} %get-tuple-element.70), channel_id=1, source_target_pairs={{0,20},{4,16},{8,28},{12,24},{16,4},{20,0},{24,12},{28,8},{1,21},{... | collective-permute-start | bytes 52232 | tf_op jit(solution)/shard_map/ppermute | solution.py:360
  57.4 5.6 %collective-permute-start.22 = (bf16[34,256]{1,0:T(8,128)(2,1)S(1)}, bf16[34,256]{1,0:T(8,128)(2,1)S(1)}, u32[]{:S(2)}, u32[]{:S(2)}) collective-permute-start(bf16[34,256]{1,0:T(8,128)(2,1)S(1)} %get-tuple-element.71), channel_id=1, source_target_pairs={{0,24},{4,28},{8,16},{12,20},{16,8},{20,12},{24,0},{28,4},{1,25},{... | collective-permute-start | bytes 52232 | tf_op jit(solution)/shard_map/ppermute | solution.py:360
  61.0 6.5 %collective-permute-start.23 = (bf16[34,256]{1,0:T(8,128)(2,1)S(1)}, bf16[34,256]{1,0:T(8,128)(2,1)S(1)}, u32[]{:S(2)}, u32[]{:S(2)}) collective-permute-start(bf16[34,256]{1,0:T(8,128)(2,1)S(1)} %get-tuple-element.72), channel_id=1, source_target_pairs={{0,28},{4,24},{8,20},{12,16},{16,12},{20,8},{24,4},{28,0},{1,29},{... | collective-permute-start | bytes 52232 | tf_op jit(solution)/shard_map/ppermute | solution.py:360
  67.5 5.4 %collective-permute-start.25 = (bf16[8,34,256]{2,1,0:T(8,128)(2,1)S(1)}, bf16[8,34,256]{2,1,0:T(8,128)(2,1)S(1)}, u32[]{:S(2)}, u32[]{:S(2)}) collective-permute-start(bf16[8,34,256]{2,1,0:T(8,128)(2,1)S(1)} %pack.3.refs_0_.refs_4_), channel_id=1, source_target_pairs={{0,2},{1,3},{2,0},{3,1},{4,6},{5,7},{6,4},{7,5},{8,10},{9,11},{10,... | collective-permute-start | bytes 417800 | tf_op jit(solution)/shard_map/ppermute | solution.py:366
  69.0 11.8 %collective-permute-start.24 = (bf16[8,34,256]{2,1,0:T(8,128)(2,1)S(1)}, bf16[8,34,256]{2,1,0:T(8,128)(2,1)S(1)}, u32[]{:S(2)}, u32[]{:S(2)}) collective-permute-start(bf16[8,34,256]{2,1,0:T(8,128)(2,1)S(1)} %pack.3.refs_0_.refs_4_), channel_id=1, source_target_pairs={{0,1},{1,0},{2,3},{3,2},{4,5},{5,4},{6,7},{7,6},{8,9},{9,8},{10,11... | collective-permute-start | bytes 417800 | tf_op jit(solution)/shard_map/ppermute | solution.py:366
  72.9 8.9 %collective-permute-start.26 = (bf16[8,34,256]{2,1,0:T(8,128)(2,1)S(1)}, bf16[8,34,256]{2,1,0:T(8,128)(2,1)S(1)}, u32[]{:S(2)}, u32[]{:S(2)}) collective-permute-start(bf16[8,34,256]{2,1,0:T(8,128)(2,1)S(1)} %collective-permute-done.25.refs_2_.refs_6_), channel_id=1, source_target_pairs={{0,1},{1,0},{2,3},{3,2},{4,5},{5,4},{6,7},{7,6},{8,9},{9,8},{10,11... | collective-permute-start | bytes 417800 | tf_op jit(solution)/shard_map/ppermute | solution.py:366
  74.2 3.8 %collective-permute-start.27 = (bf16[32,256]{1,0:T(8,128)(2,1)S(1)}, bf16[32,256]{1,0:T(8,128)(2,1)S(1)}, u32[]{:S(2)}, u32[]{:S(2)}) collective-permute-start(bf16[32,256]{1,0:T(8,128)(2,1)S(1)} %get-tuple-element.75), channel_id=1, source_target_pairs={{0,4},{4,0},{8,12},{12,8},{16,20},{20,16},{24,28},{28,24},{1,5},{5... | collective-permute-start | bytes 49160 | tf_op jit(solution)/shard_map/ppermute | solution.py:360
  74.7 16.8 %collective-permute-start.29 = (bf16[32,256]{1,0:T(8,128)(2,1)S(1)}, bf16[32,256]{1,0:T(8,128)(2,1)S(1)}, u32[]{:S(2)}, u32[]{:S(2)}) collective-permute-start(bf16[32,256]{1,0:T(8,128)(2,1)S(1)} %get-tuple-element.77), channel_id=1, source_target_pairs={{0,12},{4,8},{8,4},{12,0},{16,28},{20,24},{24,20},{28,16},{1,13},{... | collective-permute-start | bytes 49160 | tf_op jit(solution)/shard_map/ppermute | solution.py:360
  78.0 13.6 %collective-permute-start.30 = (bf16[32,256]{1,0:T(8,128)(2,1)S(1)}, bf16[32,256]{1,0:T(8,128)(2,1)S(1)}, u32[]{:S(2)}, u32[]{:S(2)}) collective-permute-start(bf16[32,256]{1,0:T(8,128)(2,1)S(1)} %get-tuple-element.78), channel_id=1, source_target_pairs={{0,16},{4,20},{8,24},{12,28},{16,0},{20,4},{24,8},{28,12},{1,17},{... | collective-permute-start | bytes 49160 | tf_op jit(solution)/shard_map/ppermute | solution.py:360
  78.5 13.1 %collective-permute-start.31 = (bf16[32,256]{1,0:T(8,128)(2,1)S(1)}, bf16[32,256]{1,0:T(8,128)(2,1)S(1)}, u32[]{:S(2)}, u32[]{:S(2)}) collective-permute-start(bf16[32,256]{1,0:T(8,128)(2,1)S(1)} %get-tuple-element.79), channel_id=1, source_target_pairs={{0,20},{4,16},{8,28},{12,24},{16,4},{20,0},{24,12},{28,8},{1,21},{... | collective-permute-start | bytes 49160 | tf_op jit(solution)/shard_map/ppermute | solution.py:360
  80.8 10.7 %collective-permute-start.32 = (bf16[32,256]{1,0:T(8,128)(2,1)S(1)}, bf16[32,256]{1,0:T(8,128)(2,1)S(1)}, u32[]{:S(2)}, u32[]{:S(2)}) collective-permute-start(bf16[32,256]{1,0:T(8,128)(2,1)S(1)} %get-tuple-element.80), channel_id=1, source_target_pairs={{0,24},{4,28},{8,16},{12,20},{16,8},{20,12},{24,0},{28,4},{1,25},{... | collective-permute-start | bytes 49160 | tf_op jit(solution)/shard_map/ppermute | solution.py:360
  81.8 9.8 %collective-permute-start.33 = (bf16[32,256]{1,0:T(8,128)(2,1)S(1)}, bf16[32,256]{1,0:T(8,128)(2,1)S(1)}, u32[]{:S(2)}, u32[]{:S(2)}) collective-permute-start(bf16[32,256]{1,0:T(8,128)(2,1)S(1)} %get-tuple-element.81), channel_id=1, source_target_pairs={{0,28},{4,24},{8,20},{12,16},{16,12},{20,8},{24,4},{28,0},{1,29},{... | collective-permute-start | bytes 49160 | tf_op jit(solution)/shard_map/ppermute | solution.py:360
  (16 other events, 233.2 us)

commit v3 on v2

v3 whole, which is shorter than its diff:
```python
import functools
import math

import jax
import jax.numpy as jnp
import ml_dtypes
import numpy as np
from jax import lax
from jax.experimental import pallas as pl
from jax.experimental.pallas import tpu as pltpu
from jax.sharding import PartitionSpec as P

COUPLING = 0.125
TILE = 256
LANES = 128
GELU_S = math.sqrt(2.0 / math.pi)
GELU_C = 0.044715
VMEM = pl.BlockSpec(memory_space=pltpu.VMEM)
SMEM = pl.BlockSpec(memory_space=pltpu.SMEM)
HBM = pl.BlockSpec(memory_space=pltpu.HBM)
MIB = 1024 * 1024


def forward_table(cell_count, mode_count, groups):
    product_index = np.arange(mode_count)[:, None] * np.arange(cell_count)[None, :] % cell_count
    angles = product_index.astype(np.float32) * np.float32(2.0 * math.pi / cell_count)
    norm_scale = np.float32(1.0 / math.sqrt(cell_count))
    cosine = (np.cos(angles) * norm_scale).reshape(groups, -1, cell_count)
    sine = (np.sin(angles) * norm_scale).reshape(groups, -1, cell_count)
    table = np.concatenate([cosine, -sine], axis=1).reshape(2 * mode_count, cell_count)
    return table.astype(ml_dtypes.bfloat16)


def dot(left, right, left_dim=1, right_dim=0):
    return lax.dot_general(
        left,
        right,
        (((left_dim,), (right_dim,)), ((), ())),
        preferred_element_type=jnp.float32,
    )


def put(ref, at, value):
    for lane in range(ref.shape[0]):
        ref[lane, at, :] = value[:, lane * LANES : (lane + 1) * LANES]


def take(ref, at):
    return jnp.concatenate([ref[lane, at, :] for lane in range(ref.shape[0])], axis=1)


def spectrum_kernel(x_ref, f_ref, msg_ref, x_tiles, f_tiles, x_sems, f_sems):
    groups, rows = msg_ref.shape[0], msg_ref.shape[1]
    tiles, all_rows, tile = f_ref.shape
    channels = x_ref.shape[1]
    span = all_rows // groups
    copies = []
    for at in range(tiles):
        rows_in = pl.ds(at * tile, tile)
        copies.append(
            (
                pltpu.make_async_copy(x_ref.at[rows_in], x_tiles.at[at], x_sems.at[at]),
                pltpu.make_async_copy(f_ref.at[at], f_tiles.at[at], f_sems.at[at]),
            )
        )
    for pair in copies:
        pair[0].start()
        pair[1].start()
    total = None
    for at, pair in enumerate(copies):
        pair[0].wait()
        pair[1].wait()
        part = dot(f_tiles[at], x_tiles[at])
        total = part if total is None else total + part
    spectra = total.astype(jnp.bfloat16)
    ends = extra_rows(
        x_tiles[0, 0:1, :], x_tiles[tiles - 1, tile - 1 : tile, :], rows - span, channels
    )
    for at in range(groups):
        msg_ref[at, 0:span, :] = spectra[at * span : (at + 1) * span]
        msg_ref[at, span:rows, :] = ends


def extra_rows(first, second, count, channels):
    parts = [first.astype(jnp.float32), second.astype(jnp.float32)]
    if count > 2:
        parts.append(jnp.zeros((count - 2, channels), jnp.float32))
    return jnp.concatenate(parts, axis=0).astype(jnp.bfloat16)


def mix_kernel(backward, r_ref, real_ref, imag_ref, out_ref, ends_ref, *refs):
    x_ref, y_ref = refs[-2:]
    groups, modes = r_ref.shape[0], real_ref.shape[0]
    span = 2 * modes
    for source in range(groups):
        rows = r_ref[source].astype(jnp.float32)
        put(x_ref, pl.ds(source * span, span), rows[0:span])
        if backward:
            ends_ref[source : source + 1, :] = rows[span : span + 1] + rows[span + 1 : span + 2]
        else:
            ends_ref[source : source + 1, :] = rows[span : span + 1]
            ends_ref[groups + source : groups + source + 1, :] = rows[span + 1 : span + 2]
    for mode in range(modes):
        first = pl.ds(mode, groups, stride=span)
        second = pl.ds(modes + mode, groups, stride=span)
        rows = jnp.concatenate([take(x_ref, first), take(x_ref, second)], axis=0).astype(
            jnp.bfloat16
        )
        dim = 1 if backward else 0
        by_real = dot(rows, real_ref[mode], 1, dim)
        by_imag = dot(rows, imag_ref[mode], 1, dim)
        if backward:
            put(y_ref, first, by_real[:groups] + by_imag[groups:])
            put(y_ref, second, by_real[groups:] - by_imag[:groups])
        else:
            refs[0][mode] = rows
            put(y_ref, first, by_real[:groups] - by_imag[groups:])
            put(y_ref, second, by_imag[:groups] + by_real[groups:])
    for source in range(groups):
        rows = take(y_ref, pl.ds(source * span, span))
        out_ref[source] = rows.astype(jnp.bfloat16)


def own_pipe(pipes):
    return lax.axis_index("len") * pipes + lax.axis_index("pipe")


def two_rows(first, second, channels):
    return jnp.concatenate([first, second, jnp.zeros((6, channels), jnp.float32)], axis=0)


def junction_sums(pipes, ends, inlet_ref, outlet_ref, both):
    channels = ends[0].shape[1]
    groups = ends[0].shape[0] if both else ends[0].shape[0] // 2
    column = lax.axis_index("pipe")
    me = own_pipe(pipes)
    owns = inlet_ref[me], outlet_ref[me]

    def add(group, carried):
        for step in range(pipes):
            pipe = group * pipes + lax.bitwise_xor(column, step)
            first = ends[step][pl.ds(group, 1), :]
            last = first if both else ends[step][pl.ds(groups + group, 1), :]
            carried = tuple(
                total
                + first * (inlet_ref[pipe] == own).astype(jnp.float32)
                + last * (outlet_ref[pipe] == own).astype(jnp.float32)
                for total, own in zip(carried, owns)
            )
        return carried

    zero = jnp.zeros((1, channels), jnp.float32)
    totals = lax.fori_loop(0, groups, add, (zero, zero), unroll=min(groups, 8))
    return two_rows(totals[0], totals[1], channels)


def junction_forward_kernel(pipes, *refs):
    ends, (inlet_ref, outlet_ref, weight_ref, bias_ref, cond_ref, slope_ref) = (
        refs[:pipes],
        refs[pipes:],
    )
    sums = junction_sums(pipes, ends, inlet_ref, outlet_ref, False)
    act = dot(sums.astype(jnp.bfloat16), weight_ref[...]) + bias_ref[...]
    sigmoid_part = jax.nn.sigmoid(act)
    junc_rows = (act * sigmoid_part).astype(jnp.bfloat16).astype(jnp.float32)
    cond_ref[...] = COUPLING * (junc_rows[0:1] + junc_rows[1:2])
    slope_ref[...] = sigmoid_part * (1.0 + act * (1.0 - sigmoid_part))


def junction_backward_kernel(pipes, *refs):
    ends, (inlet_ref, outlet_ref, weight_ref, slope_ref, rows_ref) = refs[:pipes], refs[pipes:]
    junc_grad = COUPLING * junction_sums(pipes, ends, inlet_ref, outlet_ref, True)
    act_grad = (junc_grad * slope_ref[...]).astype(jnp.bfloat16)
    sums_grad = dot(act_grad, weight_ref[...], 1, 1).astype(jnp.bfloat16)
    rows_ref[...] = sums_grad.astype(jnp.float32)


def layer_kernel(
    x_ref,
    cot_ref,
    weight_ref,
    bias_ref,
    cond_ref,
    f_ref,
    ft_ref,
    modes_ref,
    out_ref,
    total_ref,
    msg_ref,
    acc_ref,
):
    channels = x_ref.shape[1]
    groups, rows = msg_ref.shape[0], msg_ref.shape[1]
    tiles, all_rows, tile = f_ref.shape
    span = all_rows // groups
    row = lax.broadcasted_iota(jnp.int32, (all_rows, channels), 0)
    doubled = jnp.where((row == 0) | (row == span // 2), 1.0, 2.0).astype(jnp.float32)
    modes = (modes_ref[...].astype(jnp.float32) * doubled).astype(jnp.bfloat16)
    weight = weight_ref[...]
    cond = cond_ref[...]
    bias = bias_ref[...]
    for step in range(tiles):
        at = pl.ds(step * tile, tile)
        spectral = dot(ft_ref[at, :], modes)
        pre = (spectral + cond).astype(jnp.bfloat16).astype(jnp.float32)
        summed = dot(x_ref[at, :], weight) + bias + pre
        square = summed * summed
        half = 0.5 + 0.5 * jnp.tanh(summed * (GELU_S + (GELU_S * GELU_C) * square))
        result = summed * half
        out_ref[at, :] = result.astype(jnp.bfloat16)
        slope = half + result * (1.0 - half) * (2.0 * GELU_S + (6.0 * GELU_S * GELU_C) * square)
        total = (cot_ref[at, :].astype(jnp.float32) * slope).astype(jnp.bfloat16)
        total_ref[at, :] = total
        part = dot(f_ref[step], total)
        if step == 0:
            acc_ref[...] = part
        else:
            acc_ref[...] += part
    grad_cond = acc_ref[0:1, :] * (1.0 / f_ref[0, 0:1, 0:1].astype(jnp.float32))
    high = grad_cond.astype(jnp.bfloat16).astype(jnp.float32)
    extra = extra_rows(high, grad_cond - high, rows - span, channels)
    grad_spec = (acc_ref[...] * doubled).astype(jnp.bfloat16)
    for at in range(groups):
        msg_ref[at, 0:span, :] = grad_spec[at * span : (at + 1) * span]
        msg_ref[at, span:rows, :] = extra


def local_grad_kernel(total_ref, weight_ref, out_ref, grad_ref, copied_ref, sem):
    copy = pltpu.make_async_copy(out_ref, copied_ref, sem)
    copy.start()
    grad_ref[...] = dot(total_ref[...], weight_ref[...], 1, 1)
    copy.wait()


def input_grad_kernel(ft_ref, local_ref, rows_ref, modes_ref, out_ref, tiles_ref, sems):
    modes = modes_ref[...]
    tiles, tile, channels = tiles_ref.shape
    row = lax.broadcasted_iota(jnp.int32, (tile, channels), 0)
    copies = []
    for step in range(tiles):
        at = pl.ds(step * tile, tile)
        grad_cells = dot(ft_ref[at, :], modes)
        if step == 0:
            grad_cells = grad_cells + jnp.where(row == 0, rows_ref[0:1, :], 0.0)
        if step == tiles - 1:
            grad_cells = grad_cells + jnp.where(row == tile - 1, rows_ref[1:2, :], 0.0)
        spread = grad_cells.astype(jnp.bfloat16).astype(jnp.float32)
        tiles_ref[step] = (local_ref[at, :] + spread).astype(jnp.bfloat16)
        copies.append(pltpu.make_async_copy(tiles_ref.at[step], out_ref.at[at], sems.at[step]))
        copies[-1].start()
    for copy in copies:
        copy.wait()


def weight_grad_kernel(pipes, *refs):
    fields, grads = refs[:pipes], refs[pipes : 2 * pipes]
    real_out, imag_out, g_ref, real_ref, imag_ref, real_sems, imag_sems = refs[2 * pipes :]
    groups, modes = grads[0].shape[0], fields[0].shape[0]
    span = 2 * modes
    for step in range(pipes):
        for source in range(groups):
            at = pl.ds((step * groups + source) * span, span)
            put(g_ref, at, grads[step][source, 0:span, :].astype(jnp.float32))
    copies = []
    for mode in range(modes):
        plain, turned = [], []
        for step in range(pipes):
            base = step * groups * span + mode
            u = take(g_ref, pl.ds(base, groups, stride=span))
            v = take(g_ref, pl.ds(base + modes, groups, stride=span))
            plain += [u, v]
            turned += [v, -u]
        left = jnp.concatenate([fields[step][mode] for step in range(pipes)], axis=0)
        real_ref[mode] = dot(left, jnp.concatenate(plain, axis=0).astype(jnp.bfloat16), 0, 0)
        imag_ref[mode] = dot(left, jnp.concatenate(turned, axis=0).astype(jnp.bfloat16), 0, 0)
        copies.append(pltpu.make_async_copy(real_ref.at[mode], real_out.at[mode], real_sems.at[mode]))
        copies.append(pltpu.make_async_copy(imag_ref.at[mode], imag_out.at[mode], imag_sems.at[mode]))
        copies[-2].start()
        copies[-1].start()
    for copy in copies:
        copy.wait()


def rows_of(count, channels):
    return pltpu.VMEM((channels // LANES, count, LANES), jnp.float32)


def call(kernel, outs, specs, scratch=(), out_specs=None, name=None, limit=8):
    return pl.pallas_call(
        kernel,
        out_shape=outs,
        in_specs=specs,
        out_specs=out_specs if out_specs is not None else [VMEM] * len(outs),
        scratch_shapes=list(scratch),
        compiler_params=pltpu.CompilerParams(vmem_limit_bytes=limit * MIB),
        name=name,
    )


def body(
    inputs,
    cotangent,
    point_weight,
    point_bias,
    spec_real,
    spec_imag,
    junc_weight,
    junc_bias,
    inlet_ids,
    outlet_ids,
):
    per_dev, cell_count, channels = inputs.shape
    assert per_dev == 1
    groups, pipes = lax.axis_size("len"), lax.axis_size("pipe")
    assert pipes == 4
    modes = spec_real.shape[0]
    span = 2 * modes
    all_rows = span * groups
    tiles = cell_count // TILE
    table = forward_table(cell_count, modes * groups, groups)
    tiled = table.reshape(all_rows, tiles, TILE).transpose(1, 0, 2)
    f_table = jnp.asarray(np.ascontiguousarray(tiled))
    ft_table = jnp.asarray(np.ascontiguousarray(table.T))
    field = inputs.reshape(cell_count, channels)
    cot = cotangent.reshape(cell_count, channels)
    bias_row = point_bias.reshape(1, channels)
    junc_bias_row = junc_bias.reshape(1, channels)
    shape = jax.ShapeDtypeStruct
    bf16, f32 = jnp.bfloat16, jnp.float32
    message = shape((groups, span + (16 if span % 16 == 0 else 2), channels), bf16)
    chunks = shape((groups, span, channels), bf16)

    def exchange(value):
        return lax.all_to_all(value, "len", split_axis=0, concat_axis=0, tiled=True)

    def gather(value):
        return [value] + [
            lax.ppermute(value, "pipe", [(i, i ^ step) for i in range(pipes)])
            for step in range(1, pipes)
        ]

    def mix(backward, value):
        outs = [chunks, shape((groups if backward else 2 * groups, channels), f32)]
        if not backward:
            outs.append(shape((modes, 2 * groups, channels), bf16))
        return call(
            functools.partial(mix_kernel, backward),
            outs,
            [VMEM] * 3,
            [rows_of(all_rows, channels)] * 2,
            name="mix_grad" if backward else "mix",
        )(value, spec_real, spec_imag)

    (sent,) = call(
        spectrum_kernel,
        [message],
        [HBM] * 2,
        [
            pltpu.VMEM((tiles, TILE, channels), bf16),
            pltpu.VMEM((tiles, all_rows, TILE), bf16),
            pltpu.SemaphoreType.DMA((tiles,)),
            pltpu.SemaphoreType.DMA((tiles,)),
        ],
        name="spectrum",
        limit=60,
    )(field, f_table)
    received = exchange(sent)
    mixed, ends, rows = mix(False, received)
    returned = exchange(mixed).reshape(all_rows, channels)
    ends = gather(ends)
    fields = gather(rows)
    cond, slope = call(
        functools.partial(junction_forward_kernel, pipes),
        [shape((1, channels), f32), shape((8, channels), f32)],
        [VMEM] * pipes + [SMEM] * 2 + [VMEM] * 2,
        name="junction",
    )(*ends, inlet_ids, outlet_ids, junc_weight, junc_bias_row)
    early, total, sent = call(
        layer_kernel,
        [shape(field.shape, bf16), shape(field.shape, bf16), message],
        [VMEM] * 8,
        [pltpu.VMEM((all_rows, channels), f32)],
        name="layer",
    )(field, cot, point_weight, bias_row, cond, f_table, ft_table, returned)
    received = exchange(sent)
    grads = gather(received)
    mixed, ends = mix(True, received)
    returned = exchange(mixed).reshape(all_rows, channels)
    ends = gather(ends)
    local, outputs = call(
        local_grad_kernel,
        [shape(field.shape, f32), shape(field.shape, bf16)],
        [VMEM] * 3,
        [pltpu.SemaphoreType.DMA],
        out_specs=[VMEM, HBM],
        name="local_grad",
    )(total, point_weight, early)
    (rows,) = call(
        functools.partial(junction_backward_kernel, pipes),
        [shape((8, channels), f32)],
        [VMEM] * pipes + [SMEM] * 2 + [VMEM] * 2,
        name="junction_grad",
    )(*ends, inlet_ids, outlet_ids, junc_weight, slope)
    big = shape((modes, channels, channels), f32)
    grad_real, grad_imag = call(
        functools.partial(weight_grad_kernel, pipes),
        [big, big],
        [VMEM] * (2 * pipes),
        [rows_of(pipes * all_rows, channels)]
        + [pltpu.VMEM(big.shape, f32)] * 2
        + [pltpu.SemaphoreType.DMA((modes,))] * 2,
        out_specs=[HBM, HBM],
        name="weight_grad",
        limit=16,
    )(*fields, *grads)
    (grad_inputs,) = call(
        input_grad_kernel,
        [shape(field.shape, bf16)],
        [VMEM] * 4,
        [pltpu.VMEM((tiles, TILE, channels), bf16), pltpu.SemaphoreType.DMA((tiles,))],
        out_specs=[HBM],
        name="input_grad",
    )(ft_table, local, rows, returned)
    return (
        outputs.reshape(inputs.shape),
        grad_inputs.reshape(inputs.shape),
        grad_real,
        grad_imag,
    )


def solution(mesh):
    placed = (
        P(("len", "pipe"), None, None),
        P(("len", "pipe"), None, None),
        P(),
        P(),
        P("len", None, None),
        P("len", None, None),
        P(),
        P(),
        P(),
        P(),
    )
    return jax.shard_map(
        body,
        mesh=mesh,
        in_specs=placed,
        out_specs=(
            P(("len", "pipe"), None, None),
            P(("len", "pipe"), None, None),
            P("len", None, None),
            P("len", None, None),
        ),
        check_vma=False,
    )
```

time: 93 us -> 88 us (0.946)
  starting transfers between devices: 48.2 us -> 19.3 us
  blocking collectives: 0 us -> 15.2 us
  local copies, waits for them, and re-layouts: 4.23 us -> 15.1 us
  waiting for transfers between devices: 22.9 us -> 18.4 us
  Pallas kernels: 16.7 us -> 18.3 us
    ppermute x34 -> x12, starting transfers between devices: 48.2 us -> 7.5 us  [gather(): lax.ppermute(value, 'pipe', [(i, i ^ step) for i in range(pipes)])]
    all_to_all x0 -> x1, blocking collectives: none -> 15.2 us  [exchange(): return lax.all_to_all(value, 'len', split_axis=0, concat_axis=0, tiled=True)]
    ppermute x34 -> x12, waiting for transfers between devices: 22.9 us -> 8.87 us  [gather(): lax.ppermute(value, 'pipe', [(i, i ^ step) for i in range(pipes)])]
    all_to_all x0 -> x3, starting transfers between devices: none -> 11.8 us  [exchange(): return lax.all_to_all(value, 'len', split_axis=0, concat_axis=0, tiled=True)]
    unnamed x28 -> x46, local copies, waits for them, and re-layouts: 4.23 us -> 15.1 us
    all_to_all x0 -> x3, waiting for transfers between devices: none -> 9.57 us  [exchange(): return lax.all_to_all(value, 'len', split_axis=0, concat_axis=0, tiled=True)]
    pallas_call x8 -> x6, Pallas kernels: 13.9 us -> 15.6 us  [the longest x1 4.72 us: body(): call(functools.partial(weight_grad_kernel, pipes), [big, big], [VMEM] * (...]
  transfers between devices with their start and end apart: 34 -> 15, of which waited for: 12 -> 5; matrix products, arithmetic and copies ran while one was open for 0% -> 0% of each run, Pallas kernels for 10% -> 11%
where the time goes in v3:
time: 88 us; the launch traced here: 87.2 us
  starting transfers between devices  19.3 us (22%)
  waiting for transfers between devices  18.4 us (21%)
  Pallas kernels  18.3 us (21%)
  blocking collectives  15.2 us (17%)
  local copies, waits for them, and re-layouts  15.1 us (17%)
    all_to_all x1, blocking collectives, exchange(): return lax.all_to_all(value, 'len', split_axis=0, concat_axis=0, tiled=True)  15.2 us
    unnamed x46, local copies, waits for them, and re-layouts  15.1 us
    all_to_all x3, starting transfers between devices, exchange(): return lax.all_to_all(value, 'len', split_axis=0, concat_axis=0, tiled=True)  11.8 us
    all_to_all x3, waiting for transfers between devices, exchange(): return lax.all_to_all(value, 'len', split_axis=0, concat_axis=0, tiled=True)  9.57 us
    ppermute x12, waiting for transfers between devices, gather(): lax.ppermute(value, 'pipe', [(i, i ^ step) for i in range(pipes)])  8.87 us
    ppermute x12, starting transfers between devices, gather(): lax.ppermute(value, 'pipe', [(i, i ^ step) for i in range(pipes)])  7.5 us
    pallas_call x1, Pallas kernels, body(): call(functools.partial(weight_grad_kernel, pipes), [big, big], [VMEM] * (...  4.72 us
    pallas_call x2, Pallas kernels, mix(): call(functools.partial(mix_kernel, backward), outs, [VMEM] * 3, [rows_of(...  3.12 us
  transfers between devices with their start and end apart: 15, of which 5 were waited for; matrix products, arithmetic and copies ran while one was open for 0% of the time, Pallas kernels for 11%

profile of v3, /device:TPU:0, one launch (start us, length us, event | category | flops | bytes accessed | tf_op | source)
XLA Modules:
  0.0 87.2 jit_solution(6677951442906129317)
XLA Ops:
  0.6 3.1 %spectrum.1 = bf16[8,48,256]{2,1,0:T(8,128)(2,1)} custom-call(bf16[2048,256]{1,0:T(8,128)(2,1)} %bitcast.8, bf16[8,256,256]{2,1,0:T(8,128)(2,1)} %constant.4.clone.f_ref), custom_call_target="tpu_custom_call" | custom-call | tf_op jit(solution)/shard_map/spectrum/pallas_call | solution.py:354
  3.7 15.2 %all_to_all.20.r_ref = bf16[8,48,256]{2,1,0:T(8,128)(2,1)S(1)} all-to-all(bf16[8,48,256]{2,1,0:T(8,128)(2,1)} %spectrum.1), channel_id=1, replica_groups=mesh['len'=8,'pipe'=4] {'len'}, dimensions={0} | all-to-all | bytes 393216 | tf_op jit(solution)/shard_map/all_to_all | solution.py:334
  19.0 1.6 %copy-done.1 = bf16[16,256,256]{2,1,0:T(8,128)(2,1)S(1)} copy-done((bf16[16,256,256]{2,1,0:T(8,128)(2,1)S(1)}, bf16[16,256,256]{2,1,0:T(8,128)(2,1)}, u32[]{:S(2)}) %copy-start.1) | copy-done | bytes 2097176
  20.6 1.2 %mix.1 = (bf16[8,32,256]{2,1,0:T(8,128)(2,1)S(1)}, f32[16,256]{1,0:T(8,128)S(1)}, bf16[16,16,256]{2,1,0:T(8,128)(2,1)}) custom-call(bf16[8,48,256]{2,1,0:T(8,128)(2,1)S(1)} %all_to_all.20.r_ref, bf16[16,256,256]{2,1,0:T(8,128)(2,1)S(1)} %copy-done, bf16[16,256,256]{2,1,0:T(8,128)(2,1)S(1)} %copy-done.1), custom_call_target="tpu_custom_call" | custom-call | tf_op jit(solution)/shard_map/mix/pallas_call | solution.py:346
  22.5 3.4 %all-to-all-start.1 = ((bf16[8,32,256]{2,1,0:T(8,128)(2,1)}), bf16[8,32,256]{2,1,0:T(8,128)(2,1)S(1)}, u32[]{:S(2)}, u32[]{:S(2)}) async-start(bf16[8,32,256]{2,1,0:T(8,128)(2,1)} %copy-done.18), calls=%async_computation.1 | async-start | bytes 262144 | tf_op jit(solution)/shard_map/all_to_all | solution.py:334
  26.0 1.5 %collective-permute-start.1 = (f32[16,256]{1,0:T(8,128)S(1)}, f32[16,256]{1,0:T(8,128)S(1)}, u32[]{:S(2)}, u32[]{:S(2)}) collective-permute-start(f32[16,256]{1,0:T(8,128)S(1)} %get-tuple-element.18.refs_0_), channel_id=1, source_target_pairs={{0,2},{1,3},{2,0},{3,1},{4,6},{5,7},{6,4},{7,5},{8,10},{9,11},{10,... | collective-permute-start | bytes 49160 | tf_op jit(solution)/shard_map/ppermute | solution.py:338
  27.8 1.4 %collective-permute-done.2.refs_3_ = f32[16,256]{1,0:T(8,128)S(1)} collective-permute-done((f32[16,256]{1,0:T(8,128)S(1)}, f32[16,256]{1,0:T(8,128)S(1)}, u32[]{:S(2)}, u32[]{:S(2)}) %collective-permute-start.2) | collective-permute-done | bytes 16416 | tf_op jit(solution)/shard_map/ppermute | solution.py:338
  29.8 0.9 %copy-done.13 = bf16[256,256]{1,0:T(8,128)(2,1)S(1)} copy-done((bf16[256,256]{1,0:T(8,128)(2,1)S(1)}, bf16[256,256]{1,0:T(8,128)(2,1)}, u32[]{:S(2)}) %copy-start.13) | copy-done | bytes 131096
  30.7 0.9 junction.1
  31.5 1.6 %all-to-all-done.1 = bf16[8,32,256]{2,1,0:T(8,128)(2,1)S(1)} async-done(((bf16[8,32,256]{2,1,0:T(8,128)(2,1)}), bf16[8,32,256]{2,1,0:T(8,128)(2,1)S(1)}, u32[]{:S(2)}, u32[]{:S(2)}) %all-to-all-start.1) | async-done | bytes 131104 | tf_op jit(solution)/shard_map/all_to_all | solution.py:334
  33.1 1.2 %copy-done.4 = bf16[8,256,256]{2,1,0:T(8,128)(2,1)S(1)} copy-done((bf16[8,256,256]{2,1,0:T(8,128)(2,1)S(1)}, bf16[8,256,256]{2,1,0:T(8,128)(2,1)}, u32[]{:S(2)}) %copy-start.4) | copy-done | bytes 1048600
  34.4 1.2 %copy-done.5 = bf16[2048,256]{1,0:T(8,128)(2,1)S(1)} copy-done((bf16[2048,256]{1,0:T(8,128)(2,1)S(1)}, bf16[2048,256]{1,0:T(8,128)(2,1)}, u32[]{:S(2)}) %copy-start.5) | copy-done | bytes 1048600
  35.6 1.2 %copy-done.11 = bf16[1,2048,256]{2,1,0:T(8,128)(2,1)S(1)} copy-done((bf16[1,2048,256]{2,1,0:T(8,128)(2,1)S(1)}, bf16[1,2048,256]{2,1,0:T(8,128)(2,1)}, u32[]{:S(2)}) %copy-start.11) | copy-done | bytes 1048600
  36.8 2.5 %layer.1 = (bf16[2048,256]{1,0:T(8,128)(2,1)S(1)}, bf16[2048,256]{1,0:T(8,128)(2,1)S(1)}, bf16[8,48,256]{2,1,0:T(8,128)(2,1)S(1)}) custom-call(bf16[2048,256]{1,0:T(8,128)(2,1)S(1)} %bitcast.9, bf16[2048,256]{1,0:T(8,128)(2,1)S(1)} %bitcast.10, bf16[256,256]{1,0:T(8,128)(2,1)S(1)} %copy-done.12, f32[1,256]{1,0:T(1,128)S(1)} %bitcast.13, ...), custom_call_target="tpu_custom_call" | custom-call | tf_op jit(solution)/shard_map/layer/pallas_call | solution.py:378
  39.3 1.0 %copy-done.7 = bf16[2048,256]{1,0:T(8,128)(2,1)} copy-done((bf16[2048,256]{1,0:T(8,128)(2,1)}, bf16[2048,256]{1,0:T(8,128)(2,1)S(1)}, u32[]{:S(2)}) %copy-start.7) | copy-done | bytes 1048600
  40.3 1.0 %copy-done.9 = bf16[2048,256]{1,0:T(8,128)(2,1)} copy-done((bf16[2048,256]{1,0:T(8,128)(2,1)}, bf16[2048,256]{1,0:T(8,128)(2,1)S(1)}, u32[]{:S(2)}) %copy-start.9) | copy-done | bytes 1048600
  42.0 4.3 %all-to-all-start.2 = ((bf16[8,48,256]{2,1,0:T(8,128)(2,1)}), bf16[8,48,256]{2,1,0:T(8,128)(2,1)S(1)}, u32[]{:S(2)}, u32[]{:S(2)}) async-start(bf16[8,48,256]{2,1,0:T(8,128)(2,1)} %copy-done.15), calls=%async_computation.2 | async-start | bytes 393216 | tf_op jit(solution)/shard_map/all_to_all | solution.py:334
  46.8 8.0 %all-to-all-done.2.r_ref.refs_4_ = bf16[8,48,256]{2,1,0:T(8,128)(2,1)S(1)} async-done(((bf16[8,48,256]{2,1,0:T(8,128)(2,1)}), bf16[8,48,256]{2,1,0:T(8,128)(2,1)S(1)}, u32[]{:S(2)}, u32[]{:S(2)}) %all-to-all-start.2) | async-done | bytes 196640 | tf_op jit(solution)/shard_map/all_to_all | solution.py:334
  54.8 1.6 %copy-done.2 = bf16[16,256,256]{2,1,0:T(8,128)(2,1)S(1)} copy-done((bf16[16,256,256]{2,1,0:T(8,128)(2,1)S(1)}, bf16[16,256,256]{2,1,0:T(8,128)(2,1)}, u32[]{:S(2)}) %copy-start.2) | copy-done | bytes 2097176
  56.4 1.9 %mix_grad.1 = (bf16[8,32,256]{2,1,0:T(8,128)(2,1)}, f32[8,256]{1,0:T(8,128)S(1)}) custom-call(bf16[8,48,256]{2,1,0:T(8,128)(2,1)S(1)} %all-to-all-done.2.r_ref.refs_4_, bf16[16,256,256]{2,1,0:T(8,128)(2,1)S(1)} %copy-done, bf16[16,256,256]{2,1,0:T(8,128)(2,1)S(1)} %copy-done.2), custom_call_target="tpu_custom_call" | custom-call | tf_op jit(solution)/shard_map/mix_grad/pallas_call | solution.py:346
  58.3 4.1 %all-to-all-start.3 = ((bf16[8,32,256]{2,1,0:T(8,128)(2,1)}), bf16[8,32,256]{2,1,0:T(8,128)(2,1)}, u32[]{:S(2)}, u32[]{:S(2)}) async-start(bf16[8,32,256]{2,1,0:T(8,128)(2,1)} %get-tuple-element.28), calls=%async_computation.3 | async-start | bytes 262144 | tf_op jit(solution)/shard_map/all_to_all | solution.py:334
  62.5 0.9 %collective-permute-start.10 = (bf16[8,48,256]{2,1,0:T(8,128)(2,1)S(1)}, bf16[8,48,256]{2,1,0:T(8,128)(2,1)S(1)}, u32[]{:S(2)}, u32[]{:S(2)}) collective-permute-start(bf16[8,48,256]{2,1,0:T(8,128)(2,1)S(1)} %all-to-all-done.2.r_ref.refs_4_), channel_id=1, source_target_pairs={{0,2},{1,3},{2,0},{3,1},{4,6},{5,7},{6,4},{7,5},{8,10},{9,11},{10,... | collective-permute-start | bytes 589832 | tf_op jit(solution)/shard_map/ppermute | solution.py:338
  63.4 1.0 %collective-permute-start.9 = (bf16[8,48,256]{2,1,0:T(8,128)(2,1)S(1)}, bf16[8,48,256]{2,1,0:T(8,128)(2,1)S(1)}, u32[]{:S(2)}, u32[]{:S(2)}) collective-permute-start(bf16[8,48,256]{2,1,0:T(8,128)(2,1)S(1)} %all-to-all-done.2.r_ref.refs_4_), channel_id=1, source_target_pairs={{0,1},{1,0},{2,3},{3,2},{4,5},{5,4},{6,7},{7,6},{8,9},{9,8},{10,11... | collective-permute-start | bytes 589832 | tf_op jit(solution)/shard_map/ppermute | solution.py:338
  65.4 1.2 %collective-permute-start.4 = (f32[8,256]{1,0:T(8,128)S(1)}, f32[8,256]{1,0:T(8,128)S(1)}, u32[]{:S(2)}, u32[]{:S(2)}) collective-permute-start(f32[8,256]{1,0:T(8,128)S(1)} %get-tuple-element.26.refs_0_), channel_id=1, source_target_pairs={{0,2},{1,3},{2,0},{3,1},{4,6},{5,7},{6,4},{7,5},{8,10},{9,11},{10,... | collective-permute-start | bytes 24584 | tf_op jit(solution)/shard_map/ppermute | solution.py:338
  66.6 6.9 %collective-permute-done.5.refs_3_ = f32[8,256]{1,0:T(8,128)S(1)} collective-permute-done((f32[8,256]{1,0:T(8,128)S(1)}, f32[8,256]{1,0:T(8,128)S(1)}, u32[]{:S(2)}, u32[]{:S(2)}) %collective-permute-start.5) | collective-permute-done | bytes 8224 | tf_op jit(solution)/shard_map/ppermute | solution.py:338
  73.5 1.2 %collective-permute-start.7 = (bf16[16,16,256]{2,1,0:T(8,128)(2,1)}, bf16[16,16,256]{2,1,0:T(8,128)(2,1)S(1)}, u32[]{:S(2)}, u32[]{:S(2)}) collective-permute-start(bf16[16,16,256]{2,1,0:T(8,128)(2,1)} %get-tuple-element.29.refs_0_), channel_id=1, source_target_pairs={{0,2},{1,3},{2,0},{3,1},{4,6},{5,7},{6,4},{7,5},{8,10},{9,11},{10,... | collective-permute-start | bytes 393224 | tf_op jit(solution)/shard_map/ppermute | solution.py:338
  75.0 1.2 %copy-done.8 = bf16[2048,256]{1,0:T(8,128)(2,1)S(1)} copy-done((bf16[2048,256]{1,0:T(8,128)(2,1)S(1)}, bf16[2048,256]{1,0:T(8,128)(2,1)}, u32[]{:S(2)}) %copy-start.8) | copy-done | bytes 1048600
  76.2 1.2 %copy-done.10 = bf16[2048,256]{1,0:T(8,128)(2,1)S(1)} copy-done((bf16[2048,256]{1,0:T(8,128)(2,1)S(1)}, bf16[2048,256]{1,0:T(8,128)(2,1)}, u32[]{:S(2)}) %copy-start.10) | copy-done | bytes 1048600
  77.4 1.0 %local_grad.1 = (f32[2048,256]{1,0:T(8,128)S(1)}, bf16[2048,256]{1,0:T(8,128)(2,1)}) custom-call(bf16[2048,256]{1,0:T(8,128)(2,1)S(1)} %copy-done.10, bf16[256,256]{1,0:T(8,128)(2,1)S(1)} %copy-done.12, bf16[2048,256]{1,0:T(8,128)(2,1)S(1)} %copy-done.8), custom_call_target="tpu_custom_call" | custom-call | tf_op jit(solution)/shard_map/local_grad/pallas_call | solution.py:390
  78.4 0.9 %copy-done.14 = bf16[256,256]{1,0:T(8,128)(2,1)S(1)} copy-done((bf16[256,256]{1,0:T(8,128)(2,1)S(1)}, bf16[256,256]{1,0:T(8,128)(2,1)}, u32[]{:S(2)}) %copy-start.14) | copy-done | bytes 131096
  80.2 4.7 %weight_grad.1 = (f32[16,256,256]{2,1,0:T(8,128)}, f32[16,256,256]{2,1,0:T(8,128)}) custom-call(bf16[16,16,256]{2,1,0:T(8,128)(2,1)} %get-tuple-element.29.refs_0_, bf16[16,16,256]{2,1,0:T(8,128)(2,1)S(1)} %collective-permute-done.6.refs_1_, bf16[16,16,256]{2,1,0:T(8,128)(2,1)S(1)} %collective-permute-done.7.refs_2_, bf16[16,16,256]{2,1,0:T(8,128)(2,1)S(1)} %copy-done.17, ...), custom_call_target="tpu_custom_call" | custom-call | tf_op jit(solution)/shard_map/weight_grad/pallas_call | solution.py:405
  85.0 2.2 %input_grad.1 = bf16[2048,256]{1,0:T(8,128)(2,1)} custom-call(bf16[2048,256]{1,0:T(8,128)(2,1)S(1)} %copy-done.6, f32[2048,256]{1,0:T(8,128)S(1)} %get-tuple-element.24.local_ref, f32[8,256]{1,0:T(8,128)S(1)} %junction_grad.1.rows_ref, bf16[256,256]{1,0:T(8,128)(2,1)} %bitcast.6.modes_ref), custom_call_target="tpu_custom_call" | custom-call | tf_op jit(solution)/shard_map/input_grad/pallas_call | solution.py:416
  (54 shorter events, 5.2 us)
Async XLA Ops:
  0.6 18.3 %copy-start = (bf16[16,256,256]{2,1,0:T(8,128)(2,1)S(1)}, bf16[16,256,256]{2,1,0:T(8,128)(2,1)}, u32[]{:S(2)}) copy-start(bf16[16,256,256]{2,1,0:T(8,128)(2,1)} %real_ref.3) | copy-start | bytes 6291460
  19.0 1.6 %copy-start.1 = (bf16[16,256,256]{2,1,0:T(8,128)(2,1)S(1)}, bf16[16,256,256]{2,1,0:T(8,128)(2,1)}, u32[]{:S(2)}) copy-start(bf16[16,256,256]{2,1,0:T(8,128)(2,1)} %imag_ref.3) | copy-start | bytes 6291460
  20.6 9.2 %copy-start.19 = (s32[32]{0:T(128)S(1)}, s32[32]{0:T(128)}, u32[]{:S(2)}) copy-start(s32[32]{0:T(128)} %refs_4_.3) | copy-start | bytes 388
  20.6 9.2 %copy-start.20 = (s32[32]{0:T(128)S(1)}, s32[32]{0:T(128)}, u32[]{:S(2)}) copy-start(s32[32]{0:T(128)} %refs_5_.3) | copy-start | bytes 388
  20.6 9.2 %copy-start.21 = (f32[256]{0:T(256)S(1)}, f32[256]{0:T(256)}, u32[]{:S(2)}) copy-start(f32[256]{0:T(256)} %param.19) | copy-start | bytes 3076
  20.6 12.6 %copy-start.3 = (bf16[1,2048,256]{2,1,0:T(8,128)(2,1)S(1)}, bf16[1,2048,256]{2,1,0:T(8,128)(2,1)}, u32[]{:S(2)}) copy-start(bf16[1,2048,256]{2,1,0:T(8,128)(2,1)} %param.12) | copy-start | bytes 3145732
  20.6 12.6 %copy-start.12 = (bf16[256,256]{1,0:T(8,128)(2,1)S(1)}, bf16[256,256]{1,0:T(8,128)(2,1)}, u32[]{:S(2)}) copy-start(bf16[256,256]{1,0:T(8,128)(2,1)} %weight_ref.3) | copy-start | bytes 393220
  20.6 12.5 %copy-start.22 = (f32[256]{0:T(256)S(1)}, f32[256]{0:T(256)}, u32[]{:S(2)}) copy-start(f32[256]{0:T(256)} %param.15) | copy-start | bytes 3076
  22.5 10.7 %all-to-all-start.1 = ((bf16[8,32,256]{2,1,0:T(8,128)(2,1)}), bf16[8,32,256]{2,1,0:T(8,128)(2,1)S(1)}, u32[]{:S(2)}, u32[]{:S(2)}) async-start(bf16[8,32,256]{2,1,0:T(8,128)(2,1)} %copy-done.18), calls=%async_computation.1 | async-start | bytes 262144 | tf_op jit(solution)/shard_map/all_to_all | solution.py:334
  25.8 3.4 %collective-permute-start.2 = (f32[16,256]{1,0:T(8,128)S(1)}, f32[16,256]{1,0:T(8,128)S(1)}, u32[]{:S(2)}, u32[]{:S(2)}) collective-permute-start(f32[16,256]{1,0:T(8,128)S(1)} %get-tuple-element.18.refs_0_), channel_id=1, source_target_pairs={{0,3},{1,2},{2,1},{3,0},{4,7},{5,6},{6,5},{7,4},{8,11},{9,10},{10,... | collective-permute-start | bytes 49160 | tf_op jit(solution)/shard_map/ppermute | solution.py:338
  26.0 3.8 %collective-permute-start.1 = (f32[16,256]{1,0:T(8,128)S(1)}, f32[16,256]{1,0:T(8,128)S(1)}, u32[]{:S(2)}, u32[]{:S(2)}) collective-permute-start(f32[16,256]{1,0:T(8,128)S(1)} %get-tuple-element.18.refs_0_), channel_id=1, source_target_pairs={{0,2},{1,3},{2,0},{3,1},{4,6},{5,7},{6,4},{7,5},{8,10},{9,11},{10,... | collective-permute-start | bytes 49160 | tf_op jit(solution)/shard_map/ppermute | solution.py:338
  27.5 2.3 %collective-permute-start = (f32[16,256]{1,0:T(8,128)S(1)}, f32[16,256]{1,0:T(8,128)S(1)}, u32[]{:S(2)}, u32[]{:S(2)}) collective-permute-start(f32[16,256]{1,0:T(8,128)S(1)} %get-tuple-element.18.refs_0_), channel_id=1, source_target_pairs={{0,1},{1,0},{2,3},{3,2},{4,5},{5,4},{6,7},{7,6},{8,9},{9,8},{10,11... | collective-permute-start | bytes 49160 | tf_op jit(solution)/shard_map/ppermute | solution.py:338
  33.1 1.2 %copy-start.4 = (bf16[8,256,256]{2,1,0:T(8,128)(2,1)S(1)}, bf16[8,256,256]{2,1,0:T(8,128)(2,1)}, u32[]{:S(2)}) copy-start(bf16[8,256,256]{2,1,0:T(8,128)(2,1)} %constant.4.clone.f_ref) | copy-start | bytes 3145732
  34.4 1.2 %copy-start.5 = (bf16[2048,256]{1,0:T(8,128)(2,1)S(1)}, bf16[2048,256]{1,0:T(8,128)(2,1)}, u32[]{:S(2)}) copy-start(bf16[2048,256]{1,0:T(8,128)(2,1)} %constant.5.clone.ft_ref) | copy-start | bytes 3145732
  35.6 1.2 %copy-start.11 = (bf16[1,2048,256]{2,1,0:T(8,128)(2,1)S(1)}, bf16[1,2048,256]{2,1,0:T(8,128)(2,1)}, u32[]{:S(2)}) copy-start(bf16[1,2048,256]{2,1,0:T(8,128)(2,1)} %param.13) | copy-start | bytes 3145732
  39.3 1.0 %copy-start.7 = (bf16[2048,256]{1,0:T(8,128)(2,1)}, bf16[2048,256]{1,0:T(8,128)(2,1)S(1)}, u32[]{:S(2)}) copy-start(bf16[2048,256]{1,0:T(8,128)(2,1)S(1)} %get-tuple-element.22.out_ref) | copy-start | bytes 3145732
  42.0 12.8 %all-to-all-start.2 = ((bf16[8,48,256]{2,1,0:T(8,128)(2,1)}), bf16[8,48,256]{2,1,0:T(8,128)(2,1)S(1)}, u32[]{:S(2)}, u32[]{:S(2)}) async-start(bf16[8,48,256]{2,1,0:T(8,128)(2,1)} %copy-done.15), calls=%async_computation.2 | async-start | bytes 393216 | tf_op jit(solution)/shard_map/all_to_all | solution.py:334
  46.2 18.5 %collective-permute-start.8 = (bf16[16,16,256]{2,1,0:T(8,128)(2,1)}, bf16[16,16,256]{2,1,0:T(8,128)(2,1)S(1)}, u32[]{:S(2)}, u32[]{:S(2)}) collective-permute-start(bf16[16,16,256]{2,1,0:T(8,128)(2,1)} %get-tuple-element.29.refs_0_), channel_id=1, source_target_pairs={{0,3},{1,2},{2,1},{3,0},{4,7},{5,6},{6,5},{7,4},{8,11},{9,10},{10,... | collective-permute-start | bytes 393224 | tf_op jit(solution)/shard_map/ppermute | solution.py:338
  54.8 1.6 %copy-start.2 = (bf16[16,256,256]{2,1,0:T(8,128)(2,1)S(1)}, bf16[16,256,256]{2,1,0:T(8,128)(2,1)}, u32[]{:S(2)}) copy-start(bf16[16,256,256]{2,1,0:T(8,128)(2,1)} %imag_ref.3) | copy-start | bytes 6291460
  58.3 26.7 %copy-start.6 = (bf16[2048,256]{1,0:T(8,128)(2,1)S(1)}, bf16[2048,256]{1,0:T(8,128)(2,1)}, u32[]{:S(2)}) copy-start(bf16[2048,256]{1,0:T(8,128)(2,1)} %constant.5.clone.ft_ref) | copy-start | bytes 3145732
  58.3 26.7 %all-to-all-start.3 = ((bf16[8,32,256]{2,1,0:T(8,128)(2,1)}), bf16[8,32,256]{2,1,0:T(8,128)(2,1)}, u32[]{:S(2)}, u32[]{:S(2)}) async-start(bf16[8,32,256]{2,1,0:T(8,128)(2,1)} %get-tuple-element.28), calls=%async_computation.3 | async-start | bytes 262144 | tf_op jit(solution)/shard_map/all_to_all | solution.py:334
  62.4 17.8 %collective-permute-start.11 = (bf16[8,48,256]{2,1,0:T(8,128)(2,1)S(1)}, bf16[8,48,256]{2,1,0:T(8,128)(2,1)S(1)}, u32[]{:S(2)}, u32[]{:S(2)}) collective-permute-start(bf16[8,48,256]{2,1,0:T(8,128)(2,1)S(1)} %all-to-all-done.2.r_ref.refs_4_), channel_id=1, source_target_pairs={{0,3},{1,2},{2,1},{3,0},{4,7},{5,6},{6,5},{7,4},{8,11},{9,10},{10,... | collective-permute-start | bytes 589832 | tf_op jit(solution)/shard_map/ppermute | solution.py:338
  62.5 17.7 %collective-permute-start.10 = (bf16[8,48,256]{2,1,0:T(8,128)(2,1)S(1)}, bf16[8,48,256]{2,1,0:T(8,128)(2,1)S(1)}, u32[]{:S(2)}, u32[]{:S(2)}) collective-permute-start(bf16[8,48,256]{2,1,0:T(8,128)(2,1)S(1)} %all-to-all-done.2.r_ref.refs_4_), channel_id=1, source_target_pairs={{0,2},{1,3},{2,0},{3,1},{4,6},{5,7},{6,4},{7,5},{8,10},{9,11},{10,... | collective-permute-start | bytes 589832 | tf_op jit(solution)/shard_map/ppermute | solution.py:338
  63.4 16.9 %collective-permute-start.9 = (bf16[8,48,256]{2,1,0:T(8,128)(2,1)S(1)}, bf16[8,48,256]{2,1,0:T(8,128)(2,1)S(1)}, u32[]{:S(2)}, u32[]{:S(2)}) collective-permute-start(bf16[8,48,256]{2,1,0:T(8,128)(2,1)S(1)} %all-to-all-done.2.r_ref.refs_4_), channel_id=1, source_target_pairs={{0,1},{1,0},{2,3},{3,2},{4,5},{5,4},{6,7},{7,6},{8,9},{9,8},{10,11... | collective-permute-start | bytes 589832 | tf_op jit(solution)/shard_map/ppermute | solution.py:338
  64.3 9.2 %collective-permute-start.5 = (f32[8,256]{1,0:T(8,128)S(1)}, f32[8,256]{1,0:T(8,128)S(1)}, u32[]{:S(2)}, u32[]{:S(2)}) collective-permute-start(f32[8,256]{1,0:T(8,128)S(1)} %get-tuple-element.26.refs_0_), channel_id=1, source_target_pairs={{0,3},{1,2},{2,1},{3,0},{4,7},{5,6},{6,5},{7,4},{8,11},{9,10},{10,... | collective-permute-start | bytes 24584 | tf_op jit(solution)/shard_map/ppermute | solution.py:338
  65.4 8.1 %collective-permute-start.4 = (f32[8,256]{1,0:T(8,128)S(1)}, f32[8,256]{1,0:T(8,128)S(1)}, u32[]{:S(2)}, u32[]{:S(2)}) collective-permute-start(f32[8,256]{1,0:T(8,128)S(1)} %get-tuple-element.26.refs_0_), channel_id=1, source_target_pairs={{0,2},{1,3},{2,0},{3,1},{4,6},{5,7},{6,4},{7,5},{8,10},{9,11},{10,... | collective-permute-start | bytes 24584 | tf_op jit(solution)/shard_map/ppermute | solution.py:338
  73.5 1.2 %collective-permute-start.3 = (f32[8,256]{1,0:T(8,128)S(1)}, f32[8,256]{1,0:T(8,128)S(1)}, u32[]{:S(2)}, u32[]{:S(2)}) collective-permute-start(f32[8,256]{1,0:T(8,128)S(1)} %get-tuple-element.26.refs_0_), channel_id=1, source_target_pairs={{0,1},{1,0},{2,3},{3,2},{4,5},{5,4},{6,7},{7,6},{8,9},{9,8},{10,11... | collective-permute-start | bytes 24584 | tf_op jit(solution)/shard_map/ppermute | solution.py:338
  73.5 6.7 %collective-permute-start.7 = (bf16[16,16,256]{2,1,0:T(8,128)(2,1)}, bf16[16,16,256]{2,1,0:T(8,128)(2,1)S(1)}, u32[]{:S(2)}, u32[]{:S(2)}) collective-permute-start(bf16[16,16,256]{2,1,0:T(8,128)(2,1)} %get-tuple-element.29.refs_0_), channel_id=1, source_target_pairs={{0,2},{1,3},{2,0},{3,1},{4,6},{5,7},{6,4},{7,5},{8,10},{9,11},{10,... | collective-permute-start | bytes 393224 | tf_op jit(solution)/shard_map/ppermute | solution.py:338
  74.7 5.4 %collective-permute-start.6 = (bf16[16,16,256]{2,1,0:T(8,128)(2,1)}, bf16[16,16,256]{2,1,0:T(8,128)(2,1)S(1)}, u32[]{:S(2)}, u32[]{:S(2)}) collective-permute-start(bf16[16,16,256]{2,1,0:T(8,128)(2,1)} %get-tuple-element.29.refs_0_), channel_id=1, source_target_pairs={{0,1},{1,0},{2,3},{3,2},{4,5},{5,4},{6,7},{7,6},{8,9},{9,8},{10,11... | collective-permute-start | bytes 393224 | tf_op jit(solution)/shard_map/ppermute | solution.py:338
  75.0 1.2 %copy-start.8 = (bf16[2048,256]{1,0:T(8,128)(2,1)S(1)}, bf16[2048,256]{1,0:T(8,128)(2,1)}, u32[]{:S(2)}) copy-start(bf16[2048,256]{1,0:T(8,128)(2,1)} %copy-done.7) | copy-start | bytes 3145732
  76.2 1.2 %copy-start.10 = (bf16[2048,256]{1,0:T(8,128)(2,1)S(1)}, bf16[2048,256]{1,0:T(8,128)(2,1)}, u32[]{:S(2)}) copy-start(bf16[2048,256]{1,0:T(8,128)(2,1)} %copy-done.9) | copy-start | bytes 3145732
  77.4 2.8 %copy-start.17 = (bf16[16,16,256]{2,1,0:T(8,128)(2,1)S(1)}, bf16[16,16,256]{2,1,0:T(8,128)(2,1)}, u32[]{:S(2)}) copy-start(bf16[16,16,256]{2,1,0:T(8,128)(2,1)} %copy-done.16) | copy-start | bytes 393220
  (6 other events, 4.8 us)

commit v4 on v3

v4 whole, which is shorter than its diff:
```python
import functools
import math

import jax
import jax.numpy as jnp
import ml_dtypes
import numpy as np
from jax import lax
from jax.experimental import pallas as pl
from jax.experimental.pallas import tpu as pltpu
from jax.sharding import PartitionSpec as P

COUPLING = 0.125
TILE = 256
LANES = 128
GELU_S = math.sqrt(2.0 / math.pi)
GELU_C = 0.044715
VMEM = pl.BlockSpec(memory_space=pltpu.VMEM)
SMEM = pl.BlockSpec(memory_space=pltpu.SMEM)
HBM = pl.BlockSpec(memory_space=pltpu.HBM)
MIB = 1024 * 1024


def forward_table(cell_count, mode_count, groups):
    product_index = np.arange(mode_count)[:, None] * np.arange(cell_count)[None, :] % cell_count
    angles = product_index.astype(np.float32) * np.float32(2.0 * math.pi / cell_count)
    norm_scale = np.float32(1.0 / math.sqrt(cell_count))
    cosine = (np.cos(angles) * norm_scale).reshape(groups, -1, cell_count)
    sine = (np.sin(angles) * norm_scale).reshape(groups, -1, cell_count)
    table = np.concatenate([cosine, -sine], axis=1).reshape(2 * mode_count, cell_count)
    return table.astype(ml_dtypes.bfloat16)


def dot(left, right, left_dim=1, right_dim=0):
    return lax.dot_general(
        left,
        right,
        (((left_dim,), (right_dim,)), ((), ())),
        preferred_element_type=jnp.float32,
    )


def put(ref, at, value):
    for lane in range(ref.shape[0]):
        ref[lane, at, :] = value[:, lane * LANES : (lane + 1) * LANES]


def take(ref, at):
    return jnp.concatenate([ref[lane, at, :] for lane in range(ref.shape[0])], axis=1)


def spectrum_kernel(x_ref, f_ref, msg_ref, x_tiles, f_tiles, x_sems, f_sems):
    groups, rows = msg_ref.shape[0], msg_ref.shape[1]
    tiles, all_rows, tile = f_ref.shape
    channels = x_ref.shape[1]
    span = all_rows // groups
    copies = []
    for at in range(tiles):
        rows_in = pl.ds(at * tile, tile)
        copies.append(
            (
                pltpu.make_async_copy(x_ref.at[rows_in], x_tiles.at[at], x_sems.at[at]),
                pltpu.make_async_copy(f_ref.at[at], f_tiles.at[at], f_sems.at[at]),
            )
        )
    for pair in copies:
        pair[0].start()
        pair[1].start()
    total = None
    for at, pair in enumerate(copies):
        pair[0].wait()
        pair[1].wait()
        part = dot(f_tiles[at], x_tiles[at])
        total = part if total is None else total + part
    spectra = total.astype(jnp.bfloat16)
    ends = extra_rows(
        x_tiles[0, 0:1, :], x_tiles[tiles - 1, tile - 1 : tile, :], rows - span, channels
    )
    for at in range(groups):
        msg_ref[at, 0:span, :] = spectra[at * span : (at + 1) * span]
        msg_ref[at, span:rows, :] = ends


def extra_rows(first, second, count, channels):
    parts = [first.astype(jnp.float32), second.astype(jnp.float32)]
    if count > 2:
        parts.append(jnp.zeros((count - 2, channels), jnp.float32))
    return jnp.concatenate(parts, axis=0).astype(jnp.bfloat16)


def mix_kernel(backward, r_ref, real_ref, imag_ref, out_ref, x_ref, y_ref):
    groups, modes = r_ref.shape[0], real_ref.shape[0]
    span = 2 * modes
    for source in range(groups):
        put(x_ref, pl.ds(source * span, span), r_ref[source, 0:span, :].astype(jnp.float32))
    for mode in range(modes):
        first = pl.ds(mode, groups, stride=span)
        second = pl.ds(modes + mode, groups, stride=span)
        rows = jnp.concatenate([take(x_ref, first), take(x_ref, second)], axis=0).astype(
            jnp.bfloat16
        )
        dim = 1 if backward else 0
        by_real = dot(rows, real_ref[mode], 1, dim)
        by_imag = dot(rows, imag_ref[mode], 1, dim)
        if backward:
            put(y_ref, first, by_real[:groups] + by_imag[groups:])
            put(y_ref, second, by_real[groups:] - by_imag[:groups])
        else:
            put(y_ref, first, by_real[:groups] - by_imag[groups:])
            put(y_ref, second, by_imag[:groups] + by_real[groups:])
    for source in range(groups):
        rows = take(y_ref, pl.ds(source * span, span))
        out_ref[source] = rows.astype(jnp.bfloat16)


def own_pipe(pipes):
    return lax.axis_index("len") * pipes + lax.axis_index("pipe")


def two_rows(first, second, channels):
    return jnp.concatenate([first, second, jnp.zeros((6, channels), jnp.float32)], axis=0)


def junction_sums(pipes, msgs, inlet_ref, outlet_ref, both):
    groups, rows, channels = msgs[0].shape
    column = lax.axis_index("pipe")
    me = own_pipe(pipes)
    owns = inlet_ref[me], outlet_ref[me]
    is_first = lax.broadcasted_iota(jnp.int32, (2, channels), 0) == 0

    def matches(pipe, junction):
        first = (inlet_ref[pipe] == junction).astype(jnp.float32)
        last = (outlet_ref[pipe] == junction).astype(jnp.float32)
        return first + last if both else jnp.where(is_first, first, last)

    def add(group, carried):
        for step in range(pipes):
            pipe = group * pipes + lax.bitwise_xor(column, step)
            ends = msgs[step][group, rows - 2 : rows, :].astype(jnp.float32)
            carried = tuple(
                total + ends * matches(pipe, own) for total, own in zip(carried, owns)
            )
        return carried

    zero = jnp.zeros((2, channels), jnp.float32)
    totals = lax.fori_loop(0, groups, add, (zero, zero), unroll=min(groups, 8))
    return two_rows(
        jnp.sum(totals[0], axis=0, keepdims=True),
        jnp.sum(totals[1], axis=0, keepdims=True),
        channels,
    )


def started(copies):
    for copy in copies:
        copy.start()
    return copies


def wait(copies):
    for copy in copies:
        copy.wait()


def brought(pairs, sems, base=0):
    return started(
        [
            pltpu.make_async_copy(source, target, sems.at[base + place])
            for place, (source, target) in enumerate(pairs)
        ]
    )


def layer_kernel(pipes, *refs):
    msgs, refs = refs[:pipes], refs[pipes:]
    (x_ref, cot_ref, f_ref, ft_ref), refs = refs[:4], refs[4:]
    small, refs = refs[:7], refs[7:]
    (out_ref, total_ref, msg_ref, slope_ref), refs = refs[:4], refs[4:]
    x_tiles, cot_tiles, f_tiles, ft_tiles, out_tiles, total_tiles, acc_ref = refs[:7]
    msg_bufs, refs = refs[7 : 7 + pipes], refs[7 + pipes :]
    small_bufs, (first_sems, in_sems, out_sems) = refs[:7], refs[7:]
    inlet, outlet, junc_weight, junc_bias, weight_ref, bias_ref, modes_ref = small_bufs
    channels = x_ref.shape[1]
    groups, rows = msg_ref.shape[0], msg_ref.shape[1]
    tiles, all_rows, tile = f_ref.shape
    span = all_rows // groups
    junction = brought(list(zip(small[:4], small_bufs[:4])) + list(zip(msgs, msg_bufs)), first_sems)
    shared = brought(zip(small[4:], small_bufs[4:]), first_sems, 4 + pipes)
    coming = []
    for step in range(tiles):
        at = pl.ds(step * tile, tile)
        coming.append(
            brought(
                [
                    (ft_ref.at[at], ft_tiles.at[step]),
                    (x_ref.at[at], x_tiles.at[step]),
                    (cot_ref.at[at], cot_tiles.at[step]),
                    (f_ref.at[step], f_tiles.at[step]),
                ],
                in_sems,
                4 * step,
            )
        )
    wait(junction)
    sums = junction_sums(pipes, msg_bufs, inlet, outlet, False)
    act = dot(sums.astype(jnp.bfloat16), junc_weight[...]) + junc_bias[...]
    sigmoid_part = jax.nn.sigmoid(act)
    junc_rows = (act * sigmoid_part).astype(jnp.bfloat16).astype(jnp.float32)
    cond = COUPLING * (junc_rows[0:1] + junc_rows[1:2])
    slope_ref[...] = sigmoid_part * (1.0 + act * (1.0 - sigmoid_part))
    wait(shared)
    row = lax.broadcasted_iota(jnp.int32, (all_rows, channels), 0)
    doubled = jnp.where((row == 0) | (row == span // 2), 1.0, 2.0).astype(jnp.float32)
    modes = (modes_ref[...].astype(jnp.float32) * doubled).astype(jnp.bfloat16)
    weight = weight_ref[...]
    bias = bias_ref[...]
    going = []
    for step in range(tiles):
        at = pl.ds(step * tile, tile)
        wait(coming[step])
        spectral = dot(ft_tiles[step], modes)
        pre = (spectral + cond).astype(jnp.bfloat16).astype(jnp.float32)
        summed = dot(x_tiles[step], weight) + bias + pre
        square = summed * summed
        half = 0.5 + 0.5 * jnp.tanh(summed * (GELU_S + (GELU_S * GELU_C) * square))
        result = summed * half
        out_tiles[step] = result.astype(jnp.bfloat16)
        slope = half + result * (1.0 - half) * (2.0 * GELU_S + (6.0 * GELU_S * GELU_C) * square)
        total = (cot_tiles[step].astype(jnp.float32) * slope).astype(jnp.bfloat16)
        total_tiles[step] = total
        going += brought(
            [(out_tiles.at[step], out_ref.at[at]), (total_tiles.at[step], total_ref.at[at])],
            out_sems,
            2 * step,
        )
        part = dot(f_tiles[step], total)
        if step == 0:
            acc_ref[...] = part
        else:
            acc_ref[...] += part
    grad_cond = acc_ref[0:1, :] * (1.0 / f_tiles[0, 0:1, 0:1].astype(jnp.float32))
    high = grad_cond.astype(jnp.bfloat16).astype(jnp.float32)
    extra = extra_rows(high, grad_cond - high, rows - span, channels)
    grad_spec = (acc_ref[...] * doubled).astype(jnp.bfloat16)
    for at in range(groups):
        msg_ref[at, 0:span, :] = grad_spec[at * span : (at + 1) * span]
        msg_ref[at, span:rows, :] = extra
    wait(going)


def input_grad_kernel(pipes, *refs):
    msgs, refs = refs[:pipes], refs[pipes:]
    (total_ref, ft_ref), small, out_ref = refs[:2], refs[2:8], refs[8]
    total_tiles, ft_tiles, out_tiles = refs[9:12]
    msg_bufs, refs = refs[12 : 12 + pipes], refs[12 + pipes :]
    small_bufs, (first_sems, in_sems, out_sems) = refs[:6], refs[6:]
    inlet, outlet, junc_weight, slope_ref, weight_ref, modes_ref = small_bufs
    tiles, tile, channels = out_tiles.shape
    shared = brought(zip(small[4:], small_bufs[4:]), first_sems)
    order = list(range(1, tiles - 1)) + [0, tiles - 1]
    coming = {}
    for step in order:
        at = pl.ds(step * tile, tile)
        coming[step] = brought(
            [(ft_ref.at[at], ft_tiles.at[step]), (total_ref.at[at], total_tiles.at[step])],
            in_sems,
            2 * step,
        )
    junction = brought(
        list(zip(small[:4], small_bufs[:4])) + list(zip(msgs, msg_bufs)), first_sems, 2
    )
    wait(shared)
    modes = modes_ref[...]
    weight = weight_ref[...]
    row = lax.broadcasted_iota(jnp.int32, (tile, channels), 0)
    going = []
    for step in order:
        at = pl.ds(step * tile, tile)
        if step == 0:
            wait(junction)
            junc_grad = COUPLING * junction_sums(pipes, msg_bufs, inlet, outlet, True)
            act_grad = (junc_grad * slope_ref[...]).astype(jnp.bfloat16)
            sums_grad = dot(act_grad, junc_weight[...], 1, 1)
            sums_grad = sums_grad.astype(jnp.bfloat16).astype(jnp.float32)
        wait(coming[step])
        grad_cells = dot(ft_tiles[step], modes)
        if step == 0:
            grad_cells = grad_cells + jnp.where(row == 0, sums_grad[0:1, :], 0.0)
        if step == tiles - 1:
            grad_cells = grad_cells + jnp.where(row == tile - 1, sums_grad[1:2, :], 0.0)
        spread = grad_cells.astype(jnp.bfloat16).astype(jnp.float32)
        local = dot(total_tiles[step], weight, 1, 1)
        out_tiles[step] = (local + spread).astype(jnp.bfloat16)
        going += brought([(out_tiles.at[step], out_ref.at[at])], out_sems, step)
    wait(going)


def weight_grad_kernel(pipes, modes, *refs):
    fields, grads = refs[:pipes], refs[pipes : 2 * pipes]
    real_out, imag_out, x_ref, g_ref, real_ref, imag_ref, sems = refs[2 * pipes :]
    groups = fields[0].shape[0]
    span = 2 * modes
    for step in range(pipes):
        for source in range(groups):
            at = pl.ds((step * groups + source) * span, span)
            put(x_ref, at, fields[step][source, 0:span, :].astype(jnp.float32))
            put(g_ref, at, grads[step][source, 0:span, :].astype(jnp.float32))
    count = pipes * groups
    going = []
    for mode in range(modes):
        first = pl.ds(mode, count, stride=span)
        second = pl.ds(modes + mode, count, stride=span)
        a, b = take(x_ref, first), take(x_ref, second)
        u, v = take(g_ref, first), take(g_ref, second)
        left = jnp.concatenate([a, b], axis=0).astype(jnp.bfloat16)
        real_ref[mode] = dot(left, jnp.concatenate([u, v], axis=0).astype(jnp.bfloat16), 0, 0)
        imag_ref[mode] = dot(left, jnp.concatenate([v, -u], axis=0).astype(jnp.bfloat16), 0, 0)
        going += started(
            [
                pltpu.make_async_copy(real_ref.at[mode], real_out.at[mode], sems.at[mode, 0]),
                pltpu.make_async_copy(imag_ref.at[mode], imag_out.at[mode], sems.at[mode, 1]),
            ]
        )
    wait(going)


def rows_of(count, channels):
    return pltpu.VMEM((channels // LANES, count, LANES), jnp.float32)


def call(kernel, outs, specs, scratch=(), out_specs=None, name=None, limit=8):
    return pl.pallas_call(
        kernel,
        out_shape=outs,
        in_specs=specs,
        out_specs=out_specs if out_specs is not None else [VMEM] * len(outs),
        scratch_shapes=list(scratch),
        compiler_params=pltpu.CompilerParams(vmem_limit_bytes=limit * MIB),
        name=name,
    )


def body(
    inputs,
    cotangent,
    point_weight,
    point_bias,
    spec_real,
    spec_imag,
    junc_weight,
    junc_bias,
    inlet_ids,
    outlet_ids,
):
    per_dev, cell_count, channels = inputs.shape
    assert per_dev == 1
    groups, pipes = lax.axis_size("len"), lax.axis_size("pipe")
    assert pipes == 4
    modes = spec_real.shape[0]
    span = 2 * modes
    all_rows = span * groups
    tiles = cell_count // TILE
    table = forward_table(cell_count, modes * groups, groups)
    tiled = table.reshape(all_rows, tiles, TILE).transpose(1, 0, 2)
    f_table = jnp.asarray(np.ascontiguousarray(tiled))
    ft_table = jnp.asarray(np.ascontiguousarray(table.T))
    field = inputs.reshape(cell_count, channels)
    cot = cotangent.reshape(cell_count, channels)
    bias_row = point_bias.reshape(1, channels)
    junc_bias_row = junc_bias.reshape(1, channels)
    shape = jax.ShapeDtypeStruct
    bf16, f32 = jnp.bfloat16, jnp.float32
    message = shape((groups, span + 2, channels), bf16)
    chunks = shape((groups, span, channels), bf16)
    cell_tiles = pltpu.VMEM((tiles, TILE, channels), bf16)
    table_tiles = pltpu.VMEM((tiles, all_rows, TILE), bf16)
    back_tiles = pltpu.VMEM((tiles, TILE, all_rows), bf16)
    dma = pltpu.SemaphoreType.DMA

    def exchange(value):
        return lax.all_to_all(value, "len", split_axis=0, concat_axis=0, tiled=True)

    def swap(value, step):
        return lax.ppermute(value, "pipe", [(i, i ^ step) for i in range(pipes)])

    def gather(own, behind):
        across = swap(own, 2)
        tied, tied_across, _ = lax.optimization_barrier((own, across, behind))
        return [own, swap(tied, 1), across, swap(tied_across, 1)]

    def mix(backward, value):
        return call(
            functools.partial(mix_kernel, backward),
            [chunks],
            [VMEM] * 3,
            [rows_of(all_rows, channels)] * 2,
            name="mix_grad" if backward else "mix",
        )(value, spec_real, spec_imag)[0]

    (sent,) = call(
        spectrum_kernel,
        [message],
        [HBM] * 2,
        [cell_tiles, table_tiles, dma((tiles,)), dma((tiles,))],
        name="spectrum",
        limit=60,
    )(field, f_table)
    received = exchange(sent)
    mixed = mix(False, received)
    returned = exchange(mixed).reshape(all_rows, channels)
    fields = gather(received, mixed)
    ids = pltpu.SMEM(inlet_ids.shape, jnp.int32)
    square = pltpu.VMEM((channels, channels), bf16)
    flat = pltpu.VMEM((1, channels), f32)
    modes_buf = pltpu.VMEM((all_rows, channels), bf16)
    msg_bufs = [pltpu.VMEM(message.shape, bf16)] * pipes
    outputs, total, sent, slope = call(
        functools.partial(layer_kernel, pipes),
        [shape(field.shape, bf16)] * 2 + [message, shape((8, channels), f32)],
        [HBM] * (pipes + 11),
        [cell_tiles, cell_tiles, table_tiles, back_tiles, cell_tiles, cell_tiles]
        + [pltpu.VMEM((all_rows, channels), f32)]
        + msg_bufs
        + [ids, ids, square, flat, square, flat, modes_buf]
        + [dma((pipes + 7,)), dma((4 * tiles,)), dma((2 * tiles,))],
        out_specs=[HBM, HBM, VMEM, VMEM],
        name="layer",
        limit=60,
    )(
        *fields,
        field,
        cot,
        f_table,
        ft_table,
        inlet_ids,
        outlet_ids,
        junc_weight,
        junc_bias_row,
        point_weight,
        bias_row,
        returned,
    )
    received = exchange(sent)
    mixed = mix(True, received)
    returned = exchange(mixed).reshape(all_rows, channels)
    grads = gather(received, mixed)
    big = shape((modes, channels, channels), f32)
    grad_real, grad_imag = call(
        functools.partial(weight_grad_kernel, pipes, modes),
        [big, big],
        [VMEM] * (2 * pipes),
        [rows_of(pipes * all_rows, channels)] * 2
        + [pltpu.VMEM(big.shape, f32)] * 2
        + [dma((modes, 2))],
        out_specs=[HBM, HBM],
        name="weight_grad",
        limit=16,
    )(*fields, *grads)
    (grad_inputs,) = call(
        functools.partial(input_grad_kernel, pipes),
        [shape(field.shape, bf16)],
        [HBM] * (pipes + 8),
        [cell_tiles, back_tiles, cell_tiles]
        + msg_bufs
        + [ids, ids, square, pltpu.VMEM((8, channels), f32), square, modes_buf]
        + [dma((pipes + 6,)), dma((2 * tiles,)), dma((tiles,))],
        out_specs=[HBM],
        name="input_grad",
        limit=60,
    )(
        *grads,
        total,
        ft_table,
        inlet_ids,
        outlet_ids,
        junc_weight,
        slope,
        point_weight,
        returned,
    )
    return (
        outputs.reshape(inputs.shape),
        grad_inputs.reshape(inputs.shape),
        grad_real,
        grad_imag,
    )


def solution(mesh):
    placed = (
        P(("len", "pipe"), None, None),
        P(("len", "pipe"), None, None),
        P(),
        P(),
        P("len", None, None),
        P("len", None, None),
        P(),
        P(),
        P(),
        P(),
    )
    return jax.shard_map(
        body,
        mesh=mesh,
        in_specs=placed,
        out_specs=(
            P(("len", "pipe"), None, None),
            P(("len", "pipe"), None, None),
            P("len", None, None),
            P("len", None, None),
        ),
        check_vma=False,
    )
```

time: 88 us -> 75.8 us (0.86)
  blocking collectives: 15.2 us -> 25.9 us
  starting transfers between devices: 19.3 us -> 9.89 us
  waiting for transfers between devices: 18.4 us -> 9.33 us
  local copies, waits for them, and re-layouts: 15.1 us -> 6.16 us
  Pallas kernels: 18.3 us -> 23.1 us
    all_to_all x1 -> x2, blocking collectives: 15.2 us -> 25.9 us  [exchange(): return lax.all_to_all(value, 'len', split_axis=0, concat_axis=0, tiled=True)]
    unnamed x46 -> x36, local copies, waits for them, and re-layouts: 15.1 us -> 6.16 us
    ppermute x12 -> x6, waiting for transfers between devices: 8.87 us -> 1.13 us  [swap(): return lax.ppermute(value, 'pipe', [(i, i ^ step) for i in range(pipes)])]
    all_to_all x3 -> x2, starting transfers between devices: 11.8 us -> 6.74 us  [exchange(): return lax.all_to_all(value, 'len', split_axis=0, concat_axis=0, tiled=True)]
    pallas_call x9 -> x6, Pallas kernels: 18.3 us -> 23.1 us  [the longest x1 8.15 us: body(): call(functools.partial(layer_kernel, pipes), [shape(field.shape, bf16)] *...]
    ppermute x12 -> x6, starting transfers between devices: 7.5 us -> 3.15 us  [swap(): return lax.ppermute(value, 'pipe', [(i, i ^ step) for i in range(pipes)])]
    all_to_all x3 -> x2, waiting for transfers between devices: 9.57 us -> 8.21 us  [exchange(): return lax.all_to_all(value, 'len', split_axis=0, concat_axis=0, tiled=True)]
  transfers between devices with their start and end apart: 15 -> 8, of which waited for: 5 -> 4; matrix products, arithmetic and copies ran while one was open for 0% -> 0% of each run, Pallas kernels for 11% -> 10%
where the time goes in v4:
time: 75.8 us; the launch traced here: 75.1 us
  blocking collectives  25.9 us (34%)
  Pallas kernels  23.1 us (30%)
  starting transfers between devices  9.89 us (13%)
  waiting for transfers between devices  9.33 us (12%)
  local copies, waits for them, and re-layouts  6.16 us (8%)
  between operations  0.81 us (1%)
    all_to_all x2, blocking collectives, exchange(): return lax.all_to_all(value, 'len', split_axis=0, concat_axis=0, tiled=True)  25.9 us
    all_to_all x2, waiting for transfers between devices, exchange(): return lax.all_to_all(value, 'len', split_axis=0, concat_axis=0, tiled=True)  8.21 us
    pallas_call x1, Pallas kernels, body(): call(functools.partial(layer_kernel, pipes), [shape(field.shape, bf16)] *...  8.15 us
    all_to_all x2, starting transfers between devices, exchange(): return lax.all_to_all(value, 'len', split_axis=0, concat_axis=0, tiled=True)  6.74 us
    unnamed x36, local copies, waits for them, and re-layouts  6.16 us
    pallas_call x1, Pallas kernels, body(): call(functools.partial(input_grad_kernel, pipes), [shape(field.shape, bf1...  4.74 us
    pallas_call x1, Pallas kernels, body(): call(functools.partial(weight_grad_kernel, pipes, modes), [big, big], [VM...  4 us
    pallas_call x2, Pallas kernels, mix(): call(functools.partial(mix_kernel, backward), [chunks], [VMEM] * 3, [rows...  3.28 us
  transfers between devices with their start and end apart: 8, of which 4 were waited for; matrix products, arithmetic and copies ran while one was open for 0% of the time, Pallas kernels for 10%

profile of v4, /device:TPU:0, one launch (start us, length us, event | category | flops | bytes accessed | tf_op | source)
XLA Modules:
  0.0 75.1 jit_solution(4918433749552508971)
XLA Ops:
  0.6 2.9 %spectrum.1 = bf16[8,34,256]{2,1,0:T(8,128)(2,1)} custom-call(bf16[2048,256]{1,0:T(8,128)(2,1)} %bitcast.8, bf16[8,256,256]{2,1,0:T(8,128)(2,1)} %constant.4.clone.f_ref.refs_6_), custom_call_target="tpu_custom_call" | custom-call | tf_op jit(solution)/shard_map/spectrum/pallas_call | solution.py:400
  3.6 14.9 %all_to_all.20.r_ref.refs_0_ = bf16[8,34,256]{2,1,0:T(8,128)(2,1)S(1)} all-to-all(bf16[8,34,256]{2,1,0:T(8,128)(2,1)} %spectrum.1), channel_id=1, replica_groups=mesh['len'=8,'pipe'=4] {'len'}, dimensions={0} | all-to-all | bytes 278528 | tf_op jit(solution)/shard_map/all_to_all | solution.py:381
  18.4 1.5 %collective-permute-start = (bf16[8,34,256]{2,1,0:T(8,128)(2,1)S(1)}, bf16[8,34,256]{2,1,0:T(8,128)(2,1)S(1)}, u32[]{:S(2)}, u32[]{:S(2)}) collective-permute-start(bf16[8,34,256]{2,1,0:T(8,128)(2,1)S(1)} %all_to_all.20.r_ref.refs_0_), channel_id=1, source_target_pairs={{0,2},{1,3},{2,0},{3,1},{4,6},{5,7},{6,4},{7,5},{8,10},{9,11},{10,... | collective-permute-start | bytes 417800 | tf_op jit(solution)/shard_map/ppermute | solution.py:384
  19.9 1.6 %copy-done = bf16[16,256,256]{2,1,0:T(8,128)(2,1)S(1)} copy-done((bf16[16,256,256]{2,1,0:T(8,128)(2,1)S(1)}, bf16[16,256,256]{2,1,0:T(8,128)(2,1)}, u32[]{:S(2)}) %copy-start) | copy-done | bytes 2097176
  21.5 1.6 %copy-done.2 = bf16[16,256,256]{2,1,0:T(8,128)(2,1)S(1)} copy-done((bf16[16,256,256]{2,1,0:T(8,128)(2,1)S(1)}, bf16[16,256,256]{2,1,0:T(8,128)(2,1)}, u32[]{:S(2)}) %copy-start.2) | copy-done | bytes 2097176
  23.1 1.4 %mix.1 = bf16[8,32,256]{2,1,0:T(8,128)(2,1)} custom-call(bf16[8,34,256]{2,1,0:T(8,128)(2,1)S(1)} %all_to_all.20.r_ref.refs_0_, bf16[16,256,256]{2,1,0:T(8,128)(2,1)S(1)} %copy-done, bf16[16,256,256]{2,1,0:T(8,128)(2,1)S(1)} %copy-done.2), custom_call_target="tpu_custom_call" | custom-call | tf_op jit(solution)/shard_map/mix/pallas_call | solution.py:392
  24.5 3.4 %all-to-all-start.1 = ((bf16[8,32,256]{2,1,0:T(8,128)(2,1)}), bf16[8,32,256]{2,1,0:T(8,128)(2,1)S(1)}, u32[]{:S(2)}, u32[]{:S(2)}) async-start(bf16[8,32,256]{2,1,0:T(8,128)(2,1)} %mix.1), calls=%async_computation.1 | async-start | bytes 262144 | tf_op jit(solution)/shard_map/all_to_all | solution.py:381
  27.8 0.0 collective-permute-done.refs_2_
  27.9 0.0 copy-start.10
  27.9 0.1 collective-permute-start.1
  27.9 0.5 collective-permute-start.2
  28.4 6.7 %all-to-all-done.1 = bf16[8,32,256]{2,1,0:T(8,128)(2,1)S(1)} async-done(((bf16[8,32,256]{2,1,0:T(8,128)(2,1)}), bf16[8,32,256]{2,1,0:T(8,128)(2,1)S(1)}, u32[]{:S(2)}, u32[]{:S(2)}) %all-to-all-start.1) | async-done | bytes 131104 | tf_op jit(solution)/shard_map/all_to_all | solution.py:381
  35.1 0.0 collective-permute-done.2.refs_3_
  35.2 0.6 copy-done.17
  35.8 0.1 copy-done.12
  35.8 0.0 copy-done.14
  35.9 8.1 %layer.1 = (bf16[2048,256]{1,0:T(8,128)(2,1)}, bf16[2048,256]{1,0:T(8,128)(2,1)}, bf16[8,34,256]{2,1,0:T(8,128)(2,1)}, f32[8,256]{1,0:T(8,128)}) custom-call(bf16[8,34,256]{2,1,0:T(8,128)(2,1)} %copy-done.5, bf16[8,34,256]{2,1,0:T(8,128)(2,1)} %copy-done.12, bf16[8,34,256]{2,1,0:T(8,128)(2,1)} %copy-done.10, bf16[8,34,256]{2,1,0:T(8,128)(2,1)} %copy-done.14, ...), custom_call_target="tpu_custom_call" | custom-call | tf_op jit(solution)/shard_map/layer/pallas_call | solution.py:417
  44.0 0.0 copy-start.6
  44.0 0.0 copy-start.11
  44.1 11.0 %all_to_all.21.r_ref.refs_0_.refs_4_ = bf16[8,34,256]{2,1,0:T(8,128)(2,1)S(1)} all-to-all(bf16[8,34,256]{2,1,0:T(8,128)(2,1)} %get-tuple-element.17), channel_id=1, replica_groups=mesh['len'=8,'pipe'=4] {'len'}, dimensions={0} | all-to-all | bytes 278528 | tf_op jit(solution)/shard_map/all_to_all | solution.py:381
  55.1 0.5 collective-permute-start.3
  55.6 1.6 %copy-done.3 = bf16[16,256,256]{2,1,0:T(8,128)(2,1)S(1)} copy-done((bf16[16,256,256]{2,1,0:T(8,128)(2,1)S(1)}, bf16[16,256,256]{2,1,0:T(8,128)(2,1)}, u32[]{:S(2)}) %copy-start.3) | copy-done | bytes 2097176
  57.2 1.9 %mix_grad.1 = bf16[8,32,256]{2,1,0:T(8,128)(2,1)} custom-call(bf16[8,34,256]{2,1,0:T(8,128)(2,1)S(1)} %all_to_all.21.r_ref.refs_0_.refs_4_, bf16[16,256,256]{2,1,0:T(8,128)(2,1)S(1)} %copy-done.1, bf16[16,256,256]{2,1,0:T(8,128)(2,1)S(1)} %copy-done.3), custom_call_target="tpu_custom_call" | custom-call | tf_op jit(solution)/shard_map/mix_grad/pallas_call | solution.py:392
  59.1 3.4 %all-to-all-start.3 = ((bf16[8,32,256]{2,1,0:T(8,128)(2,1)}), bf16[8,32,256]{2,1,0:T(8,128)(2,1)S(1)}, u32[]{:S(2)}, u32[]{:S(2)}) async-start(bf16[8,32,256]{2,1,0:T(8,128)(2,1)} %mix_grad.1), calls=%async_computation.3 | async-start | bytes 262144 | tf_op jit(solution)/shard_map/all_to_all | solution.py:381
  62.5 0.1 collective-permute-start.4
  62.6 0.5 collective-permute-start.5
  63.1 0.9 %collective-permute-done.4.refs_1_.refs_5_ = bf16[8,34,256]{2,1,0:T(8,128)(2,1)S(1)} collective-permute-done((bf16[8,34,256]{2,1,0:T(8,128)(2,1)S(1)}, bf16[8,34,256]{2,1,0:T(8,128)(2,1)S(1)}, u32[]{:S(2)}, u32[]{:S(2)}) %collective-permute-start.4) | collective-permute-done | bytes 139296 | tf_op jit(solution)/shard_map/ppermute | solution.py:384
  64.0 0.2 collective-permute-done.5.refs_3_.refs_7_
  64.2 4.0 %weight_grad.1 = (f32[16,256,256]{2,1,0:T(8,128)}, f32[16,256,256]{2,1,0:T(8,128)}) custom-call(bf16[8,34,256]{2,1,0:T(8,128)(2,1)S(1)} %copy-done.6, bf16[8,34,256]{2,1,0:T(8,128)(2,1)S(1)} %copy-done.13, bf16[8,34,256]{2,1,0:T(8,128)(2,1)S(1)} %copy-done.11, bf16[8,34,256]{2,1,0:T(8,128)(2,1)S(1)} %copy-done.15, ...), custom_call_target="tpu_custom_call" | custom-call | tf_op jit(solution)/shard_map/weight_grad/pallas_call | solution.py:448
  68.2 1.5 %all-to-all-done.3 = bf16[8,32,256]{2,1,0:T(8,128)(2,1)S(1)} async-done(((bf16[8,32,256]{2,1,0:T(8,128)(2,1)}), bf16[8,32,256]{2,1,0:T(8,128)(2,1)S(1)}, u32[]{:S(2)}, u32[]{:S(2)}) %all-to-all-start.3) | async-done | bytes 131104 | tf_op jit(solution)/shard_map/all_to_all | solution.py:381
  69.8 0.6 copy-done.16
  70.4 4.7 %input_grad.1 = bf16[2048,256]{1,0:T(8,128)(2,1)} custom-call(bf16[8,34,256]{2,1,0:T(8,128)(2,1)} %copy-done.4, bf16[8,34,256]{2,1,0:T(8,128)(2,1)} %copy-done.8, bf16[8,34,256]{2,1,0:T(8,128)(2,1)} %copy-done.7, bf16[8,34,256]{2,1,0:T(8,128)(2,1)} %copy-done.9, bf16[2048,256]{1,0:T(8,128)(2,1)} %get-tuple-element.20.refs_4_, ...), custom_call_target="tpu_custom_call" | custom-call | tf_op jit(solution)/shard_map/input_grad/pallas_call | solution.py:459
  (28 shorter events, 0.1 us)
Async XLA Ops:
  18.4 16.7 %copy-start.5 = (bf16[8,34,256]{2,1,0:T(8,128)(2,1)}, bf16[8,34,256]{2,1,0:T(8,128)(2,1)S(1)}, u32[]{:S(2)}) copy-start(bf16[8,34,256]{2,1,0:T(8,128)(2,1)S(1)} %all_to_all.20.r_ref.refs_0_) | copy-start | bytes 417796
  18.4 9.4 %collective-permute-start = (bf16[8,34,256]{2,1,0:T(8,128)(2,1)S(1)}, bf16[8,34,256]{2,1,0:T(8,128)(2,1)S(1)}, u32[]{:S(2)}, u32[]{:S(2)}) collective-permute-start(bf16[8,34,256]{2,1,0:T(8,128)(2,1)S(1)} %all_to_all.20.r_ref.refs_0_), channel_id=1, source_target_pairs={{0,2},{1,3},{2,0},{3,1},{4,6},{5,7},{6,4},{7,5},{8,10},{9,11},{10,... | collective-permute-start | bytes 417800 | tf_op jit(solution)/shard_map/ppermute | solution.py:384
  19.9 1.6 %copy-start = (bf16[16,256,256]{2,1,0:T(8,128)(2,1)S(1)}, bf16[16,256,256]{2,1,0:T(8,128)(2,1)}, u32[]{:S(2)}) copy-start(bf16[16,256,256]{2,1,0:T(8,128)(2,1)} %real_ref.3) | copy-start | bytes 6291460
  21.5 1.6 %copy-start.2 = (bf16[16,256,256]{2,1,0:T(8,128)(2,1)S(1)}, bf16[16,256,256]{2,1,0:T(8,128)(2,1)}, u32[]{:S(2)}) copy-start(bf16[16,256,256]{2,1,0:T(8,128)(2,1)} %imag_ref.3) | copy-start | bytes 6291460
  23.1 32.5 %copy-start.1 = (bf16[16,256,256]{2,1,0:T(8,128)(2,1)S(1)}, bf16[16,256,256]{2,1,0:T(8,128)(2,1)}, u32[]{:S(2)}) copy-start(bf16[16,256,256]{2,1,0:T(8,128)(2,1)} %real_ref.3) | copy-start | bytes 6291460
  24.5 10.7 %all-to-all-start.1 = ((bf16[8,32,256]{2,1,0:T(8,128)(2,1)}), bf16[8,32,256]{2,1,0:T(8,128)(2,1)S(1)}, u32[]{:S(2)}, u32[]{:S(2)}) async-start(bf16[8,32,256]{2,1,0:T(8,128)(2,1)} %mix.1), calls=%async_computation.1 | async-start | bytes 262144 | tf_op jit(solution)/shard_map/all_to_all | solution.py:381
  27.9 7.3 %copy-start.10 = (bf16[8,34,256]{2,1,0:T(8,128)(2,1)}, bf16[8,34,256]{2,1,0:T(8,128)(2,1)S(1)}, u32[]{:S(2)}) copy-start(bf16[8,34,256]{2,1,0:T(8,128)(2,1)S(1)} %collective-permute-done.refs_2_) | copy-start | bytes 417796
  27.9 7.3 %collective-permute-start.1 = (bf16[8,34,256]{2,1,0:T(8,128)(2,1)S(1)}, bf16[8,34,256]{2,1,0:T(8,128)(2,1)S(1)}, u32[]{:S(2)}, u32[]{:S(2)}) collective-permute-start(bf16[8,34,256]{2,1,0:T(8,128)(2,1)S(1)} %all_to_all.20.r_ref.refs_0_), channel_id=1, source_target_pairs={{0,1},{1,0},{2,3},{3,2},{4,5},{5,4},{6,7},{7,6},{8,9},{9,8},{10,11... | collective-permute-start | bytes 417800 | tf_op jit(solution)/shard_map/ppermute | solution.py:384
  27.9 7.2 %collective-permute-start.2 = (bf16[8,34,256]{2,1,0:T(8,128)(2,1)S(1)}, bf16[8,34,256]{2,1,0:T(8,128)(2,1)S(1)}, u32[]{:S(2)}, u32[]{:S(2)}) collective-permute-start(bf16[8,34,256]{2,1,0:T(8,128)(2,1)S(1)} %collective-permute-done.refs_2_), channel_id=1, source_target_pairs={{0,1},{1,0},{2,3},{3,2},{4,5},{5,4},{6,7},{7,6},{8,9},{9,8},{10,11... | collective-permute-start | bytes 417800 | tf_op jit(solution)/shard_map/ppermute | solution.py:384
  35.1 0.6 copy-start.17
  35.1 0.7 copy-start.12
  35.1 0.7 copy-start.14
  44.0 20.2 %copy-start.6 = (bf16[8,34,256]{2,1,0:T(8,128)(2,1)S(1)}, bf16[8,34,256]{2,1,0:T(8,128)(2,1)}, u32[]{:S(2)}) copy-start(bf16[8,34,256]{2,1,0:T(8,128)(2,1)} %copy-done.5) | copy-start | bytes 417796
  44.0 20.1 %copy-start.11 = (bf16[8,34,256]{2,1,0:T(8,128)(2,1)S(1)}, bf16[8,34,256]{2,1,0:T(8,128)(2,1)}, u32[]{:S(2)}) copy-start(bf16[8,34,256]{2,1,0:T(8,128)(2,1)} %copy-done.10) | copy-start | bytes 417796
  55.1 14.7 %copy-start.4 = (bf16[8,34,256]{2,1,0:T(8,128)(2,1)}, bf16[8,34,256]{2,1,0:T(8,128)(2,1)S(1)}, u32[]{:S(2)}) copy-start(bf16[8,34,256]{2,1,0:T(8,128)(2,1)S(1)} %all_to_all.21.r_ref.refs_0_.refs_4_) | copy-start | bytes 417796
  55.1 7.4 %collective-permute-start.3 = (bf16[8,34,256]{2,1,0:T(8,128)(2,1)S(1)}, bf16[8,34,256]{2,1,0:T(8,128)(2,1)S(1)}, u32[]{:S(2)}, u32[]{:S(2)}) collective-permute-start(bf16[8,34,256]{2,1,0:T(8,128)(2,1)S(1)} %all_to_all.21.r_ref.refs_0_.refs_4_), channel_id=1, source_target_pairs={{0,2},{1,3},{2,0},{3,1},{4,6},{5,7},{6,4},{7,5},{8,10},{9,11},{10,... | collective-permute-start | bytes 417800 | tf_op jit(solution)/shard_map/ppermute | solution.py:384
  55.6 1.6 %copy-start.3 = (bf16[16,256,256]{2,1,0:T(8,128)(2,1)S(1)}, bf16[16,256,256]{2,1,0:T(8,128)(2,1)}, u32[]{:S(2)}) copy-start(bf16[16,256,256]{2,1,0:T(8,128)(2,1)} %imag_ref.3) | copy-start | bytes 6291460
  57.2 7.0 %copy-start.13 = (bf16[8,34,256]{2,1,0:T(8,128)(2,1)S(1)}, bf16[8,34,256]{2,1,0:T(8,128)(2,1)}, u32[]{:S(2)}) copy-start(bf16[8,34,256]{2,1,0:T(8,128)(2,1)} %copy-done.12) | copy-start | bytes 417796
  57.2 7.0 %copy-start.15 = (bf16[8,34,256]{2,1,0:T(8,128)(2,1)S(1)}, bf16[8,34,256]{2,1,0:T(8,128)(2,1)}, u32[]{:S(2)}) copy-start(bf16[8,34,256]{2,1,0:T(8,128)(2,1)} %copy-done.14) | copy-start | bytes 417796
  59.1 10.7 %all-to-all-start.3 = ((bf16[8,32,256]{2,1,0:T(8,128)(2,1)}), bf16[8,32,256]{2,1,0:T(8,128)(2,1)S(1)}, u32[]{:S(2)}, u32[]{:S(2)}) async-start(bf16[8,32,256]{2,1,0:T(8,128)(2,1)} %mix_grad.1), calls=%async_computation.3 | async-start | bytes 262144 | tf_op jit(solution)/shard_map/all_to_all | solution.py:381
  62.5 7.3 %copy-start.7 = (bf16[8,34,256]{2,1,0:T(8,128)(2,1)}, bf16[8,34,256]{2,1,0:T(8,128)(2,1)S(1)}, u32[]{:S(2)}) copy-start(bf16[8,34,256]{2,1,0:T(8,128)(2,1)S(1)} %collective-permute-done.3.refs_2_.refs_6_) | copy-start | bytes 417796
  62.5 1.5 %collective-permute-start.4 = (bf16[8,34,256]{2,1,0:T(8,128)(2,1)S(1)}, bf16[8,34,256]{2,1,0:T(8,128)(2,1)S(1)}, u32[]{:S(2)}, u32[]{:S(2)}) collective-permute-start(bf16[8,34,256]{2,1,0:T(8,128)(2,1)S(1)} %all_to_all.21.r_ref.refs_0_.refs_4_), channel_id=1, source_target_pairs={{0,1},{1,0},{2,3},{3,2},{4,5},{5,4},{6,7},{7,6},{8,9},{9,8},{10,11... | collective-permute-start | bytes 417800 | tf_op jit(solution)/shard_map/ppermute | solution.py:384
  62.6 1.6 %collective-permute-start.5 = (bf16[8,34,256]{2,1,0:T(8,128)(2,1)S(1)}, bf16[8,34,256]{2,1,0:T(8,128)(2,1)S(1)}, u32[]{:S(2)}, u32[]{:S(2)}) collective-permute-start(bf16[8,34,256]{2,1,0:T(8,128)(2,1)S(1)} %collective-permute-done.3.refs_2_.refs_6_), channel_id=1, source_target_pairs={{0,1},{1,0},{2,3},{3,2},{4,5},{5,4},{6,7},{7,6},{8,9},{9,8},{10,11... | collective-permute-start | bytes 417800 | tf_op jit(solution)/shard_map/ppermute | solution.py:384
  63.9 5.8 %copy-start.8 = (bf16[8,34,256]{2,1,0:T(8,128)(2,1)}, bf16[8,34,256]{2,1,0:T(8,128)(2,1)S(1)}, u32[]{:S(2)}) copy-start(bf16[8,34,256]{2,1,0:T(8,128)(2,1)S(1)} %collective-permute-done.4.refs_1_.refs_5_) | copy-start | bytes 417796
  64.2 5.6 %copy-start.9 = (bf16[8,34,256]{2,1,0:T(8,128)(2,1)}, bf16[8,34,256]{2,1,0:T(8,128)(2,1)S(1)}, u32[]{:S(2)}) copy-start(bf16[8,34,256]{2,1,0:T(8,128)(2,1)S(1)} %collective-permute-done.5.refs_3_.refs_7_) | copy-start | bytes 417796
  69.7 0.7 copy-start.16

commit v5 on v3

v5 whole, which is shorter than its diff:
```python
import functools
import math

import jax
import jax.numpy as jnp
import ml_dtypes
import numpy as np
from jax import lax
from jax.experimental import pallas as pl
from jax.experimental.pallas import tpu as pltpu
from jax.sharding import PartitionSpec as P

COUPLING = 0.125
TILE = 256
LANES = 128
GELU_S = math.sqrt(2.0 / math.pi)
GELU_C = 0.044715
VMEM = pl.BlockSpec(memory_space=pltpu.VMEM)
SMEM = pl.BlockSpec(memory_space=pltpu.SMEM)
HBM = pl.BlockSpec(memory_space=pltpu.HBM)
MIB = 1024 * 1024


def forward_table(cell_count, mode_count, groups):
    product_index = np.arange(mode_count)[:, None] * np.arange(cell_count)[None, :] % cell_count
    angles = product_index.astype(np.float32) * np.float32(2.0 * math.pi / cell_count)
    norm_scale = np.float32(1.0 / math.sqrt(cell_count))
    cosine = (np.cos(angles) * norm_scale).reshape(groups, -1, cell_count)
    sine = (np.sin(angles) * norm_scale).reshape(groups, -1, cell_count)
    table = np.concatenate([cosine, -sine], axis=1).reshape(2 * mode_count, cell_count)
    return table.astype(ml_dtypes.bfloat16)


def dot(left, right, left_dim=1, right_dim=0):
    return lax.dot_general(
        left,
        right,
        (((left_dim,), (right_dim,)), ((), ())),
        preferred_element_type=jnp.float32,
    )


def put(ref, at, value):
    for lane in range(ref.shape[0]):
        ref[lane, at, :] = value[:, lane * LANES : (lane + 1) * LANES]


def take(ref, at):
    return jnp.concatenate([ref[lane, at, :] for lane in range(ref.shape[0])], axis=1)


def spectrum_kernel(x_ref, f_ref, msg_ref):
    groups, rows = msg_ref.shape[0], msg_ref.shape[1]
    tiles, all_rows, tile = f_ref.shape
    cells, channels = x_ref.shape
    span = all_rows // groups
    total = None
    for step in range(tiles):
        part = dot(f_ref[step], x_ref[step * tile : (step + 1) * tile, :])
        total = part if total is None else total + part
    spectra = total.astype(jnp.bfloat16)
    ends = extra_rows(x_ref[0:1, :], x_ref[cells - 1 : cells, :], rows - span, channels)
    for at in range(groups):
        msg_ref[at, 0:span, :] = spectra[at * span : (at + 1) * span]
        msg_ref[at, span:rows, :] = ends


def extra_rows(first, second, count, channels):
    parts = [first.astype(jnp.float32), second.astype(jnp.float32)]
    if count > 2:
        parts.append(jnp.zeros((count - 2, channels), jnp.float32))
    return jnp.concatenate(parts, axis=0).astype(jnp.bfloat16)


def mix_kernel(backward, r_ref, real_ref, imag_ref, *refs):
    x_ref, y_ref = refs[-2:]
    groups, modes = r_ref.shape[0], real_ref.shape[0]
    span = 2 * modes
    if backward:
        early_ref, out_ref, copied_ref, sem = refs[:4]
        copy = pltpu.make_async_copy(early_ref, copied_ref, sem)
        copy.start()
    else:
        out_ref = refs[0]
    for source in range(groups):
        put(x_ref, pl.ds(source * span, span), r_ref[source, 0:span, :].astype(jnp.float32))
    for mode in range(modes):
        first = pl.ds(mode, groups, stride=span)
        second = pl.ds(modes + mode, groups, stride=span)
        rows = jnp.concatenate([take(x_ref, first), take(x_ref, second)], axis=0).astype(
            jnp.bfloat16
        )
        dim = 1 if backward else 0
        by_real = dot(rows, real_ref[mode], 1, dim)
        by_imag = dot(rows, imag_ref[mode], 1, dim)
        if backward:
            put(y_ref, first, by_real[:groups] + by_imag[groups:])
            put(y_ref, second, by_real[groups:] - by_imag[:groups])
        else:
            put(y_ref, first, by_real[:groups] - by_imag[groups:])
            put(y_ref, second, by_imag[:groups] + by_real[groups:])
    for source in range(groups):
        rows = take(y_ref, pl.ds(source * span, span)).astype(jnp.bfloat16)
        out_ref[source, 0:span, :] = rows
        if out_ref.shape[1] > span:
            out_ref[source, span:, :] = jnp.zeros((2, rows.shape[1]), jnp.bfloat16)
    if backward:
        copy.wait()


def own_pipe(pipes):
    return lax.axis_index("len") * pipes + lax.axis_index("pipe")


def two_rows(first, second, channels):
    return jnp.concatenate([first, second, jnp.zeros((6, channels), jnp.float32)], axis=0)


def junction_sums(pipes, msgs, inlet_ref, outlet_ref, both):
    groups, rows, channels = msgs[0].shape
    column = lax.axis_index("pipe")
    me = own_pipe(pipes)
    owns = inlet_ref[me], outlet_ref[me]
    is_first = lax.broadcasted_iota(jnp.int32, (2, channels), 0) == 0

    def matches(pipe, junction):
        first = (inlet_ref[pipe] == junction).astype(jnp.float32)
        last = (outlet_ref[pipe] == junction).astype(jnp.float32)
        return first + last if both else jnp.where(is_first, first, last)

    def add(group, carried):
        for step in range(pipes):
            pipe = group * pipes + lax.bitwise_xor(column, step)
            ends = msgs[step][group, rows - 2 : rows, :].astype(jnp.float32)
            carried = tuple(
                total + ends * matches(pipe, own) for total, own in zip(carried, owns)
            )
        return carried

    zero = jnp.zeros((2, channels), jnp.float32)
    totals = lax.fori_loop(0, groups, add, (zero, zero), unroll=min(groups, 8))
    return two_rows(
        jnp.sum(totals[0], axis=0, keepdims=True),
        jnp.sum(totals[1], axis=0, keepdims=True),
        channels,
    )


def junction_forward_kernel(pipes, *refs):
    msgs, (inlet_ref, outlet_ref, weight_ref, bias_ref, cond_ref, slope_ref) = (
        refs[:pipes],
        refs[pipes:],
    )
    sums = junction_sums(pipes, msgs, inlet_ref, outlet_ref, False)
    act = dot(sums.astype(jnp.bfloat16), weight_ref[...]) + bias_ref[...]
    sigmoid_part = jax.nn.sigmoid(act)
    junc_rows = (act * sigmoid_part).astype(jnp.bfloat16).astype(jnp.float32)
    cond_ref[...] = COUPLING * (junc_rows[0:1] + junc_rows[1:2])
    slope_ref[...] = sigmoid_part * (1.0 + act * (1.0 - sigmoid_part))


def junction_backward_kernel(pipes, *refs):
    msgs, (inlet_ref, outlet_ref, weight_ref, slope_ref, rows_ref) = refs[:pipes], refs[pipes:]
    junc_grad = COUPLING * junction_sums(pipes, msgs, inlet_ref, outlet_ref, True)
    act_grad = (junc_grad * slope_ref[...]).astype(jnp.bfloat16)
    sums_grad = dot(act_grad, weight_ref[...], 1, 1).astype(jnp.bfloat16)
    rows_ref[...] = sums_grad.astype(jnp.float32)


def started(copies):
    for copy in copies:
        copy.start()
    return copies


def wait(copies):
    for copy in copies:
        copy.wait()


def layer_kernel(
    x_ref,
    cot_ref,
    f_ref,
    ft_ref,
    weight_ref,
    bias_ref,
    cond_ref,
    modes_ref,
    out_ref,
    total_ref,
    msg_ref,
    acc_ref,
):
    channels = x_ref.shape[1]
    groups, rows = msg_ref.shape[0], msg_ref.shape[1]
    tiles, all_rows, tile = f_ref.shape
    span = all_rows // groups
    row = lax.broadcasted_iota(jnp.int32, (all_rows, channels), 0)
    doubled = jnp.where((row == 0) | (row == span // 2), 1.0, 2.0).astype(jnp.float32)
    modes = jnp.concatenate(
        [modes_ref[at, 0:span, :].astype(jnp.float32) for at in range(groups)], axis=0
    )
    modes = (modes * doubled).astype(jnp.bfloat16)
    weight = weight_ref[...]
    cond = cond_ref[...]
    bias = bias_ref[...]
    for step in range(tiles):
        at = pl.ds(step * tile, tile)
        spectral = dot(ft_ref[at, :], modes)
        pre = (spectral + cond).astype(jnp.bfloat16).astype(jnp.float32)
        summed = dot(x_ref[at, :], weight) + bias + pre
        square = summed * summed
        half = 0.5 + 0.5 * jnp.tanh(summed * (GELU_S + (GELU_S * GELU_C) * square))
        result = summed * half
        out_ref[at, :] = result.astype(jnp.bfloat16)
        slope = half + result * (1.0 - half) * (2.0 * GELU_S + (6.0 * GELU_S * GELU_C) * square)
        total = (cot_ref[at, :].astype(jnp.float32) * slope).astype(jnp.bfloat16)
        total_ref[at, :] = total
        part = dot(f_ref[step], total)
        if step == 0:
            acc_ref[...] = part
        else:
            acc_ref[...] += part
    grad_cond = acc_ref[0:1, :] * (1.0 / f_ref[0, 0:1, 0:1].astype(jnp.float32))
    high = grad_cond.astype(jnp.bfloat16).astype(jnp.float32)
    extra = extra_rows(high, grad_cond - high, rows - span, channels)
    grad_spec = (acc_ref[...] * doubled).astype(jnp.bfloat16)
    for at in range(groups):
        msg_ref[at, 0:span, :] = grad_spec[at * span : (at + 1) * span]
        msg_ref[at, span:rows, :] = extra


def input_grad_kernel(
    total_ref, ft_ref, weight_ref, rows_ref, modes_ref, out_ref, tiles_ref, sems
):
    modes = modes_ref[...]
    weight = weight_ref[...]
    tiles, tile, channels = tiles_ref.shape
    row = lax.broadcasted_iota(jnp.int32, (tile, channels), 0)
    going = []
    for step in range(tiles):
        at = pl.ds(step * tile, tile)
        grad_cells = dot(ft_ref[at, :], modes)
        if step == 0:
            grad_cells = grad_cells + jnp.where(row == 0, rows_ref[0:1, :], 0.0)
        if step == tiles - 1:
            grad_cells = grad_cells + jnp.where(row == tile - 1, rows_ref[1:2, :], 0.0)
        spread = grad_cells.astype(jnp.bfloat16).astype(jnp.float32)
        local = dot(total_ref[at, :], weight, 1, 1)
        tiles_ref[step] = (local + spread).astype(jnp.bfloat16)
        going += started(
            [pltpu.make_async_copy(tiles_ref.at[step], out_ref.at[at], sems.at[step])]
        )
    wait(going)


def weight_grad_kernel(pipes, modes, *refs):
    fields, grads = refs[:pipes], refs[pipes : 2 * pipes]
    real_out, imag_out, x_ref, g_ref, real_ref, imag_ref, sems = refs[2 * pipes :]
    groups = fields[0].shape[0]
    span = 2 * modes
    for step in range(pipes):
        for source in range(groups):
            at = pl.ds((step * groups + source) * span, span)
            put(x_ref, at, fields[step][source, 0:span, :].astype(jnp.float32))
            put(g_ref, at, grads[step][source, 0:span, :].astype(jnp.float32))
    count = pipes * groups
    going = []
    for mode in range(modes):
        first = pl.ds(mode, count, stride=span)
        second = pl.ds(modes + mode, count, stride=span)
        a, b = take(x_ref, first), take(x_ref, second)
        u, v = take(g_ref, first), take(g_ref, second)
        left = jnp.concatenate([a, b], axis=0).astype(jnp.bfloat16)
        real_ref[mode] = dot(left, jnp.concatenate([u, v], axis=0).astype(jnp.bfloat16), 0, 0)
        imag_ref[mode] = dot(left, jnp.concatenate([v, -u], axis=0).astype(jnp.bfloat16), 0, 0)
        going += started(
            [
                pltpu.make_async_copy(real_ref.at[mode], real_out.at[mode], sems.at[mode, 0]),
                pltpu.make_async_copy(imag_ref.at[mode], imag_out.at[mode], sems.at[mode, 1]),
            ]
        )
    wait(going)


def rows_of(count, channels):
    return pltpu.VMEM((channels // LANES, count, LANES), jnp.float32)


def call(kernel, outs, specs, scratch=(), out_specs=None, name=None, limit=8, busy=1):
    return pl.pallas_call(
        kernel,
        out_shape=outs,
        in_specs=specs,
        out_specs=out_specs if out_specs is not None else [VMEM] * len(outs),
        scratch_shapes=list(scratch),
        compiler_params=pltpu.CompilerParams(vmem_limit_bytes=limit * MIB),
        cost_estimate=pl.CostEstimate(
            flops=busy * 1_000_000_000, bytes_accessed=busy * MIB, transcendentals=0
        ),
        name=name,
    )


def body(
    inputs,
    cotangent,
    point_weight,
    point_bias,
    spec_real,
    spec_imag,
    junc_weight,
    junc_bias,
    inlet_ids,
    outlet_ids,
):
    per_dev, cell_count, channels = inputs.shape
    assert per_dev == 1
    groups, pipes = lax.axis_size("len"), lax.axis_size("pipe")
    assert pipes == 4
    modes = spec_real.shape[0]
    span = 2 * modes
    all_rows = span * groups
    tiles = cell_count // TILE
    table = forward_table(cell_count, modes * groups, groups)
    tiled = table.reshape(all_rows, tiles, TILE).transpose(1, 0, 2)
    f_table = jnp.asarray(np.ascontiguousarray(tiled))
    ft_table = jnp.asarray(np.ascontiguousarray(table.T))
    field = inputs.reshape(cell_count, channels)
    cot = cotangent.reshape(cell_count, channels)
    bias_row = point_bias.reshape(1, channels)
    junc_bias_row = junc_bias.reshape(1, channels)
    shape = jax.ShapeDtypeStruct
    bf16, f32 = jnp.bfloat16, jnp.float32
    message = shape((groups, span + 2, channels), bf16)
    chunks = shape((groups, span, channels), bf16)
    dma = pltpu.SemaphoreType.DMA

    def exchange(value):
        return lax.all_to_all(value, "len", split_axis=0, concat_axis=0, tiled=True)

    def swap(value, step):
        return lax.ppermute(value, "pipe", [(i, i ^ step) for i in range(pipes)])

    def gather(own, behind):
        across = swap(own, 2)
        tied, tied_across, _ = lax.optimization_barrier((own, across, behind))
        return [own, swap(tied, 1), across, swap(tied_across, 1)]

    def mix(backward, value, *early):
        return call(
            functools.partial(mix_kernel, backward),
            [chunks, early[0]] if backward else [message],
            [VMEM] * (4 if backward else 3),
            ([dma] if backward else []) + [rows_of(all_rows, channels)] * 2,
            out_specs=[VMEM, HBM] if backward else [VMEM],
            name="mix_grad" if backward else "mix",
            busy=12,
        )(value, spec_real, spec_imag, *early)

    (sent,) = call(spectrum_kernel, [message], [VMEM] * 2, name="spectrum", busy=12)(
        field, f_table
    )
    received = exchange(sent)
    (mixed,) = mix(False, received)
    returned = exchange(mixed)
    fields = gather(received, mixed)
    cond, slope = call(
        functools.partial(junction_forward_kernel, pipes),
        [shape((1, channels), f32), shape((8, channels), f32)],
        [VMEM] * pipes + [SMEM] * 2 + [VMEM] * 2,
        name="junction",
    )(*fields, inlet_ids, outlet_ids, junc_weight, junc_bias_row)
    early, total, sent = call(
        layer_kernel,
        [shape(field.shape, bf16), shape(field.shape, bf16), message],
        [VMEM] * 8,
        [pltpu.VMEM((all_rows, channels), f32)],
        name="layer",
        busy=12,
    )(field, cot, f_table, ft_table, point_weight, bias_row, cond, returned)
    received = exchange(sent)
    mixed, outputs = mix(True, received, early)
    returned = exchange(mixed).reshape(all_rows, channels)
    grads = gather(received, mixed)
    (rows,) = call(
        functools.partial(junction_backward_kernel, pipes),
        [shape((8, channels), f32)],
        [VMEM] * pipes + [SMEM] * 2 + [VMEM] * 2,
        name="junction_grad",
    )(*grads, inlet_ids, outlet_ids, junc_weight, slope)
    big = shape((modes, channels, channels), f32)
    grad_real, grad_imag = call(
        functools.partial(weight_grad_kernel, pipes, modes),
        [big, big],
        [VMEM] * (2 * pipes),
        [rows_of(pipes * all_rows, channels)] * 2
        + [pltpu.VMEM(big.shape, f32)] * 2
        + [dma((modes, 2))],
        out_specs=[HBM, HBM],
        name="weight_grad",
        limit=16,
    )(*fields, *grads)
    (grad_inputs,) = call(
        input_grad_kernel,
        [shape(field.shape, bf16)],
        [VMEM] * 5,
        [pltpu.VMEM((tiles, TILE, channels), bf16), dma((tiles,))],
        out_specs=[HBM],
        name="input_grad",
    )(total, ft_table, point_weight, rows, returned)
    return (
        outputs.reshape(inputs.shape),
        grad_inputs.reshape(inputs.shape),
        grad_real,
        grad_imag,
    )


def solution(mesh):
    placed = (
        P(("len", "pipe"), None, None),
        P(("len", "pipe"), None, None),
        P(),
        P(),
        P("len", None, None),
        P("len", None, None),
        P(),
        P(),
        P(),
        P(),
    )
    return jax.shard_map(
        body,
        mesh=mesh,
        in_specs=placed,
        out_specs=(
            P(("len", "pipe"), None, None),
            P(("len", "pipe"), None, None),
            P("len", None, None),
            P("len", None, None),
        ),
        check_vma=False,
    )
```

time: 88 us -> 78.1 us (0.89)
  blocking collectives: 15.2 us -> 26.4 us
  starting transfers between devices: 19.3 us -> 9.95 us
  waiting for transfers between devices: 18.4 us -> 12.6 us
  Pallas kernels: 18.3 us -> 14.9 us
  local copies, waits for them, and re-layouts: 15.1 us -> 12.7 us
    all_to_all x1 -> x2, blocking collectives: 15.2 us -> 26.4 us  [exchange(): return lax.all_to_all(value, 'len', split_axis=0, concat_axis=0, tiled=True)]
    all_to_all x3 -> x2, starting transfers between devices: 11.8 us -> 6.78 us  [exchange(): return lax.all_to_all(value, 'len', split_axis=0, concat_axis=0, tiled=True)]
    ppermute x12 -> x6, waiting for transfers between devices: 8.87 us -> 4.12 us  [swap(): return lax.ppermute(value, 'pipe', [(i, i ^ step) for i in range(pipes)])]
    ppermute x12 -> x6, starting transfers between devices: 7.5 us -> 3.17 us  [swap(): return lax.ppermute(value, 'pipe', [(i, i ^ step) for i in range(pipes)])]
    pallas_call x6 -> x5, Pallas kernels: 14.1 us -> 10.2 us  [the longest x1 4.92 us: body(): call(functools.partial(weight_grad_kernel, pipes, modes), [big, big], [VM...]
    unnamed x46 -> x48, local copies, waits for them, and re-layouts: 15.1 us -> 12.7 us
    all_to_all x3 -> x2, waiting for transfers between devices: 9.57 us -> 8.45 us  [exchange(): return lax.all_to_all(value, 'len', split_axis=0, concat_axis=0, tiled=True)]
  transfers between devices with their start and end apart: 15 -> 8, of which waited for: 5 -> 5; matrix products, arithmetic and copies ran while one was open for 0% -> 0% of each run, Pallas kernels for 11% -> 7%
where the time goes in v5:
time: 78.1 us; the launch traced here: 77.4 us
  blocking collectives  26.4 us (34%)
  Pallas kernels  14.9 us (19%)
  local copies, waits for them, and re-layouts  12.7 us (16%)
  waiting for transfers between devices  12.6 us (16%)
  starting transfers between devices  9.95 us (13%)
  between operations  0.81 us (1%)
    all_to_all x2, blocking collectives, exchange(): return lax.all_to_all(value, 'len', split_axis=0, concat_axis=0, tiled=True)  26.4 us
    unnamed x48, local copies, waits for them, and re-layouts  12.7 us
    all_to_all x2, waiting for transfers between devices, exchange(): return lax.all_to_all(value, 'len', split_axis=0, concat_axis=0, tiled=True)  8.45 us
    all_to_all x2, starting transfers between devices, exchange(): return lax.all_to_all(value, 'len', split_axis=0, concat_axis=0, tiled=True)  6.78 us
    pallas_call x1, Pallas kernels, body(): call(functools.partial(weight_grad_kernel, pipes, modes), [big, big], [VM...  4.92 us
    ppermute x6, waiting for transfers between devices, swap(): return lax.ppermute(value, 'pipe', [(i, i ^ step) for i in range(pipes)])  4.12 us
    pallas_call x2, Pallas kernels, mix(): call(functools.partial(mix_kernel, backward), [chunks, early[0]] if backw...  3.35 us
    ppermute x6, starting transfers between devices, swap(): return lax.ppermute(value, 'pipe', [(i, i ^ step) for i in range(pipes)])  3.17 us
  transfers between devices with their start and end apart: 8, of which 5 were waited for; matrix products, arithmetic and copies ran while one was open for 0% of the time, Pallas kernels for 7%

profile of v5, /device:TPU:0, one launch (start us, length us, event | category | flops | bytes accessed | tf_op | source)
XLA Modules:
  0.0 77.4 jit_solution(13817878344503482948)
XLA Ops:
  0.6 1.2 %copy-done.3 = bf16[1,2048,256]{2,1,0:T(8,128)(2,1)S(1)} copy-done((bf16[1,2048,256]{2,1,0:T(8,128)(2,1)S(1)}, bf16[1,2048,256]{2,1,0:T(8,128)(2,1)}, u32[]{:S(2)}) %copy-start.3) | copy-done | bytes 1048600
  1.9 1.2 %copy-done.20 = bf16[8,256,256]{2,1,0:T(8,128)(2,1)S(1)} copy-done((bf16[8,256,256]{2,1,0:T(8,128)(2,1)S(1)}, bf16[8,256,256]{2,1,0:T(8,128)(2,1)}, u32[]{:S(2)}) %copy-start.20) | copy-done | bytes 1048600
  3.5 14.9 %all_to_all.20.r_ref.refs_0_ = bf16[8,34,256]{2,1,0:T(8,128)(2,1)S(1)} all-to-all(bf16[8,34,256]{2,1,0:T(8,128)(2,1)S(1)} %spectrum.1), channel_id=1, replica_groups=mesh['len'=8,'pipe'=4] {'len'}, dimensions={0} | all-to-all | bytes 278528 | tf_op jit(solution)/shard_map/all_to_all | solution.py:341
  18.5 1.6 %collective-permute-start = (bf16[8,34,256]{2,1,0:T(8,128)(2,1)S(1)}, bf16[8,34,256]{2,1,0:T(8,128)(2,1)}, u32[]{:S(2)}, u32[]{:S(2)}) collective-permute-start(bf16[8,34,256]{2,1,0:T(8,128)(2,1)S(1)} %all_to_all.20.r_ref.refs_0_), channel_id=1, source_target_pairs={{0,2},{1,3},{2,0},{3,1},{4,6},{5,7},{6,4},{7,5},{8,10},{9,11},{10,... | collective-permute-start | bytes 417800 | tf_op jit(solution)/shard_map/ppermute | solution.py:344
  20.0 1.4 %mix.1 = bf16[8,34,256]{2,1,0:T(8,128)(2,1)} custom-call(bf16[8,34,256]{2,1,0:T(8,128)(2,1)S(1)} %all_to_all.20.r_ref.refs_0_, bf16[16,256,256]{2,1,0:T(8,128)(2,1)S(1)} %copy-done, bf16[16,256,256]{2,1,0:T(8,128)(2,1)S(1)} %copy-done.1), custom_call_target="tpu_custom_call" | custom-call | flops 12000000000 | bytes 12582912 | tf_op jit(solution)/shard_map/mix/pallas_call | solution.py:352
  21.4 3.4 %all-to-all-start.1 = ((bf16[8,34,256]{2,1,0:T(8,128)(2,1)}), bf16[8,34,256]{2,1,0:T(8,128)(2,1)S(1)}, u32[]{:S(2)}, u32[]{:S(2)}) async-start(bf16[8,34,256]{2,1,0:T(8,128)(2,1)} %mix.1), calls=%async_computation.1 | async-start | bytes 327680 | tf_op jit(solution)/shard_map/all_to_all | solution.py:341
  24.9 0.5 collective-permute-start.2
  25.4 0.9 %collective-permute-done.1.refs_1_ = bf16[8,34,256]{2,1,0:T(8,128)(2,1)S(1)} collective-permute-done((bf16[8,34,256]{2,1,0:T(8,128)(2,1)S(1)}, bf16[8,34,256]{2,1,0:T(8,128)(2,1)S(1)}, u32[]{:S(2)}, u32[]{:S(2)}) %collective-permute-start.1) | collective-permute-done | bytes 139296 | tf_op jit(solution)/shard_map/ppermute | solution.py:344
  26.3 0.4 collective-permute-done.2.refs_3_
  26.7 0.9 %copy-done.10 = bf16[256,256]{1,0:T(8,128)(2,1)S(1)} copy-done((bf16[256,256]{1,0:T(8,128)(2,1)S(1)}, bf16[256,256]{1,0:T(8,128)(2,1)}, u32[]{:S(2)}) %copy-start.10) | copy-done | bytes 131096
  27.6 1.3 %junction.1 = (f32[1,256]{1,0:T(1,128)S(1)}, f32[8,256]{1,0:T(8,128)S(1)}) custom-call(bf16[8,34,256]{2,1,0:T(8,128)(2,1)S(1)} %all_to_all.20.r_ref.refs_0_, bf16[8,34,256]{2,1,0:T(8,128)(2,1)S(1)} %collective-permute-done.1.refs_1_, bf16[8,34,256]{2,1,0:T(8,128)(2,1)} %collective-permute-done.refs_2_, ...), custom_call_target="tpu_custom_call" | custom-call | flops 1000000000 | bytes 1048576 | tf_op jit(solution)/shard_map/junction/pallas_call | solution.py:369
  28.9 0.7 copy-done.6
  29.6 0.7 copy-done.8
  30.3 2.0 %all-to-all-done.1.modes_ref = bf16[8,34,256]{2,1,0:T(8,128)(2,1)S(1)} async-done(((bf16[8,34,256]{2,1,0:T(8,128)(2,1)}), bf16[8,34,256]{2,1,0:T(8,128)(2,1)S(1)}, u32[]{:S(2)}, u32[]{:S(2)}) %all-to-all-start.1) | async-done | bytes 139296 | tf_op jit(solution)/shard_map/all_to_all | solution.py:341
  32.3 1.2 %copy-done.5 = bf16[1,2048,256]{2,1,0:T(8,128)(2,1)S(1)} copy-done((bf16[1,2048,256]{2,1,0:T(8,128)(2,1)S(1)}, bf16[1,2048,256]{2,1,0:T(8,128)(2,1)}, u32[]{:S(2)}) %copy-start.5) | copy-done | bytes 1048600
  33.5 0.9 %copy-done.12 = bf16[256,256]{1,0:T(8,128)(2,1)S(1)} copy-done((bf16[256,256]{1,0:T(8,128)(2,1)S(1)}, bf16[256,256]{1,0:T(8,128)(2,1)}, u32[]{:S(2)}) %copy-start.12) | copy-done | bytes 131096
  34.4 1.2 %copy-done.18 = bf16[2048,256]{1,0:T(8,128)(2,1)S(1)} copy-done((bf16[2048,256]{1,0:T(8,128)(2,1)S(1)}, bf16[2048,256]{1,0:T(8,128)(2,1)}, u32[]{:S(2)}) %copy-start.18) | copy-done | bytes 1048600
  35.7 1.2 %copy-done.21 = bf16[8,256,256]{2,1,0:T(8,128)(2,1)S(1)} copy-done((bf16[8,256,256]{2,1,0:T(8,128)(2,1)S(1)}, bf16[8,256,256]{2,1,0:T(8,128)(2,1)}, u32[]{:S(2)}) %copy-start.21) | copy-done | bytes 1048600
  36.9 2.5 %layer.1 = (bf16[2048,256]{1,0:T(8,128)(2,1)S(1)}, bf16[2048,256]{1,0:T(8,128)(2,1)S(1)}, bf16[8,34,256]{2,1,0:T(8,128)(2,1)S(1)}) custom-call(bf16[2048,256]{1,0:T(8,128)(2,1)S(1)} %bitcast.9, bf16[2048,256]{1,0:T(8,128)(2,1)S(1)} %bitcast.10, bf16[8,256,256]{2,1,0:T(8,128)(2,1)S(1)} %copy-done.21, bf16[2048,256]{1,0:T(8,128)(2,1)S(1)} %copy-done.18, ...), custom_call_target="tpu_custom_call" | custom-call | flops 12000000000 | bytes 12582912 | tf_op jit(solution)/shard_map/layer/pallas_call | solution.py:375
  39.4 1.0 %copy-done.22 = bf16[2048,256]{1,0:T(8,128)(2,1)} copy-done((bf16[2048,256]{1,0:T(8,128)(2,1)}, bf16[2048,256]{1,0:T(8,128)(2,1)S(1)}, u32[]{:S(2)}) %copy-start.22) | copy-done | bytes 1048600
  40.4 11.5 %all_to_all.21.r_ref.refs_0_.refs_4_ = bf16[8,34,256]{2,1,0:T(8,128)(2,1)S(1)} all-to-all(bf16[8,34,256]{2,1,0:T(8,128)(2,1)S(1)} %get-tuple-element.20), channel_id=1, replica_groups=mesh['len'=8,'pipe'=4] {'len'}, dimensions={0} | all-to-all | bytes 278528 | tf_op jit(solution)/shard_map/all_to_all | solution.py:341
  51.9 0.5 collective-permute-start.3
  52.5 2.0 %mix_grad.1 = (bf16[8,32,256]{2,1,0:T(8,128)(2,1)}, bf16[2048,256]{1,0:T(8,128)(2,1)}) custom-call(bf16[8,34,256]{2,1,0:T(8,128)(2,1)S(1)} %all_to_all.21.r_ref.refs_0_.refs_4_, bf16[16,256,256]{2,1,0:T(8,128)(2,1)S(1)} %copy-done, bf16[16,256,256]{2,1,0:T(8,128)(2,1)S(1)} %copy-done.2, bf16[2048,256]{1,0:T(8,128)(2,1)S(1)} %get-tuple-element.21.refs_0_), custom_call_target="tpu_custom_call" | custom-call | flops 12000000000 | bytes 12582912 | tf_op jit(solution)/shard_map/mix_grad/pallas_call | solution.py:352
  54.5 2.8 %collective-permute-done.3.refs_2_.refs_6_ = bf16[8,34,256]{2,1,0:T(8,128)(2,1)S(1)} collective-permute-done((bf16[8,34,256]{2,1,0:T(8,128)(2,1)S(1)}, bf16[8,34,256]{2,1,0:T(8,128)(2,1)S(1)}, u32[]{:S(2)}, u32[]{:S(2)}) %collective-permute-start.3) | collective-permute-done | bytes 139296 | tf_op jit(solution)/shard_map/ppermute | solution.py:344
  57.3 0.5 collective-permute-start.5
  57.8 3.4 %all-to-all-start.3 = ((bf16[8,32,256]{2,1,0:T(8,128)(2,1)}), bf16[8,32,256]{2,1,0:T(8,128)(2,1)S(1)}, u32[]{:S(2)}, u32[]{:S(2)}) async-start(bf16[8,32,256]{2,1,0:T(8,128)(2,1)} %get-tuple-element.24), calls=%async_computation.3 | async-start | bytes 262144 | tf_op jit(solution)/shard_map/all_to_all | solution.py:341
  61.2 0.9 %junction_grad.1.rows_ref = f32[8,256]{1,0:T(8,128)S(1)} custom-call(bf16[8,34,256]{2,1,0:T(8,128)(2,1)S(1)} %all_to_all.21.r_ref.refs_0_.refs_4_, bf16[8,34,256]{2,1,0:T(8,128)(2,1)S(1)} %collective-permute-done.4.refs_1_.refs_5_, bf16[8,34,256]{2,1,0:T(8,128)(2,1)S(1)} %collective-permute-done.3.refs_2_.refs_6_, ...), custom_call_target="tpu_custom_call" | custom-call | flops 1000000000 | bytes 1048576 | tf_op jit(solution)/shard_map/junction_grad/pallas_call | solution.py:387
  62.1 6.4 %all-to-all-done.3 = bf16[8,32,256]{2,1,0:T(8,128)(2,1)S(1)} async-done(((bf16[8,32,256]{2,1,0:T(8,128)(2,1)}), bf16[8,32,256]{2,1,0:T(8,128)(2,1)S(1)}, u32[]{:S(2)}, u32[]{:S(2)}) %all-to-all-start.3) | async-done | bytes 131104 | tf_op jit(solution)/shard_map/all_to_all | solution.py:341
  68.5 1.2 %copy-done.19 = bf16[2048,256]{1,0:T(8,128)(2,1)S(1)} copy-done((bf16[2048,256]{1,0:T(8,128)(2,1)S(1)}, bf16[2048,256]{1,0:T(8,128)(2,1)}, u32[]{:S(2)}) %copy-start.19) | copy-done | bytes 1048600
  69.7 1.2 %copy-done.23 = bf16[2048,256]{1,0:T(8,128)(2,1)S(1)} copy-done((bf16[2048,256]{1,0:T(8,128)(2,1)S(1)}, bf16[2048,256]{1,0:T(8,128)(2,1)}, u32[]{:S(2)}) %copy-start.23) | copy-done | bytes 1048600
  71.0 1.4 %input_grad.1 = bf16[2048,256]{1,0:T(8,128)(2,1)} custom-call(bf16[2048,256]{1,0:T(8,128)(2,1)S(1)} %copy-done.23, bf16[2048,256]{1,0:T(8,128)(2,1)S(1)} %copy-done.19, bf16[256,256]{1,0:T(8,128)(2,1)S(1)} %copy-done.13, f32[8,256]{1,0:T(8,128)S(1)} %junction_grad.1.rows_ref, bf16[256,256]{1,0:T(8,128)(2,1)S(1)} %bitcast.7), custom_call_target="tpu_custom_call" | custom-call | flops 1000000000 | bytes 1048576 | tf_op jit(solution)/shard_map/input_grad/pallas_call | solution.py:405
  72.4 4.9 %weight_grad.1 = (f32[16,256,256]{2,1,0:T(8,128)}, f32[16,256,256]{2,1,0:T(8,128)}) custom-call(bf16[8,34,256]{2,1,0:T(8,128)(2,1)S(1)} %all_to_all.20.r_ref.refs_0_, bf16[8,34,256]{2,1,0:T(8,128)(2,1)S(1)} %copy-done.7, bf16[8,34,256]{2,1,0:T(8,128)(2,1)} %collective-permute-done.refs_2_, bf16[8,34,256]{2,1,0:T(8,128)(2,1)S(1)} %copy-done.9, ...), custom_call_target="tpu_custom_call" | custom-call | flops 1000000000 | bytes 1048576 | tf_op jit(solution)/shard_map/weight_grad/pallas_call | solution.py:394
  (42 shorter events, 0.6 us)
Async XLA Ops:
  0.6 1.2 %copy-start.3 = (bf16[1,2048,256]{2,1,0:T(8,128)(2,1)S(1)}, bf16[1,2048,256]{2,1,0:T(8,128)(2,1)}, u32[]{:S(2)}) copy-start(bf16[1,2048,256]{2,1,0:T(8,128)(2,1)} %param.12) | copy-start | bytes 3145732
  1.9 1.2 %copy-start.20 = (bf16[8,256,256]{2,1,0:T(8,128)(2,1)S(1)}, bf16[8,256,256]{2,1,0:T(8,128)(2,1)}, u32[]{:S(2)}) copy-start(bf16[8,256,256]{2,1,0:T(8,128)(2,1)} %constant.4.clone.f_ref) | copy-start | bytes 3145732
  3.1 16.9 %copy-start = (bf16[16,256,256]{2,1,0:T(8,128)(2,1)S(1)}, bf16[16,256,256]{2,1,0:T(8,128)(2,1)}, u32[]{:S(2)}) copy-start(bf16[16,256,256]{2,1,0:T(8,128)(2,1)} %real_ref.3) | copy-start | bytes 6291460
  3.1 16.9 %copy-start.1 = (bf16[16,256,256]{2,1,0:T(8,128)(2,1)S(1)}, bf16[16,256,256]{2,1,0:T(8,128)(2,1)}, u32[]{:S(2)}) copy-start(bf16[16,256,256]{2,1,0:T(8,128)(2,1)} %imag_ref.3) | copy-start | bytes 6291460
  18.4 8.3 %copy-start.14 = (f32[256]{0:T(256)S(1)}, f32[256]{0:T(256)}, u32[]{:S(2)}) copy-start(f32[256]{0:T(256)} %param.19) | copy-start | bytes 3076
  18.4 8.3 %copy-start.16 = (s32[32]{0:T(128)S(1)}, s32[32]{0:T(128)}, u32[]{:S(2)}) copy-start(s32[32]{0:T(128)} %refs_4_.3) | copy-start | bytes 388
  18.4 8.3 %copy-start.17 = (s32[32]{0:T(128)S(1)}, s32[32]{0:T(128)}, u32[]{:S(2)}) copy-start(s32[32]{0:T(128)} %refs_5_.3) | copy-start | bytes 388
  18.4 13.9 %copy-start.4 = (bf16[1,2048,256]{2,1,0:T(8,128)(2,1)S(1)}, bf16[1,2048,256]{2,1,0:T(8,128)(2,1)}, u32[]{:S(2)}) copy-start(bf16[1,2048,256]{2,1,0:T(8,128)(2,1)} %param.12) | copy-start | bytes 3145732
  18.4 13.9 %copy-start.15 = (f32[256]{0:T(256)S(1)}, f32[256]{0:T(256)}, u32[]{:S(2)}) copy-start(f32[256]{0:T(256)} %param.15) | copy-start | bytes 3076
  18.5 6.3 %collective-permute-start = (bf16[8,34,256]{2,1,0:T(8,128)(2,1)S(1)}, bf16[8,34,256]{2,1,0:T(8,128)(2,1)}, u32[]{:S(2)}, u32[]{:S(2)}) collective-permute-start(bf16[8,34,256]{2,1,0:T(8,128)(2,1)S(1)} %all_to_all.20.r_ref.refs_0_), channel_id=1, source_target_pairs={{0,2},{1,3},{2,0},{3,1},{4,6},{5,7},{6,4},{7,5},{8,10},{9,11},{10,... | collective-permute-start | bytes 417800 | tf_op jit(solution)/shard_map/ppermute | solution.py:344
  21.4 10.9 %all-to-all-start.1 = ((bf16[8,34,256]{2,1,0:T(8,128)(2,1)}), bf16[8,34,256]{2,1,0:T(8,128)(2,1)S(1)}, u32[]{:S(2)}, u32[]{:S(2)}) async-start(bf16[8,34,256]{2,1,0:T(8,128)(2,1)} %mix.1), calls=%async_computation.1 | async-start | bytes 327680 | tf_op jit(solution)/shard_map/all_to_all | solution.py:341
  24.8 1.5 %collective-permute-start.1 = (bf16[8,34,256]{2,1,0:T(8,128)(2,1)S(1)}, bf16[8,34,256]{2,1,0:T(8,128)(2,1)S(1)}, u32[]{:S(2)}, u32[]{:S(2)}) collective-permute-start(bf16[8,34,256]{2,1,0:T(8,128)(2,1)S(1)} %all_to_all.20.r_ref.refs_0_), channel_id=1, source_target_pairs={{0,1},{1,0},{2,3},{3,2},{4,5},{5,4},{6,7},{7,6},{8,9},{9,8},{10,11... | collective-permute-start | bytes 417800 | tf_op jit(solution)/shard_map/ppermute | solution.py:344
  24.9 1.8 %collective-permute-start.2 = (bf16[8,34,256]{2,1,0:T(8,128)(2,1)}, bf16[8,34,256]{2,1,0:T(8,128)(2,1)S(1)}, u32[]{:S(2)}, u32[]{:S(2)}) collective-permute-start(bf16[8,34,256]{2,1,0:T(8,128)(2,1)} %collective-permute-done.refs_2_), channel_id=1, source_target_pairs={{0,1},{1,0},{2,3},{3,2},{4,5},{5,4},{6,7},{7,6},{8,9},{9,8},{10,11... | collective-permute-start | bytes 417800 | tf_op jit(solution)/shard_map/ppermute | solution.py:344
  26.7 0.9 %copy-start.10 = (bf16[256,256]{1,0:T(8,128)(2,1)S(1)}, bf16[256,256]{1,0:T(8,128)(2,1)}, u32[]{:S(2)}) copy-start(bf16[256,256]{1,0:T(8,128)(2,1)} %refs_6_.3) | copy-start | bytes 393220
  28.9 0.7 copy-start.6
  29.6 0.7 copy-start.8
  32.3 1.2 %copy-start.5 = (bf16[1,2048,256]{2,1,0:T(8,128)(2,1)S(1)}, bf16[1,2048,256]{2,1,0:T(8,128)(2,1)}, u32[]{:S(2)}) copy-start(bf16[1,2048,256]{2,1,0:T(8,128)(2,1)} %param.13) | copy-start | bytes 3145732
  33.5 0.9 %copy-start.12 = (bf16[256,256]{1,0:T(8,128)(2,1)S(1)}, bf16[256,256]{1,0:T(8,128)(2,1)}, u32[]{:S(2)}) copy-start(bf16[256,256]{1,0:T(8,128)(2,1)} %weight_ref.3) | copy-start | bytes 393220
  34.4 1.2 %copy-start.18 = (bf16[2048,256]{1,0:T(8,128)(2,1)S(1)}, bf16[2048,256]{1,0:T(8,128)(2,1)}, u32[]{:S(2)}) copy-start(bf16[2048,256]{1,0:T(8,128)(2,1)} %constant.5.clone.ft_ref) | copy-start | bytes 3145732
  35.7 1.2 %copy-start.21 = (bf16[8,256,256]{2,1,0:T(8,128)(2,1)S(1)}, bf16[8,256,256]{2,1,0:T(8,128)(2,1)}, u32[]{:S(2)}) copy-start(bf16[8,256,256]{2,1,0:T(8,128)(2,1)} %constant.4.clone.f_ref) | copy-start | bytes 3145732
  36.9 15.6 %copy-start.2 = (bf16[16,256,256]{2,1,0:T(8,128)(2,1)S(1)}, bf16[16,256,256]{2,1,0:T(8,128)(2,1)}, u32[]{:S(2)}) copy-start(bf16[16,256,256]{2,1,0:T(8,128)(2,1)} %imag_ref.3) | copy-start | bytes 6291460
  39.4 1.0 %copy-start.22 = (bf16[2048,256]{1,0:T(8,128)(2,1)}, bf16[2048,256]{1,0:T(8,128)(2,1)S(1)}, u32[]{:S(2)}) copy-start(bf16[2048,256]{1,0:T(8,128)(2,1)S(1)} %get-tuple-element.23.total_ref) | copy-start | bytes 3145732
  51.9 5.3 %collective-permute-start.3 = (bf16[8,34,256]{2,1,0:T(8,128)(2,1)S(1)}, bf16[8,34,256]{2,1,0:T(8,128)(2,1)S(1)}, u32[]{:S(2)}, u32[]{:S(2)}) collective-permute-start(bf16[8,34,256]{2,1,0:T(8,128)(2,1)S(1)} %all_to_all.21.r_ref.refs_0_.refs_4_), channel_id=1, source_target_pairs={{0,2},{1,3},{2,0},{3,1},{4,6},{5,7},{6,4},{7,5},{8,10},{9,11},{10,... | collective-permute-start | bytes 417800 | tf_op jit(solution)/shard_map/ppermute | solution.py:344
  52.5 8.7 %copy-start.11 = (bf16[256,256]{1,0:T(8,128)(2,1)S(1)}, bf16[256,256]{1,0:T(8,128)(2,1)}, u32[]{:S(2)}) copy-start(bf16[256,256]{1,0:T(8,128)(2,1)} %refs_6_.3) | copy-start | bytes 393220
  52.5 16.0 %copy-start.13 = (bf16[256,256]{1,0:T(8,128)(2,1)S(1)}, bf16[256,256]{1,0:T(8,128)(2,1)}, u32[]{:S(2)}) copy-start(bf16[256,256]{1,0:T(8,128)(2,1)} %weight_ref.3) | copy-start | bytes 393220
  54.4 18.0 %copy-start.7 = (bf16[8,34,256]{2,1,0:T(8,128)(2,1)S(1)}, bf16[8,34,256]{2,1,0:T(8,128)(2,1)}, u32[]{:S(2)}) copy-start(bf16[8,34,256]{2,1,0:T(8,128)(2,1)} %copy-done.6) | copy-start | bytes 417796
  54.5 18.0 %copy-start.9 = (bf16[8,34,256]{2,1,0:T(8,128)(2,1)S(1)}, bf16[8,34,256]{2,1,0:T(8,128)(2,1)}, u32[]{:S(2)}) copy-start(bf16[8,34,256]{2,1,0:T(8,128)(2,1)} %copy-done.8) | copy-start | bytes 417796
  57.3 3.9 %collective-permute-start.4 = (bf16[8,34,256]{2,1,0:T(8,128)(2,1)S(1)}, bf16[8,34,256]{2,1,0:T(8,128)(2,1)S(1)}, u32[]{:S(2)}, u32[]{:S(2)}) collective-permute-start(bf16[8,34,256]{2,1,0:T(8,128)(2,1)S(1)} %all_to_all.21.r_ref.refs_0_.refs_4_), channel_id=1, source_target_pairs={{0,1},{1,0},{2,3},{3,2},{4,5},{5,4},{6,7},{7,6},{8,9},{9,8},{10,11... | collective-permute-start | bytes 417800 | tf_op jit(solution)/shard_map/ppermute | solution.py:344
  57.3 3.9 %collective-permute-start.5 = (bf16[8,34,256]{2,1,0:T(8,128)(2,1)S(1)}, bf16[8,34,256]{2,1,0:T(8,128)(2,1)S(1)}, u32[]{:S(2)}, u32[]{:S(2)}) collective-permute-start(bf16[8,34,256]{2,1,0:T(8,128)(2,1)S(1)} %collective-permute-done.3.refs_2_.refs_6_), channel_id=1, source_target_pairs={{0,1},{1,0},{2,3},{3,2},{4,5},{5,4},{6,7},{7,6},{8,9},{9,8},{10,11... | collective-permute-start | bytes 417800 | tf_op jit(solution)/shard_map/ppermute | solution.py:344
  57.8 10.7 %all-to-all-start.3 = ((bf16[8,32,256]{2,1,0:T(8,128)(2,1)}), bf16[8,32,256]{2,1,0:T(8,128)(2,1)S(1)}, u32[]{:S(2)}, u32[]{:S(2)}) async-start(bf16[8,32,256]{2,1,0:T(8,128)(2,1)} %get-tuple-element.24), calls=%async_computation.3 | async-start | bytes 262144 | tf_op jit(solution)/shard_map/all_to_all | solution.py:341
  68.5 1.2 %copy-start.19 = (bf16[2048,256]{1,0:T(8,128)(2,1)S(1)}, bf16[2048,256]{1,0:T(8,128)(2,1)}, u32[]{:S(2)}) copy-start(bf16[2048,256]{1,0:T(8,128)(2,1)} %constant.5.clone.ft_ref) | copy-start | bytes 3145732
  69.7 1.2 %copy-start.23 = (bf16[2048,256]{1,0:T(8,128)(2,1)S(1)}, bf16[2048,256]{1,0:T(8,128)(2,1)}, u32[]{:S(2)}) copy-start(bf16[2048,256]{1,0:T(8,128)(2,1)} %copy-done.22) | copy-start | bytes 3145732

commit v6 on v5

--- a/solution.py
+++ b/solution.py
@@ -21,14 +21,22 @@
 MIB = 1024 * 1024
 
 
-def forward_table(cell_count, mode_count, groups):
-    product_index = np.arange(mode_count)[:, None] * np.arange(cell_count)[None, :] % cell_count
+def half_table(cell_count, mode_count, groups):
+    half = cell_count // 2
+    product_index = np.arange(mode_count)[:, None] * np.arange(half)[None, :] % cell_count
     angles = product_index.astype(np.float32) * np.float32(2.0 * math.pi / cell_count)
     norm_scale = np.float32(1.0 / math.sqrt(cell_count))
-    cosine = (np.cos(angles) * norm_scale).reshape(groups, -1, cell_count)
-    sine = (np.sin(angles) * norm_scale).reshape(groups, -1, cell_count)
-    table = np.concatenate([cosine, -sine], axis=1).reshape(2 * mode_count, cell_count)
+    cosine = (np.cos(angles) * norm_scale).reshape(groups, -1, half)
+    sine = (np.sin(angles) * norm_scale).reshape(groups, -1, half)
+    table = np.concatenate([cosine, -sine], axis=1).reshape(2 * mode_count, half)
     return table.astype(ml_dtypes.bfloat16)
+
+
+def row_signs(all_rows, span, channels):
+    row = lax.broadcasted_iota(jnp.int32, (all_rows, channels), 0)
+    per_owner = span // 2
+    mode = (row // span) * per_owner + lax.rem(row, per_owner)
+    return jnp.where(lax.rem(mode, 2) == 0, 1.0, -1.0).astype(jnp.float32)
 
 
 def dot(left, right, left_dim=1, right_dim=0):
@@ -51,14 +59,19 @@
 
 def spectrum_kernel(x_ref, f_ref, msg_ref):
     groups, rows = msg_ref.shape[0], msg_ref.shape[1]
-    tiles, all_rows, tile = f_ref.shape
+    steps, all_rows, tile = f_ref.shape
     cells, channels = x_ref.shape
+    half = cells // 2
     span = all_rows // groups
-    total = None
-    for step in range(tiles):
-        part = dot(f_ref[step], x_ref[step * tile : (step + 1) * tile, :])
-        total = part if total is None else total + part
-    spectra = total.astype(jnp.bfloat16)
+    sums = []
+    for base in (0, half):
+        total = None
+        for step in range(steps):
+            at = base + step * tile
+            part = dot(f_ref[step], x_ref[at : at + tile, :])
+            total = part if total is None else total + part
+        sums.append(total)
+    spectra = (sums[0] + row_signs(all_rows, span, channels) * sums[1]).astype(jnp.bfloat16)
     ends = extra_rows(x_ref[0:1, :], x_ref[cells - 1 : cells, :], rows - span, channels)
     for at in range(groups):
         msg_ref[at, 0:span, :] = spectra[at * span : (at + 1) * span]
@@ -72,16 +85,9 @@
     return jnp.concatenate(parts, axis=0).astype(jnp.bfloat16)
 
 
-def mix_kernel(backward, r_ref, real_ref, imag_ref, *refs):
-    x_ref, y_ref = refs[-2:]
+def mix_kernel(backward, r_ref, real_ref, imag_ref, out_ref, x_ref, y_ref):
     groups, modes = r_ref.shape[0], real_ref.shape[0]
     span = 2 * modes
-    if backward:
-        early_ref, out_ref, copied_ref, sem = refs[:4]
-        copy = pltpu.make_async_copy(early_ref, copied_ref, sem)
-        copy.start()
-    else:
-        out_ref = refs[0]
     for source in range(groups):
         put(x_ref, pl.ds(source * span, span), r_ref[source, 0:span, :].astype(jnp.float32))
     for mode in range(modes):
@@ -100,12 +106,8 @@
             put(y_ref, first, by_real[:groups] - by_imag[groups:])
             put(y_ref, second, by_imag[:groups] + by_real[groups:])
     for source in range(groups):
-        rows = take(y_ref, pl.ds(source * span, span)).astype(jnp.bfloat16)
-        out_ref[source, 0:span, :] = rows
-        if out_ref.shape[1] > span:
-            out_ref[source, span:, :] = jnp.zeros((2, rows.shape[1]), jnp.bfloat16)
-    if backward:
-        copy.wait()
+        rows = take(y_ref, pl.ds(source * span, span))
+        out_ref[source] = rows.astype(jnp.bfloat16)
 
 
 def own_pipe(pipes):
@@ -176,6 +178,15 @@
 def wait(copies):
     for copy in copies:
         copy.wait()
+
+
+def brought(pairs, sems, base=0):
+    return started(
+        [
+            pltpu.make_async_copy(source, target, sems.at[base + place])
+            for place, (source, target) in enumerate(pairs)
+        ]
+    )
 
 
 def layer_kernel(
@@ -190,67 +201,201 @@
     out_ref,
     total_ref,
     msg_ref,
-    acc_ref,
+    x_tiles,
+    cot_tiles,
+    f_tiles,
+    ft_tiles,
+    weight_buf,
+    bias_buf,
+    cond_buf,
+    modes_buf,
+    summed_tiles,
+    out_tiles,
+    total_tiles,
+    low_ref,
+    high_ref,
+    small_sems,
+    in_sems,
+    out_sems,
 ):
+    steps, all_rows, tile = f_ref.shape
+    half = steps * tile
     channels = x_ref.shape[1]
     groups, rows = msg_ref.shape[0], msg_ref.shape[1]
-    tiles, all_rows, tile = f_ref.shape
     span = all_rows // groups
+    low = [pl.ds(step * tile, tile) for step in range(steps)]
+    high = [pl.ds(half + step * tile, tile) for step in range(steps)]
+    small = brought(
+        [
+            (modes_ref, modes_buf),
+            (weight_ref, weight_buf),
+            (bias_ref, bias_buf),
+            (cond_ref, cond_buf),
+        ],
+        small_sems,
+    )
+    first, second, third = {}, {}, {}
+
+    def bring_first(step):
+        first[step] = brought(
+            [
+                (ft_ref.at[low[step]], ft_tiles.at[step]),
+                (x_ref.at[low[step]], x_tiles.at[step, 0]),
+                (x_ref.at[high[step]], x_tiles.at[step, 1]),
+            ],
+            in_sems,
+            6 * step,
+        )
+
+    def bring_rest(step):
+        second[step] = brought(
+            [
+                (cot_ref.at[low[step]], cot_tiles.at[step, 0]),
+                (cot_ref.at[high[step]], cot_tiles.at[step, 1]),
+            ],
+            in_sems,
+            6 * step + 3,
+        )
+        third[step] = brought([(f_ref.at[step], f_tiles.at[step])], in_sems, 6 * step + 5)
+
+    for step in range(steps + 1):
+        if step < steps:
+            bring_first(step)
+        if step > 0:
+            bring_rest(step - 1)
+    wait(small)
     row = lax.broadcasted_iota(jnp.int32, (all_rows, channels), 0)
     doubled = jnp.where((row == 0) | (row == span // 2), 1.0, 2.0).astype(jnp.float32)
+    signs = row_signs(all_rows, span, channels)
     modes = jnp.concatenate(
-        [modes_ref[at, 0:span, :].astype(jnp.float32) for at in range(groups)], axis=0
-    )
-    modes = (modes * doubled).astype(jnp.bfloat16)
-    weight = weight_ref[...]
-    cond = cond_ref[...]
-    bias = bias_ref[...]
-    for step in range(tiles):
-        at = pl.ds(step * tile, tile)
-        spectral = dot(ft_ref[at, :], modes)
-        pre = (spectral + cond).astype(jnp.bfloat16).astype(jnp.float32)
-        summed = dot(x_ref[at, :], weight) + bias + pre
-        square = summed * summed
-        half = 0.5 + 0.5 * jnp.tanh(summed * (GELU_S + (GELU_S * GELU_C) * square))
-        result = summed * half
-        out_ref[at, :] = result.astype(jnp.bfloat16)
-        slope = half + result * (1.0 - half) * (2.0 * GELU_S + (6.0 * GELU_S * GELU_C) * square)
-        total = (cot_ref[at, :].astype(jnp.float32) * slope).astype(jnp.bfloat16)
-        total_ref[at, :] = total
-        part = dot(f_ref[step], total)
-        if step == 0:
-            acc_ref[...] = part
-        else:
-            acc_ref[...] += part
-    grad_cond = acc_ref[0:1, :] * (1.0 / f_ref[0, 0:1, 0:1].astype(jnp.float32))
-    high = grad_cond.astype(jnp.bfloat16).astype(jnp.float32)
-    extra = extra_rows(high, grad_cond - high, rows - span, channels)
-    grad_spec = (acc_ref[...] * doubled).astype(jnp.bfloat16)
+        [modes_buf[at, 0:span, :].astype(jnp.float32) for at in range(groups)], axis=0
+    )
+    modes = modes * doubled
+    modes = (modes.astype(jnp.bfloat16), (modes * signs).astype(jnp.bfloat16))
+    weight = weight_buf[...]
+    cond = cond_buf[...]
+    bias = bias_buf[...]
+    going = []
+    for block in range(steps + 2):
+        if block < steps:
+            wait(first[block])
+        if 1 <= block <= steps:
+            wait(second[block - 1])
+        if 2 <= block:
+            wait(third[block - 2])
+        if block < steps:
+            for side in range(2):
+                spectral = dot(ft_tiles[block], modes[side])
+                pre = (spectral + cond).astype(jnp.bfloat16).astype(jnp.float32)
+                summed_tiles[block, side] = dot(x_tiles[block, side], weight) + bias + pre
+        if 1 <= block <= steps:
+            step = block - 1
+            for side in range(2):
+                summed = summed_tiles[step, side]
+                square = summed * summed
+                part = 0.5 + 0.5 * jnp.tanh(summed * (GELU_S + (GELU_S * GELU_C) * square))
+                result = summed * part
+                out_tiles[step, side] = result.astype(jnp.bfloat16)
+                slope = part + result * (1.0 - part) * (
+                    2.0 * GELU_S + (6.0 * GELU_S * GELU_C) * square
+                )
+                total = cot_tiles[step, side].astype(jnp.float32) * slope
+                total_tiles[step, side] = total.astype(jnp.bfloat16)
+        if 2 <= block:
+            step = block - 2
+            for side, acc_ref in enumerate((low_ref, high_ref)):
+                part = dot(f_tiles[step], total_tiles[step, side])
+                if step == 0:
+                    acc_ref[...] = part
+                else:
+                    acc_ref[...] += part
+        if 1 <= block <= steps:
+            step = block - 1
+            going += brought(
+                [
+                    (out_tiles.at[step, 0], out_ref.at[low[step]]),
+                    (out_tiles.at[step, 1], out_ref.at[high[step]]),
+                    (total_tiles.at[step, 0], total_ref.at[low[step]]),
+                    (total_tiles.at[step, 1], total_ref.at[high[step]]),
+                ],
+                out_sems,
+                4 * step,
+            )
+    acc = low_ref[...] + signs * high_ref[...]
+    grad_cond = acc[0:1, :] * (1.0 / f_tiles[0, 0:1, 0:1].astype(jnp.float32))
+    upper = grad_cond.astype(jnp.bfloat16).astype(jnp.float32)
+    extra = extra_rows(upper, grad_cond - upper, rows - span, channels)
+    grad_spec = (acc * doubled).astype(jnp.bfloat16)
     for at in range(groups):
         msg_ref[at, 0:span, :] = grad_spec[at * span : (at + 1) * span]
         msg_ref[at, span:rows, :] = extra
+    wait(going)
 
 
 def input_grad_kernel(
-    total_ref, ft_ref, weight_ref, rows_ref, modes_ref, out_ref, tiles_ref, sems
+    total_ref,
+    ft_ref,
+    weight_ref,
+    rows_ref,
+    modes_ref,
+    out_ref,
+    total_tiles,
+    ft_tiles,
+    weight_buf,
+    rows_buf,
+    modes_buf,
+    out_tiles,
+    small_sems,
+    in_sems,
+    out_sems,
 ):
-    modes = modes_ref[...]
-    weight = weight_ref[...]
-    tiles, tile, channels = tiles_ref.shape
+    steps, tile, all_rows = ft_tiles.shape
+    half = steps * tile
+    groups, span, channels = modes_ref.shape
+    low = [pl.ds(step * tile, tile) for step in range(steps)]
+    high = [pl.ds(half + step * tile, tile) for step in range(steps)]
+    small = brought(
+        [(modes_ref, modes_buf), (weight_ref, weight_buf), (rows_ref, rows_buf)], small_sems
+    )
+    coming = [
+        brought(
+            [
+                (ft_ref.at[low[step]], ft_tiles.at[step]),
+                (total_ref.at[low[step]], total_tiles.at[step, 0]),
+                (total_ref.at[high[step]], total_tiles.at[step, 1]),
+            ],
+            in_sems,
+            3 * step,
+        )
+        for step in range(steps)
+    ]
     row = lax.broadcasted_iota(jnp.int32, (tile, channels), 0)
+    wait(small)
+    modes = jnp.concatenate(
+        [modes_buf[at, 0:span, :].astype(jnp.float32) for at in range(groups)], axis=0
+    )
+    signs = row_signs(all_rows, span, channels)
+    modes = (modes.astype(jnp.bfloat16), (modes * signs).astype(jnp.bfloat16))
+    weight = weight_buf[...]
     going = []
-    for step in range(tiles):
-        at = pl.ds(step * tile, tile)
-        grad_cells = dot(ft_ref[at, :], modes)
-        if step == 0:
-            grad_cells = grad_cells + jnp.where(row == 0, rows_ref[0:1, :], 0.0)
-        if step == tiles - 1:
-            grad_cells = grad_cells + jnp.where(row == tile - 1, rows_ref[1:2, :], 0.0)
-        spread = grad_cells.astype(jnp.bfloat16).astype(jnp.float32)
-        local = dot(total_ref[at, :], weight, 1, 1)
-        tiles_ref[step] = (local + spread).astype(jnp.bfloat16)
-        going += started(
-            [pltpu.make_async_copy(tiles_ref.at[step], out_ref.at[at], sems.at[step])]
+    for step in range(steps):
+        wait(coming[step])
+        for side, at in enumerate((low[step], high[step])):
+            grad_cells = dot(ft_tiles[step], modes[side])
+            if step == 0 and side == 0:
+                grad_cells = grad_cells + jnp.where(row == 0, rows_buf[0:1, :], 0.0)
+            if step == steps - 1 and side == 1:
+                grad_cells = grad_cells + jnp.where(row == tile - 1, rows_buf[1:2, :], 0.0)
+            spread = grad_cells.astype(jnp.bfloat16).astype(jnp.float32)
+            local = dot(total_tiles[step, side], weight, 1, 1)
+            out_tiles[step, side] = (local + spread).astype(jnp.bfloat16)
+        going += brought(
+            [
+                (out_tiles.at[step, 0], out_ref.at[low[step]]),
+                (out_tiles.at[step, 1], out_ref.at[high[step]]),
+            ],
+            out_sems,
+            2 * step,
         )
     wait(going)
 
@@ -322,9 +467,9 @@
     modes = spec_real.shape[0]
     span = 2 * modes
     all_rows = span * groups
-    tiles = cell_count // TILE
-    table = forward_table(cell_count, modes * groups, groups)
-    tiled = table.reshape(all_rows, tiles, TILE).transpose(1, 0, 2)
+    steps = cell_count // (2 * TILE)
+    table = half_table(cell_count, modes * groups, groups)
+    tiled = table.reshape(all_rows, steps, TILE).transpose(1, 0, 2)
     f_table = jnp.asarray(np.ascontiguousarray(tiled))
     ft_table = jnp.asarray(np.ascontiguousarray(table.T))
     field = inputs.reshape(cell_count, channels)
@@ -348,22 +493,21 @@
         tied, tied_across, _ = lax.optimization_barrier((own, across, behind))
         return [own, swap(tied, 1), across, swap(tied_across, 1)]
 
-    def mix(backward, value, *early):
+    def mix(backward, value):
         return call(
             functools.partial(mix_kernel, backward),
-            [chunks, early[0]] if backward else [message],
-            [VMEM] * (4 if backward else 3),
-            ([dma] if backward else []) + [rows_of(all_rows, channels)] * 2,
-            out_specs=[VMEM, HBM] if backward else [VMEM],
+            [chunks],
+            [VMEM] * 3,
+            [rows_of(all_rows, channels)] * 2,
             name="mix_grad" if backward else "mix",
             busy=12,
-        )(value, spec_real, spec_imag, *early)
+        )(value, spec_real, spec_imag)[0]
 
     (sent,) = call(spectrum_kernel, [message], [VMEM] * 2, name="spectrum", busy=12)(
         field, f_table
     )
     received = exchange(sent)
-    (mixed,) = mix(False, received)
+    mixed = mix(False, received)
     returned = exchange(mixed)
     fields = gather(received, mixed)
     cond, slope = call(
@@ -372,17 +516,28 @@
         [VMEM] * pipes + [SMEM] * 2 + [VMEM] * 2,
         name="junction",
     )(*fields, inlet_ids, outlet_ids, junc_weight, junc_bias_row)
-    early, total, sent = call(
+    sides = pltpu.VMEM((steps, 2, TILE, channels), bf16)
+    table_tiles = pltpu.VMEM((steps, all_rows, TILE), bf16)
+    back_tiles = pltpu.VMEM((steps, TILE, all_rows), bf16)
+    square = pltpu.VMEM((channels, channels), bf16)
+    flat = pltpu.VMEM((1, channels), f32)
+    outputs, total, sent = call(
         layer_kernel,
         [shape(field.shape, bf16), shape(field.shape, bf16), message],
-        [VMEM] * 8,
-        [pltpu.VMEM((all_rows, channels), f32)],
+        [HBM] * 8,
+        [sides, sides, table_tiles, back_tiles, square, flat, flat]
+        + [pltpu.VMEM(chunks.shape, bf16), pltpu.VMEM((steps, 2, TILE, channels), f32)]
+        + [sides, sides]
+        + [pltpu.VMEM((all_rows, channels), f32)] * 2
+        + [dma((4,)), dma((6 * steps,)), dma((4 * steps,))],
+        out_specs=[HBM, HBM, VMEM],
         name="layer",
         busy=12,
+        limit=60,
     )(field, cot, f_table, ft_table, point_weight, bias_row, cond, returned)
     received = exchange(sent)
-    mixed, outputs = mix(True, received, early)
-    returned = exchange(mixed).reshape(all_rows, channels)
+    mixed = mix(True, received)
+    returned = exchange(mixed)
     grads = gather(received, mixed)
     (rows,) = call(
         functools.partial(junction_backward_kernel, pipes),
@@ -402,13 +557,17 @@
         name="weight_grad",
         limit=16,
     )(*fields, *grads)
+    total, grad_real, grad_imag = lax.optimization_barrier((total, grad_real, grad_imag))
     (grad_inputs,) = call(
         input_grad_kernel,
         [shape(field.shape, bf16)],
-        [VMEM] * 5,
-        [pltpu.VMEM((tiles, TILE, channels), bf16), dma((tiles,))],
+        [HBM] * 5,
+        [sides, back_tiles, square, pltpu.VMEM((8, channels), f32)]
+        + [pltpu.VMEM(chunks.shape, bf16), sides]
+        + [dma((3,)), dma((3 * steps,)), dma((2 * steps,))],
         out_specs=[HBM],
         name="input_grad",
+        limit=60,
     )(total, ft_table, point_weight, rows, returned)
     return (
         outputs.reshape(inputs.shape),

time: 78.1 us -> 74.6 us (0.955)
  local copies, waits for them, and re-layouts: 12.7 us -> 5.78 us
  Pallas kernels: 14.9 us -> 19.9 us
  waiting for transfers between devices: 12.6 us -> 11 us
  starting transfers between devices: 9.95 us -> 10.8 us
    unnamed x48 -> x26, local copies, waits for them, and re-layouts: 12.7 us -> 5.78 us
    pallas_call x1, Pallas kernels: 2.53 us -> 6.62 us  [body(): call(layer_kernel, [shape(field.shape, bf16), shape(field.shape, bf16), m...]
    pallas_call x3, Pallas kernels: 4.8 us -> 7.04 us  [the longest x1 3.75 us: body(): call(input_grad_kernel, [shape(field.shape, bf16)], [HBM] * 5, [sides, ba...]
    ppermute x6, waiting for transfers between devices: 4.12 us -> 2.77 us  [swap(): return lax.ppermute(value, 'pipe', [(i, i ^ step) for i in range(pipes)])]
    pallas_call x1, Pallas kernels: 4.92 us -> 4.01 us  [body(): call(functools.partial(weight_grad_kernel, pipes, modes), [big, big], [VM...]
    ppermute x6, starting transfers between devices: 3.17 us -> 4.08 us  [swap(): return lax.ppermute(value, 'pipe', [(i, i ^ step) for i in range(pipes)])]
  transfers between devices with their start and end apart: 8 -> 8, of which waited for: 5 -> 4; matrix products, arithmetic and copies ran while one was open for 0% -> 0% of each run, Pallas kernels for 7% -> 12%
where the time goes in v6:
time: 74.6 us; the launch traced here: 74 us
  blocking collectives  25.8 us (35%)
  Pallas kernels  19.9 us (27%)
  waiting for transfers between devices  11 us (15%)
  starting transfers between devices  10.8 us (14%)
  local copies, waits for them, and re-layouts  5.78 us (8%)
  between operations  0.78 us (1%)
    all_to_all x2, blocking collectives, exchange(): return lax.all_to_all(value, 'len', split_axis=0, concat_axis=0, tiled=True)  25.8 us
    all_to_all x2, waiting for transfers between devices, exchange(): return lax.all_to_all(value, 'len', split_axis=0, concat_axis=0, tiled=True)  8.2 us
    all_to_all x2, starting transfers between devices, exchange(): return lax.all_to_all(value, 'len', split_axis=0, concat_axis=0, tiled=True)  6.74 us
    pallas_call x1, Pallas kernels, body(): call(layer_kernel, [shape(field.shape, bf16), shape(field.shape, bf16), m...  6.62 us
    unnamed x26, local copies, waits for them, and re-layouts  5.78 us
    ppermute x6, starting transfers between devices, swap(): return lax.ppermute(value, 'pipe', [(i, i ^ step) for i in range(pipes)])  4.08 us
    pallas_call x1, Pallas kernels, body(): call(functools.partial(weight_grad_kernel, pipes, modes), [big, big], [VM...  4.01 us
    pallas_call x1, Pallas kernels, body(): call(input_grad_kernel, [shape(field.shape, bf16)], [HBM] * 5, [sides, ba...  3.75 us
  transfers between devices with their start and end apart: 8, of which 4 were waited for; matrix products, arithmetic and copies ran while one was open for 0% of the time, Pallas kernels for 12%

profile of v6, /device:TPU:0, one launch (start us, length us, event | category | flops | bytes accessed | tf_op | source)
XLA Modules:
  0.0 74.0 jit_solution(8034220640651565188)
XLA Ops:
  0.6 0.0 copy-start.3
  0.6 1.2 %copy-done.3 = bf16[1,2048,256]{2,1,0:T(8,128)(2,1)S(1)} copy-done((bf16[1,2048,256]{2,1,0:T(8,128)(2,1)S(1)}, bf16[1,2048,256]{2,1,0:T(8,128)(2,1)}, u32[]{:S(2)}) %copy-start.3) | copy-done | bytes 1048600
  1.9 1.0 %copy-done.8 = bf16[4,256,256]{2,1,0:T(8,128)(2,1)S(1)} copy-done((bf16[4,256,256]{2,1,0:T(8,128)(2,1)S(1)}, bf16[4,256,256]{2,1,0:T(8,128)(2,1)}, u32[]{:S(2)}) %copy-start.8) | copy-done | bytes 524312
  2.9 0.4 spectrum.1
  3.3 14.9 %all_to_all.20.r_ref.refs_0_ = bf16[8,34,256]{2,1,0:T(8,128)(2,1)S(1)} all-to-all(bf16[8,34,256]{2,1,0:T(8,128)(2,1)S(1)} %spectrum.1), channel_id=1, replica_groups=mesh['len'=8,'pipe'=4] {'len'}, dimensions={0} | all-to-all | bytes 278528 | tf_op jit(solution)/shard_map/all_to_all | solution.py:486
  18.3 1.6 %collective-permute-start = (bf16[8,34,256]{2,1,0:T(8,128)(2,1)S(1)}, bf16[8,34,256]{2,1,0:T(8,128)(2,1)S(1)}, u32[]{:S(2)}, u32[]{:S(2)}) collective-permute-start(bf16[8,34,256]{2,1,0:T(8,128)(2,1)S(1)} %all_to_all.20.r_ref.refs_0_), channel_id=1, source_target_pairs={{0,2},{1,3},{2,0},{3,1},{4,6},{5,7},{6,4},{7,5},{8,10},{9,11},{10,... | collective-permute-start | bytes 417800 | tf_op jit(solution)/shard_map/ppermute | solution.py:489
  19.8 1.4 %mix.1 = bf16[8,32,256]{2,1,0:T(8,128)(2,1)} custom-call(bf16[8,34,256]{2,1,0:T(8,128)(2,1)S(1)} %all_to_all.20.r_ref.refs_0_, bf16[16,256,256]{2,1,0:T(8,128)(2,1)S(1)} %copy-done, bf16[16,256,256]{2,1,0:T(8,128)(2,1)S(1)} %copy-done.1), custom_call_target="tpu_custom_call" | custom-call | flops 12000000000 | bytes 12582912 | tf_op jit(solution)/shard_map/mix/pallas_call | solution.py:497
  21.2 2.4 %collective-permute-done.refs_2_ = bf16[8,34,256]{2,1,0:T(8,128)(2,1)S(1)} collective-permute-done((bf16[8,34,256]{2,1,0:T(8,128)(2,1)S(1)}, bf16[8,34,256]{2,1,0:T(8,128)(2,1)S(1)}, u32[]{:S(2)}, u32[]{:S(2)}) %collective-permute-start) | collective-permute-done | bytes 139296 | tf_op jit(solution)/shard_map/ppermute | solution.py:489
  23.6 0.0 collective-permute-start.1
  23.7 0.5 collective-permute-start.2
  24.2 3.4 %all-to-all-start.1 = ((bf16[8,32,256]{2,1,0:T(8,128)(2,1)}), bf16[8,32,256]{2,1,0:T(8,128)(2,1)S(1)}, u32[]{:S(2)}, u32[]{:S(2)}) async-start(bf16[8,32,256]{2,1,0:T(8,128)(2,1)} %mix.1), calls=%async_computation.1 | async-start | bytes 262144 | tf_op jit(solution)/shard_map/all_to_all | solution.py:486
  27.5 0.0 collective-permute-done.1.refs_1_
  27.6 0.0 collective-permute-done.2.refs_3_
  27.6 0.9 %junction.1 = (f32[1,256]{1,0:T(1,128)S(1)}, f32[8,256]{1,0:T(8,128)S(1)}) custom-call(bf16[8,34,256]{2,1,0:T(8,128)(2,1)S(1)} %all_to_all.20.r_ref.refs_0_, bf16[8,34,256]{2,1,0:T(8,128)(2,1)S(1)} %collective-permute-done.1.refs_1_, bf16[8,34,256]{2,1,0:T(8,128)(2,1)S(1)} %collective-permute-done.refs_2_, ...), custom_call_target="tpu_custom_call" | custom-call | flops 1000000000 | bytes 1048576 | tf_op jit(solution)/shard_map/junction/pallas_call | solution.py:513
  28.5 0.0 copy-start.10
  28.5 6.4 %all-to-all-done.1.modes_ref = bf16[8,32,256]{2,1,0:T(8,128)(2,1)S(1)} async-done(((bf16[8,32,256]{2,1,0:T(8,128)(2,1)}), bf16[8,32,256]{2,1,0:T(8,128)(2,1)S(1)}, u32[]{:S(2)}, u32[]{:S(2)}) %all-to-all-start.1) | async-done | bytes 131104 | tf_op jit(solution)/shard_map/all_to_all | solution.py:486
  34.9 0.7 copy-done.12
  35.6 6.6 %layer.1 = (bf16[2048,256]{1,0:T(8,128)(2,1)}, bf16[2048,256]{1,0:T(8,128)(2,1)}, bf16[8,34,256]{2,1,0:T(8,128)(2,1)}) custom-call(bf16[2048,256]{1,0:T(8,128)(2,1)} %bitcast.6, bf16[2048,256]{1,0:T(8,128)(2,1)} %bitcast.9, bf16[4,256,256]{2,1,0:T(8,128)(2,1)} %constant.4.clone.f_ref, bf16[1024,256]{1,0:T(8,128)(2,1)} %constant.5.clone.ft_ref, ...), custom_call_target="tpu_custom_call" | custom-call | flops 12000000000 | bytes 12582912 | tf_op jit(solution)/shard_map/layer/pallas_call | solution.py:524
  42.2 10.9 %all_to_all.21.r_ref.refs_4_.refs_0_ = bf16[8,34,256]{2,1,0:T(8,128)(2,1)S(1)} all-to-all(bf16[8,34,256]{2,1,0:T(8,128)(2,1)} %get-tuple-element.23), channel_id=1, replica_groups=mesh['len'=8,'pipe'=4] {'len'}, dimensions={0} | all-to-all | bytes 278528 | tf_op jit(solution)/shard_map/all_to_all | solution.py:486
  53.1 1.5 %collective-permute-start.3 = (bf16[8,34,256]{2,1,0:T(8,128)(2,1)S(1)}, bf16[8,34,256]{2,1,0:T(8,128)(2,1)S(1)}, u32[]{:S(2)}, u32[]{:S(2)}) collective-permute-start(bf16[8,34,256]{2,1,0:T(8,128)(2,1)S(1)} %all_to_all.21.r_ref.refs_4_.refs_0_), channel_id=1, source_target_pairs={{0,2},{1,3},{2,0},{3,1},{4,6},{5,7},{6,4},{7,5},{8,10},{9,11},{10,... | collective-permute-start | bytes 417800 | tf_op jit(solution)/shard_map/ppermute | solution.py:489
  54.6 1.6 %copy-done.2 = bf16[16,256,256]{2,1,0:T(8,128)(2,1)S(1)} copy-done((bf16[16,256,256]{2,1,0:T(8,128)(2,1)S(1)}, bf16[16,256,256]{2,1,0:T(8,128)(2,1)}, u32[]{:S(2)}) %copy-start.2) | copy-done | bytes 2097176
  56.1 1.9 %mix_grad.1 = bf16[8,32,256]{2,1,0:T(8,128)(2,1)} custom-call(bf16[8,34,256]{2,1,0:T(8,128)(2,1)S(1)} %all_to_all.21.r_ref.refs_4_.refs_0_, bf16[16,256,256]{2,1,0:T(8,128)(2,1)S(1)} %copy-done, bf16[16,256,256]{2,1,0:T(8,128)(2,1)S(1)} %copy-done.2), custom_call_target="tpu_custom_call" | custom-call | flops 12000000000 | bytes 12582912 | tf_op jit(solution)/shard_map/mix_grad/pallas_call | solution.py:497
  58.1 0.3 collective-permute-done.3.refs_6_.refs_2_
  58.4 0.5 collective-permute-start.5
  58.9 3.4 %all-to-all-start.3 = ((bf16[8,32,256]{2,1,0:T(8,128)(2,1)}), bf16[8,32,256]{2,1,0:T(8,128)(2,1)S(1)}, u32[]{:S(2)}, u32[]{:S(2)}) async-start(bf16[8,32,256]{2,1,0:T(8,128)(2,1)} %mix_grad.1), calls=%async_computation.3 | async-start | bytes 262144 | tf_op jit(solution)/shard_map/all_to_all | solution.py:486
  62.3 0.0 collective-permute-done.4.refs_5_.refs_1_
  62.3 4.0 %weight_grad.1 = (f32[16,256,256]{2,1,0:T(8,128)}, f32[16,256,256]{2,1,0:T(8,128)}) custom-call(bf16[8,34,256]{2,1,0:T(8,128)(2,1)S(1)} %all_to_all.20.r_ref.refs_0_, bf16[8,34,256]{2,1,0:T(8,128)(2,1)S(1)} %collective-permute-done.1.refs_1_, bf16[8,34,256]{2,1,0:T(8,128)(2,1)S(1)} %collective-permute-done.refs_2_, ...), custom_call_target="tpu_custom_call" | custom-call | flops 1000000000 | bytes 1048576 | tf_op jit(solution)/shard_map/weight_grad/pallas_call | solution.py:549
  66.3 0.9 %junction_grad.1.rows_ref = f32[8,256]{1,0:T(8,128)S(1)} custom-call(bf16[8,34,256]{2,1,0:T(8,128)(2,1)S(1)} %all_to_all.21.r_ref.refs_4_.refs_0_, bf16[8,34,256]{2,1,0:T(8,128)(2,1)S(1)} %collective-permute-done.4.refs_5_.refs_1_, bf16[8,34,256]{2,1,0:T(8,128)(2,1)S(1)} %collective-permute-done.3.refs_6_.refs_2_, ...), custom_call_target="tpu_custom_call" | custom-call | flops 1000000000 | bytes 1048576 | tf_op jit(solution)/shard_map/junction_grad/pallas_call | solution.py:542
  67.2 0.6 copy-done.9
  67.8 1.8 %all-to-all-done.3.modes_ref = bf16[8,32,256]{2,1,0:T(8,128)(2,1)S(1)} async-done(((bf16[8,32,256]{2,1,0:T(8,128)(2,1)}), bf16[8,32,256]{2,1,0:T(8,128)(2,1)S(1)}, u32[]{:S(2)}, u32[]{:S(2)}) %all-to-all-start.3) | async-done | bytes 131104 | tf_op jit(solution)/shard_map/all_to_all | solution.py:486
  69.6 0.6 copy-done.11
  70.3 3.7 %input_grad.1 = bf16[2048,256]{1,0:T(8,128)(2,1)} custom-call(bf16[2048,256]{1,0:T(8,128)(2,1)} %get-tuple-element.28.total_ref, bf16[1024,256]{1,0:T(8,128)(2,1)} %constant.5.clone.ft_ref, bf16[256,256]{1,0:T(8,128)(2,1)} %weight_ref.3, f32[8,256]{1,0:T(8,128)} %copy-done.9, bf16[8,32,256]{2,1,0:T(8,128)(2,1)} %copy-done.11), custom_call_target="tpu_custom_call" | custom-call | flops 1000000000 | bytes 1048576 | tf_op jit(solution)/shard_map/input_grad/pallas_call | solution.py:561
  (20 shorter events, 0.0 us)
Async XLA Ops:
  0.6 1.2 %copy-start.3 = (bf16[1,2048,256]{2,1,0:T(8,128)(2,1)S(1)}, bf16[1,2048,256]{2,1,0:T(8,128)(2,1)}, u32[]{:S(2)}) copy-start(bf16[1,2048,256]{2,1,0:T(8,128)(2,1)} %param.12) | copy-start | bytes 3145732
  1.9 1.0 %copy-start.8 = (bf16[4,256,256]{2,1,0:T(8,128)(2,1)S(1)}, bf16[4,256,256]{2,1,0:T(8,128)(2,1)}, u32[]{:S(2)}) copy-start(bf16[4,256,256]{2,1,0:T(8,128)(2,1)} %constant.4.clone.f_ref) | copy-start | bytes 1572868
  2.9 16.9 %copy-start = (bf16[16,256,256]{2,1,0:T(8,128)(2,1)S(1)}, bf16[16,256,256]{2,1,0:T(8,128)(2,1)}, u32[]{:S(2)}) copy-start(bf16[16,256,256]{2,1,0:T(8,128)(2,1)} %real_ref.3) | copy-start | bytes 6291460
  2.9 16.9 %copy-start.1 = (bf16[16,256,256]{2,1,0:T(8,128)(2,1)S(1)}, bf16[16,256,256]{2,1,0:T(8,128)(2,1)}, u32[]{:S(2)}) copy-start(bf16[16,256,256]{2,1,0:T(8,128)(2,1)} %imag_ref.3) | copy-start | bytes 6291460
  18.3 9.3 %copy-start.4 = (bf16[256,256]{1,0:T(8,128)(2,1)S(1)}, bf16[256,256]{1,0:T(8,128)(2,1)}, u32[]{:S(2)}) copy-start(bf16[256,256]{1,0:T(8,128)(2,1)} %refs_6_.3) | copy-start | bytes 393220
  18.3 9.3 %copy-start.5 = (f32[256]{0:T(256)S(1)}, f32[256]{0:T(256)}, u32[]{:S(2)}) copy-start(f32[256]{0:T(256)} %param.19) | copy-start | bytes 3076
  18.3 9.3 %copy-start.6 = (s32[32]{0:T(128)S(1)}, s32[32]{0:T(128)}, u32[]{:S(2)}) copy-start(s32[32]{0:T(128)} %refs_4_.3) | copy-start | bytes 388
  18.3 9.3 %copy-start.7 = (s32[32]{0:T(128)S(1)}, s32[32]{0:T(128)}, u32[]{:S(2)}) copy-start(s32[32]{0:T(128)} %refs_5_.3) | copy-start | bytes 388
  18.3 5.4 %collective-permute-start = (bf16[8,34,256]{2,1,0:T(8,128)(2,1)S(1)}, bf16[8,34,256]{2,1,0:T(8,128)(2,1)S(1)}, u32[]{:S(2)}, u32[]{:S(2)}) collective-permute-start(bf16[8,34,256]{2,1,0:T(8,128)(2,1)S(1)} %all_to_all.20.r_ref.refs_0_), channel_id=1, source_target_pairs={{0,2},{1,3},{2,0},{3,1},{4,6},{5,7},{6,4},{7,5},{8,10},{9,11},{10,... | collective-permute-start | bytes 417800 | tf_op jit(solution)/shard_map/ppermute | solution.py:489
  23.6 3.9 %collective-permute-start.1 = (bf16[8,34,256]{2,1,0:T(8,128)(2,1)S(1)}, bf16[8,34,256]{2,1,0:T(8,128)(2,1)S(1)}, u32[]{:S(2)}, u32[]{:S(2)}) collective-permute-start(bf16[8,34,256]{2,1,0:T(8,128)(2,1)S(1)} %all_to_all.20.r_ref.refs_0_), channel_id=1, source_target_pairs={{0,1},{1,0},{2,3},{3,2},{4,5},{5,4},{6,7},{7,6},{8,9},{9,8},{10,11... | collective-permute-start | bytes 417800 | tf_op jit(solution)/shard_map/ppermute | solution.py:489
  23.7 3.9 %collective-permute-start.2 = (bf16[8,34,256]{2,1,0:T(8,128)(2,1)S(1)}, bf16[8,34,256]{2,1,0:T(8,128)(2,1)S(1)}, u32[]{:S(2)}, u32[]{:S(2)}) collective-permute-start(bf16[8,34,256]{2,1,0:T(8,128)(2,1)S(1)} %collective-permute-done.refs_2_), channel_id=1, source_target_pairs={{0,1},{1,0},{2,3},{3,2},{4,5},{5,4},{6,7},{7,6},{8,9},{9,8},{10,11... | collective-permute-start | bytes 417800 | tf_op jit(solution)/shard_map/ppermute | solution.py:489
  24.2 10.7 %all-to-all-start.1 = ((bf16[8,32,256]{2,1,0:T(8,128)(2,1)}), bf16[8,32,256]{2,1,0:T(8,128)(2,1)S(1)}, u32[]{:S(2)}, u32[]{:S(2)}) async-start(bf16[8,32,256]{2,1,0:T(8,128)(2,1)} %mix.1), calls=%async_computation.1 | async-start | bytes 262144 | tf_op jit(solution)/shard_map/all_to_all | solution.py:486
  28.5 6.4 %copy-start.10 = (f32[1,256]{1,0:T(1,128)}, f32[1,256]{1,0:T(1,128)S(1)}, u32[]{:S(2)}) copy-start(f32[1,256]{1,0:T(1,128)S(1)} %get-tuple-element.20.cond_ref) | copy-start | bytes 3076
  34.9 0.7 copy-start.12
  53.1 5.3 %collective-permute-start.3 = (bf16[8,34,256]{2,1,0:T(8,128)(2,1)S(1)}, bf16[8,34,256]{2,1,0:T(8,128)(2,1)S(1)}, u32[]{:S(2)}, u32[]{:S(2)}) collective-permute-start(bf16[8,34,256]{2,1,0:T(8,128)(2,1)S(1)} %all_to_all.21.r_ref.refs_4_.refs_0_), channel_id=1, source_target_pairs={{0,2},{1,3},{2,0},{3,1},{4,6},{5,7},{6,4},{7,5},{8,10},{9,11},{10,... | collective-permute-start | bytes 417800 | tf_op jit(solution)/shard_map/ppermute | solution.py:489
  54.6 1.6 %copy-start.2 = (bf16[16,256,256]{2,1,0:T(8,128)(2,1)S(1)}, bf16[16,256,256]{2,1,0:T(8,128)(2,1)}, u32[]{:S(2)}) copy-start(bf16[16,256,256]{2,1,0:T(8,128)(2,1)} %imag_ref.3) | copy-start | bytes 6291460
  58.4 3.9 %collective-permute-start.4 = (bf16[8,34,256]{2,1,0:T(8,128)(2,1)S(1)}, bf16[8,34,256]{2,1,0:T(8,128)(2,1)S(1)}, u32[]{:S(2)}, u32[]{:S(2)}) collective-permute-start(bf16[8,34,256]{2,1,0:T(8,128)(2,1)S(1)} %all_to_all.21.r_ref.refs_4_.refs_0_), channel_id=1, source_target_pairs={{0,1},{1,0},{2,3},{3,2},{4,5},{5,4},{6,7},{7,6},{8,9},{9,8},{10,11... | collective-permute-start | bytes 417800 | tf_op jit(solution)/shard_map/ppermute | solution.py:489
  58.4 3.9 %collective-permute-start.5 = (bf16[8,34,256]{2,1,0:T(8,128)(2,1)S(1)}, bf16[8,34,256]{2,1,0:T(8,128)(2,1)S(1)}, u32[]{:S(2)}, u32[]{:S(2)}) collective-permute-start(bf16[8,34,256]{2,1,0:T(8,128)(2,1)S(1)} %collective-permute-done.3.refs_6_.refs_2_), channel_id=1, source_target_pairs={{0,1},{1,0},{2,3},{3,2},{4,5},{5,4},{6,7},{7,6},{8,9},{9,8},{10,11... | collective-permute-start | bytes 417800 | tf_op jit(solution)/shard_map/ppermute | solution.py:489
  58.9 10.7 %all-to-all-start.3 = ((bf16[8,32,256]{2,1,0:T(8,128)(2,1)}), bf16[8,32,256]{2,1,0:T(8,128)(2,1)S(1)}, u32[]{:S(2)}, u32[]{:S(2)}) async-start(bf16[8,32,256]{2,1,0:T(8,128)(2,1)} %mix_grad.1), calls=%async_computation.3 | async-start | bytes 262144 | tf_op jit(solution)/shard_map/all_to_all | solution.py:486
  67.2 0.6 copy-start.9
  69.6 0.6 copy-start.11

commit v7 on v5

v7 whole, which is shorter than its diff:
```python
import functools
import math

import jax
import jax.numpy as jnp
import ml_dtypes
import numpy as np
from jax import lax
from jax.experimental import pallas as pl
from jax.experimental.pallas import tpu as pltpu
from jax.sharding import PartitionSpec as P

COUPLING = 0.125
TILE = 256
LANES = 128
GELU_S = math.sqrt(2.0 / math.pi)
GELU_C = 0.044715
VMEM = pl.BlockSpec(memory_space=pltpu.VMEM)
SMEM = pl.BlockSpec(memory_space=pltpu.SMEM)
HBM = pl.BlockSpec(memory_space=pltpu.HBM)
MIB = 1024 * 1024


def half_table(cell_count, mode_count, groups):
    half = cell_count // 2
    product_index = np.arange(mode_count)[:, None] * np.arange(half)[None, :] % cell_count
    angles = product_index.astype(np.float32) * np.float32(2.0 * math.pi / cell_count)
    norm_scale = np.float32(1.0 / math.sqrt(cell_count))
    cosine = (np.cos(angles) * norm_scale).reshape(groups, -1, half)
    sine = (np.sin(angles) * norm_scale).reshape(groups, -1, half)
    table = np.concatenate([cosine, -sine], axis=1).reshape(2 * mode_count, half)
    return table.astype(ml_dtypes.bfloat16)


def row_signs(all_rows, span, channels):
    row = lax.broadcasted_iota(jnp.int32, (all_rows, channels), 0)
    per_owner = span // 2
    mode = (row // span) * per_owner + lax.rem(row, per_owner)
    return jnp.where(lax.rem(mode, 2) == 0, 1.0, -1.0).astype(jnp.float32)


def dot(left, right, left_dim=1, right_dim=0):
    return lax.dot_general(
        left,
        right,
        (((left_dim,), (right_dim,)), ((), ())),
        preferred_element_type=jnp.float32,
    )


def put(ref, at, value):
    for lane in range(ref.shape[0]):
        ref[lane, at, :] = value[:, lane * LANES : (lane + 1) * LANES]


def take(ref, at):
    return jnp.concatenate([ref[lane, at, :] for lane in range(ref.shape[0])], axis=1)


def spectrum_kernel(x_ref, f_ref, msg_ref):
    groups, rows = msg_ref.shape[0], msg_ref.shape[1]
    steps, all_rows, tile = f_ref.shape
    cells, channels = x_ref.shape
    half = cells // 2
    span = all_rows // groups
    sums = []
    for base in (0, half):
        total = None
        for step in range(steps):
            at = base + step * tile
            part = dot(f_ref[step], x_ref[at : at + tile, :])
            total = part if total is None else total + part
        sums.append(total)
    spectra = (sums[0] + row_signs(all_rows, span, channels) * sums[1]).astype(jnp.bfloat16)
    ends = extra_rows(x_ref[0:1, :], x_ref[cells - 1 : cells, :], rows - span, channels)
    for at in range(groups):
        msg_ref[at, 0:span, :] = spectra[at * span : (at + 1) * span]
        msg_ref[at, span:rows, :] = ends


def extra_rows(first, second, count, channels):
    parts = [first.astype(jnp.float32), second.astype(jnp.float32)]
    if count > 2:
        parts.append(jnp.zeros((count - 2, channels), jnp.float32))
    return jnp.concatenate(parts, axis=0).astype(jnp.bfloat16)


def mix_kernel(backward, r_ref, real_ref, imag_ref, *refs):
    x_ref, y_ref = refs[-2:]
    groups, modes = r_ref.shape[0], real_ref.shape[0]
    span = 2 * modes
    if backward:
        early_ref, out_ref, copied_ref, sem = refs[:4]
        copy = pltpu.make_async_copy(early_ref, copied_ref, sem)
        copy.start()
    else:
        out_ref = refs[0]
    for source in range(groups):
        put(x_ref, pl.ds(source * span, span), r_ref[source, 0:span, :].astype(jnp.float32))
    for mode in range(modes):
        first = pl.ds(mode, groups, stride=span)
        second = pl.ds(modes + mode, groups, stride=span)
        rows = jnp.concatenate([take(x_ref, first), take(x_ref, second)], axis=0).astype(
            jnp.bfloat16
        )
        dim = 1 if backward else 0
        by_real = dot(rows, real_ref[mode], 1, dim)
        by_imag = dot(rows, imag_ref[mode], 1, dim)
        if backward:
            put(y_ref, first, by_real[:groups] + by_imag[groups:])
            put(y_ref, second, by_real[groups:] - by_imag[:groups])
        else:
            put(y_ref, first, by_real[:groups] - by_imag[groups:])
            put(y_ref, second, by_imag[:groups] + by_real[groups:])
    for source in range(groups):
        rows = take(y_ref, pl.ds(source * span, span)).astype(jnp.bfloat16)
        out_ref[source] = rows
    if backward:
        copy.wait()


def own_pipe(pipes):
    return lax.axis_index("len") * pipes + lax.axis_index("pipe")


def two_rows(first, second, channels):
    return jnp.concatenate([first, second, jnp.zeros((6, channels), jnp.float32)], axis=0)


def junction_sums(pipes, msgs, inlet_ref, outlet_ref, both):
    groups, rows, channels = msgs[0].shape
    column = lax.axis_index("pipe")
    me = own_pipe(pipes)
    owns = inlet_ref[me], outlet_ref[me]
    is_first = lax.broadcasted_iota(jnp.int32, (2, channels), 0) == 0

    def matches(pipe, junction):
        first = (inlet_ref[pipe] == junction).astype(jnp.float32)
        last = (outlet_ref[pipe] == junction).astype(jnp.float32)
        return first + last if both else jnp.where(is_first, first, last)

    def add(group, carried):
        for step in range(pipes):
            pipe = group * pipes + lax.bitwise_xor(column, step)
            ends = msgs[step][group, rows - 2 : rows, :].astype(jnp.float32)
            carried = tuple(
                total + ends * matches(pipe, own) for total, own in zip(carried, owns)
            )
        return carried

    zero = jnp.zeros((2, channels), jnp.float32)
    totals = lax.fori_loop(0, groups, add, (zero, zero), unroll=min(groups, 8))
    return two_rows(
        jnp.sum(totals[0], axis=0, keepdims=True),
        jnp.sum(totals[1], axis=0, keepdims=True),
        channels,
    )


def junction_forward(pipes, msgs, inlet_ref, outlet_ref, weight_ref, bias_ref):
    sums = junction_sums(pipes, msgs, inlet_ref, outlet_ref, False)
    act = dot(sums.astype(jnp.bfloat16), weight_ref[...]) + bias_ref[...]
    sigmoid_part = jax.nn.sigmoid(act)
    junc_rows = (act * sigmoid_part).astype(jnp.bfloat16).astype(jnp.float32)
    cond = COUPLING * (junc_rows[0:1] + junc_rows[1:2])
    return cond, sigmoid_part * (1.0 + act * (1.0 - sigmoid_part))


def junction_backward(pipes, msgs, inlet_ref, outlet_ref, weight_ref, slope_ref):
    junc_grad = COUPLING * junction_sums(pipes, msgs, inlet_ref, outlet_ref, True)
    act_grad = (junc_grad * slope_ref[...]).astype(jnp.bfloat16)
    return dot(act_grad, weight_ref[...], 1, 1).astype(jnp.bfloat16).astype(jnp.float32)


def started(copies):
    for copy in copies:
        copy.start()
    return copies


def wait(copies):
    for copy in copies:
        copy.wait()


def brought(pairs, sems, base=0):
    return started(
        [
            pltpu.make_async_copy(source, target, sems.at[base + place])
            for place, (source, target) in enumerate(pairs)
        ]
    )


def layer_kernel(pipes, *refs):
    msgs, refs = refs[:pipes], refs[pipes:]
    (inlet_ref, outlet_ref, junc_weight_ref, junc_bias_ref), refs = refs[:4], refs[4:]
    x_ref, cot_ref, f_ref, ft_ref, weight_ref, bias_ref, modes_ref = refs[:7]
    out_ref, total_ref, msg_ref, slope_ref, low_ref, high_ref = refs[7:]
    steps, all_rows, tile = f_ref.shape
    half = steps * tile
    channels = x_ref.shape[1]
    groups, rows = msg_ref.shape[0], msg_ref.shape[1]
    span = all_rows // groups
    cond, slope = junction_forward(
        pipes, msgs, inlet_ref, outlet_ref, junc_weight_ref, junc_bias_ref
    )
    slope_ref[...] = slope
    row = lax.broadcasted_iota(jnp.int32, (all_rows, channels), 0)
    doubled = jnp.where((row == 0) | (row == span // 2), 1.0, 2.0).astype(jnp.float32)
    signs = row_signs(all_rows, span, channels)
    modes = jnp.concatenate(
        [modes_ref[at, 0:span, :].astype(jnp.float32) for at in range(groups)], axis=0
    )
    modes = modes * doubled
    modes = (modes.astype(jnp.bfloat16), (modes * signs).astype(jnp.bfloat16))
    weight = weight_ref[...]
    bias = bias_ref[...]
    for step in range(steps):
        for side, acc_ref in enumerate((low_ref, high_ref)):
            at = pl.ds(side * half + step * tile, tile)
            pointwise = dot(x_ref[at, :], weight) + bias
            spectral = dot(ft_ref[pl.ds(step * tile, tile), :], modes[side])
            summed = pointwise + (spectral + cond).astype(jnp.bfloat16).astype(jnp.float32)
            square = summed * summed
            part = 0.5 + 0.5 * jnp.tanh(summed * (GELU_S + (GELU_S * GELU_C) * square))
            result = summed * part
            out_ref[at, :] = result.astype(jnp.bfloat16)
            slope = part + result * (1.0 - part) * (
                2.0 * GELU_S + (6.0 * GELU_S * GELU_C) * square
            )
            total = (cot_ref[at, :].astype(jnp.float32) * slope).astype(jnp.bfloat16)
            total_ref[at, :] = total
            term = dot(f_ref[step], total)
            if step == 0:
                acc_ref[...] = term
            else:
                acc_ref[...] += term
    acc = low_ref[...] + signs * high_ref[...]
    grad_cond = acc[0:1, :] * (1.0 / f_ref[0, 0:1, 0:1].astype(jnp.float32))
    upper = grad_cond.astype(jnp.bfloat16).astype(jnp.float32)
    extra = extra_rows(upper, grad_cond - upper, rows - span, channels)
    grad_spec = (acc * doubled).astype(jnp.bfloat16)
    for at in range(groups):
        msg_ref[at, 0:span, :] = grad_spec[at * span : (at + 1) * span]
        msg_ref[at, span:rows, :] = extra


def last_kernel(pipes, modes, per_copy, *refs):
    fields, grads, refs = refs[:pipes], refs[pipes : 2 * pipes], refs[2 * pipes :]
    (inlet_ref, outlet_ref, junc_weight_ref, slope_ref), refs = refs[:4], refs[4:]
    total_ref, ft_ref, weight_ref, modes_ref = refs[:4]
    real_out, imag_out, field_out = refs[4:7]
    x_ref, g_ref, real_ref, imag_ref, tiles_ref, weight_sems, field_sems = refs[7:]
    groups, span, channels = modes_ref.shape
    steps, tile = tiles_ref.shape[0], tiles_ref.shape[2]
    half, all_rows = steps * tile, groups * span
    for step in range(pipes):
        for source in range(groups):
            at = pl.ds((step * groups + source) * span, span)
            put(x_ref, at, fields[step][source, 0:span, :].astype(jnp.float32))
            put(g_ref, at, grads[step][source, 0:span, :].astype(jnp.float32))
    count = pipes * groups
    going = []

    def weight_part(number):
        for mode in range(number * per_copy, (number + 1) * per_copy):
            first = pl.ds(mode, count, stride=span)
            second = pl.ds(modes + mode, count, stride=span)
            a, b = take(x_ref, first), take(x_ref, second)
            u, v = take(g_ref, first), take(g_ref, second)
            left = jnp.concatenate([a, b], axis=0).astype(jnp.bfloat16)
            right = jnp.concatenate([u, v], axis=0).astype(jnp.bfloat16)
            turned = jnp.concatenate([v, -u], axis=0).astype(jnp.bfloat16)
            real_ref[mode] = dot(left, right, 0, 0)
            imag_ref[mode] = dot(left, turned, 0, 0)
        at = pl.ds(number * per_copy, per_copy)
        return started(
            [
                pltpu.make_async_copy(real_ref.at[at], real_out.at[at], weight_sems.at[number, 0]),
                pltpu.make_async_copy(imag_ref.at[at], imag_out.at[at], weight_sems.at[number, 1]),
            ]
        )

    back = jnp.concatenate(
        [modes_ref[at, 0:span, :].astype(jnp.float32) for at in range(groups)], axis=0
    )
    signs = row_signs(all_rows, span, channels)
    back = (back.astype(jnp.bfloat16), (back * signs).astype(jnp.bfloat16))
    weight = weight_ref[...]
    row = lax.broadcasted_iota(jnp.int32, (tile, channels), 0)
    sums_grad = junction_backward(
        pipes, grads, inlet_ref, outlet_ref, junc_weight_ref, slope_ref
    )

    def field_part(step):
        for side in range(2):
            at = pl.ds(side * half + step * tile, tile)
            grad_cells = dot(ft_ref[pl.ds(step * tile, tile), :], back[side])
            if step == 0 and side == 0:
                grad_cells = grad_cells + jnp.where(row == 0, sums_grad[0:1, :], 0.0)
            if step == steps - 1 and side == 1:
                grad_cells = grad_cells + jnp.where(row == tile - 1, sums_grad[1:2, :], 0.0)
            spread = grad_cells.astype(jnp.bfloat16).astype(jnp.float32)
            local = dot(total_ref[at, :], weight, 1, 1)
            tiles_ref[step, side] = (local + spread).astype(jnp.bfloat16)
        copies = []
        for side in range(2):
            at = pl.ds(side * half + step * tile, tile)
            copies.append(
                pltpu.make_async_copy(
                    tiles_ref.at[step, side], field_out.at[at], field_sems.at[step, side]
                )
            )
        return started(copies)

    numbers = modes // per_copy
    for place in range(max(numbers, steps)):
        if place < numbers:
            going += weight_part(place)
        if place < steps:
            going += field_part(place)
    wait(going)


def rows_of(count, channels):
    return pltpu.VMEM((channels // LANES, count, LANES), jnp.float32)


def call(kernel, outs, specs, scratch=(), out_specs=None, name=None, limit=8, busy=1):
    return pl.pallas_call(
        kernel,
        out_shape=outs,
        in_specs=specs,
        out_specs=out_specs if out_specs is not None else [VMEM] * len(outs),
        scratch_shapes=list(scratch),
        compiler_params=pltpu.CompilerParams(vmem_limit_bytes=limit * MIB),
        cost_estimate=pl.CostEstimate(
            flops=busy * 1_000_000_000, bytes_accessed=busy * MIB, transcendentals=0
        ),
        name=name,
    )


def body(
    inputs,
    cotangent,
    point_weight,
    point_bias,
    spec_real,
    spec_imag,
    junc_weight,
    junc_bias,
    inlet_ids,
    outlet_ids,
):
    per_dev, cell_count, channels = inputs.shape
    assert per_dev == 1
    groups, pipes = lax.axis_size("len"), lax.axis_size("pipe")
    assert pipes == 4
    modes = spec_real.shape[0]
    span = 2 * modes
    all_rows = span * groups
    steps = cell_count // (2 * TILE)
    table = half_table(cell_count, modes * groups, groups)
    tiled = table.reshape(all_rows, steps, TILE).transpose(1, 0, 2)
    f_table = jnp.asarray(np.ascontiguousarray(tiled))
    ft_table = jnp.asarray(np.ascontiguousarray(table.T))
    field = inputs.reshape(cell_count, channels)
    cot = cotangent.reshape(cell_count, channels)
    bias_row = point_bias.reshape(1, channels)
    junc_bias_row = junc_bias.reshape(1, channels)
    shape = jax.ShapeDtypeStruct
    bf16, f32 = jnp.bfloat16, jnp.float32
    message = shape((groups, span + 2, channels), bf16)
    chunks = shape((groups, span, channels), bf16)
    dma = pltpu.SemaphoreType.DMA

    def exchange(value):
        return lax.all_to_all(value, "len", split_axis=0, concat_axis=0, tiled=True)

    def swap(value, step):
        return lax.ppermute(value, "pipe", [(i, i ^ step) for i in range(pipes)])

    def gather(own):
        return [own] + [swap(own, step) for step in range(1, pipes)]

    def mix(backward, value, *early):
        return call(
            functools.partial(mix_kernel, backward),
            [chunks, early[0]] if backward else [chunks],
            [VMEM] * (4 if backward else 3),
            ([dma] if backward else []) + [rows_of(all_rows, channels)] * 2,
            out_specs=[VMEM, HBM] if backward else [VMEM],
            name="mix_grad" if backward else "mix",
            busy=12,
        )(value, spec_real, spec_imag, *early)

    (sent,) = call(spectrum_kernel, [message], [VMEM] * 2, name="spectrum", busy=12)(
        field, f_table
    )
    received = exchange(sent)
    fields = gather(received)
    (mixed,) = mix(False, received)
    returned = exchange(mixed)
    early, total, sent, slope = call(
        functools.partial(layer_kernel, pipes),
        [shape(field.shape, bf16)] * 2 + [message, shape((8, channels), f32)],
        [VMEM] * pipes + [SMEM] * 2 + [VMEM] * 9,
        [pltpu.VMEM((all_rows, channels), f32)] * 2,
        name="layer",
        busy=12,
    )(
        *fields,
        inlet_ids,
        outlet_ids,
        junc_weight,
        junc_bias_row,
        field,
        cot,
        f_table,
        ft_table,
        point_weight,
        bias_row,
        returned,
    )
    received = exchange(sent)
    grads = gather(received)
    mixed, outputs = mix(True, received, early)
    returned = exchange(mixed)
    big = shape((modes, channels, channels), f32)
    per_copy = math.gcd(modes, 2)
    grad_real, grad_imag, grad_inputs = call(
        functools.partial(last_kernel, pipes, modes, per_copy),
        [big, big, shape(field.shape, bf16)],
        [VMEM] * (2 * pipes) + [SMEM] * 2 + [VMEM] * 6,
        [rows_of(pipes * all_rows, channels)] * 2
        + [pltpu.VMEM(big.shape, f32)] * 2
        + [pltpu.VMEM((steps, 2, TILE, channels), bf16)]
        + [dma((modes // per_copy, 2)), dma((steps, 2))],
        out_specs=[HBM] * 3,
        name="last",
        limit=20,
    )(
        *fields,
        *grads,
        inlet_ids,
        outlet_ids,
        junc_weight,
        slope,
        total,
        ft_table,
        point_weight,
        returned,
    )
    return (
        outputs.reshape(inputs.shape),
        grad_inputs.reshape(inputs.shape),
        grad_real,
        grad_imag,
    )


def solution(mesh):
    placed = (
        P(("len", "pipe"), None, None),
        P(("len", "pipe"), None, None),
        P(),
        P(),
        P("len", None, None),
        P("len", None, None),
        P(),
        P(),
        P(),
        P(),
    )
    return jax.shard_map(
        body,
        mesh=mesh,
        in_specs=placed,
        out_specs=(
            P(("len", "pipe"), None, None),
            P(("len", "pipe"), None, None),
            P("len", None, None),
            P("len", None, None),
        ),
        check_vma=False,
    )
```

time: 78.1 us -> 81.9 us (1.049)
  Pallas kernels: 14.9 us -> 12.9 us
  blocking collectives: 26.4 us -> 28.3 us
  local copies, waits for them, and re-layouts: 12.7 us -> 14.4 us
  waiting for transfers between devices: 12.6 us -> 13.7 us
    ppermute x6, waiting for transfers between devices: 4.12 us -> 13.7 us  [swap(): return lax.ppermute(value, 'pipe', [(i, i ^ step) for i in range(pipes)])]
    all_to_all x2, waiting for transfers between devices: 8.45 us -> 0.01 us  [exchange(): return lax.all_to_all(value, 'len', split_axis=0, concat_axis=0, tiled=True)]
    pallas_call x5 -> x2, Pallas kernels: 11.1 us -> 9.11 us  [the longest x1 5.04 us: body(): call(functools.partial(last_kernel, pipes, modes, per_copy), [big, big, s...]
    all_to_all x2, blocking collectives: 26.4 us -> 28.3 us  [exchange(): return lax.all_to_all(value, 'len', split_axis=0, concat_axis=0, tiled=True)]
    unnamed x48 -> x58, local copies, waits for them, and re-layouts: 12.7 us -> 14.4 us
  transfers between devices with their start and end apart: 8 -> 8, of which waited for: 5 -> 4; matrix products, arithmetic and copies ran while one was open for 0% -> 0% of each run, Pallas kernels for 7% -> 0%
where the time goes in v7:
time: 81.9 us; the launch traced here: 80.8 us
  blocking collectives  28.3 us (35%)
  local copies, waits for them, and re-layouts  14.4 us (18%)
  waiting for transfers between devices  13.7 us (17%)
  Pallas kernels  12.9 us (16%)
  starting transfers between devices  10.6 us (13%)
  between operations  0.86 us (1%)
    all_to_all x2, blocking collectives, exchange(): return lax.all_to_all(value, 'len', split_axis=0, concat_axis=0, tiled=True)  28.3 us
    unnamed x58, local copies, waits for them, and re-layouts  14.4 us
    ppermute x6, waiting for transfers between devices, swap(): return lax.ppermute(value, 'pipe', [(i, i ^ step) for i in range(pipes)])  13.7 us
    all_to_all x2, starting transfers between devices, exchange(): return lax.all_to_all(value, 'len', split_axis=0, concat_axis=0, tiled=True)  6.75 us
    pallas_call x1, Pallas kernels, body(): call(functools.partial(last_kernel, pipes, modes, per_copy), [big, big, s...  5.04 us
    pallas_call x1, Pallas kernels, body(): call(functools.partial(layer_kernel, pipes), [shape(field.shape, bf16)] *...  4.08 us
    ppermute x6, starting transfers between devices, swap(): return lax.ppermute(value, 'pipe', [(i, i ^ step) for i in range(pipes)])  3.84 us
    pallas_call x2, Pallas kernels, mix(): call(functools.partial(mix_kernel, backward), [chunks, early[0]] if backw...  3.34 us
  transfers between devices with their start and end apart: 8, of which 4 were waited for; matrix products, arithmetic and copies ran while one was open for 0% of the time, Pallas kernels for 0%

profile of v7, /device:TPU:0, one launch (start us, length us, event | category | flops | bytes accessed | tf_op | source)
XLA Modules:
  0.0 80.8 jit_solution(9322065544689771533)
XLA Ops:
  0.6 1.2 %copy-done.3 = bf16[1,2048,256]{2,1,0:T(8,128)(2,1)S(1)} copy-done((bf16[1,2048,256]{2,1,0:T(8,128)(2,1)S(1)}, bf16[1,2048,256]{2,1,0:T(8,128)(2,1)}, u32[]{:S(2)}) %copy-start.3) | copy-done | bytes 1048600
  1.9 1.0 %copy-done.25 = bf16[4,256,256]{2,1,0:T(8,128)(2,1)S(1)} copy-done((bf16[4,256,256]{2,1,0:T(8,128)(2,1)S(1)}, bf16[4,256,256]{2,1,0:T(8,128)(2,1)}, u32[]{:S(2)}) %copy-start.25) | copy-done | bytes 524312
  2.9 0.4 spectrum.1
  3.3 14.9 %all_to_all.20.r_ref.refs_0_ = bf16[8,34,256]{2,1,0:T(8,128)(2,1)S(1)} all-to-all(bf16[8,34,256]{2,1,0:T(8,128)(2,1)S(1)} %spectrum.1), channel_id=1, replica_groups=mesh['len'=8,'pipe'=4] {'len'}, dimensions={0} | all-to-all | bytes 278528 | tf_op jit(solution)/shard_map/all_to_all | solution.py:380
  18.3 1.4 %mix.1 = bf16[8,32,256]{2,1,0:T(8,128)(2,1)} custom-call(bf16[8,34,256]{2,1,0:T(8,128)(2,1)S(1)} %all_to_all.20.r_ref.refs_0_, bf16[16,256,256]{2,1,0:T(8,128)(2,1)S(1)} %copy-done, bf16[16,256,256]{2,1,0:T(8,128)(2,1)S(1)} %copy-done.1), custom_call_target="tpu_custom_call" | custom-call | flops 12000000000 | bytes 12582912 | tf_op jit(solution)/shard_map/mix/pallas_call | solution.py:389
  19.7 3.4 %all-to-all-start.1 = ((bf16[8,32,256]{2,1,0:T(8,128)(2,1)}), bf16[8,32,256]{2,1,0:T(8,128)(2,1)S(1)}, u32[]{:S(2)}, u32[]{:S(2)}) async-start(bf16[8,32,256]{2,1,0:T(8,128)(2,1)} %mix.1), calls=%async_computation.1 | async-start | bytes 262144 | tf_op jit(solution)/shard_map/all_to_all | solution.py:380
  23.1 1.6 %collective-permute-start.1 = (bf16[8,34,256]{2,1,0:T(8,128)(2,1)S(1)}, bf16[8,34,256]{2,1,0:T(8,128)(2,1)S(1)}, u32[]{:S(2)}, u32[]{:S(2)}) collective-permute-start(bf16[8,34,256]{2,1,0:T(8,128)(2,1)S(1)} %all_to_all.20.r_ref.refs_0_), channel_id=1, source_target_pairs={{0,2},{1,3},{2,0},{3,1},{4,6},{5,7},{6,4},{7,5},{8,10},{9,11},{10,... | collective-permute-start | bytes 417800 | tf_op jit(solution)/shard_map/ppermute | solution.py:383
  24.7 0.3 collective-permute-start
  25.0 4.6 %collective-permute-done.2.refs_3_ = bf16[8,34,256]{2,1,0:T(8,128)(2,1)S(1)} collective-permute-done((bf16[8,34,256]{2,1,0:T(8,128)(2,1)S(1)}, bf16[8,34,256]{2,1,0:T(8,128)(2,1)S(1)}, u32[]{:S(2)}, u32[]{:S(2)}) %collective-permute-start.2) | collective-permute-done | bytes 139296 | tf_op jit(solution)/shard_map/ppermute | solution.py:383
  29.6 0.7 copy-done.6
  30.2 2.9 %collective-permute-done.1.refs_2_ = bf16[8,34,256]{2,1,0:T(8,128)(2,1)S(1)} collective-permute-done((bf16[8,34,256]{2,1,0:T(8,128)(2,1)S(1)}, bf16[8,34,256]{2,1,0:T(8,128)(2,1)S(1)}, u32[]{:S(2)}, u32[]{:S(2)}) %collective-permute-start.1) | collective-permute-done | bytes 139296 | tf_op jit(solution)/shard_map/ppermute | solution.py:383
  33.1 0.7 copy-done.9
  33.8 0.7 copy-done.12
  34.5 1.2 %copy-done.5 = bf16[1,2048,256]{2,1,0:T(8,128)(2,1)S(1)} copy-done((bf16[1,2048,256]{2,1,0:T(8,128)(2,1)S(1)}, bf16[1,2048,256]{2,1,0:T(8,128)(2,1)}, u32[]{:S(2)}) %copy-start.5) | copy-done | bytes 1048600
  35.8 0.9 %copy-done.7 = bf16[8,34,256]{2,1,0:T(8,128)(2,1)S(1)} copy-done((bf16[8,34,256]{2,1,0:T(8,128)(2,1)S(1)}, bf16[8,34,256]{2,1,0:T(8,128)(2,1)}, u32[]{:S(2)}) %copy-start.7) | copy-done | bytes 139288
  36.7 0.9 %copy-done.10 = bf16[8,34,256]{2,1,0:T(8,128)(2,1)S(1)} copy-done((bf16[8,34,256]{2,1,0:T(8,128)(2,1)S(1)}, bf16[8,34,256]{2,1,0:T(8,128)(2,1)}, u32[]{:S(2)}) %copy-start.10) | copy-done | bytes 139288
  37.6 0.9 %copy-done.13 = bf16[8,34,256]{2,1,0:T(8,128)(2,1)S(1)} copy-done((bf16[8,34,256]{2,1,0:T(8,128)(2,1)S(1)}, bf16[8,34,256]{2,1,0:T(8,128)(2,1)}, u32[]{:S(2)}) %copy-start.13) | copy-done | bytes 139288
  38.5 0.9 %copy-done.15 = bf16[256,256]{1,0:T(8,128)(2,1)S(1)} copy-done((bf16[256,256]{1,0:T(8,128)(2,1)S(1)}, bf16[256,256]{1,0:T(8,128)(2,1)}, u32[]{:S(2)}) %copy-start.15) | copy-done | bytes 131096
  39.4 0.9 %copy-done.17 = bf16[256,256]{1,0:T(8,128)(2,1)S(1)} copy-done((bf16[256,256]{1,0:T(8,128)(2,1)S(1)}, bf16[256,256]{1,0:T(8,128)(2,1)}, u32[]{:S(2)}) %copy-start.17) | copy-done | bytes 131096
  40.3 1.0 %copy-done.23 = bf16[1024,256]{1,0:T(8,128)(2,1)S(1)} copy-done((bf16[1024,256]{1,0:T(8,128)(2,1)S(1)}, bf16[1024,256]{1,0:T(8,128)(2,1)}, u32[]{:S(2)}) %copy-start.23) | copy-done | bytes 524312
  41.4 1.0 %copy-done.26 = bf16[4,256,256]{2,1,0:T(8,128)(2,1)S(1)} copy-done((bf16[4,256,256]{2,1,0:T(8,128)(2,1)S(1)}, bf16[4,256,256]{2,1,0:T(8,128)(2,1)}, u32[]{:S(2)}) %copy-start.26) | copy-done | bytes 524312
  42.4 4.1 %layer.1 = (bf16[2048,256]{1,0:T(8,128)(2,1)S(1)}, bf16[2048,256]{1,0:T(8,128)(2,1)S(1)}, bf16[8,34,256]{2,1,0:T(8,128)(2,1)S(1)}, f32[8,256]{1,0:T(8,128)S(1)}) custom-call(bf16[8,34,256]{2,1,0:T(8,128)(2,1)S(1)} %all_to_all.20.r_ref.refs_0_, bf16[8,34,256]{2,1,0:T(8,128)(2,1)S(1)} %copy-done.13, bf16[8,34,256]{2,1,0:T(8,128)(2,1)S(1)} %copy-done.10, ...), custom_call_target="tpu_custom_call" | custom-call | flops 12000000000 | bytes 12582912 | tf_op jit(solution)/shard_map/layer/pallas_call | solution.py:406
  46.5 13.4 %all_to_all.21.r_ref.refs_4_ = bf16[8,34,256]{2,1,0:T(8,128)(2,1)S(1)} all-to-all(bf16[8,34,256]{2,1,0:T(8,128)(2,1)S(1)} %get-tuple-element.13), channel_id=1, replica_groups=mesh['len'=8,'pipe'=4] {'len'}, dimensions={0} | all-to-all | bytes 278528 | tf_op jit(solution)/shard_map/all_to_all | solution.py:380
  59.9 2.0 %mix_grad.1 = (bf16[8,32,256]{2,1,0:T(8,128)(2,1)}, bf16[2048,256]{1,0:T(8,128)(2,1)}) custom-call(bf16[8,34,256]{2,1,0:T(8,128)(2,1)S(1)} %all_to_all.21.r_ref.refs_4_, bf16[16,256,256]{2,1,0:T(8,128)(2,1)S(1)} %copy-done, bf16[16,256,256]{2,1,0:T(8,128)(2,1)S(1)} %copy-done.2, bf16[2048,256]{1,0:T(8,128)(2,1)S(1)} %get-tuple-element.14.refs_0_), custom_call_target="tpu_custom_call" | custom-call | flops 12000000000 | bytes 12582912 | tf_op jit(solution)/shard_map/mix_grad/pallas_call | solution.py:389
  61.9 3.4 %all-to-all-start.3 = ((bf16[8,32,256]{2,1,0:T(8,128)(2,1)}), bf16[8,32,256]{2,1,0:T(8,128)(2,1)S(1)}, u32[]{:S(2)}, u32[]{:S(2)}) async-start(bf16[8,32,256]{2,1,0:T(8,128)(2,1)} %get-tuple-element.18), calls=%async_computation.3 | async-start | bytes 262144 | tf_op jit(solution)/shard_map/all_to_all | solution.py:380
  65.3 0.5 collective-permute-start.4
  65.8 1.4 %collective-permute-start.3 = (bf16[8,34,256]{2,1,0:T(8,128)(2,1)S(1)}, bf16[8,34,256]{2,1,0:T(8,128)(2,1)S(1)}, u32[]{:S(2)}, u32[]{:S(2)}) collective-permute-start(bf16[8,34,256]{2,1,0:T(8,128)(2,1)S(1)} %all_to_all.21.r_ref.refs_4_), channel_id=1, source_target_pairs={{0,1},{1,0},{2,3},{3,2},{4,5},{5,4},{6,7},{7,6},{8,9},{9,8},{10,11... | collective-permute-start | bytes 417800 | tf_op jit(solution)/shard_map/ppermute | solution.py:383
  67.2 4.6 %collective-permute-done.5.refs_7_ = bf16[8,34,256]{2,1,0:T(8,128)(2,1)S(1)} collective-permute-done((bf16[8,34,256]{2,1,0:T(8,128)(2,1)S(1)}, bf16[8,34,256]{2,1,0:T(8,128)(2,1)S(1)}, u32[]{:S(2)}, u32[]{:S(2)}) %collective-permute-start.5) | collective-permute-done | bytes 139296 | tf_op jit(solution)/shard_map/ppermute | solution.py:383
  71.8 1.6 %collective-permute-done.4.refs_6_ = bf16[8,34,256]{2,1,0:T(8,128)(2,1)S(1)} collective-permute-done((bf16[8,34,256]{2,1,0:T(8,128)(2,1)S(1)}, bf16[8,34,256]{2,1,0:T(8,128)(2,1)S(1)}, u32[]{:S(2)}, u32[]{:S(2)}) %collective-permute-start.4) | collective-permute-done | bytes 139296 | tf_op jit(solution)/shard_map/ppermute | solution.py:383
  73.5 1.0 %copy-done.24 = bf16[1024,256]{1,0:T(8,128)(2,1)S(1)} copy-done((bf16[1024,256]{1,0:T(8,128)(2,1)S(1)}, bf16[1024,256]{1,0:T(8,128)(2,1)}, u32[]{:S(2)}) %copy-start.24) | copy-done | bytes 524312
  74.5 1.2 %copy-done.28 = bf16[2048,256]{1,0:T(8,128)(2,1)S(1)} copy-done((bf16[2048,256]{1,0:T(8,128)(2,1)S(1)}, bf16[2048,256]{1,0:T(8,128)(2,1)}, u32[]{:S(2)}) %copy-start.28) | copy-done | bytes 1048600
  75.8 5.0 %last.1 = (f32[16,256,256]{2,1,0:T(8,128)}, f32[16,256,256]{2,1,0:T(8,128)}, bf16[2048,256]{1,0:T(8,128)(2,1)}) custom-call(bf16[8,34,256]{2,1,0:T(8,128)(2,1)S(1)} %all_to_all.20.r_ref.refs_0_, bf16[8,34,256]{2,1,0:T(8,128)(2,1)S(1)} %copy-done.14, bf16[8,34,256]{2,1,0:T(8,128)(2,1)S(1)} %copy-done.11, bf16[8,34,256]{2,1,0:T(8,128)(2,1)S(1)} %copy-done.8, ...), custom_call_target="tpu_custom_call" | custom-call | flops 1000000000 | bytes 1048576 | tf_op jit(solution)/shard_map/last/pallas_call | solution.py:433
  (49 shorter events, 0.3 us)
Async XLA Ops:
  0.6 1.2 %copy-start.3 = (bf16[1,2048,256]{2,1,0:T(8,128)(2,1)S(1)}, bf16[1,2048,256]{2,1,0:T(8,128)(2,1)}, u32[]{:S(2)}) copy-start(bf16[1,2048,256]{2,1,0:T(8,128)(2,1)} %param.12) | copy-start | bytes 3145732
  1.9 1.0 %copy-start.25 = (bf16[4,256,256]{2,1,0:T(8,128)(2,1)S(1)}, bf16[4,256,256]{2,1,0:T(8,128)(2,1)}, u32[]{:S(2)}) copy-start(bf16[4,256,256]{2,1,0:T(8,128)(2,1)} %constant.4.clone.f_ref.refs_10_) | copy-start | bytes 1572868
  2.9 15.4 %copy-start = (bf16[16,256,256]{2,1,0:T(8,128)(2,1)S(1)}, bf16[16,256,256]{2,1,0:T(8,128)(2,1)}, u32[]{:S(2)}) copy-start(bf16[16,256,256]{2,1,0:T(8,128)(2,1)} %real_ref.3) | copy-start | bytes 6291460
  2.9 15.4 %copy-start.1 = (bf16[16,256,256]{2,1,0:T(8,128)(2,1)S(1)}, bf16[16,256,256]{2,1,0:T(8,128)(2,1)}, u32[]{:S(2)}) copy-start(bf16[16,256,256]{2,1,0:T(8,128)(2,1)} %imag_ref.3) | copy-start | bytes 6291460
  18.3 16.2 %copy-start.4 = (bf16[1,2048,256]{2,1,0:T(8,128)(2,1)S(1)}, bf16[1,2048,256]{2,1,0:T(8,128)(2,1)}, u32[]{:S(2)}) copy-start(bf16[1,2048,256]{2,1,0:T(8,128)(2,1)} %param.12) | copy-start | bytes 3145732
  18.3 16.2 %copy-start.19 = (f32[256]{0:T(256)S(1)}, f32[256]{0:T(256)}, u32[]{:S(2)}) copy-start(f32[256]{0:T(256)} %param.19) | copy-start | bytes 3076
  18.3 16.2 %copy-start.20 = (f32[256]{0:T(256)S(1)}, f32[256]{0:T(256)}, u32[]{:S(2)}) copy-start(f32[256]{0:T(256)} %param.15) | copy-start | bytes 3076
  18.3 16.2 %copy-start.21 = (s32[32]{0:T(128)S(1)}, s32[32]{0:T(128)}, u32[]{:S(2)}) copy-start(s32[32]{0:T(128)} %refs_8_.1) | copy-start | bytes 388
  18.3 16.2 %copy-start.22 = (s32[32]{0:T(128)S(1)}, s32[32]{0:T(128)}, u32[]{:S(2)}) copy-start(s32[32]{0:T(128)} %refs_9_.1) | copy-start | bytes 388
  19.7 14.8 %all-to-all-start.1 = ((bf16[8,32,256]{2,1,0:T(8,128)(2,1)}), bf16[8,32,256]{2,1,0:T(8,128)(2,1)S(1)}, u32[]{:S(2)}, u32[]{:S(2)}) async-start(bf16[8,32,256]{2,1,0:T(8,128)(2,1)} %mix.1), calls=%async_computation.1 | async-start | bytes 262144 | tf_op jit(solution)/shard_map/all_to_all | solution.py:380
  23.1 6.5 %collective-permute-start.2 = (bf16[8,34,256]{2,1,0:T(8,128)(2,1)S(1)}, bf16[8,34,256]{2,1,0:T(8,128)(2,1)S(1)}, u32[]{:S(2)}, u32[]{:S(2)}) collective-permute-start(bf16[8,34,256]{2,1,0:T(8,128)(2,1)S(1)} %all_to_all.20.r_ref.refs_0_), channel_id=1, source_target_pairs={{0,3},{1,2},{2,1},{3,0},{4,7},{5,6},{6,5},{7,4},{8,11},{9,10},{10,... | collective-permute-start | bytes 417800 | tf_op jit(solution)/shard_map/ppermute | solution.py:383
  23.1 10.0 %collective-permute-start.1 = (bf16[8,34,256]{2,1,0:T(8,128)(2,1)S(1)}, bf16[8,34,256]{2,1,0:T(8,128)(2,1)S(1)}, u32[]{:S(2)}, u32[]{:S(2)}) collective-permute-start(bf16[8,34,256]{2,1,0:T(8,128)(2,1)S(1)} %all_to_all.20.r_ref.refs_0_), channel_id=1, source_target_pairs={{0,2},{1,3},{2,0},{3,1},{4,6},{5,7},{6,4},{7,5},{8,10},{9,11},{10,... | collective-permute-start | bytes 417800 | tf_op jit(solution)/shard_map/ppermute | solution.py:383
  24.7 9.1 %collective-permute-start = (bf16[8,34,256]{2,1,0:T(8,128)(2,1)S(1)}, bf16[8,34,256]{2,1,0:T(8,128)(2,1)S(1)}, u32[]{:S(2)}, u32[]{:S(2)}) collective-permute-start(bf16[8,34,256]{2,1,0:T(8,128)(2,1)S(1)} %all_to_all.20.r_ref.refs_0_), channel_id=1, source_target_pairs={{0,1},{1,0},{2,3},{3,2},{4,5},{5,4},{6,7},{7,6},{8,9},{9,8},{10,11... | collective-permute-start | bytes 417800 | tf_op jit(solution)/shard_map/ppermute | solution.py:383
  34.5 1.2 %copy-start.5 = (bf16[1,2048,256]{2,1,0:T(8,128)(2,1)S(1)}, bf16[1,2048,256]{2,1,0:T(8,128)(2,1)}, u32[]{:S(2)}) copy-start(bf16[1,2048,256]{2,1,0:T(8,128)(2,1)} %param.13) | copy-start | bytes 3145732
  35.7 0.9 %copy-start.7 = (bf16[8,34,256]{2,1,0:T(8,128)(2,1)S(1)}, bf16[8,34,256]{2,1,0:T(8,128)(2,1)}, u32[]{:S(2)}) copy-start(bf16[8,34,256]{2,1,0:T(8,128)(2,1)} %copy-done.6) | copy-start | bytes 417796
  36.7 0.9 %copy-start.10 = (bf16[8,34,256]{2,1,0:T(8,128)(2,1)S(1)}, bf16[8,34,256]{2,1,0:T(8,128)(2,1)}, u32[]{:S(2)}) copy-start(bf16[8,34,256]{2,1,0:T(8,128)(2,1)} %copy-done.9) | copy-start | bytes 417796
  37.6 0.9 %copy-start.13 = (bf16[8,34,256]{2,1,0:T(8,128)(2,1)S(1)}, bf16[8,34,256]{2,1,0:T(8,128)(2,1)}, u32[]{:S(2)}) copy-start(bf16[8,34,256]{2,1,0:T(8,128)(2,1)} %copy-done.12) | copy-start | bytes 417796
  40.3 1.0 %copy-start.23 = (bf16[1024,256]{1,0:T(8,128)(2,1)S(1)}, bf16[1024,256]{1,0:T(8,128)(2,1)}, u32[]{:S(2)}) copy-start(bf16[1024,256]{1,0:T(8,128)(2,1)} %constant.5.clone.refs_11_.refs_13_) | copy-start | bytes 1572868
  41.3 1.0 %copy-start.26 = (bf16[4,256,256]{2,1,0:T(8,128)(2,1)S(1)}, bf16[4,256,256]{2,1,0:T(8,128)(2,1)}, u32[]{:S(2)}) copy-start(bf16[4,256,256]{2,1,0:T(8,128)(2,1)} %constant.4.clone.f_ref.refs_10_) | copy-start | bytes 1572868
  42.4 17.5 %copy-start.2 = (bf16[16,256,256]{2,1,0:T(8,128)(2,1)S(1)}, bf16[16,256,256]{2,1,0:T(8,128)(2,1)}, u32[]{:S(2)}) copy-start(bf16[16,256,256]{2,1,0:T(8,128)(2,1)} %imag_ref.3) | copy-start | bytes 6291460
  46.5 15.4 %copy-start.27 = (bf16[2048,256]{1,0:T(8,128)(2,1)}, bf16[2048,256]{1,0:T(8,128)(2,1)S(1)}, u32[]{:S(2)}) copy-start(bf16[2048,256]{1,0:T(8,128)(2,1)S(1)} %get-tuple-element.17.refs_12_) | copy-start | bytes 3145732
  59.9 13.6 %copy-start.8 = (bf16[8,34,256]{2,1,0:T(8,128)(2,1)S(1)}, bf16[8,34,256]{2,1,0:T(8,128)(2,1)}, u32[]{:S(2)}) copy-start(bf16[8,34,256]{2,1,0:T(8,128)(2,1)} %copy-done.6) | copy-start | bytes 417796
  59.9 13.6 %copy-start.11 = (bf16[8,34,256]{2,1,0:T(8,128)(2,1)S(1)}, bf16[8,34,256]{2,1,0:T(8,128)(2,1)}, u32[]{:S(2)}) copy-start(bf16[8,34,256]{2,1,0:T(8,128)(2,1)} %copy-done.9) | copy-start | bytes 417796
  59.9 13.6 %copy-start.14 = (bf16[8,34,256]{2,1,0:T(8,128)(2,1)S(1)}, bf16[8,34,256]{2,1,0:T(8,128)(2,1)}, u32[]{:S(2)}) copy-start(bf16[8,34,256]{2,1,0:T(8,128)(2,1)} %copy-done.12) | copy-start | bytes 417796
  59.9 13.6 %copy-start.16 = (bf16[256,256]{1,0:T(8,128)(2,1)S(1)}, bf16[256,256]{1,0:T(8,128)(2,1)}, u32[]{:S(2)}) copy-start(bf16[256,256]{1,0:T(8,128)(2,1)} %refs_10_.2) | copy-start | bytes 393220
  59.9 13.6 %copy-start.18 = (bf16[256,256]{1,0:T(8,128)(2,1)S(1)}, bf16[256,256]{1,0:T(8,128)(2,1)}, u32[]{:S(2)}) copy-start(bf16[256,256]{1,0:T(8,128)(2,1)} %refs_14_.1) | copy-start | bytes 393220
  61.9 11.6 %all-to-all-start.3 = ((bf16[8,32,256]{2,1,0:T(8,128)(2,1)}), bf16[8,32,256]{2,1,0:T(8,128)(2,1)S(1)}, u32[]{:S(2)}, u32[]{:S(2)}) async-start(bf16[8,32,256]{2,1,0:T(8,128)(2,1)} %get-tuple-element.18), calls=%async_computation.3 | async-start | bytes 262144 | tf_op jit(solution)/shard_map/all_to_all | solution.py:380
  65.3 6.6 %collective-permute-start.5 = (bf16[8,34,256]{2,1,0:T(8,128)(2,1)S(1)}, bf16[8,34,256]{2,1,0:T(8,128)(2,1)S(1)}, u32[]{:S(2)}, u32[]{:S(2)}) collective-permute-start(bf16[8,34,256]{2,1,0:T(8,128)(2,1)S(1)} %all_to_all.21.r_ref.refs_4_), channel_id=1, source_target_pairs={{0,3},{1,2},{2,1},{3,0},{4,7},{5,6},{6,5},{7,4},{8,11},{9,10},{10,... | collective-permute-start | bytes 417800 | tf_op jit(solution)/shard_map/ppermute | solution.py:383
  65.3 8.1 %collective-permute-start.4 = (bf16[8,34,256]{2,1,0:T(8,128)(2,1)S(1)}, bf16[8,34,256]{2,1,0:T(8,128)(2,1)S(1)}, u32[]{:S(2)}, u32[]{:S(2)}) collective-permute-start(bf16[8,34,256]{2,1,0:T(8,128)(2,1)S(1)} %all_to_all.21.r_ref.refs_4_), channel_id=1, source_target_pairs={{0,2},{1,3},{2,0},{3,1},{4,6},{5,7},{6,4},{7,5},{8,10},{9,11},{10,... | collective-permute-start | bytes 417800 | tf_op jit(solution)/shard_map/ppermute | solution.py:383
  65.8 7.6 %collective-permute-start.3 = (bf16[8,34,256]{2,1,0:T(8,128)(2,1)S(1)}, bf16[8,34,256]{2,1,0:T(8,128)(2,1)S(1)}, u32[]{:S(2)}, u32[]{:S(2)}) collective-permute-start(bf16[8,34,256]{2,1,0:T(8,128)(2,1)S(1)} %all_to_all.21.r_ref.refs_4_), channel_id=1, source_target_pairs={{0,1},{1,0},{2,3},{3,2},{4,5},{5,4},{6,7},{7,6},{8,9},{9,8},{10,11... | collective-permute-start | bytes 417800 | tf_op jit(solution)/shard_map/ppermute | solution.py:383
  73.5 1.0 %copy-start.24 = (bf16[1024,256]{1,0:T(8,128)(2,1)S(1)}, bf16[1024,256]{1,0:T(8,128)(2,1)}, u32[]{:S(2)}) copy-start(bf16[1024,256]{1,0:T(8,128)(2,1)} %constant.5.clone.refs_11_.refs_13_) | copy-start | bytes 1572868
  74.5 1.2 %copy-start.28 = (bf16[2048,256]{1,0:T(8,128)(2,1)S(1)}, bf16[2048,256]{1,0:T(8,128)(2,1)}, u32[]{:S(2)}) copy-start(bf16[2048,256]{1,0:T(8,128)(2,1)} %copy-done.27) | copy-start | bytes 3145732
  (5 other events, 3.8 us)

commit v8 on v7

--- a/solution.py
+++ b/solution.py
@@ -123,53 +123,40 @@
     return lax.axis_index("len") * pipes + lax.axis_index("pipe")
 
 
-def two_rows(first, second, channels):
-    return jnp.concatenate([first, second, jnp.zeros((6, channels), jnp.float32)], axis=0)
-
-
-def junction_sums(pipes, msgs, inlet_ref, outlet_ref, both):
-    groups, rows, channels = msgs[0].shape
-    column = lax.axis_index("pipe")
+def selection(inlet_ref, outlet_ref, pipes, groups, both):
     me = own_pipe(pipes)
-    owns = inlet_ref[me], outlet_ref[me]
-    is_first = lax.broadcasted_iota(jnp.int32, (2, channels), 0) == 0
-
-    def matches(pipe, junction):
-        first = (inlet_ref[pipe] == junction).astype(jnp.float32)
-        last = (outlet_ref[pipe] == junction).astype(jnp.float32)
-        return first + last if both else jnp.where(is_first, first, last)
-
-    def add(group, carried):
-        for step in range(pipes):
-            pipe = group * pipes + lax.bitwise_xor(column, step)
-            ends = msgs[step][group, rows - 2 : rows, :].astype(jnp.float32)
-            carried = tuple(
-                total + ends * matches(pipe, own) for total, own in zip(carried, owns)
-            )
-        return carried
-
-    zero = jnp.zeros((2, channels), jnp.float32)
-    totals = lax.fori_loop(0, groups, add, (zero, zero), unroll=min(groups, 8))
-    return two_rows(
-        jnp.sum(totals[0], axis=0, keepdims=True),
-        jnp.sum(totals[1], axis=0, keepdims=True),
-        channels,
-    )
-
-
-def junction_forward(pipes, msgs, inlet_ref, outlet_ref, weight_ref, bias_ref):
-    sums = junction_sums(pipes, msgs, inlet_ref, outlet_ref, False)
-    act = dot(sums.astype(jnp.bfloat16), weight_ref[...]) + bias_ref[...]
-    sigmoid_part = jax.nn.sigmoid(act)
-    junc_rows = (act * sigmoid_part).astype(jnp.bfloat16).astype(jnp.float32)
-    cond = COUPLING * (junc_rows[0:1] + junc_rows[1:2])
-    return cond, sigmoid_part * (1.0 + act * (1.0 - sigmoid_part))
-
-
-def junction_backward(pipes, msgs, inlet_ref, outlet_ref, weight_ref, slope_ref):
-    junc_grad = COUPLING * junction_sums(pipes, msgs, inlet_ref, outlet_ref, True)
-    act_grad = (junc_grad * slope_ref[...]).astype(jnp.bfloat16)
-    return dot(act_grad, weight_ref[...], 1, 1).astype(jnp.bfloat16).astype(jnp.float32)
+    shape = (8, 2 * pipes * groups)
+    lane = lax.broadcasted_iota(jnp.int32, shape, 1)
+    row = lax.broadcasted_iota(jnp.int32, shape, 0)
+    own = jnp.where(row == 0, inlet_ref[me], outlet_ref[me])
+    first = jnp.full(shape, -1, jnp.int32)
+    last = jnp.full(shape, -1, jnp.int32)
+    for column in range(pipes):
+        for group in range(groups):
+            base = 2 * (column * groups + group)
+            pipe = group * pipes + column
+            here, there = lane == base, lane == base + 1
+            if both:
+                here = there = here | there
+            first = jnp.where(here, inlet_ref[pipe], first)
+            last = jnp.where(there, outlet_ref[pipe], last)
+    picked = (first == own).astype(jnp.float32) + (last == own).astype(jnp.float32)
+    return picked.astype(jnp.bfloat16)
+
+
+def junction_sums(ends_ref, inlet_ref, outlet_ref, both):
+    pipes, twice, channels = ends_ref.shape
+    picked = selection(inlet_ref, outlet_ref, pipes, twice // 2, both)
+    ends = ends_ref[...].reshape(pipes * twice, channels).astype(jnp.bfloat16)
+    return dot(picked, ends)
+
+
+def ends_kernel(r_ref, ends_ref):
+    groups, rows = r_ref.shape[0], r_ref.shape[1]
+    for group in range(groups):
+        ends_ref[2 * group : 2 * group + 2, :] = r_ref[group, rows - 2 : rows, :].astype(
+            jnp.float32
+        )
 
 
 def started(copies):
@@ -193,19 +180,24 @@
 
 
 def layer_kernel(pipes, *refs):
-    msgs, refs = refs[:pipes], refs[pipes:]
+    ends, refs = refs[:pipes], refs[pipes:]
     (inlet_ref, outlet_ref, junc_weight_ref, junc_bias_ref), refs = refs[:4], refs[4:]
     x_ref, cot_ref, f_ref, ft_ref, weight_ref, bias_ref, modes_ref = refs[:7]
-    out_ref, total_ref, msg_ref, slope_ref, low_ref, high_ref = refs[7:]
+    out_ref, total_ref, msg_ref, slope_ref, low_ref, high_ref, ends_ref = refs[7:]
     steps, all_rows, tile = f_ref.shape
     half = steps * tile
     channels = x_ref.shape[1]
     groups, rows = msg_ref.shape[0], msg_ref.shape[1]
     span = all_rows // groups
-    cond, slope = junction_forward(
-        pipes, msgs, inlet_ref, outlet_ref, junc_weight_ref, junc_bias_ref
-    )
-    slope_ref[...] = slope
+    column = lax.axis_index("pipe")
+    for step in range(pipes):
+        ends_ref[lax.bitwise_xor(column, step)] = ends[step][...]
+    sums = junction_sums(ends_ref, inlet_ref, outlet_ref, False)
+    act = dot(sums.astype(jnp.bfloat16), junc_weight_ref[...]) + junc_bias_ref[...]
+    sigmoid_part = jax.nn.sigmoid(act)
+    junc_rows = (act * sigmoid_part).astype(jnp.bfloat16).astype(jnp.float32)
+    cond = COUPLING * (junc_rows[0:1] + junc_rows[1:2])
+    slope_ref[...] = sigmoid_part * (1.0 + act * (1.0 - sigmoid_part))
     row = lax.broadcasted_iota(jnp.int32, (all_rows, channels), 0)
     doubled = jnp.where((row == 0) | (row == span // 2), 1.0, 2.0).astype(jnp.float32)
     signs = row_signs(all_rows, span, channels)
@@ -246,15 +238,12 @@
         msg_ref[at, span:rows, :] = extra
 
 
-def last_kernel(pipes, modes, per_copy, *refs):
+def weight_grad_kernel(pipes, modes, per_copy, *refs):
     fields, grads, refs = refs[:pipes], refs[pipes : 2 * pipes], refs[2 * pipes :]
     (inlet_ref, outlet_ref, junc_weight_ref, slope_ref), refs = refs[:4], refs[4:]
-    total_ref, ft_ref, weight_ref, modes_ref = refs[:4]
-    real_out, imag_out, field_out = refs[4:7]
-    x_ref, g_ref, real_ref, imag_ref, tiles_ref, weight_sems, field_sems = refs[7:]
-    groups, span, channels = modes_ref.shape
-    steps, tile = tiles_ref.shape[0], tiles_ref.shape[2]
-    half, all_rows = steps * tile, groups * span
+    real_out, imag_out, rows_ref, x_ref, g_ref, real_ref, imag_ref, ends_ref, sems = refs
+    groups, rows = fields[0].shape[0], fields[0].shape[1]
+    span = 2 * modes
     for step in range(pipes):
         for source in range(groups):
             at = pl.ds((step * groups + source) * span, span)
@@ -262,8 +251,7 @@
             put(g_ref, at, grads[step][source, 0:span, :].astype(jnp.float32))
     count = pipes * groups
     going = []
-
-    def weight_part(number):
+    for number in range(modes // per_copy):
         for mode in range(number * per_copy, (number + 1) * per_copy):
             first = pl.ds(mode, count, stride=span)
             second = pl.ds(modes + mode, count, stride=span)
@@ -275,13 +263,31 @@
             real_ref[mode] = dot(left, right, 0, 0)
             imag_ref[mode] = dot(left, turned, 0, 0)
         at = pl.ds(number * per_copy, per_copy)
-        return started(
+        going += started(
             [
-                pltpu.make_async_copy(real_ref.at[at], real_out.at[at], weight_sems.at[number, 0]),
-                pltpu.make_async_copy(imag_ref.at[at], imag_out.at[at], weight_sems.at[number, 1]),
+                pltpu.make_async_copy(real_ref.at[at], real_out.at[at], sems.at[number, 0]),
+                pltpu.make_async_copy(imag_ref.at[at], imag_out.at[at], sems.at[number, 1]),
             ]
         )
-
+    column = lax.axis_index("pipe")
+    for step in range(pipes):
+        place = lax.bitwise_xor(column, step)
+        for group in range(groups):
+            parts = grads[step][group, rows - 2 : rows, :].astype(jnp.float32)
+            ends_ref[place, 2 * group : 2 * group + 2, :] = parts
+    junc_grad = COUPLING * junction_sums(ends_ref, inlet_ref, outlet_ref, True)
+    act_grad = (junc_grad * slope_ref[...]).astype(jnp.bfloat16)
+    sums_grad = dot(act_grad, junc_weight_ref[...], 1, 1)
+    rows_ref[...] = sums_grad.astype(jnp.bfloat16).astype(jnp.float32)
+    wait(going)
+
+
+def input_grad_kernel(
+    total_ref, ft_ref, weight_ref, rows_ref, modes_ref, out_ref, tiles_ref, sems
+):
+    groups, span, channels = modes_ref.shape
+    steps, tile = tiles_ref.shape[0], tiles_ref.shape[2]
+    half, all_rows = steps * tile, groups * span
     back = jnp.concatenate(
         [modes_ref[at, 0:span, :].astype(jnp.float32) for at in range(groups)], axis=0
     )
@@ -289,37 +295,25 @@
     back = (back.astype(jnp.bfloat16), (back * signs).astype(jnp.bfloat16))
     weight = weight_ref[...]
     row = lax.broadcasted_iota(jnp.int32, (tile, channels), 0)
-    sums_grad = junction_backward(
-        pipes, grads, inlet_ref, outlet_ref, junc_weight_ref, slope_ref
-    )
-
-    def field_part(step):
+    going = []
+    for step in range(steps):
         for side in range(2):
             at = pl.ds(side * half + step * tile, tile)
             grad_cells = dot(ft_ref[pl.ds(step * tile, tile), :], back[side])
             if step == 0 and side == 0:
-                grad_cells = grad_cells + jnp.where(row == 0, sums_grad[0:1, :], 0.0)
+                grad_cells = grad_cells + jnp.where(row == 0, rows_ref[0:1, :], 0.0)
             if step == steps - 1 and side == 1:
-                grad_cells = grad_cells + jnp.where(row == tile - 1, sums_grad[1:2, :], 0.0)
+                grad_cells = grad_cells + jnp.where(row == tile - 1, rows_ref[1:2, :], 0.0)
             spread = grad_cells.astype(jnp.bfloat16).astype(jnp.float32)
             local = dot(total_ref[at, :], weight, 1, 1)
             tiles_ref[step, side] = (local + spread).astype(jnp.bfloat16)
-        copies = []
-        for side in range(2):
-            at = pl.ds(side * half + step * tile, tile)
-            copies.append(
-                pltpu.make_async_copy(
-                    tiles_ref.at[step, side], field_out.at[at], field_sems.at[step, side]
-                )
+            going += started(
+                [
+                    pltpu.make_async_copy(
+                        tiles_ref.at[step, side], out_ref.at[at], sems.at[step, side]
+                    )
+                ]
             )
-        return started(copies)
-
-    numbers = modes // per_copy
-    for place in range(max(numbers, steps)):
-        if place < numbers:
-            going += weight_part(place)
-        if place < steps:
-            going += field_part(place)
     wait(going)
 
 
@@ -383,7 +377,8 @@
         return lax.ppermute(value, "pipe", [(i, i ^ step) for i in range(pipes)])
 
     def gather(own):
-        return [own] + [swap(own, step) for step in range(1, pipes)]
+        across = swap(own, 2)
+        return [own, swap(own, 1), across, swap(across, 1)]
 
     def mix(backward, value, *early):
         return call(
@@ -400,18 +395,24 @@
         field, f_table
     )
     received = exchange(sent)
-    fields = gather(received)
+    (ends,) = call(
+        ends_kernel, [shape((2 * groups, channels), f32)], [VMEM], name="pipe_ends"
+    )(received)
+    ends = [ends] + [swap(ends, step) for step in range(1, pipes)]
     (mixed,) = mix(False, received)
+    mixed, *ends = lax.optimization_barrier((mixed, *ends))
     returned = exchange(mixed)
+    spectra = received
+    ends_buf = pltpu.VMEM((pipes, 2 * groups, channels), f32)
     early, total, sent, slope = call(
         functools.partial(layer_kernel, pipes),
         [shape(field.shape, bf16)] * 2 + [message, shape((8, channels), f32)],
         [VMEM] * pipes + [SMEM] * 2 + [VMEM] * 9,
-        [pltpu.VMEM((all_rows, channels), f32)] * 2,
+        [pltpu.VMEM((all_rows, channels), f32)] * 2 + [ends_buf],
         name="layer",
         busy=12,
     )(
-        *fields,
+        *ends,
         inlet_ids,
         outlet_ids,
         junc_weight,
@@ -425,34 +426,32 @@
         returned,
     )
     received = exchange(sent)
+    received, spectra = lax.optimization_barrier((received, spectra))
+    fields = gather(spectra)
     grads = gather(received)
     mixed, outputs = mix(True, received, early)
     returned = exchange(mixed)
     big = shape((modes, channels, channels), f32)
     per_copy = math.gcd(modes, 2)
-    grad_real, grad_imag, grad_inputs = call(
-        functools.partial(last_kernel, pipes, modes, per_copy),
-        [big, big, shape(field.shape, bf16)],
-        [VMEM] * (2 * pipes) + [SMEM] * 2 + [VMEM] * 6,
+    grad_real, grad_imag, rows = call(
+        functools.partial(weight_grad_kernel, pipes, modes, per_copy),
+        [big, big, shape((8, channels), f32)],
+        [VMEM] * (2 * pipes) + [SMEM] * 2 + [VMEM] * 2,
         [rows_of(pipes * all_rows, channels)] * 2
         + [pltpu.VMEM(big.shape, f32)] * 2
-        + [pltpu.VMEM((steps, 2, TILE, channels), bf16)]
-        + [dma((modes // per_copy, 2)), dma((steps, 2))],
-        out_specs=[HBM] * 3,
-        name="last",
-        limit=20,
-    )(
-        *fields,
-        *grads,
-        inlet_ids,
-        outlet_ids,
-        junc_weight,
-        slope,
-        total,
-        ft_table,
-        point_weight,
-        returned,
-    )
+        + [ends_buf, dma((modes // per_copy, 2))],
+        out_specs=[HBM, HBM, VMEM],
+        name="weight_grad",
+        limit=16,
+    )(*fields, *grads, inlet_ids, outlet_ids, junc_weight, slope)
+    (grad_inputs,) = call(
+        input_grad_kernel,
+        [shape(field.shape, bf16)],
+        [VMEM] * 5,
+        [pltpu.VMEM((steps, 2, TILE, channels), bf16), dma((steps, 2))],
+        out_specs=[HBM],
+        name="input_grad",
+    )(total, ft_table, point_weight, rows, returned)
     return (
         outputs.reshape(inputs.shape),
         grad_inputs.reshape(inputs.shape),

time: 81.9 us -> 70.6 us (0.86)
  local copies, waits for them, and re-layouts: 14.4 us -> 2.32 us
  blocking collectives: 28.3 us -> 34.9 us
  waiting for transfers between devices: 13.7 us -> 10.6 us
  starting transfers between devices: 10.6 us -> 8.33 us
    unnamed x58 -> x26, local copies, waits for them, and re-layouts: 14.4 us -> 2.32 us
    all_to_all x2 -> x3, blocking collectives: 28.3 us -> 34.9 us  [exchange(): return lax.all_to_all(value, 'len', split_axis=0, concat_axis=0, tiled=True)]
    ppermute x6 -> x9, waiting for transfers between devices: 13.7 us -> 7.52 us  [swap(): return lax.ppermute(value, 'pipe', [(i, i ^ step) for i in range(pipes)])]
    all_to_all x2 -> x1, waiting for transfers between devices: 0.01 us -> 3.07 us  [exchange(): return lax.all_to_all(value, 'len', split_axis=0, concat_axis=0, tiled=True)]
    all_to_all x2 -> x1, starting transfers between devices: 6.75 us -> 3.85 us  [exchange(): return lax.all_to_all(value, 'len', split_axis=0, concat_axis=0, tiled=True)]
    pallas_call x1 -> x3, Pallas kernels: 5.04 us -> 6.02 us  [the longest x1 4.54 us: body(): call(functools.partial(weight_grad_kernel, pipes, modes, per_copy), [big,...]
    ppermute x6 -> x9, starting transfers between devices: 3.84 us -> 4.47 us  [swap(): return lax.ppermute(value, 'pipe', [(i, i ^ step) for i in range(pipes)])]
  transfers between devices with their start and end apart: 8 -> 10, of which waited for: 4 -> 5; matrix products, arithmetic and copies ran while one was open for 0% -> 0% of each run, Pallas kernels for 0% -> 10%
where the time goes in v8:
time: 70.6 us; the launch traced here: 70.2 us
  blocking collectives  34.9 us (49%)
  Pallas kernels  13.2 us (19%)
  waiting for transfers between devices  10.6 us (15%)
  starting transfers between devices  8.33 us (12%)
  local copies, waits for them, and re-layouts  2.32 us (3%)
  between operations  0.85 us (1%)
    all_to_all x3, blocking collectives, exchange(): return lax.all_to_all(value, 'len', split_axis=0, concat_axis=0, tiled=True)  34.9 us
    ppermute x9, waiting for transfers between devices, swap(): return lax.ppermute(value, 'pipe', [(i, i ^ step) for i in range(pipes)])  7.52 us
    pallas_call x1, Pallas kernels, body(): call(functools.partial(weight_grad_kernel, pipes, modes, per_copy), [big,...  4.54 us
    ppermute x9, starting transfers between devices, swap(): return lax.ppermute(value, 'pipe', [(i, i ^ step) for i in range(pipes)])  4.47 us
    pallas_call x1, Pallas kernels, body(): call(functools.partial(layer_kernel, pipes), [shape(field.shape, bf16)] *...  4 us
    all_to_all x1, starting transfers between devices, exchange(): return lax.all_to_all(value, 'len', split_axis=0, concat_axis=0, tiled=True)  3.85 us
    all_to_all x1, waiting for transfers between devices, exchange(): return lax.all_to_all(value, 'len', split_axis=0, concat_axis=0, tiled=True)  3.07 us
    pallas_call x2, Pallas kernels, mix(): call(functools.partial(mix_kernel, backward), [chunks, early[0]] if backw...  2.71 us
  transfers between devices with their start and end apart: 10, of which 5 were waited for; matrix products, arithmetic and copies ran while one was open for 0% of the time, Pallas kernels for 10%

profile of v8, /device:TPU:0, one launch (start us, length us, event | category | flops | bytes accessed | tf_op | source)
XLA Modules:
  0.0 70.2 jit_solution(4835311631158308013)
XLA Ops:
  0.6 0.0 copy-start.2
  0.6 1.2 %copy-done.2 = bf16[1,2048,256]{2,1,0:T(8,128)(2,1)S(1)} copy-done((bf16[1,2048,256]{2,1,0:T(8,128)(2,1)S(1)}, bf16[1,2048,256]{2,1,0:T(8,128)(2,1)}, u32[]{:S(2)}) %copy-start.2) | copy-done | bytes 1048600
  1.9 1.0 %copy-done.12 = bf16[4,256,256]{2,1,0:T(8,128)(2,1)S(1)} copy-done((bf16[4,256,256]{2,1,0:T(8,128)(2,1)S(1)}, bf16[4,256,256]{2,1,0:T(8,128)(2,1)}, u32[]{:S(2)}) %copy-start.12) | copy-done | bytes 524312
  2.9 0.4 spectrum.1
  3.3 14.9 %all_to_all.20.r_ref.refs_0_ = bf16[8,34,256]{2,1,0:T(8,128)(2,1)S(1)} all-to-all(bf16[8,34,256]{2,1,0:T(8,128)(2,1)S(1)} %spectrum.1), channel_id=1, replica_groups=mesh['len'=8,'pipe'=4] {'len'}, dimensions={0} | all-to-all | bytes 278528 | tf_op jit(solution)/shard_map/all_to_all | solution.py:374
  18.3 0.0 copy-start.4
  18.3 0.0 copy-start.5
  18.3 0.0 copy-start.6
  18.3 0.0 copy-start.7
  18.3 0.0 copy-start.8
  18.3 0.0 copy-start.9
  18.3 0.0 copy-start.10
  18.4 0.0 copy-start.11
  18.4 0.1 collective-permute-start
  18.4 1.6 %collective-permute-start.1 = (f32[16,256]{1,0:T(8,128)S(1)}, f32[16,256]{1,0:T(8,128)S(1)}, u32[]{:S(2)}, u32[]{:S(2)}) collective-permute-start(f32[16,256]{1,0:T(8,128)S(1)} %pipe_ends.1.refs_0_), channel_id=1, source_target_pairs={{0,2},{1,3},{2,0},{3,1},{4,6},{5,7},{6,4},{7,5},{8,10},{9,11},{10,... | collective-permute-start | bytes 49160 | tf_op jit(solution)/shard_map/ppermute | solution.py:377
  20.0 0.3 collective-permute-start.2
  20.3 0.8 %mix.1 = bf16[8,32,256]{2,1,0:T(8,128)(2,1)S(1)} custom-call(bf16[8,34,256]{2,1,0:T(8,128)(2,1)S(1)} %all_to_all.20.r_ref.refs_0_, bf16[16,256,256]{2,1,0:T(8,128)(2,1)S(1)} %copy-done, bf16[16,256,256]{2,1,0:T(8,128)(2,1)S(1)} %copy-done.1), custom_call_target="tpu_custom_call" | custom-call | flops 12000000000 | bytes 12582912 | tf_op jit(solution)/shard_map/mix/pallas_call | solution.py:384
  21.1 1.2 %collective-permute-done.1.refs_2_ = f32[16,256]{1,0:T(8,128)S(1)} collective-permute-done((f32[16,256]{1,0:T(8,128)S(1)}, f32[16,256]{1,0:T(8,128)S(1)}, u32[]{:S(2)}, u32[]{:S(2)}) %collective-permute-start.1) | collective-permute-done | bytes 16416 | tf_op jit(solution)/shard_map/ppermute | solution.py:377
  22.3 0.9 %collective-permute-done.2.refs_3_ = f32[16,256]{1,0:T(8,128)S(1)} collective-permute-done((f32[16,256]{1,0:T(8,128)S(1)}, f32[16,256]{1,0:T(8,128)S(1)}, u32[]{:S(2)}, u32[]{:S(2)}) %collective-permute-start.2) | collective-permute-done | bytes 16416 | tf_op jit(solution)/shard_map/ppermute | solution.py:377
  23.2 10.0 %all_to_all.21.refs_14_ = bf16[8,32,256]{2,1,0:T(8,128)(2,1)S(1)} all-to-all(bf16[8,32,256]{2,1,0:T(8,128)(2,1)S(1)} %mix.1), channel_id=1, replica_groups=mesh['len'=8,'pipe'=4] {'len'}, dimensions={0} | all-to-all | bytes 262144 | tf_op jit(solution)/shard_map/all_to_all | solution.py:374
  33.2 4.0 %layer.1 = (bf16[2048,256]{1,0:T(8,128)(2,1)S(1)}, bf16[2048,256]{1,0:T(8,128)(2,1)S(1)}, bf16[8,34,256]{2,1,0:T(8,128)(2,1)S(1)}, f32[8,256]{1,0:T(8,128)S(1)}) custom-call(f32[16,256]{1,0:T(8,128)S(1)} %pipe_ends.1.refs_0_, f32[16,256]{1,0:T(8,128)S(1)} %collective-permute-done.refs_1_, f32[16,256]{1,0:T(8,128)S(1)} %collective-permute-done.1.refs_2_, ...), custom_call_target="tpu_custom_call" | custom-call | flops 12000000000 | bytes 12582912 | tf_op jit(solution)/shard_map/layer/pallas_call | solution.py:407
  37.2 10.1 %all_to_all.22.r_ref.refs_4_ = bf16[8,34,256]{2,1,0:T(8,128)(2,1)S(1)} all-to-all(bf16[8,34,256]{2,1,0:T(8,128)(2,1)S(1)} %get-tuple-element.25), channel_id=1, replica_groups=mesh['len'=8,'pipe'=4] {'len'}, dimensions={0} | all-to-all | bytes 278528 | tf_op jit(solution)/shard_map/all_to_all | solution.py:374
  47.3 0.7 collective-permute-start.4
  47.9 1.4 %collective-permute-start.7 = (bf16[8,34,256]{2,1,0:T(8,128)(2,1)S(1)}, bf16[8,34,256]{2,1,0:T(8,128)(2,1)S(1)}, u32[]{:S(2)}, u32[]{:S(2)}) collective-permute-start(bf16[8,34,256]{2,1,0:T(8,128)(2,1)S(1)} %all_to_all.22.r_ref.refs_4_), channel_id=1, source_target_pairs={{0,2},{1,3},{2,0},{3,1},{4,6},{5,7},{6,4},{7,5},{8,10},{9,11},{10,... | collective-permute-start | bytes 417800 | tf_op jit(solution)/shard_map/ppermute | solution.py:377
  49.3 0.5 collective-permute-start.6
  49.8 3.7 %collective-permute-done.4.refs_2_ = bf16[8,34,256]{2,1,0:T(8,128)(2,1)S(1)} collective-permute-done((bf16[8,34,256]{2,1,0:T(8,128)(2,1)S(1)}, bf16[8,34,256]{2,1,0:T(8,128)(2,1)S(1)}, u32[]{:S(2)}, u32[]{:S(2)}) %collective-permute-start.4) | collective-permute-done | bytes 139296 | tf_op jit(solution)/shard_map/ppermute | solution.py:377
  53.5 1.8 %collective-permute-done.7.refs_6_ = bf16[8,34,256]{2,1,0:T(8,128)(2,1)S(1)} collective-permute-done((bf16[8,34,256]{2,1,0:T(8,128)(2,1)S(1)}, bf16[8,34,256]{2,1,0:T(8,128)(2,1)S(1)}, u32[]{:S(2)}, u32[]{:S(2)}) %collective-permute-start.7) | collective-permute-done | bytes 139296 | tf_op jit(solution)/shard_map/ppermute | solution.py:377
  55.2 1.9 %mix_grad.1 = (bf16[8,32,256]{2,1,0:T(8,128)(2,1)}, bf16[2048,256]{1,0:T(8,128)(2,1)}) custom-call(bf16[8,34,256]{2,1,0:T(8,128)(2,1)S(1)} %all_to_all.22.r_ref.refs_4_, bf16[16,256,256]{2,1,0:T(8,128)(2,1)S(1)} %copy-done, bf16[16,256,256]{2,1,0:T(8,128)(2,1)S(1)} %copy-done.1, bf16[2048,256]{1,0:T(8,128)(2,1)S(1)} %get-tuple-element.27.refs_0_), custom_call_target="tpu_custom_call" | custom-call | flops 12000000000 | bytes 12582912 | tf_op jit(solution)/shard_map/mix_grad/pallas_call | solution.py:384
  57.2 3.9 %all-to-all-start.3 = ((bf16[8,32,256]{2,1,0:T(8,128)(2,1)}), bf16[8,32,256]{2,1,0:T(8,128)(2,1)S(1)}, u32[]{:S(2)}, u32[]{:S(2)}) async-start(bf16[8,32,256]{2,1,0:T(8,128)(2,1)} %get-tuple-element.33), calls=%async_computation.3 | async-start | bytes 262144 | tf_op jit(solution)/shard_map/all_to_all | solution.py:374
  61.1 4.5 %weight_grad.1 = (f32[16,256,256]{2,1,0:T(8,128)}, f32[16,256,256]{2,1,0:T(8,128)}, f32[8,256]{1,0:T(8,128)S(1)}) custom-call(bf16[8,34,256]{2,1,0:T(8,128)(2,1)S(1)} %all_to_all.20.r_ref.refs_0_, bf16[8,34,256]{2,1,0:T(8,128)(2,1)S(1)} %collective-permute-done.3.refs_1_, bf16[8,34,256]{2,1,0:T(8,128)(2,1)S(1)} %collective-permute-done.4.refs_2_, ...), custom_call_target="tpu_custom_call" | custom-call | flops 1000000000 | bytes 1048576 | tf_op jit(solution)/shard_map/weight_grad/pallas_call | solution.py:436
  65.6 3.1 %all-to-all-done.3.modes_ref = bf16[8,32,256]{2,1,0:T(8,128)(2,1)S(1)} async-done(((bf16[8,32,256]{2,1,0:T(8,128)(2,1)}), bf16[8,32,256]{2,1,0:T(8,128)(2,1)S(1)}, u32[]{:S(2)}, u32[]{:S(2)}) %all-to-all-start.3) | async-done | bytes 131104 | tf_op jit(solution)/shard_map/all_to_all | solution.py:374
  68.7 1.5 %input_grad.1 = bf16[2048,256]{1,0:T(8,128)(2,1)} custom-call(bf16[2048,256]{1,0:T(8,128)(2,1)S(1)} %get-tuple-element.29.total_ref, bf16[1024,256]{1,0:T(8,128)(2,1)S(1)} %copy-done.11, bf16[256,256]{1,0:T(8,128)(2,1)S(1)} %copy-done.6, f32[8,256]{1,0:T(8,128)S(1)} %get-tuple-element.32.rows_ref, bf16[8,32,256]{2,1,0:T(8,128)(2,1)S(1)} %all-to-all-done.3.modes_ref), custom_call_target="tpu_custom_call" | custom-call | flops 1000000000 | bytes 1048576 | tf_op jit(solution)/shard_map/input_grad/pallas_call | solution.py:447
  (24 shorter events, 0.1 us)
Async XLA Ops:
  0.6 1.2 %copy-start.2 = (bf16[1,2048,256]{2,1,0:T(8,128)(2,1)S(1)}, bf16[1,2048,256]{2,1,0:T(8,128)(2,1)}, u32[]{:S(2)}) copy-start(bf16[1,2048,256]{2,1,0:T(8,128)(2,1)} %param.12) | copy-start | bytes 3145732
  1.9 1.0 %copy-start.12 = (bf16[4,256,256]{2,1,0:T(8,128)(2,1)S(1)}, bf16[4,256,256]{2,1,0:T(8,128)(2,1)}, u32[]{:S(2)}) copy-start(bf16[4,256,256]{2,1,0:T(8,128)(2,1)} %constant.4.clone.f_ref.refs_10_) | copy-start | bytes 1572868
  2.9 17.4 %copy-start = (bf16[16,256,256]{2,1,0:T(8,128)(2,1)S(1)}, bf16[16,256,256]{2,1,0:T(8,128)(2,1)}, u32[]{:S(2)}) copy-start(bf16[16,256,256]{2,1,0:T(8,128)(2,1)} %real_ref.3) | copy-start | bytes 6291460
  2.9 17.4 %copy-start.1 = (bf16[16,256,256]{2,1,0:T(8,128)(2,1)S(1)}, bf16[16,256,256]{2,1,0:T(8,128)(2,1)}, u32[]{:S(2)}) copy-start(bf16[16,256,256]{2,1,0:T(8,128)(2,1)} %imag_ref.3) | copy-start | bytes 6291460
  18.3 14.9 %copy-start.3 = (bf16[1,2048,256]{2,1,0:T(8,128)(2,1)S(1)}, bf16[1,2048,256]{2,1,0:T(8,128)(2,1)}, u32[]{:S(2)}) copy-start(bf16[1,2048,256]{2,1,0:T(8,128)(2,1)} %param.12) | copy-start | bytes 3145732
  18.3 14.9 %copy-start.4 = (bf16[1,2048,256]{2,1,0:T(8,128)(2,1)S(1)}, bf16[1,2048,256]{2,1,0:T(8,128)(2,1)}, u32[]{:S(2)}) copy-start(bf16[1,2048,256]{2,1,0:T(8,128)(2,1)} %param.13) | copy-start | bytes 3145732
  18.3 14.9 %copy-start.5 = (bf16[256,256]{1,0:T(8,128)(2,1)S(1)}, bf16[256,256]{1,0:T(8,128)(2,1)}, u32[]{:S(2)}) copy-start(bf16[256,256]{1,0:T(8,128)(2,1)} %refs_10_.2) | copy-start | bytes 393220
  18.3 14.9 %copy-start.6 = (bf16[256,256]{1,0:T(8,128)(2,1)S(1)}, bf16[256,256]{1,0:T(8,128)(2,1)}, u32[]{:S(2)}) copy-start(bf16[256,256]{1,0:T(8,128)(2,1)} %weight_ref.1) | copy-start | bytes 393220
  18.3 14.9 %copy-start.7 = (f32[256]{0:T(256)S(1)}, f32[256]{0:T(256)}, u32[]{:S(2)}) copy-start(f32[256]{0:T(256)} %param.19) | copy-start | bytes 3076
  18.3 14.9 %copy-start.8 = (f32[256]{0:T(256)S(1)}, f32[256]{0:T(256)}, u32[]{:S(2)}) copy-start(f32[256]{0:T(256)} %param.15) | copy-start | bytes 3076
  18.3 14.9 %copy-start.9 = (s32[32]{0:T(128)S(1)}, s32[32]{0:T(128)}, u32[]{:S(2)}) copy-start(s32[32]{0:T(128)} %refs_8_.1) | copy-start | bytes 388
  18.3 14.9 %copy-start.10 = (s32[32]{0:T(128)S(1)}, s32[32]{0:T(128)}, u32[]{:S(2)}) copy-start(s32[32]{0:T(128)} %refs_9_.1) | copy-start | bytes 388
  18.4 14.9 %copy-start.11 = (bf16[1024,256]{1,0:T(8,128)(2,1)S(1)}, bf16[1024,256]{1,0:T(8,128)(2,1)}, u32[]{:S(2)}) copy-start(bf16[1024,256]{1,0:T(8,128)(2,1)} %constant.5.clone.refs_11_.ft_ref) | copy-start | bytes 1572868
  18.4 2.7 %collective-permute-start = (f32[16,256]{1,0:T(8,128)S(1)}, f32[16,256]{1,0:T(8,128)S(1)}, u32[]{:S(2)}, u32[]{:S(2)}) collective-permute-start(f32[16,256]{1,0:T(8,128)S(1)} %pipe_ends.1.refs_0_), channel_id=1, source_target_pairs={{0,1},{1,0},{2,3},{3,2},{4,5},{5,4},{6,7},{7,6},{8,9},{9,8},{10,11... | collective-permute-start | bytes 49160 | tf_op jit(solution)/shard_map/ppermute | solution.py:377
  18.4 3.8 %collective-permute-start.1 = (f32[16,256]{1,0:T(8,128)S(1)}, f32[16,256]{1,0:T(8,128)S(1)}, u32[]{:S(2)}, u32[]{:S(2)}) collective-permute-start(f32[16,256]{1,0:T(8,128)S(1)} %pipe_ends.1.refs_0_), channel_id=1, source_target_pairs={{0,2},{1,3},{2,0},{3,1},{4,6},{5,7},{6,4},{7,5},{8,10},{9,11},{10,... | collective-permute-start | bytes 49160 | tf_op jit(solution)/shard_map/ppermute | solution.py:377
  20.0 3.2 %collective-permute-start.2 = (f32[16,256]{1,0:T(8,128)S(1)}, f32[16,256]{1,0:T(8,128)S(1)}, u32[]{:S(2)}, u32[]{:S(2)}) collective-permute-start(f32[16,256]{1,0:T(8,128)S(1)} %pipe_ends.1.refs_0_), channel_id=1, source_target_pairs={{0,3},{1,2},{2,1},{3,0},{4,7},{5,6},{6,5},{7,4},{8,11},{9,10},{10,... | collective-permute-start | bytes 49160 | tf_op jit(solution)/shard_map/ppermute | solution.py:377
  47.3 6.2 %collective-permute-start.4 = (bf16[8,34,256]{2,1,0:T(8,128)(2,1)S(1)}, bf16[8,34,256]{2,1,0:T(8,128)(2,1)S(1)}, u32[]{:S(2)}, u32[]{:S(2)}) collective-permute-start(bf16[8,34,256]{2,1,0:T(8,128)(2,1)S(1)} %all_to_all.20.r_ref.refs_0_), channel_id=1, source_target_pairs={{0,2},{1,3},{2,0},{3,1},{4,6},{5,7},{6,4},{7,5},{8,10},{9,11},{10,... | collective-permute-start | bytes 417800 | tf_op jit(solution)/shard_map/ppermute | solution.py:377
  47.9 7.3 %collective-permute-start.7 = (bf16[8,34,256]{2,1,0:T(8,128)(2,1)S(1)}, bf16[8,34,256]{2,1,0:T(8,128)(2,1)S(1)}, u32[]{:S(2)}, u32[]{:S(2)}) collective-permute-start(bf16[8,34,256]{2,1,0:T(8,128)(2,1)S(1)} %all_to_all.22.r_ref.refs_4_), channel_id=1, source_target_pairs={{0,2},{1,3},{2,0},{3,1},{4,6},{5,7},{6,4},{7,5},{8,10},{9,11},{10,... | collective-permute-start | bytes 417800 | tf_op jit(solution)/shard_map/ppermute | solution.py:377
  49.3 11.8 %collective-permute-start.3 = (bf16[8,34,256]{2,1,0:T(8,128)(2,1)S(1)}, bf16[8,34,256]{2,1,0:T(8,128)(2,1)S(1)}, u32[]{:S(2)}, u32[]{:S(2)}) collective-permute-start(bf16[8,34,256]{2,1,0:T(8,128)(2,1)S(1)} %all_to_all.20.r_ref.refs_0_), channel_id=1, source_target_pairs={{0,1},{1,0},{2,3},{3,2},{4,5},{5,4},{6,7},{7,6},{8,9},{9,8},{10,11... | collective-permute-start | bytes 417800 | tf_op jit(solution)/shard_map/ppermute | solution.py:377
  49.3 11.8 %collective-permute-start.6 = (bf16[8,34,256]{2,1,0:T(8,128)(2,1)S(1)}, bf16[8,34,256]{2,1,0:T(8,128)(2,1)S(1)}, u32[]{:S(2)}, u32[]{:S(2)}) collective-permute-start(bf16[8,34,256]{2,1,0:T(8,128)(2,1)S(1)} %all_to_all.22.r_ref.refs_4_), channel_id=1, source_target_pairs={{0,1},{1,0},{2,3},{3,2},{4,5},{5,4},{6,7},{7,6},{8,9},{9,8},{10,11... | collective-permute-start | bytes 417800 | tf_op jit(solution)/shard_map/ppermute | solution.py:377
  53.5 7.6 %collective-permute-start.5 = (bf16[8,34,256]{2,1,0:T(8,128)(2,1)S(1)}, bf16[8,34,256]{2,1,0:T(8,128)(2,1)S(1)}, u32[]{:S(2)}, u32[]{:S(2)}) collective-permute-start(bf16[8,34,256]{2,1,0:T(8,128)(2,1)S(1)} %collective-permute-done.4.refs_2_), channel_id=1, source_target_pairs={{0,1},{1,0},{2,3},{3,2},{4,5},{5,4},{6,7},{7,6},{8,9},{9,8},{10,11... | collective-permute-start | bytes 417800 | tf_op jit(solution)/shard_map/ppermute | solution.py:377
  55.2 5.8 %collective-permute-start.8 = (bf16[8,34,256]{2,1,0:T(8,128)(2,1)S(1)}, bf16[8,34,256]{2,1,0:T(8,128)(2,1)S(1)}, u32[]{:S(2)}, u32[]{:S(2)}) collective-permute-start(bf16[8,34,256]{2,1,0:T(8,128)(2,1)S(1)} %collective-permute-done.7.refs_6_), channel_id=1, source_target_pairs={{0,1},{1,0},{2,3},{3,2},{4,5},{5,4},{6,7},{7,6},{8,9},{9,8},{10,11... | collective-permute-start | bytes 417800 | tf_op jit(solution)/shard_map/ppermute | solution.py:377
  57.2 11.5 %all-to-all-start.3 = ((bf16[8,32,256]{2,1,0:T(8,128)(2,1)}), bf16[8,32,256]{2,1,0:T(8,128)(2,1)S(1)}, u32[]{:S(2)}, u32[]{:S(2)}) async-start(bf16[8,32,256]{2,1,0:T(8,128)(2,1)} %get-tuple-element.33), calls=%async_computation.3 | async-start | bytes 262144 | tf_op jit(solution)/shard_map/all_to_all | solution.py:374

commit v9 on v8

--- a/solution.py
+++ b/solution.py
@@ -16,7 +16,6 @@
 GELU_S = math.sqrt(2.0 / math.pi)
 GELU_C = 0.044715
 VMEM = pl.BlockSpec(memory_space=pltpu.VMEM)
-SMEM = pl.BlockSpec(memory_space=pltpu.SMEM)
 HBM = pl.BlockSpec(memory_space=pltpu.HBM)
 MIB = 1024 * 1024
 
@@ -123,40 +122,27 @@
     return lax.axis_index("len") * pipes + lax.axis_index("pipe")
 
 
-def selection(inlet_ref, outlet_ref, pipes, groups, both):
-    me = own_pipe(pipes)
-    shape = (8, 2 * pipes * groups)
-    lane = lax.broadcasted_iota(jnp.int32, shape, 1)
-    row = lax.broadcasted_iota(jnp.int32, shape, 0)
-    own = jnp.where(row == 0, inlet_ref[me], outlet_ref[me])
-    first = jnp.full(shape, -1, jnp.int32)
-    last = jnp.full(shape, -1, jnp.int32)
-    for column in range(pipes):
-        for group in range(groups):
-            base = 2 * (column * groups + group)
-            pipe = group * pipes + column
-            here, there = lane == base, lane == base + 1
-            if both:
-                here = there = here | there
-            first = jnp.where(here, inlet_ref[pipe], first)
-            last = jnp.where(there, outlet_ref[pipe], last)
-    picked = (first == own).astype(jnp.float32) + (last == own).astype(jnp.float32)
-    return picked.astype(jnp.bfloat16)
-
-
-def junction_sums(ends_ref, inlet_ref, outlet_ref, both):
-    pipes, twice, channels = ends_ref.shape
-    picked = selection(inlet_ref, outlet_ref, pipes, twice // 2, both)
-    ends = ends_ref[...].reshape(pipes * twice, channels).astype(jnp.bfloat16)
-    return dot(picked, ends)
+def selection(inlet_ref, outlet_ref, pipes):
+    count = inlet_ref.shape[1]
+    lane = lax.broadcasted_iota(jnp.int32, (8, count), 1)
+    row = lax.broadcasted_iota(jnp.int32, (8, count), 0)
+    inlets = jnp.broadcast_to(inlet_ref[...], (8, count)).astype(jnp.float32)
+    outlets = jnp.broadcast_to(outlet_ref[...], (8, count)).astype(jnp.float32)
+    mine = jnp.where(row == 0, inlets, outlets)
+    own = jnp.sum(jnp.where(lane == own_pipe(pipes), mine, 0.0), axis=1, keepdims=True)
+    return (inlets == own).astype(jnp.bfloat16), (outlets == own).astype(jnp.bfloat16)
+
+
+def whole(ref):
+    return take(ref, pl.ds(0, ref.shape[1])).astype(jnp.bfloat16)
 
 
 def ends_kernel(r_ref, ends_ref):
     groups, rows = r_ref.shape[0], r_ref.shape[1]
     for group in range(groups):
-        ends_ref[2 * group : 2 * group + 2, :] = r_ref[group, rows - 2 : rows, :].astype(
-            jnp.float32
-        )
+        ends = r_ref[group, rows - 2 : rows, :].astype(jnp.float32)
+        ends_ref[group : group + 1, :] = ends[0:1]
+        ends_ref[groups + group : groups + group + 1, :] = ends[1:2]
 
 
 def started(copies):
@@ -183,7 +169,7 @@
     ends, refs = refs[:pipes], refs[pipes:]
     (inlet_ref, outlet_ref, junc_weight_ref, junc_bias_ref), refs = refs[:4], refs[4:]
     x_ref, cot_ref, f_ref, ft_ref, weight_ref, bias_ref, modes_ref = refs[:7]
-    out_ref, total_ref, msg_ref, slope_ref, low_ref, high_ref, ends_ref = refs[7:]
+    out_ref, total_ref, msg_ref, slope_ref, low_ref, high_ref, first_ref, last_ref = refs[7:]
     steps, all_rows, tile = f_ref.shape
     half = steps * tile
     channels = x_ref.shape[1]
@@ -191,8 +177,11 @@
     span = all_rows // groups
     column = lax.axis_index("pipe")
     for step in range(pipes):
-        ends_ref[lax.bitwise_xor(column, step)] = ends[step][...]
-    sums = junction_sums(ends_ref, inlet_ref, outlet_ref, False)
+        at = pl.ds(lax.bitwise_xor(column, step), groups, stride=pipes)
+        put(first_ref, at, ends[step][0:groups, :])
+        put(last_ref, at, ends[step][groups : 2 * groups, :])
+    picked_in, picked_out = selection(inlet_ref, outlet_ref, pipes)
+    sums = dot(picked_in, whole(first_ref)) + dot(picked_out, whole(last_ref))
     act = dot(sums.astype(jnp.bfloat16), junc_weight_ref[...]) + junc_bias_ref[...]
     sigmoid_part = jax.nn.sigmoid(act)
     junc_rows = (act * sigmoid_part).astype(jnp.bfloat16).astype(jnp.float32)
@@ -241,7 +230,8 @@
 def weight_grad_kernel(pipes, modes, per_copy, *refs):
     fields, grads, refs = refs[:pipes], refs[pipes : 2 * pipes], refs[2 * pipes :]
     (inlet_ref, outlet_ref, junc_weight_ref, slope_ref), refs = refs[:4], refs[4:]
-    real_out, imag_out, rows_ref, x_ref, g_ref, real_ref, imag_ref, ends_ref, sems = refs
+    real_out, imag_out, rows_ref, x_ref, g_ref, real_ref, imag_ref = refs[:7]
+    first_ref, last_ref, upper_ref, lower_ref, sems = refs[7:]
     groups, rows = fields[0].shape[0], fields[0].shape[1]
     span = 2 * modes
     for step in range(pipes):
@@ -271,11 +261,16 @@
         )
     column = lax.axis_index("pipe")
     for step in range(pipes):
-        place = lax.bitwise_xor(column, step)
         for group in range(groups):
             parts = grads[step][group, rows - 2 : rows, :].astype(jnp.float32)
-            ends_ref[place, 2 * group : 2 * group + 2, :] = parts
-    junc_grad = COUPLING * junction_sums(ends_ref, inlet_ref, outlet_ref, True)
+            upper_ref[group : group + 1, :] = parts[0:1]
+            lower_ref[group : group + 1, :] = parts[1:2]
+        at = pl.ds(lax.bitwise_xor(column, step), groups, stride=pipes)
+        put(first_ref, at, upper_ref[...])
+        put(last_ref, at, lower_ref[...])
+    picked_in, picked_out = selection(inlet_ref, outlet_ref, pipes)
+    picked = picked_in + picked_out
+    junc_grad = COUPLING * (dot(picked, whole(first_ref)) + dot(picked, whole(last_ref)))
     act_grad = (junc_grad * slope_ref[...]).astype(jnp.bfloat16)
     sums_grad = dot(act_grad, junc_weight_ref[...], 1, 1)
     rows_ref[...] = sums_grad.astype(jnp.bfloat16).astype(jnp.float32)
@@ -321,7 +316,7 @@
     return pltpu.VMEM((channels // LANES, count, LANES), jnp.float32)
 
 
-def call(kernel, outs, specs, scratch=(), out_specs=None, name=None, limit=8, busy=1):
+def call(kernel, outs, specs, scratch=(), out_specs=None, name=None, limit=8, busy=0):
     return pl.pallas_call(
         kernel,
         out_shape=outs,
@@ -331,7 +326,9 @@
         compiler_params=pltpu.CompilerParams(vmem_limit_bytes=limit * MIB),
         cost_estimate=pl.CostEstimate(
             flops=busy * 1_000_000_000, bytes_accessed=busy * MIB, transcendentals=0
-        ),
+        )
+        if busy
+        else None,
         name=name,
     )
 
@@ -376,9 +373,10 @@
     def swap(value, step):
         return lax.ppermute(value, "pipe", [(i, i ^ step) for i in range(pipes)])
 
-    def gather(own):
+    def gather(own, behind):
         across = swap(own, 2)
-        return [own, swap(own, 1), across, swap(across, 1)]
+        tied, tied_across, _ = lax.optimization_barrier((own, across, behind))
+        return [own, swap(tied, 1), across, swap(tied_across, 1)]
 
     def mix(backward, value, *early):
         return call(
@@ -403,18 +401,20 @@
     mixed, *ends = lax.optimization_barrier((mixed, *ends))
     returned = exchange(mixed)
     spectra = received
-    ends_buf = pltpu.VMEM((pipes, 2 * groups, channels), f32)
+    pipe_rows = [rows_of(pipes * groups, channels)] * 2
+    inlet_row = inlet_ids.reshape(1, -1)
+    outlet_row = outlet_ids.reshape(1, -1)
     early, total, sent, slope = call(
         functools.partial(layer_kernel, pipes),
         [shape(field.shape, bf16)] * 2 + [message, shape((8, channels), f32)],
-        [VMEM] * pipes + [SMEM] * 2 + [VMEM] * 9,
-        [pltpu.VMEM((all_rows, channels), f32)] * 2 + [ends_buf],
+        [VMEM] * (pipes + 11),
+        [pltpu.VMEM((all_rows, channels), f32)] * 2 + pipe_rows,
         name="layer",
         busy=12,
     )(
         *ends,
-        inlet_ids,
-        outlet_ids,
+        inlet_row,
+        outlet_row,
         junc_weight,
         junc_bias_row,
         field,
@@ -427,23 +427,25 @@
     )
     received = exchange(sent)
     received, spectra = lax.optimization_barrier((received, spectra))
-    fields = gather(spectra)
-    grads = gather(received)
     mixed, outputs = mix(True, received, early)
+    fields = gather(spectra, mixed)
+    grads = gather(received, mixed)
     returned = exchange(mixed)
     big = shape((modes, channels, channels), f32)
     per_copy = math.gcd(modes, 2)
     grad_real, grad_imag, rows = call(
         functools.partial(weight_grad_kernel, pipes, modes, per_copy),
         [big, big, shape((8, channels), f32)],
-        [VMEM] * (2 * pipes) + [SMEM] * 2 + [VMEM] * 2,
+        [VMEM] * (2 * pipes + 4),
         [rows_of(pipes * all_rows, channels)] * 2
         + [pltpu.VMEM(big.shape, f32)] * 2
-        + [ends_buf, dma((modes // per_copy, 2))],
+        + pipe_rows
+        + [pltpu.VMEM((groups, channels), f32)] * 2
+        + [dma((modes // per_copy, 2))],
         out_specs=[HBM, HBM, VMEM],
         name="weight_grad",
         limit=16,
-    )(*fields, *grads, inlet_ids, outlet_ids, junc_weight, slope)
+    )(*fields, *grads, inlet_row, outlet_row, junc_weight, slope)
     (grad_inputs,) = call(
         input_grad_kernel,
         [shape(field.shape, bf16)],

time: 70.6 us -> 63 us (0.89)
  waiting for transfers between devices: 10.6 us -> 3.41 us
  Pallas kernels: 13.2 us -> 12.1 us
    ppermute x9, waiting for transfers between devices: 7.52 us -> 2.35 us  [swap(): return lax.ppermute(value, 'pipe', [(i, i ^ step) for i in range(pipes)])]
    all_to_all x1, waiting for transfers between devices: 3.07 us -> 1.06 us  [exchange(): return lax.all_to_all(value, 'len', split_axis=0, concat_axis=0, tiled=True)]
  transfers between devices with their start and end apart: 10 -> 10, of which waited for: 5 -> 7; matrix products, arithmetic and copies ran while one was open for 0% -> 0% of each run, Pallas kernels for 10% -> 11%
where the time goes in v9:
time: 63 us; the launch traced here: 62.6 us
  blocking collectives  35.5 us (56%)
  Pallas kernels  12.1 us (19%)
  starting transfers between devices  8.41 us (13%)
  waiting for transfers between devices  3.41 us (5%)
  local copies, waits for them, and re-layouts  2.33 us (4%)
  between operations  0.85 us (1%)
    all_to_all x3, blocking collectives, exchange(): return lax.all_to_all(value, 'len', split_axis=0, concat_axis=0, tiled=True)  35.5 us
    ppermute x9, starting transfers between devices, swap(): return lax.ppermute(value, 'pipe', [(i, i ^ step) for i in range(pipes)])  5.02 us
    pallas_call x1, Pallas kernels, body(): call(functools.partial(weight_grad_kernel, pipes, modes, per_copy), [big,...  3.99 us
    pallas_call x1, Pallas kernels, body(): call(functools.partial(layer_kernel, pipes), [shape(field.shape, bf16)] *...  3.52 us
    all_to_all x1, starting transfers between devices, exchange(): return lax.all_to_all(value, 'len', split_axis=0, concat_axis=0, tiled=True)  3.38 us
    pallas_call x2, Pallas kernels, mix(): call(functools.partial(mix_kernel, backward), [chunks, early[0]] if backw...  2.65 us
    ppermute x9, waiting for transfers between devices, swap(): return lax.ppermute(value, 'pipe', [(i, i ^ step) for i in range(pipes)])  2.35 us
    unnamed x26, local copies, waits for them, and re-layouts  2.33 us
  transfers between devices with their start and end apart: 10, of which 7 were waited for; matrix products, arithmetic and copies ran while one was open for 0% of the time, Pallas kernels for 11%

profile of v9, /device:TPU:0, one launch (start us, length us, event | category | flops | bytes accessed | tf_op | source)
XLA Modules:
  0.0 62.6 jit_solution(6828085255980504204)
XLA Ops:
  0.6 0.0 copy-start.7
  0.6 1.2 %copy-done.7 = bf16[1,2048,256]{2,1,0:T(8,128)(2,1)S(1)} copy-done((bf16[1,2048,256]{2,1,0:T(8,128)(2,1)S(1)}, bf16[1,2048,256]{2,1,0:T(8,128)(2,1)}, u32[]{:S(2)}) %copy-start.7) | copy-done | bytes 1048600
  1.9 1.0 %copy-done.12 = bf16[4,256,256]{2,1,0:T(8,128)(2,1)S(1)} copy-done((bf16[4,256,256]{2,1,0:T(8,128)(2,1)S(1)}, bf16[4,256,256]{2,1,0:T(8,128)(2,1)}, u32[]{:S(2)}) %copy-start.12) | copy-done | bytes 524312
  2.9 0.4 spectrum.1
  3.3 14.9 %all_to_all.20.r_ref.refs_0_ = bf16[8,34,256]{2,1,0:T(8,128)(2,1)S(1)} all-to-all(bf16[8,34,256]{2,1,0:T(8,128)(2,1)S(1)} %spectrum.1), channel_id=1, replica_groups=mesh['len'=8,'pipe'=4] {'len'}, dimensions={0} | all-to-all | bytes 278528 | tf_op jit(solution)/shard_map/all_to_all | solution.py:371
  18.3 0.0 copy-start
  18.3 0.0 copy-start.1
  18.3 0.0 copy-start.2
  18.4 0.1 collective-permute-start.2
  18.5 1.6 %collective-permute-start.1 = (f32[16,256]{1,0:T(8,128)S(1)}, f32[16,256]{1,0:T(8,128)S(1)}, u32[]{:S(2)}, u32[]{:S(2)}) collective-permute-start(f32[16,256]{1,0:T(8,128)S(1)} %pipe_ends.1.refs_0_), channel_id=1, source_target_pairs={{0,2},{1,3},{2,0},{3,1},{4,6},{5,7},{6,4},{7,5},{8,10},{9,11},{10,... | collective-permute-start | bytes 49160 | tf_op jit(solution)/shard_map/ppermute | solution.py:374
  20.0 0.3 collective-permute-start
  20.3 0.7 %mix.1 = bf16[8,32,256]{2,1,0:T(8,128)(2,1)S(1)} custom-call(bf16[8,34,256]{2,1,0:T(8,128)(2,1)S(1)} %all_to_all.20.r_ref.refs_0_, bf16[16,256,256]{2,1,0:T(8,128)(2,1)S(1)} %copy-done.5, bf16[16,256,256]{2,1,0:T(8,128)(2,1)S(1)} %copy-done.6), custom_call_target="tpu_custom_call" | custom-call | flops 12000000000 | bytes 12582912 | tf_op jit(solution)/shard_map/mix/pallas_call | solution.py:382
  21.0 0.7 %collective-permute-done.2.refs_3_ = f32[16,256]{1,0:T(8,128)S(1)} collective-permute-done((f32[16,256]{1,0:T(8,128)S(1)}, f32[16,256]{1,0:T(8,128)S(1)}, u32[]{:S(2)}, u32[]{:S(2)}) %collective-permute-start.2) | collective-permute-done | bytes 16416 | tf_op jit(solution)/shard_map/ppermute | solution.py:374
  21.7 0.5 collective-permute-done.1.refs_2_
  22.3 10.6 %all_to_all.21.refs_14_ = bf16[8,32,256]{2,1,0:T(8,128)(2,1)S(1)} all-to-all(bf16[8,32,256]{2,1,0:T(8,128)(2,1)S(1)} %mix.1), channel_id=1, replica_groups=mesh['len'=8,'pipe'=4] {'len'}, dimensions={0} | all-to-all | bytes 262144 | tf_op jit(solution)/shard_map/all_to_all | solution.py:371
  33.0 3.5 %layer.1 = (bf16[2048,256]{1,0:T(8,128)(2,1)S(1)}, bf16[2048,256]{1,0:T(8,128)(2,1)S(1)}, bf16[8,34,256]{2,1,0:T(8,128)(2,1)S(1)}, f32[8,256]{1,0:T(8,128)S(1)}) custom-call(f32[16,256]{1,0:T(8,128)S(1)} %pipe_ends.1.refs_0_, f32[16,256]{1,0:T(8,128)S(1)} %collective-permute-done.refs_1_, f32[16,256]{1,0:T(8,128)S(1)} %collective-permute-done.1.refs_2_, ...), custom_call_target="tpu_custom_call" | custom-call | flops 12000000000 | bytes 12582912 | tf_op jit(solution)/shard_map/layer/pallas_call | solution.py:407
  36.5 10.0 %all_to_all.22.r_ref.refs_4_ = bf16[8,34,256]{2,1,0:T(8,128)(2,1)S(1)} all-to-all(bf16[8,34,256]{2,1,0:T(8,128)(2,1)S(1)} %get-tuple-element.29), channel_id=1, replica_groups=mesh['len'=8,'pipe'=4] {'len'}, dimensions={0} | all-to-all | bytes 278528 | tf_op jit(solution)/shard_map/all_to_all | solution.py:371
  46.5 0.8 %collective-permute-start.3 = (bf16[8,34,256]{2,1,0:T(8,128)(2,1)S(1)}, bf16[8,34,256]{2,1,0:T(8,128)(2,1)S(1)}, u32[]{:S(2)}, u32[]{:S(2)}) collective-permute-start(bf16[8,34,256]{2,1,0:T(8,128)(2,1)S(1)} %all_to_all.20.r_ref.refs_0_), channel_id=1, source_target_pairs={{0,2},{1,3},{2,0},{3,1},{4,6},{5,7},{6,4},{7,5},{8,10},{9,11},{10,... | collective-permute-start | bytes 417800 | tf_op jit(solution)/shard_map/ppermute | solution.py:374
  47.3 1.3 %collective-permute-start.6 = (bf16[8,34,256]{2,1,0:T(8,128)(2,1)S(1)}, bf16[8,34,256]{2,1,0:T(8,128)(2,1)S(1)}, u32[]{:S(2)}, u32[]{:S(2)}) collective-permute-start(bf16[8,34,256]{2,1,0:T(8,128)(2,1)S(1)} %all_to_all.22.r_ref.refs_4_), channel_id=1, source_target_pairs={{0,2},{1,3},{2,0},{3,1},{4,6},{5,7},{6,4},{7,5},{8,10},{9,11},{10,... | collective-permute-start | bytes 417800 | tf_op jit(solution)/shard_map/ppermute | solution.py:374
  48.5 1.9 %mix_grad.1 = (bf16[8,32,256]{2,1,0:T(8,128)(2,1)}, bf16[2048,256]{1,0:T(8,128)(2,1)}) custom-call(bf16[8,34,256]{2,1,0:T(8,128)(2,1)S(1)} %all_to_all.22.r_ref.refs_4_, bf16[16,256,256]{2,1,0:T(8,128)(2,1)S(1)} %copy-done.5, bf16[16,256,256]{2,1,0:T(8,128)(2,1)S(1)} %copy-done.6, bf16[2048,256]{1,0:T(8,128)(2,1)S(1)} %get-tuple-element.31.refs_0_), custom_call_target="tpu_custom_call" | custom-call | flops 12000000000 | bytes 12582912 | tf_op jit(solution)/shard_map/mix_grad/pallas_call | solution.py:382
  50.5 3.4 %all-to-all-start.3 = ((bf16[8,32,256]{2,1,0:T(8,128)(2,1)}), bf16[8,32,256]{2,1,0:T(8,128)(2,1)S(1)}, u32[]{:S(2)}, u32[]{:S(2)}) async-start(bf16[8,32,256]{2,1,0:T(8,128)(2,1)} %get-tuple-element.35), calls=%async_computation.3 | async-start | bytes 262144 | tf_op jit(solution)/shard_map/all_to_all | solution.py:371
  53.9 0.1 collective-permute-start.4
  54.0 0.5 collective-permute-start.5
  54.5 0.1 collective-permute-start.7
  54.5 0.4 collective-permute-start.8
  55.0 0.4 collective-permute-done.4.refs_1_
  55.3 0.2 collective-permute-done.5.refs_3_
  55.6 0.3 collective-permute-done.7.refs_5_
  55.9 0.2 collective-permute-done.8.refs_7_
  56.1 4.0 %weight_grad.1 = (f32[16,256,256]{2,1,0:T(8,128)}, f32[16,256,256]{2,1,0:T(8,128)}, f32[8,256]{1,0:T(8,128)S(1)}) custom-call(bf16[8,34,256]{2,1,0:T(8,128)(2,1)S(1)} %all_to_all.20.r_ref.refs_0_, bf16[8,34,256]{2,1,0:T(8,128)(2,1)S(1)} %collective-permute-done.4.refs_1_, bf16[8,34,256]{2,1,0:T(8,128)(2,1)S(1)} %collective-permute-done.3.refs_2_, ...), custom_call_target="tpu_custom_call" | custom-call | tf_op jit(solution)/shard_map/weight_grad/pallas_call | solution.py:436
  60.1 1.1 %all-to-all-done.3.modes_ref = bf16[8,32,256]{2,1,0:T(8,128)(2,1)S(1)} async-done(((bf16[8,32,256]{2,1,0:T(8,128)(2,1)}), bf16[8,32,256]{2,1,0:T(8,128)(2,1)S(1)}, u32[]{:S(2)}, u32[]{:S(2)}) %all-to-all-start.3) | async-done | bytes 131104 | tf_op jit(solution)/shard_map/all_to_all | solution.py:371
  61.1 1.5 %input_grad.1 = bf16[2048,256]{1,0:T(8,128)(2,1)} custom-call(bf16[2048,256]{1,0:T(8,128)(2,1)S(1)} %get-tuple-element.33.total_ref, bf16[1024,256]{1,0:T(8,128)(2,1)S(1)} %copy-done, bf16[256,256]{1,0:T(8,128)(2,1)S(1)} %copy-done.2, f32[8,256]{1,0:T(8,128)S(1)} %get-tuple-element.41.rows_ref, bf16[8,32,256]{2,1,0:T(8,128)(2,1)S(1)} %all-to-all-done.3.modes_ref), custom_call_target="tpu_custom_call" | custom-call | tf_op jit(solution)/shard_map/input_grad/pallas_call | solution.py:449
  (24 shorter events, 0.1 us)
Async XLA Ops:
  0.6 1.2 %copy-start.7 = (bf16[1,2048,256]{2,1,0:T(8,128)(2,1)S(1)}, bf16[1,2048,256]{2,1,0:T(8,128)(2,1)}, u32[]{:S(2)}) copy-start(bf16[1,2048,256]{2,1,0:T(8,128)(2,1)} %param.12) | copy-start | bytes 3145732
  1.9 1.0 %copy-start.12 = (bf16[4,256,256]{2,1,0:T(8,128)(2,1)S(1)}, bf16[4,256,256]{2,1,0:T(8,128)(2,1)}, u32[]{:S(2)}) copy-start(bf16[4,256,256]{2,1,0:T(8,128)(2,1)} %constant.4.clone.f_ref.refs_10_) | copy-start | bytes 1572868
  2.9 17.4 %copy-start.5 = (bf16[16,256,256]{2,1,0:T(8,128)(2,1)S(1)}, bf16[16,256,256]{2,1,0:T(8,128)(2,1)}, u32[]{:S(2)}) copy-start(bf16[16,256,256]{2,1,0:T(8,128)(2,1)} %real_ref.3) | copy-start | bytes 6291460
  2.9 17.4 %copy-start.6 = (bf16[16,256,256]{2,1,0:T(8,128)(2,1)S(1)}, bf16[16,256,256]{2,1,0:T(8,128)(2,1)}, u32[]{:S(2)}) copy-start(bf16[16,256,256]{2,1,0:T(8,128)(2,1)} %imag_ref.3) | copy-start | bytes 6291460
  18.3 14.6 %copy-start = (bf16[1024,256]{1,0:T(8,128)(2,1)S(1)}, bf16[1024,256]{1,0:T(8,128)(2,1)}, u32[]{:S(2)}) copy-start(bf16[1024,256]{1,0:T(8,128)(2,1)} %constant.5.clone.refs_11_.ft_ref) | copy-start | bytes 1572868
  18.3 14.6 %copy-start.1 = (bf16[256,256]{1,0:T(8,128)(2,1)S(1)}, bf16[256,256]{1,0:T(8,128)(2,1)}, u32[]{:S(2)}) copy-start(bf16[256,256]{1,0:T(8,128)(2,1)} %refs_10_.2) | copy-start | bytes 393220
  18.3 14.6 %copy-start.2 = (bf16[256,256]{1,0:T(8,128)(2,1)S(1)}, bf16[256,256]{1,0:T(8,128)(2,1)}, u32[]{:S(2)}) copy-start(bf16[256,256]{1,0:T(8,128)(2,1)} %weight_ref.1) | copy-start | bytes 393220
  18.3 14.6 %copy-start.3 = (s32[32]{0:T(128)S(1)}, s32[32]{0:T(128)}, u32[]{:S(2)}) copy-start(s32[32]{0:T(128)} %param.20) | copy-start | bytes 388
  18.3 14.6 %copy-start.4 = (s32[32]{0:T(128)S(1)}, s32[32]{0:T(128)}, u32[]{:S(2)}) copy-start(s32[32]{0:T(128)} %param.21) | copy-start | bytes 388
  18.3 14.6 %copy-start.8 = (bf16[1,2048,256]{2,1,0:T(8,128)(2,1)S(1)}, bf16[1,2048,256]{2,1,0:T(8,128)(2,1)}, u32[]{:S(2)}) copy-start(bf16[1,2048,256]{2,1,0:T(8,128)(2,1)} %param.12) | copy-start | bytes 3145732
  18.3 14.6 %copy-start.9 = (bf16[1,2048,256]{2,1,0:T(8,128)(2,1)S(1)}, bf16[1,2048,256]{2,1,0:T(8,128)(2,1)}, u32[]{:S(2)}) copy-start(bf16[1,2048,256]{2,1,0:T(8,128)(2,1)} %param.13) | copy-start | bytes 3145732
  18.4 14.6 %copy-start.10 = (f32[256]{0:T(256)S(1)}, f32[256]{0:T(256)}, u32[]{:S(2)}) copy-start(f32[256]{0:T(256)} %param.19) | copy-start | bytes 3076
  18.4 14.6 %copy-start.11 = (f32[256]{0:T(256)S(1)}, f32[256]{0:T(256)}, u32[]{:S(2)}) copy-start(f32[256]{0:T(256)} %param.15) | copy-start | bytes 3076
  18.4 3.4 %collective-permute-start.2 = (f32[16,256]{1,0:T(8,128)S(1)}, f32[16,256]{1,0:T(8,128)S(1)}, u32[]{:S(2)}, u32[]{:S(2)}) collective-permute-start(f32[16,256]{1,0:T(8,128)S(1)} %pipe_ends.1.refs_0_), channel_id=1, source_target_pairs={{0,3},{1,2},{2,1},{3,0},{4,7},{5,6},{6,5},{7,4},{8,11},{9,10},{10,... | collective-permute-start | bytes 49160 | tf_op jit(solution)/shard_map/ppermute | solution.py:374
  18.5 3.8 %collective-permute-start.1 = (f32[16,256]{1,0:T(8,128)S(1)}, f32[16,256]{1,0:T(8,128)S(1)}, u32[]{:S(2)}, u32[]{:S(2)}) collective-permute-start(f32[16,256]{1,0:T(8,128)S(1)} %pipe_ends.1.refs_0_), channel_id=1, source_target_pairs={{0,2},{1,3},{2,0},{3,1},{4,6},{5,7},{6,4},{7,5},{8,10},{9,11},{10,... | collective-permute-start | bytes 49160 | tf_op jit(solution)/shard_map/ppermute | solution.py:374
  20.0 2.2 %collective-permute-start = (f32[16,256]{1,0:T(8,128)S(1)}, f32[16,256]{1,0:T(8,128)S(1)}, u32[]{:S(2)}, u32[]{:S(2)}) collective-permute-start(f32[16,256]{1,0:T(8,128)S(1)} %pipe_ends.1.refs_0_), channel_id=1, source_target_pairs={{0,1},{1,0},{2,3},{3,2},{4,5},{5,4},{6,7},{7,6},{8,9},{9,8},{10,11... | collective-permute-start | bytes 49160 | tf_op jit(solution)/shard_map/ppermute | solution.py:374
  46.5 7.4 %collective-permute-start.3 = (bf16[8,34,256]{2,1,0:T(8,128)(2,1)S(1)}, bf16[8,34,256]{2,1,0:T(8,128)(2,1)S(1)}, u32[]{:S(2)}, u32[]{:S(2)}) collective-permute-start(bf16[8,34,256]{2,1,0:T(8,128)(2,1)S(1)} %all_to_all.20.r_ref.refs_0_), channel_id=1, source_target_pairs={{0,2},{1,3},{2,0},{3,1},{4,6},{5,7},{6,4},{7,5},{8,10},{9,11},{10,... | collective-permute-start | bytes 417800 | tf_op jit(solution)/shard_map/ppermute | solution.py:374
  47.3 7.2 %collective-permute-start.6 = (bf16[8,34,256]{2,1,0:T(8,128)(2,1)S(1)}, bf16[8,34,256]{2,1,0:T(8,128)(2,1)S(1)}, u32[]{:S(2)}, u32[]{:S(2)}) collective-permute-start(bf16[8,34,256]{2,1,0:T(8,128)(2,1)S(1)} %all_to_all.22.r_ref.refs_4_), channel_id=1, source_target_pairs={{0,2},{1,3},{2,0},{3,1},{4,6},{5,7},{6,4},{7,5},{8,10},{9,11},{10,... | collective-permute-start | bytes 417800 | tf_op jit(solution)/shard_map/ppermute | solution.py:374
  50.5 10.7 %all-to-all-start.3 = ((bf16[8,32,256]{2,1,0:T(8,128)(2,1)}), bf16[8,32,256]{2,1,0:T(8,128)(2,1)S(1)}, u32[]{:S(2)}, u32[]{:S(2)}) async-start(bf16[8,32,256]{2,1,0:T(8,128)(2,1)} %get-tuple-element.35), calls=%async_computation.3 | async-start | bytes 262144 | tf_op jit(solution)/shard_map/all_to_all | solution.py:371
  53.9 1.5 %collective-permute-start.4 = (bf16[8,34,256]{2,1,0:T(8,128)(2,1)S(1)}, bf16[8,34,256]{2,1,0:T(8,128)(2,1)S(1)}, u32[]{:S(2)}, u32[]{:S(2)}) collective-permute-start(bf16[8,34,256]{2,1,0:T(8,128)(2,1)S(1)} %all_to_all.20.r_ref.refs_0_), channel_id=1, source_target_pairs={{0,1},{1,0},{2,3},{3,2},{4,5},{5,4},{6,7},{7,6},{8,9},{9,8},{10,11... | collective-permute-start | bytes 417800 | tf_op jit(solution)/shard_map/ppermute | solution.py:374
  54.0 1.6 %collective-permute-start.5 = (bf16[8,34,256]{2,1,0:T(8,128)(2,1)S(1)}, bf16[8,34,256]{2,1,0:T(8,128)(2,1)S(1)}, u32[]{:S(2)}, u32[]{:S(2)}) collective-permute-start(bf16[8,34,256]{2,1,0:T(8,128)(2,1)S(1)} %collective-permute-done.3.refs_2_), channel_id=1, source_target_pairs={{0,1},{1,0},{2,3},{3,2},{4,5},{5,4},{6,7},{7,6},{8,9},{9,8},{10,11... | collective-permute-start | bytes 417800 | tf_op jit(solution)/shard_map/ppermute | solution.py:374
  54.5 1.4 %collective-permute-start.7 = (bf16[8,34,256]{2,1,0:T(8,128)(2,1)S(1)}, bf16[8,34,256]{2,1,0:T(8,128)(2,1)S(1)}, u32[]{:S(2)}, u32[]{:S(2)}) collective-permute-start(bf16[8,34,256]{2,1,0:T(8,128)(2,1)S(1)} %all_to_all.22.r_ref.refs_4_), channel_id=1, source_target_pairs={{0,1},{1,0},{2,3},{3,2},{4,5},{5,4},{6,7},{7,6},{8,9},{9,8},{10,11... | collective-permute-start | bytes 417800 | tf_op jit(solution)/shard_map/ppermute | solution.py:374
  54.5 1.6 %collective-permute-start.8 = (bf16[8,34,256]{2,1,0:T(8,128)(2,1)S(1)}, bf16[8,34,256]{2,1,0:T(8,128)(2,1)S(1)}, u32[]{:S(2)}, u32[]{:S(2)}) collective-permute-start(bf16[8,34,256]{2,1,0:T(8,128)(2,1)S(1)} %collective-permute-done.6.refs_6_), channel_id=1, source_target_pairs={{0,1},{1,0},{2,3},{3,2},{4,5},{5,4},{6,7},{7,6},{8,9},{9,8},{10,11... | collective-permute-start | bytes 417800 | tf_op jit(solution)/shard_map/ppermute | solution.py:374

commit v10 on v9

--- a/solution.py
+++ b/solution.py
@@ -31,11 +31,12 @@
     return table.astype(ml_dtypes.bfloat16)
 
 
-def row_signs(all_rows, span, channels):
-    row = lax.broadcasted_iota(jnp.int32, (all_rows, channels), 0)
+def factors_kernel(span, signs_ref, doubled_ref):
+    row = lax.broadcasted_iota(jnp.int32, signs_ref.shape, 0)
     per_owner = span // 2
     mode = (row // span) * per_owner + lax.rem(row, per_owner)
-    return jnp.where(lax.rem(mode, 2) == 0, 1.0, -1.0).astype(jnp.float32)
+    signs_ref[...] = jnp.where(lax.rem(mode, 2) == 0, 1.0, -1.0).astype(jnp.float32)
+    doubled_ref[...] = jnp.where(mode == 0, 1.0, 2.0).astype(jnp.float32)
 
 
 def dot(left, right, left_dim=1, right_dim=0):
@@ -56,7 +57,7 @@
     return jnp.concatenate([ref[lane, at, :] for lane in range(ref.shape[0])], axis=1)
 
 
-def spectrum_kernel(x_ref, f_ref, msg_ref):
+def spectrum_kernel(x_ref, f_ref, signs_ref, msg_ref):
     groups, rows = msg_ref.shape[0], msg_ref.shape[1]
     steps, all_rows, tile = f_ref.shape
     cells, channels = x_ref.shape
@@ -70,7 +71,7 @@
             part = dot(f_ref[step], x_ref[at : at + tile, :])
             total = part if total is None else total + part
         sums.append(total)
-    spectra = (sums[0] + row_signs(all_rows, span, channels) * sums[1]).astype(jnp.bfloat16)
+    spectra = (sums[0] + signs_ref[...] * sums[1]).astype(jnp.bfloat16)
     ends = extra_rows(x_ref[0:1, :], x_ref[cells - 1 : cells, :], rows - span, channels)
     for at in range(groups):
         msg_ref[at, 0:span, :] = spectra[at * span : (at + 1) * span]
@@ -169,7 +170,8 @@
     ends, refs = refs[:pipes], refs[pipes:]
     (inlet_ref, outlet_ref, junc_weight_ref, junc_bias_ref), refs = refs[:4], refs[4:]
     x_ref, cot_ref, f_ref, ft_ref, weight_ref, bias_ref, modes_ref = refs[:7]
-    out_ref, total_ref, msg_ref, slope_ref, low_ref, high_ref, first_ref, last_ref = refs[7:]
+    (signs_ref, doubled_ref), refs = refs[7:9], refs[9:]
+    out_ref, total_ref, msg_ref, slope_ref, low_ref, high_ref, first_ref, last_ref = refs
     steps, all_rows, tile = f_ref.shape
     half = steps * tile
     channels = x_ref.shape[1]
@@ -187,9 +189,8 @@
     junc_rows = (act * sigmoid_part).astype(jnp.bfloat16).astype(jnp.float32)
     cond = COUPLING * (junc_rows[0:1] + junc_rows[1:2])
     slope_ref[...] = sigmoid_part * (1.0 + act * (1.0 - sigmoid_part))
-    row = lax.broadcasted_iota(jnp.int32, (all_rows, channels), 0)
-    doubled = jnp.where((row == 0) | (row == span // 2), 1.0, 2.0).astype(jnp.float32)
-    signs = row_signs(all_rows, span, channels)
+    doubled = doubled_ref[...]
+    signs = signs_ref[...]
     modes = jnp.concatenate(
         [modes_ref[at, 0:span, :].astype(jnp.float32) for at in range(groups)], axis=0
     )
@@ -228,17 +229,17 @@
 
 
 def weight_grad_kernel(pipes, modes, per_copy, *refs):
-    fields, grads, refs = refs[:pipes], refs[pipes : 2 * pipes], refs[2 * pipes :]
+    both, refs = refs[:pipes], refs[pipes:]
     (inlet_ref, outlet_ref, junc_weight_ref, slope_ref), refs = refs[:4], refs[4:]
     real_out, imag_out, rows_ref, x_ref, g_ref, real_ref, imag_ref = refs[:7]
     first_ref, last_ref, upper_ref, lower_ref, sems = refs[7:]
-    groups, rows = fields[0].shape[0], fields[0].shape[1]
+    groups, rows = both[0].shape[0] // 2, both[0].shape[1]
     span = 2 * modes
     for step in range(pipes):
         for source in range(groups):
             at = pl.ds((step * groups + source) * span, span)
-            put(x_ref, at, fields[step][source, 0:span, :].astype(jnp.float32))
-            put(g_ref, at, grads[step][source, 0:span, :].astype(jnp.float32))
+            put(x_ref, at, both[step][source, 0:span, :].astype(jnp.float32))
+            put(g_ref, at, both[step][groups + source, 0:span, :].astype(jnp.float32))
     count = pipes * groups
     going = []
     for number in range(modes // per_copy):
@@ -262,7 +263,7 @@
     column = lax.axis_index("pipe")
     for step in range(pipes):
         for group in range(groups):
-            parts = grads[step][group, rows - 2 : rows, :].astype(jnp.float32)
+            parts = both[step][groups + group, rows - 2 : rows, :].astype(jnp.float32)
             upper_ref[group : group + 1, :] = parts[0:1]
             lower_ref[group : group + 1, :] = parts[1:2]
         at = pl.ds(lax.bitwise_xor(column, step), groups, stride=pipes)
@@ -277,16 +278,22 @@
     wait(going)
 
 
+def pack_kernel(first_ref, second_ref, out_ref):
+    groups = first_ref.shape[0]
+    out_ref[0:groups] = first_ref[...]
+    out_ref[groups : 2 * groups] = second_ref[...]
+
+
 def input_grad_kernel(
-    total_ref, ft_ref, weight_ref, rows_ref, modes_ref, out_ref, tiles_ref, sems
+    total_ref, ft_ref, weight_ref, rows_ref, signs_ref, modes_ref, out_ref, tiles_ref, sems
 ):
     groups, span, channels = modes_ref.shape
     steps, tile = tiles_ref.shape[0], tiles_ref.shape[2]
-    half, all_rows = steps * tile, groups * span
+    half = steps * tile
     back = jnp.concatenate(
         [modes_ref[at, 0:span, :].astype(jnp.float32) for at in range(groups)], axis=0
     )
-    signs = row_signs(all_rows, span, channels)
+    signs = signs_ref[...]
     back = (back.astype(jnp.bfloat16), (back * signs).astype(jnp.bfloat16))
     weight = weight_ref[...]
     row = lax.broadcasted_iota(jnp.int32, (tile, channels), 0)
@@ -389,8 +396,15 @@
             busy=12,
         )(value, spec_real, spec_imag, *early)
 
-    (sent,) = call(spectrum_kernel, [message], [VMEM] * 2, name="spectrum", busy=12)(
-        field, f_table
+    signs, doubled = call(
+        functools.partial(factors_kernel, span),
+        [shape((all_rows, channels), f32)] * 2,
+        [],
+        name="factors",
+        busy=1,
+    )()
+    (sent,) = call(spectrum_kernel, [message], [VMEM] * 3, name="spectrum", busy=12)(
+        field, f_table, signs
     )
     received = exchange(sent)
     (ends,) = call(
@@ -407,7 +421,7 @@
     early, total, sent, slope = call(
         functools.partial(layer_kernel, pipes),
         [shape(field.shape, bf16)] * 2 + [message, shape((8, channels), f32)],
-        [VMEM] * (pipes + 11),
+        [VMEM] * (pipes + 13),
         [pltpu.VMEM((all_rows, channels), f32)] * 2 + pipe_rows,
         name="layer",
         busy=12,
@@ -424,19 +438,26 @@
         point_weight,
         bias_row,
         returned,
+        signs,
+        doubled,
     )
     received = exchange(sent)
     received, spectra = lax.optimization_barrier((received, spectra))
+    (both,) = call(
+        pack_kernel,
+        [shape((2 * groups, span + 2, channels), bf16)],
+        [VMEM] * 2,
+        name="pack",
+    )(spectra, received)
     mixed, outputs = mix(True, received, early)
-    fields = gather(spectra, mixed)
-    grads = gather(received, mixed)
+    both = gather(both, mixed)
     returned = exchange(mixed)
     big = shape((modes, channels, channels), f32)
     per_copy = math.gcd(modes, 2)
     grad_real, grad_imag, rows = call(
         functools.partial(weight_grad_kernel, pipes, modes, per_copy),
         [big, big, shape((8, channels), f32)],
-        [VMEM] * (2 * pipes + 4),
+        [VMEM] * (pipes + 4),
         [rows_of(pipes * all_rows, channels)] * 2
         + [pltpu.VMEM(big.shape, f32)] * 2
         + pipe_rows
@@ -445,15 +466,15 @@
         out_specs=[HBM, HBM, VMEM],
         name="weight_grad",
         limit=16,
-    )(*fields, *grads, inlet_row, outlet_row, junc_weight, slope)
+    )(*both, inlet_row, outlet_row, junc_weight, slope)
     (grad_inputs,) = call(
         input_grad_kernel,
         [shape(field.shape, bf16)],
-        [VMEM] * 5,
+        [VMEM] * 6,
         [pltpu.VMEM((steps, 2, TILE, channels), bf16), dma((steps, 2))],
         out_specs=[HBM],
         name="input_grad",
-    )(total, ft_table, point_weight, rows, returned)
+    )(total, ft_table, point_weight, rows, signs, returned)
     return (
         outputs.reshape(inputs.shape),
         grad_inputs.reshape(inputs.shape),

time: 63 us -> 67.7 us (1.075)
  waiting for transfers between devices: 3.41 us -> 8.5 us
  local copies, waits for them, and re-layouts: 2.33 us -> 4.29 us
  starting transfers between devices: 8.41 us -> 6.64 us
    ppermute x9 -> x6, waiting for transfers between devices: 2.35 us -> 6.47 us  [swap(): return lax.ppermute(value, 'pipe', [(i, i ^ step) for i in range(pipes)])]
    unnamed x26 -> x34, local copies, waits for them, and re-layouts: 2.33 us -> 4.29 us
    ppermute x9 -> x6, starting transfers between devices: 5.02 us -> 3.27 us  [swap(): return lax.ppermute(value, 'pipe', [(i, i ^ step) for i in range(pipes)])]
    all_to_all x1, waiting for transfers between devices: 1.06 us -> 2.03 us  [exchange(): return lax.all_to_all(value, 'len', split_axis=0, concat_axis=0, tiled=True)]
    pallas_call x2 -> x4, Pallas kernels: 1.89 us -> 1.98 us  [the longest x1 1.45 us: body(): call(input_grad_kernel, [shape(field.shape, bf16)], [VMEM] * 6, [pltpu.VM...]
  transfers between devices with their start and end apart: 10 -> 7, of which waited for: 7 -> 4; matrix products, arithmetic and copies ran while one was open for 0% -> 0% of each run, Pallas kernels for 11% -> 9%
where the time goes in v10:
time: 67.7 us; the launch traced here: 67.3 us
  blocking collectives  35.5 us (52%)
  Pallas kernels  11.5 us (17%)
  waiting for transfers between devices  8.5 us (13%)
  starting transfers between devices  6.64 us (10%)
  local copies, waits for them, and re-layouts  4.29 us (6%)
  between operations  0.89 us (1%)
    all_to_all x3, blocking collectives, exchange(): return lax.all_to_all(value, 'len', split_axis=0, concat_axis=0, tiled=True)  35.5 us
    ppermute x6, waiting for transfers between devices, swap(): return lax.ppermute(value, 'pipe', [(i, i ^ step) for i in range(pipes)])  6.47 us
    unnamed x34, local copies, waits for them, and re-layouts  4.29 us
    pallas_call x1, Pallas kernels, body(): call(functools.partial(weight_grad_kernel, pipes, modes, per_copy), [big,...  3.99 us
    pallas_call x1, Pallas kernels, body(): call(functools.partial(layer_kernel, pipes), [shape(field.shape, bf16)] *...  3.49 us
    all_to_all x1, starting transfers between devices, exchange(): return lax.all_to_all(value, 'len', split_axis=0, concat_axis=0, tiled=True)  3.37 us
    ppermute x6, starting transfers between devices, swap(): return lax.ppermute(value, 'pipe', [(i, i ^ step) for i in range(pipes)])  3.27 us
    all_to_all x1, waiting for transfers between devices, exchange(): return lax.all_to_all(value, 'len', split_axis=0, concat_axis=0, tiled=True)  2.03 us
  transfers between devices with their start and end apart: 7, of which 4 were waited for; matrix products, arithmetic and copies ran while one was open for 0% of the time, Pallas kernels for 9%

profile of v10, /device:TPU:0, one launch (start us, length us, event | category | flops | bytes accessed | tf_op | source)
XLA Modules:
  0.0 67.3 jit_solution(1043368434376488098)
XLA Ops:
  0.6 0.1 factors.1
  0.7 1.2 %copy-done.10 = bf16[1,2048,256]{2,1,0:T(8,128)(2,1)S(1)} copy-done((bf16[1,2048,256]{2,1,0:T(8,128)(2,1)S(1)}, bf16[1,2048,256]{2,1,0:T(8,128)(2,1)}, u32[]{:S(2)}) %copy-start.10) | copy-done | bytes 1048600
  1.9 1.0 %copy-done.15 = bf16[4,256,256]{2,1,0:T(8,128)(2,1)S(1)} copy-done((bf16[4,256,256]{2,1,0:T(8,128)(2,1)S(1)}, bf16[4,256,256]{2,1,0:T(8,128)(2,1)}, u32[]{:S(2)}) %copy-start.15) | copy-done | bytes 524312
  3.0 0.4 spectrum.1
  3.4 14.9 %all_to_all.20.r_ref.first_ref = bf16[8,34,256]{2,1,0:T(8,128)(2,1)S(1)} all-to-all(bf16[8,34,256]{2,1,0:T(8,128)(2,1)S(1)} %spectrum.1), channel_id=1, replica_groups=mesh['len'=8,'pipe'=4] {'len'}, dimensions={0} | all-to-all | bytes 278528 | tf_op jit(solution)/shard_map/all_to_all | solution.py:378
  18.4 0.0 copy-start
  18.4 0.0 copy-start.1
  18.4 0.0 copy-start.4
  18.4 0.0 copy-start.6
  18.4 0.0 copy-start.13
  18.4 0.0 copy-start.14
  18.5 0.0 copy-start.16
  18.5 0.1 collective-permute-start.2
  18.6 1.6 %collective-permute-start.1 = (f32[16,256]{1,0:T(8,128)S(1)}, f32[16,256]{1,0:T(8,128)S(1)}, u32[]{:S(2)}, u32[]{:S(2)}) collective-permute-start(f32[16,256]{1,0:T(8,128)S(1)} %pipe_ends.1.refs_0_), channel_id=1, source_target_pairs={{0,2},{1,3},{2,0},{3,1},{4,6},{5,7},{6,4},{7,5},{8,10},{9,11},{10,... | collective-permute-start | bytes 49160 | tf_op jit(solution)/shard_map/ppermute | solution.py:381
  20.1 0.3 collective-permute-start
  20.4 0.7 %mix.1 = bf16[8,32,256]{2,1,0:T(8,128)(2,1)S(1)} custom-call(bf16[8,34,256]{2,1,0:T(8,128)(2,1)S(1)} %all_to_all.20.r_ref.first_ref, bf16[16,256,256]{2,1,0:T(8,128)(2,1)S(1)} %copy-done.8, bf16[16,256,256]{2,1,0:T(8,128)(2,1)S(1)} %copy-done.9), custom_call_target="tpu_custom_call" | custom-call | flops 12000000000 | bytes 12582912 | tf_op jit(solution)/shard_map/mix/pallas_call | solution.py:389
  21.1 0.7 %collective-permute-done.2.refs_3_ = f32[16,256]{1,0:T(8,128)S(1)} collective-permute-done((f32[16,256]{1,0:T(8,128)S(1)}, f32[16,256]{1,0:T(8,128)S(1)}, u32[]{:S(2)}, u32[]{:S(2)}) %collective-permute-start.2) | collective-permute-done | bytes 16416 | tf_op jit(solution)/shard_map/ppermute | solution.py:381
  21.8 0.5 collective-permute-done.1.refs_2_
  22.4 10.6 %all_to_all.21.refs_14_ = bf16[8,32,256]{2,1,0:T(8,128)(2,1)S(1)} all-to-all(bf16[8,32,256]{2,1,0:T(8,128)(2,1)S(1)} %mix.1), channel_id=1, replica_groups=mesh['len'=8,'pipe'=4] {'len'}, dimensions={0} | all-to-all | bytes 262144 | tf_op jit(solution)/shard_map/all_to_all | solution.py:378
  33.1 3.5 %layer.1 = (bf16[2048,256]{1,0:T(8,128)(2,1)S(1)}, bf16[2048,256]{1,0:T(8,128)(2,1)S(1)}, bf16[8,34,256]{2,1,0:T(8,128)(2,1)S(1)}, f32[8,256]{1,0:T(8,128)S(1)}) custom-call(f32[16,256]{1,0:T(8,128)S(1)} %pipe_ends.1.refs_0_, f32[16,256]{1,0:T(8,128)S(1)} %collective-permute-done.refs_1_, f32[16,256]{1,0:T(8,128)S(1)} %collective-permute-done.1.refs_2_, ...), custom_call_target="tpu_custom_call" | custom-call | flops 12000000000 | bytes 12582912 | tf_op jit(solution)/shard_map/layer/pallas_call | solution.py:421
  36.6 10.0 %all_to_all.22.r_ref.second_ref = bf16[8,34,256]{2,1,0:T(8,128)(2,1)S(1)} all-to-all(bf16[8,34,256]{2,1,0:T(8,128)(2,1)S(1)} %get-tuple-element.31), channel_id=1, replica_groups=mesh['len'=8,'pipe'=4] {'len'}, dimensions={0} | all-to-all | bytes 278528 | tf_op jit(solution)/shard_map/all_to_all | solution.py:378
  46.6 0.8 %collective-permute-start.3 = (bf16[16,34,256]{2,1,0:T(8,128)(2,1)S(1)}, bf16[16,34,256]{2,1,0:T(8,128)(2,1)S(1)}, u32[]{:S(2)}, u32[]{:S(2)}) collective-permute-start(bf16[16,34,256]{2,1,0:T(8,128)(2,1)S(1)} %pack.1.refs_0_), channel_id=1, source_target_pairs={{0,2},{1,3},{2,0},{3,1},{4,6},{5,7},{6,4},{7,5},{8,10},{9,11},{10,... | collective-permute-start | bytes 835592 | tf_op jit(solution)/shard_map/ppermute | solution.py:381
  47.4 1.3 %mix_grad.1 = (bf16[8,32,256]{2,1,0:T(8,128)(2,1)S(1)}, bf16[2048,256]{1,0:T(8,128)(2,1)}) custom-call(bf16[8,34,256]{2,1,0:T(8,128)(2,1)S(1)} %all_to_all.22.r_ref.second_ref, bf16[16,256,256]{2,1,0:T(8,128)(2,1)S(1)} %copy-done.8, bf16[16,256,256]{2,1,0:T(8,128)(2,1)S(1)} %copy-done.9, bf16[2048,256]{1,0:T(8,128)(2,1)S(1)} %get-tuple-element.33.refs_0_), custom_call_target="tpu_custom_call" | custom-call | flops 12000000000 | bytes 12582912 | tf_op jit(solution)/shard_map/mix_grad/pallas_call | solution.py:389
  48.7 0.6 copy-done.3
  49.4 5.2 %collective-permute-done.3.refs_2_ = bf16[16,34,256]{2,1,0:T(8,128)(2,1)S(1)} collective-permute-done((bf16[16,34,256]{2,1,0:T(8,128)(2,1)S(1)}, bf16[16,34,256]{2,1,0:T(8,128)(2,1)S(1)}, u32[]{:S(2)}, u32[]{:S(2)}) %collective-permute-start.3) | collective-permute-done | bytes 278560 | tf_op jit(solution)/shard_map/ppermute | solution.py:381
  54.6 0.5 collective-permute-start.5
  55.1 3.4 %all-to-all-start.3 = ((bf16[8,32,256]{2,1,0:T(8,128)(2,1)}), bf16[8,32,256]{2,1,0:T(8,128)(2,1)S(1)}, u32[]{:S(2)}, u32[]{:S(2)}) async-start(bf16[8,32,256]{2,1,0:T(8,128)(2,1)} %copy-done.3), calls=%async_computation.3 | async-start | bytes 262144 | tf_op jit(solution)/shard_map/all_to_all | solution.py:378
  58.5 0.6 copy-done.5
  59.2 0.7 copy-done.7
  59.9 4.0 %weight_grad.1 = (f32[16,256,256]{2,1,0:T(8,128)}, f32[16,256,256]{2,1,0:T(8,128)}, f32[8,256]{1,0:T(8,128)S(1)}) custom-call(bf16[16,34,256]{2,1,0:T(8,128)(2,1)S(1)} %pack.1.refs_0_, bf16[16,34,256]{2,1,0:T(8,128)(2,1)S(1)} %collective-permute-done.4.refs_1_, bf16[16,34,256]{2,1,0:T(8,128)(2,1)S(1)} %collective-permute-done.3.refs_2_, ...), custom_call_target="tpu_custom_call" | custom-call | tf_op jit(solution)/shard_map/weight_grad/pallas_call | solution.py:457
  63.9 2.0 %all-to-all-done.3.modes_ref = bf16[8,32,256]{2,1,0:T(8,128)(2,1)S(1)} async-done(((bf16[8,32,256]{2,1,0:T(8,128)(2,1)}), bf16[8,32,256]{2,1,0:T(8,128)(2,1)S(1)}, u32[]{:S(2)}, u32[]{:S(2)}) %all-to-all-start.3) | async-done | bytes 131104 | tf_op jit(solution)/shard_map/all_to_all | solution.py:378
  65.9 1.4 %input_grad.1 = bf16[2048,256]{1,0:T(8,128)(2,1)} custom-call(bf16[2048,256]{1,0:T(8,128)(2,1)S(1)} %get-tuple-element.35.total_ref, bf16[1024,256]{1,0:T(8,128)(2,1)S(1)} %copy-done, bf16[256,256]{1,0:T(8,128)(2,1)S(1)} %copy-done.2, f32[8,256]{1,0:T(8,128)S(1)} %get-tuple-element.41.rows_ref, f32[256,256]{1,0:T(8,128)S(1)} %get-tuple-element.24.signs_ref.refs_15_, ...), custom_call_target="tpu_custom_call" | custom-call | tf_op jit(solution)/shard_map/input_grad/pallas_call | solution.py:470
  (28 shorter events, 0.1 us)
Async XLA Ops:
  0.7 1.2 %copy-start.10 = (bf16[1,2048,256]{2,1,0:T(8,128)(2,1)S(1)}, bf16[1,2048,256]{2,1,0:T(8,128)(2,1)}, u32[]{:S(2)}) copy-start(bf16[1,2048,256]{2,1,0:T(8,128)(2,1)} %param.12) | copy-start | bytes 3145732
  1.9 1.0 %copy-start.15 = (bf16[4,256,256]{2,1,0:T(8,128)(2,1)S(1)}, bf16[4,256,256]{2,1,0:T(8,128)(2,1)}, u32[]{:S(2)}) copy-start(bf16[4,256,256]{2,1,0:T(8,128)(2,1)} %constant.4.clone.f_ref.refs_10_) | copy-start | bytes 1572868
  3.0 17.4 %copy-start.8 = (bf16[16,256,256]{2,1,0:T(8,128)(2,1)S(1)}, bf16[16,256,256]{2,1,0:T(8,128)(2,1)}, u32[]{:S(2)}) copy-start(bf16[16,256,256]{2,1,0:T(8,128)(2,1)} %real_ref.3) | copy-start | bytes 6291460
  3.0 17.4 %copy-start.9 = (bf16[16,256,256]{2,1,0:T(8,128)(2,1)S(1)}, bf16[16,256,256]{2,1,0:T(8,128)(2,1)}, u32[]{:S(2)}) copy-start(bf16[16,256,256]{2,1,0:T(8,128)(2,1)} %imag_ref.3) | copy-start | bytes 6291460
  18.4 14.7 %copy-start = (bf16[1024,256]{1,0:T(8,128)(2,1)S(1)}, bf16[1024,256]{1,0:T(8,128)(2,1)}, u32[]{:S(2)}) copy-start(bf16[1024,256]{1,0:T(8,128)(2,1)} %constant.5.clone.refs_11_.ft_ref) | copy-start | bytes 1572868
  18.4 14.6 %copy-start.1 = (bf16[256,256]{1,0:T(8,128)(2,1)S(1)}, bf16[256,256]{1,0:T(8,128)(2,1)}, u32[]{:S(2)}) copy-start(bf16[256,256]{1,0:T(8,128)(2,1)} %refs_6_.3) | copy-start | bytes 393220
  18.4 14.6 %copy-start.2 = (bf16[256,256]{1,0:T(8,128)(2,1)S(1)}, bf16[256,256]{1,0:T(8,128)(2,1)}, u32[]{:S(2)}) copy-start(bf16[256,256]{1,0:T(8,128)(2,1)} %weight_ref.1) | copy-start | bytes 393220
  18.4 14.6 %copy-start.4 = (s32[32]{0:T(128)S(1)}, s32[32]{0:T(128)}, u32[]{:S(2)}) copy-start(s32[32]{0:T(128)} %param.20) | copy-start | bytes 388
  18.4 14.6 %copy-start.6 = (s32[32]{0:T(128)S(1)}, s32[32]{0:T(128)}, u32[]{:S(2)}) copy-start(s32[32]{0:T(128)} %param.21) | copy-start | bytes 388
  18.4 14.6 %copy-start.11 = (bf16[1,2048,256]{2,1,0:T(8,128)(2,1)S(1)}, bf16[1,2048,256]{2,1,0:T(8,128)(2,1)}, u32[]{:S(2)}) copy-start(bf16[1,2048,256]{2,1,0:T(8,128)(2,1)} %param.12) | copy-start | bytes 3145732
  18.4 14.6 %copy-start.12 = (bf16[1,2048,256]{2,1,0:T(8,128)(2,1)S(1)}, bf16[1,2048,256]{2,1,0:T(8,128)(2,1)}, u32[]{:S(2)}) copy-start(bf16[1,2048,256]{2,1,0:T(8,128)(2,1)} %param.13) | copy-start | bytes 3145732
  18.4 14.6 %copy-start.13 = (f32[256]{0:T(256)S(1)}, f32[256]{0:T(256)}, u32[]{:S(2)}) copy-start(f32[256]{0:T(256)} %param.19) | copy-start | bytes 3076
  18.4 14.6 %copy-start.14 = (f32[256]{0:T(256)S(1)}, f32[256]{0:T(256)}, u32[]{:S(2)}) copy-start(f32[256]{0:T(256)} %param.15) | copy-start | bytes 3076
  18.5 14.6 %copy-start.16 = (bf16[4,256,256]{2,1,0:T(8,128)(2,1)S(1)}, bf16[4,256,256]{2,1,0:T(8,128)(2,1)}, u32[]{:S(2)}) copy-start(bf16[4,256,256]{2,1,0:T(8,128)(2,1)} %constant.4.clone.f_ref.refs_10_) | copy-start | bytes 1572868
  18.5 3.4 %collective-permute-start.2 = (f32[16,256]{1,0:T(8,128)S(1)}, f32[16,256]{1,0:T(8,128)S(1)}, u32[]{:S(2)}, u32[]{:S(2)}) collective-permute-start(f32[16,256]{1,0:T(8,128)S(1)} %pipe_ends.1.refs_0_), channel_id=1, source_target_pairs={{0,3},{1,2},{2,1},{3,0},{4,7},{5,6},{6,5},{7,4},{8,11},{9,10},{10,... | collective-permute-start | bytes 49160 | tf_op jit(solution)/shard_map/ppermute | solution.py:381
  18.6 3.8 %collective-permute-start.1 = (f32[16,256]{1,0:T(8,128)S(1)}, f32[16,256]{1,0:T(8,128)S(1)}, u32[]{:S(2)}, u32[]{:S(2)}) collective-permute-start(f32[16,256]{1,0:T(8,128)S(1)} %pipe_ends.1.refs_0_), channel_id=1, source_target_pairs={{0,2},{1,3},{2,0},{3,1},{4,6},{5,7},{6,4},{7,5},{8,10},{9,11},{10,... | collective-permute-start | bytes 49160 | tf_op jit(solution)/shard_map/ppermute | solution.py:381
  20.1 2.2 %collective-permute-start = (f32[16,256]{1,0:T(8,128)S(1)}, f32[16,256]{1,0:T(8,128)S(1)}, u32[]{:S(2)}, u32[]{:S(2)}) collective-permute-start(f32[16,256]{1,0:T(8,128)S(1)} %pipe_ends.1.refs_0_), channel_id=1, source_target_pairs={{0,1},{1,0},{2,3},{3,2},{4,5},{5,4},{6,7},{7,6},{8,9},{9,8},{10,11... | collective-permute-start | bytes 49160 | tf_op jit(solution)/shard_map/ppermute | solution.py:381
  46.6 8.0 %collective-permute-start.3 = (bf16[16,34,256]{2,1,0:T(8,128)(2,1)S(1)}, bf16[16,34,256]{2,1,0:T(8,128)(2,1)S(1)}, u32[]{:S(2)}, u32[]{:S(2)}) collective-permute-start(bf16[16,34,256]{2,1,0:T(8,128)(2,1)S(1)} %pack.1.refs_0_), channel_id=1, source_target_pairs={{0,2},{1,3},{2,0},{3,1},{4,6},{5,7},{6,4},{7,5},{8,10},{9,11},{10,... | collective-permute-start | bytes 835592 | tf_op jit(solution)/shard_map/ppermute | solution.py:381
  48.7 0.7 copy-start.3
  54.6 3.9 %collective-permute-start.4 = (bf16[16,34,256]{2,1,0:T(8,128)(2,1)S(1)}, bf16[16,34,256]{2,1,0:T(8,128)(2,1)S(1)}, u32[]{:S(2)}, u32[]{:S(2)}) collective-permute-start(bf16[16,34,256]{2,1,0:T(8,128)(2,1)S(1)} %pack.1.refs_0_), channel_id=1, source_target_pairs={{0,1},{1,0},{2,3},{3,2},{4,5},{5,4},{6,7},{7,6},{8,9},{9,8},{10,11... | collective-permute-start | bytes 835592 | tf_op jit(solution)/shard_map/ppermute | solution.py:381
  54.6 3.9 %collective-permute-start.5 = (bf16[16,34,256]{2,1,0:T(8,128)(2,1)S(1)}, bf16[16,34,256]{2,1,0:T(8,128)(2,1)S(1)}, u32[]{:S(2)}, u32[]{:S(2)}) collective-permute-start(bf16[16,34,256]{2,1,0:T(8,128)(2,1)S(1)} %collective-permute-done.3.refs_2_), channel_id=1, source_target_pairs={{0,1},{1,0},{2,3},{3,2},{4,5},{5,4},{6,7},{7,6},{8,9},{9,8},{10,11... | collective-permute-start | bytes 835592 | tf_op jit(solution)/shard_map/ppermute | solution.py:381
  55.1 10.7 %all-to-all-start.3 = ((bf16[8,32,256]{2,1,0:T(8,128)(2,1)}), bf16[8,32,256]{2,1,0:T(8,128)(2,1)S(1)}, u32[]{:S(2)}, u32[]{:S(2)}) async-start(bf16[8,32,256]{2,1,0:T(8,128)(2,1)} %copy-done.3), calls=%async_computation.3 | async-start | bytes 262144 | tf_op jit(solution)/shard_map/all_to_all | solution.py:378
  58.5 0.7 copy-start.5
  59.2 0.7 copy-start.7

commit v11 on v9

--- a/solution.py
+++ b/solution.py
@@ -277,6 +277,18 @@
     wait(going)
 
 
+def pack_kernel(first_ref, second_ref, out_ref):
+    groups = first_ref.shape[0]
+    out_ref[0:groups] = first_ref[...]
+    out_ref[groups : 2 * groups] = second_ref[...]
+
+
+def split_kernel(both_ref, first_ref, second_ref):
+    groups = first_ref.shape[0]
+    first_ref[...] = both_ref[0:groups]
+    second_ref[...] = both_ref[groups : 2 * groups]
+
+
 def input_grad_kernel(
     total_ref, ft_ref, weight_ref, rows_ref, modes_ref, out_ref, tiles_ref, sems
 ):
@@ -373,11 +385,6 @@
     def swap(value, step):
         return lax.ppermute(value, "pipe", [(i, i ^ step) for i in range(pipes)])
 
-    def gather(own, behind):
-        across = swap(own, 2)
-        tied, tied_across, _ = lax.optimization_barrier((own, across, behind))
-        return [own, swap(tied, 1), across, swap(tied_across, 1)]
-
     def mix(backward, value, *early):
         return call(
             functools.partial(mix_kernel, backward),
@@ -427,9 +434,18 @@
     )
     received = exchange(sent)
     received, spectra = lax.optimization_barrier((received, spectra))
+    (both,) = call(
+        pack_kernel,
+        [shape((2 * groups, span + 2, channels), bf16)],
+        [VMEM] * 2,
+        name="pack",
+    )(spectra, received)
     mixed, outputs = mix(True, received, early)
-    fields = gather(spectra, mixed)
-    grads = gather(received, mixed)
+    both, behind = lax.optimization_barrier((swap(both, 2), mixed))
+    across = call(split_kernel, [message] * 2, [VMEM], name="split")(both)
+    spectra, received, _ = lax.optimization_barrier((spectra, received, behind))
+    fields = [spectra, swap(spectra, 1), across[0], swap(across[0], 1)]
+    grads = [received, swap(received, 1), across[1], swap(across[1], 1)]
     returned = exchange(mixed)
     big = shape((modes, channels, channels), f32)
     per_copy = math.gcd(modes, 2)

time: 63 us -> 62.1 us (0.986)
  starting transfers between devices: 8.41 us -> 7.28 us
    ppermute x9 -> x8, waiting for transfers between devices: 2.35 us -> 3.61 us  [swap(): return lax.ppermute(value, 'pipe', [(i, i ^ step) for i in range(pipes)])]
    ppermute x9 -> x8, starting transfers between devices: 5.02 us -> 3.89 us  [swap(): return lax.ppermute(value, 'pipe', [(i, i ^ step) for i in range(pipes)])]
    all_to_all x1, waiting for transfers between devices: 1.06 us -> 0.01 us  [exchange(): return lax.all_to_all(value, 'len', split_axis=0, concat_axis=0, tiled=True)]
  transfers between devices with their start and end apart: 10 -> 9, of which waited for: 7 -> 5; matrix products, arithmetic and copies ran while one was open for 0% -> 0% of each run, Pallas kernels for 11% -> 11%
where the time goes in v11:
time: 62.1 us; the launch traced here: 61.7 us
  blocking collectives  35.5 us (57%)
  Pallas kernels  12.1 us (19%)
  starting transfers between devices  7.28 us (12%)
  waiting for transfers between devices  3.61 us (6%)
  local copies, waits for them, and re-layouts  2.33 us (4%)
  between operations  0.86 us (1%)
    all_to_all x3, blocking collectives, exchange(): return lax.all_to_all(value, 'len', split_axis=0, concat_axis=0, tiled=True)  35.5 us
    pallas_call x1, Pallas kernels, body(): call(functools.partial(weight_grad_kernel, pipes, modes, per_copy), [big,...  3.99 us
    ppermute x8, starting transfers between devices, swap(): return lax.ppermute(value, 'pipe', [(i, i ^ step) for i in range(pipes)])  3.89 us
    ppermute x8, waiting for transfers between devices, swap(): return lax.ppermute(value, 'pipe', [(i, i ^ step) for i in range(pipes)])  3.61 us
    pallas_call x1, Pallas kernels, body(): call(functools.partial(layer_kernel, pipes), [shape(field.shape, bf16)] *...  3.52 us
    all_to_all x1, starting transfers between devices, exchange(): return lax.all_to_all(value, 'len', split_axis=0, concat_axis=0, tiled=True)  3.38 us
    pallas_call x2, Pallas kernels, mix(): call(functools.partial(mix_kernel, backward), [chunks, early[0]] if backw...  2.65 us
    unnamed x26, local copies, waits for them, and re-layouts  2.33 us
  transfers between devices with their start and end apart: 9, of which 5 were waited for; matrix products, arithmetic and copies ran while one was open for 0% of the time, Pallas kernels for 11%

profile of v11, /device:TPU:0, one launch (start us, length us, event | category | flops | bytes accessed | tf_op | source)
XLA Modules:
  0.0 61.7 jit_solution(8269109953234599419)
XLA Ops:
  0.6 0.0 copy-start.7
  0.6 1.2 %copy-done.7 = bf16[1,2048,256]{2,1,0:T(8,128)(2,1)S(1)} copy-done((bf16[1,2048,256]{2,1,0:T(8,128)(2,1)S(1)}, bf16[1,2048,256]{2,1,0:T(8,128)(2,1)}, u32[]{:S(2)}) %copy-start.7) | copy-done | bytes 1048600
  1.9 1.0 %copy-done.12 = bf16[4,256,256]{2,1,0:T(8,128)(2,1)S(1)} copy-done((bf16[4,256,256]{2,1,0:T(8,128)(2,1)S(1)}, bf16[4,256,256]{2,1,0:T(8,128)(2,1)}, u32[]{:S(2)}) %copy-start.12) | copy-done | bytes 524312
  2.9 0.4 spectrum.1
  3.3 14.9 %all_to_all.20.r_ref.first_ref.refs_0_ = bf16[8,34,256]{2,1,0:T(8,128)(2,1)S(1)} all-to-all(bf16[8,34,256]{2,1,0:T(8,128)(2,1)S(1)} %spectrum.1), channel_id=1, replica_groups=mesh['len'=8,'pipe'=4] {'len'}, dimensions={0} | all-to-all | bytes 278528 | tf_op jit(solution)/shard_map/all_to_all | solution.py:383
  18.3 0.0 copy-start
  18.3 0.0 copy-start.1
  18.3 0.0 copy-start.3
  18.3 0.0 copy-start.4
  18.4 0.0 copy-start.10
  18.4 0.0 copy-start.11
  18.4 0.1 collective-permute-start.2
  18.5 1.6 %collective-permute-start.1 = (f32[16,256]{1,0:T(8,128)S(1)}, f32[16,256]{1,0:T(8,128)S(1)}, u32[]{:S(2)}, u32[]{:S(2)}) collective-permute-start(f32[16,256]{1,0:T(8,128)S(1)} %pipe_ends.1.refs_0_), channel_id=1, source_target_pairs={{0,2},{1,3},{2,0},{3,1},{4,6},{5,7},{6,4},{7,5},{8,10},{9,11},{10,... | collective-permute-start | bytes 49160 | tf_op jit(solution)/shard_map/ppermute | solution.py:386
  20.0 0.3 collective-permute-start
  20.3 0.7 %mix.1 = bf16[8,32,256]{2,1,0:T(8,128)(2,1)S(1)} custom-call(bf16[8,34,256]{2,1,0:T(8,128)(2,1)S(1)} %all_to_all.20.r_ref.first_ref.refs_0_, bf16[16,256,256]{2,1,0:T(8,128)(2,1)S(1)} %copy-done.5, bf16[16,256,256]{2,1,0:T(8,128)(2,1)S(1)} %copy-done.6), custom_call_target="tpu_custom_call" | custom-call | flops 12000000000 | bytes 12582912 | tf_op jit(solution)/shard_map/mix/pallas_call | solution.py:389
  21.0 0.7 %collective-permute-done.2.refs_3_ = f32[16,256]{1,0:T(8,128)S(1)} collective-permute-done((f32[16,256]{1,0:T(8,128)S(1)}, f32[16,256]{1,0:T(8,128)S(1)}, u32[]{:S(2)}, u32[]{:S(2)}) %collective-permute-start.2) | collective-permute-done | bytes 16416 | tf_op jit(solution)/shard_map/ppermute | solution.py:386
  21.7 0.5 collective-permute-done.1.refs_2_
  22.3 10.6 %all_to_all.21.refs_14_ = bf16[8,32,256]{2,1,0:T(8,128)(2,1)S(1)} all-to-all(bf16[8,32,256]{2,1,0:T(8,128)(2,1)S(1)} %mix.1), channel_id=1, replica_groups=mesh['len'=8,'pipe'=4] {'len'}, dimensions={0} | all-to-all | bytes 262144 | tf_op jit(solution)/shard_map/all_to_all | solution.py:383
  33.0 3.5 %layer.1 = (bf16[2048,256]{1,0:T(8,128)(2,1)S(1)}, bf16[2048,256]{1,0:T(8,128)(2,1)S(1)}, bf16[8,34,256]{2,1,0:T(8,128)(2,1)S(1)}, f32[8,256]{1,0:T(8,128)S(1)}) custom-call(f32[16,256]{1,0:T(8,128)S(1)} %pipe_ends.1.refs_0_, f32[16,256]{1,0:T(8,128)S(1)} %collective-permute-done.refs_1_, f32[16,256]{1,0:T(8,128)S(1)} %collective-permute-done.1.refs_2_, ...), custom_call_target="tpu_custom_call" | custom-call | flops 12000000000 | bytes 12582912 | tf_op jit(solution)/shard_map/layer/pallas_call | solution.py:414
  36.5 10.0 %all_to_all.22.r_ref.second_ref.refs_4_ = bf16[8,34,256]{2,1,0:T(8,128)(2,1)S(1)} all-to-all(bf16[8,34,256]{2,1,0:T(8,128)(2,1)S(1)} %get-tuple-element.30), channel_id=1, replica_groups=mesh['len'=8,'pipe'=4] {'len'}, dimensions={0} | all-to-all | bytes 278528 | tf_op jit(solution)/shard_map/all_to_all | solution.py:383
  46.5 0.8 %collective-permute-start.4 = (bf16[16,34,256]{2,1,0:T(8,128)(2,1)S(1)}, bf16[16,34,256]{2,1,0:T(8,128)(2,1)S(1)}, u32[]{:S(2)}, u32[]{:S(2)}) collective-permute-start(bf16[16,34,256]{2,1,0:T(8,128)(2,1)S(1)} %pack.1), channel_id=1, source_target_pairs={{0,2},{1,3},{2,0},{3,1},{4,6},{5,7},{6,4},{7,5},{8,10},{9,11},{10,... | collective-permute-start | bytes 835592 | tf_op jit(solution)/shard_map/ppermute | solution.py:386
  47.4 1.9 %mix_grad.1 = (bf16[8,32,256]{2,1,0:T(8,128)(2,1)}, bf16[2048,256]{1,0:T(8,128)(2,1)}) custom-call(bf16[8,34,256]{2,1,0:T(8,128)(2,1)S(1)} %all_to_all.22.r_ref.second_ref.refs_4_, bf16[16,256,256]{2,1,0:T(8,128)(2,1)S(1)} %copy-done.5, bf16[16,256,256]{2,1,0:T(8,128)(2,1)S(1)} %copy-done.6, bf16[2048,256]{1,0:T(8,128)(2,1)S(1)} %get-tuple-element.32.refs_0_), custom_call_target="tpu_custom_call" | custom-call | flops 12000000000 | bytes 12582912 | tf_op jit(solution)/shard_map/mix_grad/pallas_call | solution.py:389
  49.3 3.4 %all-to-all-start.3 = ((bf16[8,32,256]{2,1,0:T(8,128)(2,1)}), bf16[8,32,256]{2,1,0:T(8,128)(2,1)S(1)}, u32[]{:S(2)}, u32[]{:S(2)}) async-start(bf16[8,32,256]{2,1,0:T(8,128)(2,1)} %get-tuple-element.37), calls=%async_computation.3 | async-start | bytes 262144 | tf_op jit(solution)/shard_map/all_to_all | solution.py:383
  52.7 0.1 collective-permute-start.3
  52.8 0.5 collective-permute-start.6
  53.3 1.3 %collective-permute-done.4.both_ref = bf16[16,34,256]{2,1,0:T(8,128)(2,1)S(1)} collective-permute-done((bf16[16,34,256]{2,1,0:T(8,128)(2,1)S(1)}, bf16[16,34,256]{2,1,0:T(8,128)(2,1)S(1)}, u32[]{:S(2)}, u32[]{:S(2)}) %collective-permute-start.4) | collective-permute-done | bytes 278560 | tf_op jit(solution)/shard_map/ppermute | solution.py:386
  54.6 0.1 collective-permute-start.5
  54.7 0.5 collective-permute-start.7
  55.2 0.9 %collective-permute-done.5.refs_3_ = bf16[8,34,256]{2,1,0:T(8,128)(2,1)S(1)} collective-permute-done((bf16[8,34,256]{2,1,0:T(8,128)(2,1)S(1)}, bf16[8,34,256]{2,1,0:T(8,128)(2,1)S(1)}, u32[]{:S(2)}, u32[]{:S(2)}) %collective-permute-start.5) | collective-permute-done | bytes 139296 | tf_op jit(solution)/shard_map/ppermute | solution.py:386
  56.0 0.2 collective-permute-done.7.refs_7_
  56.3 4.0 %weight_grad.1 = (f32[16,256,256]{2,1,0:T(8,128)}, f32[16,256,256]{2,1,0:T(8,128)}, f32[8,256]{1,0:T(8,128)S(1)}) custom-call(bf16[8,34,256]{2,1,0:T(8,128)(2,1)S(1)} %all_to_all.20.r_ref.first_ref.refs_0_, bf16[8,34,256]{2,1,0:T(8,128)(2,1)S(1)} %collective-permute-done.3.refs_1_, bf16[8,34,256]{2,1,0:T(8,128)(2,1)S(1)} %get-tuple-element.39.refs_2_, ...), custom_call_target="tpu_custom_call" | custom-call | tf_op jit(solution)/shard_map/weight_grad/pallas_call | solution.py:452
  60.3 1.5 %input_grad.1 = bf16[2048,256]{1,0:T(8,128)(2,1)} custom-call(bf16[2048,256]{1,0:T(8,128)(2,1)S(1)} %get-tuple-element.34.total_ref, bf16[1024,256]{1,0:T(8,128)(2,1)S(1)} %copy-done, bf16[256,256]{1,0:T(8,128)(2,1)S(1)} %copy-done.2, f32[8,256]{1,0:T(8,128)S(1)} %get-tuple-element.43.rows_ref, bf16[8,32,256]{2,1,0:T(8,128)(2,1)S(1)} %all-to-all-done.3.modes_ref), custom_call_target="tpu_custom_call" | custom-call | tf_op jit(solution)/shard_map/input_grad/pallas_call | solution.py:465
  (24 shorter events, 0.1 us)
Async XLA Ops:
  0.6 1.2 %copy-start.7 = (bf16[1,2048,256]{2,1,0:T(8,128)(2,1)S(1)}, bf16[1,2048,256]{2,1,0:T(8,128)(2,1)}, u32[]{:S(2)}) copy-start(bf16[1,2048,256]{2,1,0:T(8,128)(2,1)} %param.12) | copy-start | bytes 3145732
  1.9 1.0 %copy-start.12 = (bf16[4,256,256]{2,1,0:T(8,128)(2,1)S(1)}, bf16[4,256,256]{2,1,0:T(8,128)(2,1)}, u32[]{:S(2)}) copy-start(bf16[4,256,256]{2,1,0:T(8,128)(2,1)} %constant.4.clone.f_ref.refs_10_) | copy-start | bytes 1572868
  2.9 17.4 %copy-start.5 = (bf16[16,256,256]{2,1,0:T(8,128)(2,1)S(1)}, bf16[16,256,256]{2,1,0:T(8,128)(2,1)}, u32[]{:S(2)}) copy-start(bf16[16,256,256]{2,1,0:T(8,128)(2,1)} %real_ref.3) | copy-start | bytes 6291460
  2.9 17.4 %copy-start.6 = (bf16[16,256,256]{2,1,0:T(8,128)(2,1)S(1)}, bf16[16,256,256]{2,1,0:T(8,128)(2,1)}, u32[]{:S(2)}) copy-start(bf16[16,256,256]{2,1,0:T(8,128)(2,1)} %imag_ref.3) | copy-start | bytes 6291460
  18.3 14.6 %copy-start = (bf16[1024,256]{1,0:T(8,128)(2,1)S(1)}, bf16[1024,256]{1,0:T(8,128)(2,1)}, u32[]{:S(2)}) copy-start(bf16[1024,256]{1,0:T(8,128)(2,1)} %constant.5.clone.refs_11_.ft_ref) | copy-start | bytes 1572868
  18.3 14.6 %copy-start.1 = (bf16[256,256]{1,0:T(8,128)(2,1)S(1)}, bf16[256,256]{1,0:T(8,128)(2,1)}, u32[]{:S(2)}) copy-start(bf16[256,256]{1,0:T(8,128)(2,1)} %refs_10_.2) | copy-start | bytes 393220
  18.3 14.6 %copy-start.2 = (bf16[256,256]{1,0:T(8,128)(2,1)S(1)}, bf16[256,256]{1,0:T(8,128)(2,1)}, u32[]{:S(2)}) copy-start(bf16[256,256]{1,0:T(8,128)(2,1)} %weight_ref.1) | copy-start | bytes 393220
  18.3 14.6 %copy-start.3 = (s32[32]{0:T(128)S(1)}, s32[32]{0:T(128)}, u32[]{:S(2)}) copy-start(s32[32]{0:T(128)} %param.20) | copy-start | bytes 388
  18.3 14.6 %copy-start.4 = (s32[32]{0:T(128)S(1)}, s32[32]{0:T(128)}, u32[]{:S(2)}) copy-start(s32[32]{0:T(128)} %param.21) | copy-start | bytes 388
  18.3 14.6 %copy-start.8 = (bf16[1,2048,256]{2,1,0:T(8,128)(2,1)S(1)}, bf16[1,2048,256]{2,1,0:T(8,128)(2,1)}, u32[]{:S(2)}) copy-start(bf16[1,2048,256]{2,1,0:T(8,128)(2,1)} %param.12) | copy-start | bytes 3145732
  18.3 14.6 %copy-start.9 = (bf16[1,2048,256]{2,1,0:T(8,128)(2,1)S(1)}, bf16[1,2048,256]{2,1,0:T(8,128)(2,1)}, u32[]{:S(2)}) copy-start(bf16[1,2048,256]{2,1,0:T(8,128)(2,1)} %param.13) | copy-start | bytes 3145732
  18.4 14.6 %copy-start.10 = (f32[256]{0:T(256)S(1)}, f32[256]{0:T(256)}, u32[]{:S(2)}) copy-start(f32[256]{0:T(256)} %param.19) | copy-start | bytes 3076
  18.4 14.6 %copy-start.11 = (f32[256]{0:T(256)S(1)}, f32[256]{0:T(256)}, u32[]{:S(2)}) copy-start(f32[256]{0:T(256)} %param.15) | copy-start | bytes 3076
  18.4 3.4 %collective-permute-start.2 = (f32[16,256]{1,0:T(8,128)S(1)}, f32[16,256]{1,0:T(8,128)S(1)}, u32[]{:S(2)}, u32[]{:S(2)}) collective-permute-start(f32[16,256]{1,0:T(8,128)S(1)} %pipe_ends.1.refs_0_), channel_id=1, source_target_pairs={{0,3},{1,2},{2,1},{3,0},{4,7},{5,6},{6,5},{7,4},{8,11},{9,10},{10,... | collective-permute-start | bytes 49160 | tf_op jit(solution)/shard_map/ppermute | solution.py:386
  18.5 3.8 %collective-permute-start.1 = (f32[16,256]{1,0:T(8,128)S(1)}, f32[16,256]{1,0:T(8,128)S(1)}, u32[]{:S(2)}, u32[]{:S(2)}) collective-permute-start(f32[16,256]{1,0:T(8,128)S(1)} %pipe_ends.1.refs_0_), channel_id=1, source_target_pairs={{0,2},{1,3},{2,0},{3,1},{4,6},{5,7},{6,4},{7,5},{8,10},{9,11},{10,... | collective-permute-start | bytes 49160 | tf_op jit(solution)/shard_map/ppermute | solution.py:386
  20.0 2.2 %collective-permute-start = (f32[16,256]{1,0:T(8,128)S(1)}, f32[16,256]{1,0:T(8,128)S(1)}, u32[]{:S(2)}, u32[]{:S(2)}) collective-permute-start(f32[16,256]{1,0:T(8,128)S(1)} %pipe_ends.1.refs_0_), channel_id=1, source_target_pairs={{0,1},{1,0},{2,3},{3,2},{4,5},{5,4},{6,7},{7,6},{8,9},{9,8},{10,11... | collective-permute-start | bytes 49160 | tf_op jit(solution)/shard_map/ppermute | solution.py:386
  46.5 8.0 %collective-permute-start.4 = (bf16[16,34,256]{2,1,0:T(8,128)(2,1)S(1)}, bf16[16,34,256]{2,1,0:T(8,128)(2,1)S(1)}, u32[]{:S(2)}, u32[]{:S(2)}) collective-permute-start(bf16[16,34,256]{2,1,0:T(8,128)(2,1)S(1)} %pack.1), channel_id=1, source_target_pairs={{0,2},{1,3},{2,0},{3,1},{4,6},{5,7},{6,4},{7,5},{8,10},{9,11},{10,... | collective-permute-start | bytes 835592 | tf_op jit(solution)/shard_map/ppermute | solution.py:386
  49.3 11.0 %all-to-all-start.3 = ((bf16[8,32,256]{2,1,0:T(8,128)(2,1)}), bf16[8,32,256]{2,1,0:T(8,128)(2,1)S(1)}, u32[]{:S(2)}, u32[]{:S(2)}) async-start(bf16[8,32,256]{2,1,0:T(8,128)(2,1)} %get-tuple-element.37), calls=%async_computation.3 | async-start | bytes 262144 | tf_op jit(solution)/shard_map/all_to_all | solution.py:383
  52.7 2.5 %collective-permute-start.3 = (bf16[8,34,256]{2,1,0:T(8,128)(2,1)S(1)}, bf16[8,34,256]{2,1,0:T(8,128)(2,1)S(1)}, u32[]{:S(2)}, u32[]{:S(2)}) collective-permute-start(bf16[8,34,256]{2,1,0:T(8,128)(2,1)S(1)} %all_to_all.20.r_ref.first_ref.refs_0_), channel_id=1, source_target_pairs={{0,1},{1,0},{2,3},{3,2},{4,5},{5,4},{6,7},{7,6},{8,9},{9,8},{10,11... | collective-permute-start | bytes 417800 | tf_op jit(solution)/shard_map/ppermute | solution.py:386
  52.8 2.4 %collective-permute-start.6 = (bf16[8,34,256]{2,1,0:T(8,128)(2,1)S(1)}, bf16[8,34,256]{2,1,0:T(8,128)(2,1)S(1)}, u32[]{:S(2)}, u32[]{:S(2)}) collective-permute-start(bf16[8,34,256]{2,1,0:T(8,128)(2,1)S(1)} %all_to_all.22.r_ref.second_ref.refs_4_), channel_id=1, source_target_pairs={{0,1},{1,0},{2,3},{3,2},{4,5},{5,4},{6,7},{7,6},{8,9},{9,8},{10,11... | collective-permute-start | bytes 417800 | tf_op jit(solution)/shard_map/ppermute | solution.py:386
  54.6 1.5 %collective-permute-start.5 = (bf16[8,34,256]{2,1,0:T(8,128)(2,1)S(1)}, bf16[8,34,256]{2,1,0:T(8,128)(2,1)S(1)}, u32[]{:S(2)}, u32[]{:S(2)}) collective-permute-start(bf16[8,34,256]{2,1,0:T(8,128)(2,1)S(1)} %get-tuple-element.39.refs_2_), channel_id=1, source_target_pairs={{0,1},{1,0},{2,3},{3,2},{4,5},{5,4},{6,7},{7,6},{8,9},{9,8},{10,11... | collective-permute-start | bytes 417800 | tf_op jit(solution)/shard_map/ppermute | solution.py:386
  54.7 1.6 %collective-permute-start.7 = (bf16[8,34,256]{2,1,0:T(8,128)(2,1)S(1)}, bf16[8,34,256]{2,1,0:T(8,128)(2,1)S(1)}, u32[]{:S(2)}, u32[]{:S(2)}) collective-permute-start(bf16[8,34,256]{2,1,0:T(8,128)(2,1)S(1)} %get-tuple-element.41.refs_6_), channel_id=1, source_target_pairs={{0,1},{1,0},{2,3},{3,2},{4,5},{5,4},{6,7},{7,6},{8,9},{9,8},{10,11... | collective-permute-start | bytes 417800 | tf_op jit(solution)/shard_map/ppermute | solution.py:386

commit v12 on v11

--- a/solution.py
+++ b/solution.py
@@ -36,6 +36,10 @@
     per_owner = span // 2
     mode = (row // span) * per_owner + lax.rem(row, per_owner)
     return jnp.where(lax.rem(mode, 2) == 0, 1.0, -1.0).astype(jnp.float32)
+
+
+def position(column, group, groups):
+    return jnp.where(lax.rem(column, 2) == 0, group, groups - 1 - group)
 
 
 def dot(left, right, left_dim=1, right_dim=0):
@@ -72,9 +76,11 @@
         sums.append(total)
     spectra = (sums[0] + row_signs(all_rows, span, channels) * sums[1]).astype(jnp.bfloat16)
     ends = extra_rows(x_ref[0:1, :], x_ref[cells - 1 : cells, :], rows - span, channels)
+    column = lax.axis_index("pipe")
     for at in range(groups):
-        msg_ref[at, 0:span, :] = spectra[at * span : (at + 1) * span]
-        msg_ref[at, span:rows, :] = ends
+        to = position(column, at, groups)
+        msg_ref[to, 0:span, :] = spectra[at * span : (at + 1) * span]
+        msg_ref[to, span:rows, :] = ends
 
 
 def extra_rows(first, second, count, channels):
@@ -139,8 +145,9 @@
 
 def ends_kernel(r_ref, ends_ref):
     groups, rows = r_ref.shape[0], r_ref.shape[1]
+    column = lax.axis_index("pipe")
     for group in range(groups):
-        ends = r_ref[group, rows - 2 : rows, :].astype(jnp.float32)
+        ends = r_ref[position(column, group, groups), rows - 2 : rows, :].astype(jnp.float32)
         ends_ref[group : group + 1, :] = ends[0:1]
         ends_ref[groups + group : groups + group + 1, :] = ends[1:2]
 
@@ -190,9 +197,8 @@
     row = lax.broadcasted_iota(jnp.int32, (all_rows, channels), 0)
     doubled = jnp.where((row == 0) | (row == span // 2), 1.0, 2.0).astype(jnp.float32)
     signs = row_signs(all_rows, span, channels)
-    modes = jnp.concatenate(
-        [modes_ref[at, 0:span, :].astype(jnp.float32) for at in range(groups)], axis=0
-    )
+    order = [position(column, at, groups) for at in range(groups)]
+    modes = jnp.concatenate([modes_ref[at].astype(jnp.float32) for at in order], axis=0)
     modes = modes * doubled
     modes = (modes.astype(jnp.bfloat16), (modes * signs).astype(jnp.bfloat16))
     weight = weight_ref[...]
@@ -223,8 +229,8 @@
     extra = extra_rows(upper, grad_cond - upper, rows - span, channels)
     grad_spec = (acc * doubled).astype(jnp.bfloat16)
     for at in range(groups):
-        msg_ref[at, 0:span, :] = grad_spec[at * span : (at + 1) * span]
-        msg_ref[at, span:rows, :] = extra
+        msg_ref[order[at], 0:span, :] = grad_spec[at * span : (at + 1) * span]
+        msg_ref[order[at], span:rows, :] = extra
 
 
 def weight_grad_kernel(pipes, modes, per_copy, *refs):
@@ -262,7 +268,8 @@
     column = lax.axis_index("pipe")
     for step in range(pipes):
         for group in range(groups):
-            parts = grads[step][group, rows - 2 : rows, :].astype(jnp.float32)
+            at = position(lax.bitwise_xor(column, step), group, groups)
+            parts = grads[step][at, rows - 2 : rows, :].astype(jnp.float32)
             upper_ref[group : group + 1, :] = parts[0:1]
             lower_ref[group : group + 1, :] = parts[1:2]
         at = pl.ds(lax.bitwise_xor(column, step), groups, stride=pipes)
@@ -295,9 +302,9 @@
     groups, span, channels = modes_ref.shape
     steps, tile = tiles_ref.shape[0], tiles_ref.shape[2]
     half, all_rows = steps * tile, groups * span
-    back = jnp.concatenate(
-        [modes_ref[at, 0:span, :].astype(jnp.float32) for at in range(groups)], axis=0
-    )
+    column = lax.axis_index("pipe")
+    order = [position(column, at, groups) for at in range(groups)]
+    back = jnp.concatenate([modes_ref[at].astype(jnp.float32) for at in order], axis=0)
     signs = row_signs(all_rows, span, channels)
     back = (back.astype(jnp.bfloat16), (back * signs).astype(jnp.bfloat16))
     weight = weight_ref[...]
@@ -379,8 +386,23 @@
     chunks = shape((groups, span, channels), bf16)
     dma = pltpu.SemaphoreType.DMA
 
+    ranks = [
+        [
+            (groups - 1 - group if column % 2 else group) * pipes + column
+            for group in range(groups)
+        ]
+        for column in range(pipes)
+    ]
+
     def exchange(value):
-        return lax.all_to_all(value, "len", split_axis=0, concat_axis=0, tiled=True)
+        return lax.all_to_all(
+            value,
+            ("len", "pipe"),
+            split_axis=0,
+            concat_axis=0,
+            tiled=True,
+            axis_index_groups=ranks,
+        )
 
     def swap(value, step):
         return lax.ppermute(value, "pipe", [(i, i ^ step) for i in range(pipes)])

time: 62.1 us -> 62.2 us (level)
  no operation moved by 1% of the time
where the time goes in v12:
time: 62.2 us; the launch traced here: 61.8 us
  blocking collectives  35.9 us (58%)
  Pallas kernels  12.1 us (19%)
  starting transfers between devices  6.75 us (11%)
  waiting for transfers between devices  3.84 us (6%)
  local copies, waits for them, and re-layouts  2.33 us (4%)
  between operations  0.85 us (1%)
    all_to_all x3, blocking collectives, exchange(): lax.all_to_all(value, ('len', 'pipe'), split_axis=0, concat_axis=0, tiled...  35.9 us
    pallas_call x1, Pallas kernels, body(): call(functools.partial(weight_grad_kernel, pipes, modes, per_copy), [big,...  3.99 us
    ppermute x8, waiting for transfers between devices, swap(): return lax.ppermute(value, 'pipe', [(i, i ^ step) for i in range(pipes)])  3.84 us
    pallas_call x1, Pallas kernels, body(): call(functools.partial(layer_kernel, pipes), [shape(field.shape, bf16)] *...  3.52 us
    all_to_all x1, starting transfers between devices, exchange(): lax.all_to_all(value, ('len', 'pipe'), split_axis=0, concat_axis=0, tiled...  3.38 us
    ppermute x8, starting transfers between devices, swap(): return lax.ppermute(value, 'pipe', [(i, i ^ step) for i in range(pipes)])  3.36 us
    pallas_call x2, Pallas kernels, mix(): call(functools.partial(mix_kernel, backward), [chunks, early[0]] if backw...  2.65 us
    unnamed x26, local copies, waits for them, and re-layouts  2.33 us
  transfers between devices with their start and end apart: 9, of which 5 were waited for; matrix products, arithmetic and copies ran while one was open for 0% of the time, Pallas kernels for 11%

profile of v12, /device:TPU:0, one launch (start us, length us, event | category | flops | bytes accessed | tf_op | source)
XLA Modules:
  0.0 61.8 jit_solution(14775767764286757950)
XLA Ops:
  0.6 0.0 copy-start.7
  0.6 1.2 %copy-done.7 = bf16[1,2048,256]{2,1,0:T(8,128)(2,1)S(1)} copy-done((bf16[1,2048,256]{2,1,0:T(8,128)(2,1)S(1)}, bf16[1,2048,256]{2,1,0:T(8,128)(2,1)}, u32[]{:S(2)}) %copy-start.7) | copy-done | bytes 1048600
  1.9 1.0 %copy-done.12 = bf16[4,256,256]{2,1,0:T(8,128)(2,1)S(1)} copy-done((bf16[4,256,256]{2,1,0:T(8,128)(2,1)S(1)}, bf16[4,256,256]{2,1,0:T(8,128)(2,1)}, u32[]{:S(2)}) %copy-start.12) | copy-done | bytes 524312
  2.9 0.4 spectrum.1
  3.3 14.9 %all_to_all.20.r_ref.first_ref.refs_0_ = bf16[8,34,256]{2,1,0:T(8,128)(2,1)S(1)} all-to-all(bf16[8,34,256]{2,1,0:T(8,128)(2,1)S(1)} %spectrum.1), channel_id=1, replica_groups={{0,4,8,12,16,20,24,28},{29,25,21,17,13,9,5,1},{2,6,10,14,18,22,26,30},{..., dimensions={0} | all-to-all | bytes 278528 | tf_op jit(solution)/shard_map/all_to_all | solution.py:398
  18.3 0.0 copy-start
  18.3 0.0 copy-start.1
  18.3 0.0 copy-start.2
  18.3 0.0 copy-start.3
  18.3 0.0 copy-start.4
  18.4 0.0 copy-start.10
  18.4 0.0 copy-start.11
  18.4 0.1 collective-permute-start.2
  18.5 1.6 %collective-permute-start.1 = (f32[16,256]{1,0:T(8,128)S(1)}, f32[16,256]{1,0:T(8,128)S(1)}, u32[]{:S(2)}, u32[]{:S(2)}) collective-permute-start(f32[16,256]{1,0:T(8,128)S(1)} %pipe_ends.1.refs_0_), channel_id=1, source_target_pairs={{0,2},{1,3},{2,0},{3,1},{4,6},{5,7},{6,4},{7,5},{8,10},{9,11},{10,... | collective-permute-start | bytes 49160 | tf_op jit(solution)/shard_map/ppermute | solution.py:408
  20.0 0.3 collective-permute-start
  20.3 0.7 %mix.1 = bf16[8,32,256]{2,1,0:T(8,128)(2,1)S(1)} custom-call(bf16[8,34,256]{2,1,0:T(8,128)(2,1)S(1)} %all_to_all.20.r_ref.first_ref.refs_0_, bf16[16,256,256]{2,1,0:T(8,128)(2,1)S(1)} %copy-done.5, bf16[16,256,256]{2,1,0:T(8,128)(2,1)S(1)} %copy-done.6), custom_call_target="tpu_custom_call" | custom-call | flops 12000000000 | bytes 12582912 | tf_op jit(solution)/shard_map/mix/pallas_call | solution.py:411
  21.0 0.7 %collective-permute-done.2.refs_3_ = f32[16,256]{1,0:T(8,128)S(1)} collective-permute-done((f32[16,256]{1,0:T(8,128)S(1)}, f32[16,256]{1,0:T(8,128)S(1)}, u32[]{:S(2)}, u32[]{:S(2)}) %collective-permute-start.2) | collective-permute-done | bytes 16416 | tf_op jit(solution)/shard_map/ppermute | solution.py:408
  21.7 0.5 collective-permute-done.1.refs_2_
  22.3 10.5 %all_to_all.21.refs_14_ = bf16[8,32,256]{2,1,0:T(8,128)(2,1)S(1)} all-to-all(bf16[8,32,256]{2,1,0:T(8,128)(2,1)S(1)} %mix.1), channel_id=1, replica_groups={{0,4,8,12,16,20,24,28},{29,25,21,17,13,9,5,1},{2,6,10,14,18,22,26,30},{..., dimensions={0} | all-to-all | bytes 262144 | tf_op jit(solution)/shard_map/all_to_all | solution.py:398
  32.9 3.5 %layer.1 = (bf16[2048,256]{1,0:T(8,128)(2,1)S(1)}, bf16[2048,256]{1,0:T(8,128)(2,1)S(1)}, bf16[8,34,256]{2,1,0:T(8,128)(2,1)S(1)}, f32[8,256]{1,0:T(8,128)S(1)}) custom-call(f32[16,256]{1,0:T(8,128)S(1)} %pipe_ends.1.refs_0_, f32[16,256]{1,0:T(8,128)S(1)} %collective-permute-done.refs_1_, f32[16,256]{1,0:T(8,128)S(1)} %collective-permute-done.1.refs_2_, ...), custom_call_target="tpu_custom_call" | custom-call | flops 12000000000 | bytes 12582912 | tf_op jit(solution)/shard_map/layer/pallas_call | solution.py:436
  36.4 10.5 %all_to_all.22.r_ref.second_ref.refs_4_ = bf16[8,34,256]{2,1,0:T(8,128)(2,1)S(1)} all-to-all(bf16[8,34,256]{2,1,0:T(8,128)(2,1)S(1)} %get-tuple-element.30), channel_id=1, replica_groups={{0,4,8,12,16,20,24,28},{29,25,21,17,13,9,5,1},{2,6,10,14,18,22,26,30},{..., dimensions={0} | all-to-all | bytes 278528 | tf_op jit(solution)/shard_map/all_to_all | solution.py:398
  46.9 0.2 collective-permute-start.4
  47.1 1.9 %mix_grad.1 = (bf16[8,32,256]{2,1,0:T(8,128)(2,1)}, bf16[2048,256]{1,0:T(8,128)(2,1)}) custom-call(bf16[8,34,256]{2,1,0:T(8,128)(2,1)S(1)} %all_to_all.22.r_ref.second_ref.refs_4_, bf16[16,256,256]{2,1,0:T(8,128)(2,1)S(1)} %copy-done.5, bf16[16,256,256]{2,1,0:T(8,128)(2,1)S(1)} %copy-done.6, bf16[2048,256]{1,0:T(8,128)(2,1)S(1)} %get-tuple-element.32.refs_0_), custom_call_target="tpu_custom_call" | custom-call | flops 12000000000 | bytes 12582912 | tf_op jit(solution)/shard_map/mix_grad/pallas_call | solution.py:411
  49.1 3.4 %all-to-all-start.3 = ((bf16[8,32,256]{2,1,0:T(8,128)(2,1)}), bf16[8,32,256]{2,1,0:T(8,128)(2,1)S(1)}, u32[]{:S(2)}, u32[]{:S(2)}) async-start(bf16[8,32,256]{2,1,0:T(8,128)(2,1)} %get-tuple-element.37), calls=%async_computation.3 | async-start | bytes 262144 | tf_op jit(solution)/shard_map/all_to_all | solution.py:398
  52.5 0.7 %collective-permute-start.3 = (bf16[8,34,256]{2,1,0:T(8,128)(2,1)S(1)}, bf16[8,34,256]{2,1,0:T(8,128)(2,1)S(1)}, u32[]{:S(2)}, u32[]{:S(2)}) collective-permute-start(bf16[8,34,256]{2,1,0:T(8,128)(2,1)S(1)} %all_to_all.20.r_ref.first_ref.refs_0_), channel_id=1, source_target_pairs={{0,1},{1,0},{2,3},{3,2},{4,5},{5,4},{6,7},{7,6},{8,9},{9,8},{10,11... | collective-permute-start | bytes 417800 | tf_op jit(solution)/shard_map/ppermute | solution.py:408
  53.1 1.5 %collective-permute-done.4.both_ref = bf16[16,34,256]{2,1,0:T(8,128)(2,1)S(1)} collective-permute-done((bf16[16,34,256]{2,1,0:T(8,128)(2,1)S(1)}, bf16[16,34,256]{2,1,0:T(8,128)(2,1)S(1)}, u32[]{:S(2)}, u32[]{:S(2)}) %collective-permute-start.4) | collective-permute-done | bytes 278560 | tf_op jit(solution)/shard_map/ppermute | solution.py:408
  54.7 0.1 collective-permute-start.5
  54.7 0.5 collective-permute-start.7
  55.2 0.9 %collective-permute-done.5.refs_3_ = bf16[8,34,256]{2,1,0:T(8,128)(2,1)S(1)} collective-permute-done((bf16[8,34,256]{2,1,0:T(8,128)(2,1)S(1)}, bf16[8,34,256]{2,1,0:T(8,128)(2,1)S(1)}, u32[]{:S(2)}, u32[]{:S(2)}) %collective-permute-start.5) | collective-permute-done | bytes 139296 | tf_op jit(solution)/shard_map/ppermute | solution.py:408
  56.1 0.2 collective-permute-done.7.refs_7_
  56.4 4.0 %weight_grad.1 = (f32[16,256,256]{2,1,0:T(8,128)}, f32[16,256,256]{2,1,0:T(8,128)}, f32[8,256]{1,0:T(8,128)S(1)}) custom-call(bf16[8,34,256]{2,1,0:T(8,128)(2,1)S(1)} %all_to_all.20.r_ref.first_ref.refs_0_, bf16[8,34,256]{2,1,0:T(8,128)(2,1)S(1)} %collective-permute-done.3.refs_1_, bf16[8,34,256]{2,1,0:T(8,128)(2,1)S(1)} %get-tuple-element.39.refs_2_, ...), custom_call_target="tpu_custom_call" | custom-call | tf_op jit(solution)/shard_map/weight_grad/pallas_call | solution.py:474
  60.4 1.5 %input_grad.1 = bf16[2048,256]{1,0:T(8,128)(2,1)} custom-call(bf16[2048,256]{1,0:T(8,128)(2,1)S(1)} %get-tuple-element.34.total_ref, bf16[1024,256]{1,0:T(8,128)(2,1)S(1)} %copy-done, bf16[256,256]{1,0:T(8,128)(2,1)S(1)} %copy-done.2, f32[8,256]{1,0:T(8,128)S(1)} %get-tuple-element.43.rows_ref, bf16[8,32,256]{2,1,0:T(8,128)(2,1)S(1)} %all-to-all-done.3.modes_ref), custom_call_target="tpu_custom_call" | custom-call | tf_op jit(solution)/shard_map/input_grad/pallas_call | solution.py:487
  (24 shorter events, 0.1 us)
Async XLA Ops:
  0.6 1.2 %copy-start.7 = (bf16[1,2048,256]{2,1,0:T(8,128)(2,1)S(1)}, bf16[1,2048,256]{2,1,0:T(8,128)(2,1)}, u32[]{:S(2)}) copy-start(bf16[1,2048,256]{2,1,0:T(8,128)(2,1)} %param.12) | copy-start | bytes 3145732
  1.9 1.0 %copy-start.12 = (bf16[4,256,256]{2,1,0:T(8,128)(2,1)S(1)}, bf16[4,256,256]{2,1,0:T(8,128)(2,1)}, u32[]{:S(2)}) copy-start(bf16[4,256,256]{2,1,0:T(8,128)(2,1)} %constant.4.clone.f_ref.refs_10_) | copy-start | bytes 1572868
  2.9 17.4 %copy-start.5 = (bf16[16,256,256]{2,1,0:T(8,128)(2,1)S(1)}, bf16[16,256,256]{2,1,0:T(8,128)(2,1)}, u32[]{:S(2)}) copy-start(bf16[16,256,256]{2,1,0:T(8,128)(2,1)} %real_ref.3) | copy-start | bytes 6291460
  2.9 17.4 %copy-start.6 = (bf16[16,256,256]{2,1,0:T(8,128)(2,1)S(1)}, bf16[16,256,256]{2,1,0:T(8,128)(2,1)}, u32[]{:S(2)}) copy-start(bf16[16,256,256]{2,1,0:T(8,128)(2,1)} %imag_ref.3) | copy-start | bytes 6291460
  18.3 14.5 %copy-start = (bf16[1024,256]{1,0:T(8,128)(2,1)S(1)}, bf16[1024,256]{1,0:T(8,128)(2,1)}, u32[]{:S(2)}) copy-start(bf16[1024,256]{1,0:T(8,128)(2,1)} %constant.5.clone.refs_11_.ft_ref) | copy-start | bytes 1572868
  18.3 14.5 %copy-start.1 = (bf16[256,256]{1,0:T(8,128)(2,1)S(1)}, bf16[256,256]{1,0:T(8,128)(2,1)}, u32[]{:S(2)}) copy-start(bf16[256,256]{1,0:T(8,128)(2,1)} %refs_10_.2) | copy-start | bytes 393220
  18.3 14.5 %copy-start.2 = (bf16[256,256]{1,0:T(8,128)(2,1)S(1)}, bf16[256,256]{1,0:T(8,128)(2,1)}, u32[]{:S(2)}) copy-start(bf16[256,256]{1,0:T(8,128)(2,1)} %weight_ref.1) | copy-start | bytes 393220
  18.3 14.5 %copy-start.3 = (s32[32]{0:T(128)S(1)}, s32[32]{0:T(128)}, u32[]{:S(2)}) copy-start(s32[32]{0:T(128)} %param.20) | copy-start | bytes 388
  18.3 14.5 %copy-start.4 = (s32[32]{0:T(128)S(1)}, s32[32]{0:T(128)}, u32[]{:S(2)}) copy-start(s32[32]{0:T(128)} %param.21) | copy-start | bytes 388
  18.3 14.5 %copy-start.8 = (bf16[1,2048,256]{2,1,0:T(8,128)(2,1)S(1)}, bf16[1,2048,256]{2,1,0:T(8,128)(2,1)}, u32[]{:S(2)}) copy-start(bf16[1,2048,256]{2,1,0:T(8,128)(2,1)} %param.12) | copy-start | bytes 3145732
  18.4 14.5 %copy-start.9 = (bf16[1,2048,256]{2,1,0:T(8,128)(2,1)S(1)}, bf16[1,2048,256]{2,1,0:T(8,128)(2,1)}, u32[]{:S(2)}) copy-start(bf16[1,2048,256]{2,1,0:T(8,128)(2,1)} %param.13) | copy-start | bytes 3145732
  18.4 14.5 %copy-start.10 = (f32[256]{0:T(256)S(1)}, f32[256]{0:T(256)}, u32[]{:S(2)}) copy-start(f32[256]{0:T(256)} %param.19) | copy-start | bytes 3076
  18.4 14.5 %copy-start.11 = (f32[256]{0:T(256)S(1)}, f32[256]{0:T(256)}, u32[]{:S(2)}) copy-start(f32[256]{0:T(256)} %param.15) | copy-start | bytes 3076
  18.4 3.4 %collective-permute-start.2 = (f32[16,256]{1,0:T(8,128)S(1)}, f32[16,256]{1,0:T(8,128)S(1)}, u32[]{:S(2)}, u32[]{:S(2)}) collective-permute-start(f32[16,256]{1,0:T(8,128)S(1)} %pipe_ends.1.refs_0_), channel_id=1, source_target_pairs={{0,3},{1,2},{2,1},{3,0},{4,7},{5,6},{6,5},{7,4},{8,11},{9,10},{10,... | collective-permute-start | bytes 49160 | tf_op jit(solution)/shard_map/ppermute | solution.py:408
  18.5 3.8 %collective-permute-start.1 = (f32[16,256]{1,0:T(8,128)S(1)}, f32[16,256]{1,0:T(8,128)S(1)}, u32[]{:S(2)}, u32[]{:S(2)}) collective-permute-start(f32[16,256]{1,0:T(8,128)S(1)} %pipe_ends.1.refs_0_), channel_id=1, source_target_pairs={{0,2},{1,3},{2,0},{3,1},{4,6},{5,7},{6,4},{7,5},{8,10},{9,11},{10,... | collective-permute-start | bytes 49160 | tf_op jit(solution)/shard_map/ppermute | solution.py:408
  20.0 2.2 %collective-permute-start = (f32[16,256]{1,0:T(8,128)S(1)}, f32[16,256]{1,0:T(8,128)S(1)}, u32[]{:S(2)}, u32[]{:S(2)}) collective-permute-start(f32[16,256]{1,0:T(8,128)S(1)} %pipe_ends.1.refs_0_), channel_id=1, source_target_pairs={{0,1},{1,0},{2,3},{3,2},{4,5},{5,4},{6,7},{7,6},{8,9},{9,8},{10,11... | collective-permute-start | bytes 49160 | tf_op jit(solution)/shard_map/ppermute | solution.py:408
  46.9 7.7 %collective-permute-start.4 = (bf16[16,34,256]{2,1,0:T(8,128)(2,1)S(1)}, bf16[16,34,256]{2,1,0:T(8,128)(2,1)S(1)}, u32[]{:S(2)}, u32[]{:S(2)}) collective-permute-start(bf16[16,34,256]{2,1,0:T(8,128)(2,1)S(1)} %pack.1), channel_id=1, source_target_pairs={{0,2},{1,3},{2,0},{3,1},{4,6},{5,7},{6,4},{7,5},{8,10},{9,11},{10,... | collective-permute-start | bytes 835592 | tf_op jit(solution)/shard_map/ppermute | solution.py:408
  49.1 11.3 %all-to-all-start.3 = ((bf16[8,32,256]{2,1,0:T(8,128)(2,1)}), bf16[8,32,256]{2,1,0:T(8,128)(2,1)S(1)}, u32[]{:S(2)}, u32[]{:S(2)}) async-start(bf16[8,32,256]{2,1,0:T(8,128)(2,1)} %get-tuple-element.37), calls=%async_computation.3 | async-start | bytes 262144 | tf_op jit(solution)/shard_map/all_to_all | solution.py:398
  52.5 2.8 %collective-permute-start.3 = (bf16[8,34,256]{2,1,0:T(8,128)(2,1)S(1)}, bf16[8,34,256]{2,1,0:T(8,128)(2,1)S(1)}, u32[]{:S(2)}, u32[]{:S(2)}) collective-permute-start(bf16[8,34,256]{2,1,0:T(8,128)(2,1)S(1)} %all_to_all.20.r_ref.first_ref.refs_0_), channel_id=1, source_target_pairs={{0,1},{1,0},{2,3},{3,2},{4,5},{5,4},{6,7},{7,6},{8,9},{9,8},{10,11... | collective-permute-start | bytes 417800 | tf_op jit(solution)/shard_map/ppermute | solution.py:408
  53.1 2.1 %collective-permute-start.6 = (bf16[8,34,256]{2,1,0:T(8,128)(2,1)S(1)}, bf16[8,34,256]{2,1,0:T(8,128)(2,1)S(1)}, u32[]{:S(2)}, u32[]{:S(2)}) collective-permute-start(bf16[8,34,256]{2,1,0:T(8,128)(2,1)S(1)} %all_to_all.22.r_ref.second_ref.refs_4_), channel_id=1, source_target_pairs={{0,1},{1,0},{2,3},{3,2},{4,5},{5,4},{6,7},{7,6},{8,9},{9,8},{10,11... | collective-permute-start | bytes 417800 | tf_op jit(solution)/shard_map/ppermute | solution.py:408
  54.7 1.5 %collective-permute-start.5 = (bf16[8,34,256]{2,1,0:T(8,128)(2,1)S(1)}, bf16[8,34,256]{2,1,0:T(8,128)(2,1)S(1)}, u32[]{:S(2)}, u32[]{:S(2)}) collective-permute-start(bf16[8,34,256]{2,1,0:T(8,128)(2,1)S(1)} %get-tuple-element.39.refs_2_), channel_id=1, source_target_pairs={{0,1},{1,0},{2,3},{3,2},{4,5},{5,4},{6,7},{7,6},{8,9},{9,8},{10,11... | collective-permute-start | bytes 417800 | tf_op jit(solution)/shard_map/ppermute | solution.py:408
  54.7 1.6 %collective-permute-start.7 = (bf16[8,34,256]{2,1,0:T(8,128)(2,1)S(1)}, bf16[8,34,256]{2,1,0:T(8,128)(2,1)S(1)}, u32[]{:S(2)}, u32[]{:S(2)}) collective-permute-start(bf16[8,34,256]{2,1,0:T(8,128)(2,1)S(1)} %get-tuple-element.41.refs_6_), channel_id=1, source_target_pairs={{0,1},{1,0},{2,3},{3,2},{4,5},{5,4},{6,7},{7,6},{8,9},{9,8},{10,11... | collective-permute-start | bytes 417800 | tf_op jit(solution)/shard_map/ppermute | solution.py:408

commit v13 on v11

--- a/solution.py
+++ b/solution.py
@@ -56,12 +56,16 @@
     return jnp.concatenate([ref[lane, at, :] for lane in range(ref.shape[0])], axis=1)
 
 
-def spectrum_kernel(x_ref, f_ref, msg_ref):
-    groups, rows = msg_ref.shape[0], msg_ref.shape[1]
+def ends_kernel(x_ref, ends_ref):
+    cells, channels = x_ref.shape
+    ends = [x_ref[0:1, :], x_ref[cells - 1 : cells, :], jnp.zeros((6, channels), x_ref.dtype)]
+    ends_ref[...] = jnp.concatenate([part.astype(jnp.float32) for part in ends], axis=0)
+
+
+def spectrum_kernel(x_ref, f_ref, spectra_ref):
     steps, all_rows, tile = f_ref.shape
-    cells, channels = x_ref.shape
-    half = cells // 2
-    span = all_rows // groups
+    half = x_ref.shape[0] // 2
+    groups, span, channels = spectra_ref.shape
     sums = []
     for base in (0, half):
         total = None
@@ -70,11 +74,20 @@
             part = dot(f_ref[step], x_ref[at : at + tile, :])
             total = part if total is None else total + part
         sums.append(total)
-    spectra = (sums[0] + row_signs(all_rows, span, channels) * sums[1]).astype(jnp.bfloat16)
-    ends = extra_rows(x_ref[0:1, :], x_ref[cells - 1 : cells, :], rows - span, channels)
+    spectra = sums[0] + row_signs(all_rows, span, channels) * sums[1]
+    spectra = spectra.astype(jnp.bfloat16)
     for at in range(groups):
-        msg_ref[at, 0:span, :] = spectra[at * span : (at + 1) * span]
-        msg_ref[at, span:rows, :] = ends
+        spectra_ref[at] = spectra[at * span : (at + 1) * span]
+
+
+def message_kernel(pipes, spectra_ref, *refs):
+    groups, span = spectra_ref.shape[0], spectra_ref.shape[1]
+    msg_ref = refs[pipes]
+    ends = jnp.concatenate([refs[step][0:2, :] for step in range(pipes)], axis=0)
+    ends = ends.astype(jnp.bfloat16)
+    for at in range(groups):
+        msg_ref[at, 0:span, :] = spectra_ref[at]
+        msg_ref[at, span:, :] = ends
 
 
 def extra_rows(first, second, count, channels):
@@ -84,16 +97,9 @@
     return jnp.concatenate(parts, axis=0).astype(jnp.bfloat16)
 
 
-def mix_kernel(backward, r_ref, real_ref, imag_ref, *refs):
-    x_ref, y_ref = refs[-2:]
+def mix_rows(backward, r_ref, real_ref, imag_ref, out_ref, x_ref, y_ref):
     groups, modes = r_ref.shape[0], real_ref.shape[0]
     span = 2 * modes
-    if backward:
-        early_ref, out_ref, copied_ref, sem = refs[:4]
-        copy = pltpu.make_async_copy(early_ref, copied_ref, sem)
-        copy.start()
-    else:
-        out_ref = refs[0]
     for source in range(groups):
         put(x_ref, pl.ds(source * span, span), r_ref[source, 0:span, :].astype(jnp.float32))
     for mode in range(modes):
@@ -114,8 +120,51 @@
     for source in range(groups):
         rows = take(y_ref, pl.ds(source * span, span)).astype(jnp.bfloat16)
         out_ref[source] = rows
-    if backward:
-        copy.wait()
+
+
+def mix_kernel(
+    pipes,
+    r_ref,
+    real_ref,
+    imag_ref,
+    inlet_ref,
+    outlet_ref,
+    junc_weight_ref,
+    junc_bias_ref,
+    out_ref,
+    cond_ref,
+    slope_ref,
+    x_ref,
+    y_ref,
+    first_ref,
+    last_ref,
+):
+    groups, rows = r_ref.shape[0], r_ref.shape[1]
+    span = rows - 2 * pipes
+    column = lax.axis_index("pipe")
+    ends = [r_ref[group, span:rows, :].astype(jnp.float32) for group in range(groups)]
+    for step in range(pipes):
+        at = pl.ds(lax.bitwise_xor(column, step), groups, stride=pipes)
+        for side, ref in enumerate((first_ref, last_ref)):
+            row = 2 * step + side
+            put(ref, at, jnp.concatenate([part[row : row + 1] for part in ends], axis=0))
+    picked_in, picked_out = selection(inlet_ref, outlet_ref, pipes)
+    sums = dot(picked_in, whole(first_ref)) + dot(picked_out, whole(last_ref))
+    act = dot(sums.astype(jnp.bfloat16), junc_weight_ref[...]) + junc_bias_ref[...]
+    sigmoid_part = jax.nn.sigmoid(act)
+    junc_rows = (act * sigmoid_part).astype(jnp.bfloat16).astype(jnp.float32)
+    cond_ref[...] = COUPLING * (junc_rows[0:1] + junc_rows[1:2])
+    slope_ref[...] = sigmoid_part * (1.0 + act * (1.0 - sigmoid_part))
+    mix_rows(False, r_ref, real_ref, imag_ref, out_ref, x_ref, y_ref)
+
+
+def mix_grad_kernel(
+    r_ref, real_ref, imag_ref, early_ref, out_ref, copied_ref, sem, x_ref, y_ref
+):
+    copy = pltpu.make_async_copy(early_ref, copied_ref, sem)
+    copy.start()
+    mix_rows(True, r_ref, real_ref, imag_ref, out_ref, x_ref, y_ref)
+    copy.wait()
 
 
 def own_pipe(pipes):
@@ -137,14 +186,6 @@
     return take(ref, pl.ds(0, ref.shape[1])).astype(jnp.bfloat16)
 
 
-def ends_kernel(r_ref, ends_ref):
-    groups, rows = r_ref.shape[0], r_ref.shape[1]
-    for group in range(groups):
-        ends = r_ref[group, rows - 2 : rows, :].astype(jnp.float32)
-        ends_ref[group : group + 1, :] = ends[0:1]
-        ends_ref[groups + group : groups + group + 1, :] = ends[1:2]
-
-
 def started(copies):
     for copy in copies:
         copy.start()
@@ -165,28 +206,27 @@
     )
 
 
-def layer_kernel(pipes, *refs):
-    ends, refs = refs[:pipes], refs[pipes:]
-    (inlet_ref, outlet_ref, junc_weight_ref, junc_bias_ref), refs = refs[:4], refs[4:]
-    x_ref, cot_ref, f_ref, ft_ref, weight_ref, bias_ref, modes_ref = refs[:7]
-    out_ref, total_ref, msg_ref, slope_ref, low_ref, high_ref, first_ref, last_ref = refs[7:]
+def layer_kernel(
+    x_ref,
+    cot_ref,
+    f_ref,
+    ft_ref,
+    weight_ref,
+    bias_ref,
+    cond_ref,
+    modes_ref,
+    out_ref,
+    total_ref,
+    msg_ref,
+    low_ref,
+    high_ref,
+):
     steps, all_rows, tile = f_ref.shape
     half = steps * tile
     channels = x_ref.shape[1]
     groups, rows = msg_ref.shape[0], msg_ref.shape[1]
     span = all_rows // groups
-    column = lax.axis_index("pipe")
-    for step in range(pipes):
-        at = pl.ds(lax.bitwise_xor(column, step), groups, stride=pipes)
-        put(first_ref, at, ends[step][0:groups, :])
-        put(last_ref, at, ends[step][groups : 2 * groups, :])
-    picked_in, picked_out = selection(inlet_ref, outlet_ref, pipes)
-    sums = dot(picked_in, whole(first_ref)) + dot(picked_out, whole(last_ref))
-    act = dot(sums.astype(jnp.bfloat16), junc_weight_ref[...]) + junc_bias_ref[...]
-    sigmoid_part = jax.nn.sigmoid(act)
-    junc_rows = (act * sigmoid_part).astype(jnp.bfloat16).astype(jnp.float32)
-    cond = COUPLING * (junc_rows[0:1] + junc_rows[1:2])
-    slope_ref[...] = sigmoid_part * (1.0 + act * (1.0 - sigmoid_part))
+    cond = cond_ref[...]
     row = lax.broadcasted_iota(jnp.int32, (all_rows, channels), 0)
     doubled = jnp.where((row == 0) | (row == span // 2), 1.0, 2.0).astype(jnp.float32)
     signs = row_signs(all_rows, span, channels)
@@ -232,7 +272,7 @@
     (inlet_ref, outlet_ref, junc_weight_ref, slope_ref), refs = refs[:4], refs[4:]
     real_out, imag_out, rows_ref, x_ref, g_ref, real_ref, imag_ref = refs[:7]
     first_ref, last_ref, upper_ref, lower_ref, sems = refs[7:]
-    groups, rows = fields[0].shape[0], fields[0].shape[1]
+    groups, rows = grads[0].shape[0], grads[0].shape[1]
     span = 2 * modes
     for step in range(pipes):
         for source in range(groups):
@@ -278,8 +318,8 @@
 
 
 def pack_kernel(first_ref, second_ref, out_ref):
-    groups = first_ref.shape[0]
-    out_ref[0:groups] = first_ref[...]
+    groups, rows = second_ref.shape[0], second_ref.shape[1]
+    out_ref[0:groups] = first_ref[:, 0:rows, :]
     out_ref[groups : 2 * groups] = second_ref[...]
 
 
@@ -385,53 +425,42 @@
     def swap(value, step):
         return lax.ppermute(value, "pipe", [(i, i ^ step) for i in range(pipes)])
 
-    def mix(backward, value, *early):
-        return call(
-            functools.partial(mix_kernel, backward),
-            [chunks, early[0]] if backward else [chunks],
-            [VMEM] * (4 if backward else 3),
-            ([dma] if backward else []) + [rows_of(all_rows, channels)] * 2,
-            out_specs=[VMEM, HBM] if backward else [VMEM],
-            name="mix_grad" if backward else "mix",
-            busy=12,
-        )(value, spec_real, spec_imag, *early)
-
-    (sent,) = call(spectrum_kernel, [message], [VMEM] * 2, name="spectrum", busy=12)(
-        field, f_table
-    )
-    received = exchange(sent)
-    (ends,) = call(
-        ends_kernel, [shape((2 * groups, channels), f32)], [VMEM], name="pipe_ends"
-    )(received)
-    ends = [ends] + [swap(ends, step) for step in range(1, pipes)]
-    (mixed,) = mix(False, received)
-    mixed, *ends = lax.optimization_barrier((mixed, *ends))
-    returned = exchange(mixed)
-    spectra = received
+    mix_bufs = [rows_of(all_rows, channels)] * 2
     pipe_rows = [rows_of(pipes * groups, channels)] * 2
     inlet_row = inlet_ids.reshape(1, -1)
     outlet_row = outlet_ids.reshape(1, -1)
-    early, total, sent, slope = call(
-        functools.partial(layer_kernel, pipes),
-        [shape(field.shape, bf16)] * 2 + [message, shape((8, channels), f32)],
-        [VMEM] * (pipes + 11),
-        [pltpu.VMEM((all_rows, channels), f32)] * 2 + pipe_rows,
+    (ends,) = call(
+        ends_kernel, [shape((8, channels), f32)], [VMEM], name="pipe_ends", busy=4
+    )(field)
+    ends = [ends] + [swap(ends, step) for step in range(1, pipes)]
+    (spectra,) = call(spectrum_kernel, [chunks], [VMEM] * 2, name="spectrum", busy=12)(
+        field, f_table
+    )
+    (sent,) = call(
+        functools.partial(message_kernel, pipes),
+        [shape((groups, span + 2 * pipes, channels), bf16)],
+        [VMEM] * (1 + pipes),
+        name="message",
+    )(spectra, *ends)
+    received = exchange(sent)
+    mixed, cond, slope = call(
+        functools.partial(mix_kernel, pipes),
+        [chunks, shape((1, channels), f32), shape((8, channels), f32)],
+        [VMEM] * 7,
+        mix_bufs + pipe_rows,
+        name="mix",
+        busy=12,
+    )(received, spec_real, spec_imag, inlet_row, outlet_row, junc_weight, junc_bias_row)
+    returned = exchange(mixed)
+    spectra = received
+    early, total, sent = call(
+        layer_kernel,
+        [shape(field.shape, bf16)] * 2 + [message],
+        [VMEM] * 8,
+        [pltpu.VMEM((all_rows, channels), f32)] * 2,
         name="layer",
         busy=12,
-    )(
-        *ends,
-        inlet_row,
-        outlet_row,
-        junc_weight,
-        junc_bias_row,
-        field,
-        cot,
-        f_table,
-        ft_table,
-        point_weight,
-        bias_row,
-        returned,
-    )
+    )(field, cot, f_table, ft_table, point_weight, bias_row, cond, returned)
     received = exchange(sent)
     received, spectra = lax.optimization_barrier((received, spectra))
     (both,) = call(
@@ -440,7 +469,15 @@
         [VMEM] * 2,
         name="pack",
     )(spectra, received)
-    mixed, outputs = mix(True, received, early)
+    mixed, outputs = call(
+        mix_grad_kernel,
+        [chunks, early],
+        [VMEM] * 4,
+        [dma] + mix_bufs,
+        out_specs=[VMEM, HBM],
+        name="mix_grad",
+        busy=12,
+    )(received, spec_real, spec_imag, early)
     both, behind = lax.optimization_barrier((swap(both, 2), mixed))
     across = call(split_kernel, [message] * 2, [VMEM], name="split")(both)
     spectra, received, _ = lax.optimization_barrier((spectra, received, behind))

time: 62.1 us -> 60.6 us (0.976)
  blocking collectives: 35.5 us -> 32.9 us
  starting transfers between devices: 7.28 us -> 8.35 us
  local copies, waits for them, and re-layouts: 2.33 us -> 1.29 us
  waiting for transfers between devices: 3.61 us -> 4.62 us
    all_to_all x3, blocking collectives: 35.5 us -> 32.9 us  [exchange(): return lax.all_to_all(value, 'len', split_axis=0, concat_axis=0, tiled=True)]
    ppermute x8, starting transfers between devices: 3.89 us -> 4.97 us  [swap(): return lax.ppermute(value, 'pipe', [(i, i ^ step) for i in range(pipes)])]
    unnamed x26, local copies, waits for them, and re-layouts: 2.33 us -> 1.29 us
    pallas_call x5 -> x6, Pallas kernels: 6.62 us -> 6.7 us  [the longest x1 3.33 us: body(): call(layer_kernel, [shape(field.shape, bf16)] * 2 + [message], [VMEM] * 8...]
  transfers between devices with their start and end apart: 9 -> 9, of which waited for: 5 -> 6; matrix products, arithmetic and copies ran while one was open for 0% -> 0% of each run, Pallas kernels for 11% -> 11%
where the time goes in v13:
time: 60.6 us; the launch traced here: 60.2 us
  blocking collectives  32.9 us (54%)
  Pallas kernels  12.2 us (20%)
  starting transfers between devices  8.35 us (14%)
  waiting for transfers between devices  4.62 us (8%)
  local copies, waits for them, and re-layouts  1.29 us (2%)
  between operations  0.85 us (1%)
    all_to_all x3, blocking collectives, exchange(): return lax.all_to_all(value, 'len', split_axis=0, concat_axis=0, tiled=True)  32.9 us
    ppermute x8, starting transfers between devices, swap(): return lax.ppermute(value, 'pipe', [(i, i ^ step) for i in range(pipes)])  4.97 us
    ppermute x8, waiting for transfers between devices, swap(): return lax.ppermute(value, 'pipe', [(i, i ^ step) for i in range(pipes)])  4.16 us
    pallas_call x1, Pallas kernels, body(): call(functools.partial(weight_grad_kernel, pipes, modes, per_copy), [big,...  3.99 us
    all_to_all x1, starting transfers between devices, exchange(): return lax.all_to_all(value, 'len', split_axis=0, concat_axis=0, tiled=True)  3.38 us
    pallas_call x1, Pallas kernels, body(): call(layer_kernel, [shape(field.shape, bf16)] * 2 + [message], [VMEM] * 8...  3.33 us
    pallas_call x1, Pallas kernels, body(): call(mix_grad_kernel, [chunks, early], [VMEM] * 4, [dma] + mix_bufs, out_...  1.93 us
    pallas_call x1, Pallas kernels, body(): call(input_grad_kernel, [shape(field.shape, bf16)], [VMEM] * 5, [pltpu.VM...  1.46 us
  transfers between devices with their start and end apart: 9, of which 6 were waited for; matrix products, arithmetic and copies ran while one was open for 0% of the time, Pallas kernels for 11%

profile of v13, /device:TPU:0, one launch (start us, length us, event | category | flops | bytes accessed | tf_op | source)
XLA Modules:
  0.0 60.2 jit_solution(564316469762829956)
XLA Ops:
  0.6 0.0 copy-start.7
  0.6 1.2 %copy-done.7 = bf16[1,2048,256]{2,1,0:T(8,128)(2,1)S(1)} copy-done((bf16[1,2048,256]{2,1,0:T(8,128)(2,1)S(1)}, bf16[1,2048,256]{2,1,0:T(8,128)(2,1)}, u32[]{:S(2)}) %copy-start.7) | copy-done | bytes 1048600
  1.9 0.0 copy-start.3
  1.9 0.0 copy-start.4
  1.9 0.0 copy-start.5
  1.9 2.4 %collective-permute-start.2 = (f32[8,256]{1,0:T(8,128)S(1)}, f32[8,256]{1,0:T(8,128)S(1)}, u32[]{:S(2)}, u32[]{:S(2)}) collective-permute-start(f32[8,256]{1,0:T(8,128)S(1)} %pipe_ends.1.refs_0_), channel_id=1, source_target_pairs={{0,3},{1,2},{2,1},{3,0},{4,7},{5,6},{6,5},{7,4},{8,11},{9,10},{10,... | collective-permute-start | bytes 24584 | tf_op jit(solution)/shard_map/ppermute | solution.py:426
  4.4 0.6 %collective-permute-start.1 = (f32[8,256]{1,0:T(8,128)S(1)}, f32[8,256]{1,0:T(8,128)S(1)}, u32[]{:S(2)}, u32[]{:S(2)}) collective-permute-start(f32[8,256]{1,0:T(8,128)S(1)} %pipe_ends.1.refs_0_), channel_id=1, source_target_pairs={{0,2},{1,3},{2,0},{3,1},{4,6},{5,7},{6,4},{7,5},{8,10},{9,11},{10,... | collective-permute-start | bytes 24584 | tf_op jit(solution)/shard_map/ppermute | solution.py:426
  5.0 0.0 collective-permute-start
  5.1 0.4 spectrum.1.spectra_ref
  5.5 0.2 collective-permute-done.2.refs_3_
  5.7 2.3 %collective-permute-done.1.refs_2_ = f32[8,256]{1,0:T(8,128)S(1)} collective-permute-done((f32[8,256]{1,0:T(8,128)S(1)}, f32[8,256]{1,0:T(8,128)S(1)}, u32[]{:S(2)}, u32[]{:S(2)}) %collective-permute-start.1) | collective-permute-done | bytes 8224 | tf_op jit(solution)/shard_map/ppermute | solution.py:426
  8.0 13.2 %all_to_all.20.r_ref.first_ref.refs_0_ = bf16[8,40,256]{2,1,0:T(8,128)(2,1)S(1)} all-to-all(bf16[8,40,256]{2,1,0:T(8,128)(2,1)S(1)} %message.1), channel_id=1, replica_groups=mesh['len'=8,'pipe'=4] {'len'}, dimensions={0} | all-to-all | bytes 327680 | tf_op jit(solution)/shard_map/all_to_all | solution.py:423
  21.3 0.0 copy-start
  21.3 0.0 copy-start.2
  21.3 0.0 copy-start.11
  21.3 1.0 %mix.1 = (bf16[8,32,256]{2,1,0:T(8,128)(2,1)S(1)}, f32[1,256]{1,0:T(1,128)S(1)}, f32[8,256]{1,0:T(8,128)S(1)}) custom-call(bf16[8,40,256]{2,1,0:T(8,128)(2,1)S(1)} %all_to_all.20.r_ref.first_ref.refs_0_, bf16[16,256,256]{2,1,0:T(8,128)(2,1)S(1)} %copy-done.5, bf16[16,256,256]{2,1,0:T(8,128)(2,1)S(1)} %copy-done.6, s32[1,32]{1,0:T(1,128)S(1)} %bitcast.8, ...), custom_call_target="tpu_custom_call" | custom-call | flops 12000000000 | bytes 12582912 | tf_op jit(solution)/shard_map/mix/pallas_call | solution.py:446
  22.3 9.7 %all_to_all.21.modes_ref = bf16[8,32,256]{2,1,0:T(8,128)(2,1)S(1)} all-to-all(bf16[8,32,256]{2,1,0:T(8,128)(2,1)S(1)} %get-tuple-element.23), channel_id=1, replica_groups=mesh['len'=8,'pipe'=4] {'len'}, dimensions={0} | all-to-all | bytes 262144 | tf_op jit(solution)/shard_map/all_to_all | solution.py:423
  32.1 3.3 %layer.1 = (bf16[2048,256]{1,0:T(8,128)(2,1)S(1)}, bf16[2048,256]{1,0:T(8,128)(2,1)S(1)}, bf16[8,34,256]{2,1,0:T(8,128)(2,1)S(1)}) custom-call(bf16[2048,256]{1,0:T(8,128)(2,1)S(1)} %bitcast.14, bf16[2048,256]{1,0:T(8,128)(2,1)S(1)} %bitcast.15, bf16[4,256,256]{2,1,0:T(8,128)(2,1)S(1)} %copy-done.12, bf16[1024,256]{1,0:T(8,128)(2,1)S(1)} %copy-done, ...), custom_call_target="tpu_custom_call" | custom-call | flops 12000000000 | bytes 12582912 | tf_op jit(solution)/shard_map/layer/pallas_call | solution.py:456
  35.4 10.0 %all_to_all.22.r_ref.second_ref.refs_4_ = bf16[8,34,256]{2,1,0:T(8,128)(2,1)S(1)} all-to-all(bf16[8,34,256]{2,1,0:T(8,128)(2,1)S(1)} %get-tuple-element.24), channel_id=1, replica_groups=mesh['len'=8,'pipe'=4] {'len'}, dimensions={0} | all-to-all | bytes 278528 | tf_op jit(solution)/shard_map/all_to_all | solution.py:423
  45.4 0.7 %collective-permute-start.4 = (bf16[16,34,256]{2,1,0:T(8,128)(2,1)S(1)}, bf16[16,34,256]{2,1,0:T(8,128)(2,1)S(1)}, u32[]{:S(2)}, u32[]{:S(2)}) collective-permute-start(bf16[16,34,256]{2,1,0:T(8,128)(2,1)S(1)} %pack.1), channel_id=1, source_target_pairs={{0,2},{1,3},{2,0},{3,1},{4,6},{5,7},{6,4},{7,5},{8,10},{9,11},{10,... | collective-permute-start | bytes 835592 | tf_op jit(solution)/shard_map/ppermute | solution.py:426
  46.1 1.9 %mix_grad.1 = (bf16[8,32,256]{2,1,0:T(8,128)(2,1)}, bf16[2048,256]{1,0:T(8,128)(2,1)}) custom-call(bf16[8,34,256]{2,1,0:T(8,128)(2,1)S(1)} %all_to_all.22.r_ref.second_ref.refs_4_, bf16[16,256,256]{2,1,0:T(8,128)(2,1)S(1)} %copy-done.5, bf16[16,256,256]{2,1,0:T(8,128)(2,1)S(1)} %copy-done.6, bf16[2048,256]{1,0:T(8,128)(2,1)S(1)} %get-tuple-element.26.early_ref), custom_call_target="tpu_custom_call" | custom-call | flops 12000000000 | bytes 12582912 | tf_op jit(solution)/shard_map/mix_grad/pallas_call | solution.py:472
  48.1 3.4 %all-to-all-start.3 = ((bf16[8,32,256]{2,1,0:T(8,128)(2,1)}), bf16[8,32,256]{2,1,0:T(8,128)(2,1)S(1)}, u32[]{:S(2)}, u32[]{:S(2)}) async-start(bf16[8,32,256]{2,1,0:T(8,128)(2,1)} %get-tuple-element.31), calls=%async_computation.3 | async-start | bytes 262144 | tf_op jit(solution)/shard_map/all_to_all | solution.py:423
  51.5 0.1 collective-permute-start.3
  51.5 0.5 collective-permute-start.6
  52.0 0.5 collective-permute-done.4.both_ref
  52.6 0.1 collective-permute-start.5
  52.7 0.5 collective-permute-start.7
  53.2 0.9 %collective-permute-done.5.refs_3_ = bf16[8,34,256]{2,1,0:T(8,128)(2,1)S(1)} collective-permute-done((bf16[8,34,256]{2,1,0:T(8,128)(2,1)S(1)}, bf16[8,34,256]{2,1,0:T(8,128)(2,1)S(1)}, u32[]{:S(2)}, u32[]{:S(2)}) %collective-permute-start.5) | collective-permute-done | bytes 139296 | tf_op jit(solution)/shard_map/ppermute | solution.py:426
  54.0 0.2 collective-permute-done.7.refs_7_
  54.3 4.0 %weight_grad.1 = (f32[16,256,256]{2,1,0:T(8,128)}, f32[16,256,256]{2,1,0:T(8,128)}, f32[8,256]{1,0:T(8,128)S(1)}) custom-call(bf16[8,40,256]{2,1,0:T(8,128)(2,1)S(1)} %all_to_all.20.r_ref.first_ref.refs_0_, bf16[8,40,256]{2,1,0:T(8,128)(2,1)S(1)} %collective-permute-done.3.refs_1_, bf16[8,34,256]{2,1,0:T(8,128)(2,1)S(1)} %get-tuple-element.33.refs_2_, ...), custom_call_target="tpu_custom_call" | custom-call | tf_op jit(solution)/shard_map/weight_grad/pallas_call | solution.py:489
  58.3 0.5 all-to-all-done.3.modes_ref
  58.7 1.5 %input_grad.1 = bf16[2048,256]{1,0:T(8,128)(2,1)} custom-call(bf16[2048,256]{1,0:T(8,128)(2,1)S(1)} %get-tuple-element.28.total_ref, bf16[1024,256]{1,0:T(8,128)(2,1)S(1)} %copy-done, bf16[256,256]{1,0:T(8,128)(2,1)S(1)} %copy-done.2, f32[8,256]{1,0:T(8,128)S(1)} %get-tuple-element.37.rows_ref, bf16[8,32,256]{2,1,0:T(8,128)(2,1)S(1)} %all-to-all-done.3.modes_ref), custom_call_target="tpu_custom_call" | custom-call | tf_op jit(solution)/shard_map/input_grad/pallas_call | solution.py:502
  (25 shorter events, 0.1 us)
Async XLA Ops:
  0.6 1.2 %copy-start.7 = (bf16[1,2048,256]{2,1,0:T(8,128)(2,1)S(1)}, bf16[1,2048,256]{2,1,0:T(8,128)(2,1)}, u32[]{:S(2)}) copy-start(bf16[1,2048,256]{2,1,0:T(8,128)(2,1)} %param.12) | copy-start | bytes 3145732
  1.9 3.2 %copy-start.12 = (bf16[4,256,256]{2,1,0:T(8,128)(2,1)S(1)}, bf16[4,256,256]{2,1,0:T(8,128)(2,1)}, u32[]{:S(2)}) copy-start(bf16[4,256,256]{2,1,0:T(8,128)(2,1)} %constant.4.clone.f_ref) | copy-start | bytes 1572868
  1.9 19.4 %copy-start.1 = (bf16[256,256]{1,0:T(8,128)(2,1)S(1)}, bf16[256,256]{1,0:T(8,128)(2,1)}, u32[]{:S(2)}) copy-start(bf16[256,256]{1,0:T(8,128)(2,1)} %refs_10_.1) | copy-start | bytes 393220
  1.9 19.4 %copy-start.3 = (s32[32]{0:T(128)S(1)}, s32[32]{0:T(128)}, u32[]{:S(2)}) copy-start(s32[32]{0:T(128)} %param.20) | copy-start | bytes 388
  1.9 19.4 %copy-start.4 = (s32[32]{0:T(128)S(1)}, s32[32]{0:T(128)}, u32[]{:S(2)}) copy-start(s32[32]{0:T(128)} %param.21) | copy-start | bytes 388
  1.9 19.4 %copy-start.5 = (bf16[16,256,256]{2,1,0:T(8,128)(2,1)S(1)}, bf16[16,256,256]{2,1,0:T(8,128)(2,1)}, u32[]{:S(2)}) copy-start(bf16[16,256,256]{2,1,0:T(8,128)(2,1)} %real_ref.3) | copy-start | bytes 6291460
  1.9 19.4 %copy-start.6 = (bf16[16,256,256]{2,1,0:T(8,128)(2,1)S(1)}, bf16[16,256,256]{2,1,0:T(8,128)(2,1)}, u32[]{:S(2)}) copy-start(bf16[16,256,256]{2,1,0:T(8,128)(2,1)} %imag_ref.3) | copy-start | bytes 6291460
  1.9 19.4 %copy-start.10 = (f32[256]{0:T(256)S(1)}, f32[256]{0:T(256)}, u32[]{:S(2)}) copy-start(f32[256]{0:T(256)} %param.19) | copy-start | bytes 3076
  1.9 3.8 %collective-permute-start.2 = (f32[8,256]{1,0:T(8,128)S(1)}, f32[8,256]{1,0:T(8,128)S(1)}, u32[]{:S(2)}, u32[]{:S(2)}) collective-permute-start(f32[8,256]{1,0:T(8,128)S(1)} %pipe_ends.1.refs_0_), channel_id=1, source_target_pairs={{0,3},{1,2},{2,1},{3,0},{4,7},{5,6},{6,5},{7,4},{8,11},{9,10},{10,... | collective-permute-start | bytes 24584 | tf_op jit(solution)/shard_map/ppermute | solution.py:426
  4.4 3.7 %collective-permute-start.1 = (f32[8,256]{1,0:T(8,128)S(1)}, f32[8,256]{1,0:T(8,128)S(1)}, u32[]{:S(2)}, u32[]{:S(2)}) collective-permute-start(f32[8,256]{1,0:T(8,128)S(1)} %pipe_ends.1.refs_0_), channel_id=1, source_target_pairs={{0,2},{1,3},{2,0},{3,1},{4,6},{5,7},{6,4},{7,5},{8,10},{9,11},{10,... | collective-permute-start | bytes 24584 | tf_op jit(solution)/shard_map/ppermute | solution.py:426
  5.0 3.0 %collective-permute-start = (f32[8,256]{1,0:T(8,128)S(1)}, f32[8,256]{1,0:T(8,128)S(1)}, u32[]{:S(2)}, u32[]{:S(2)}) collective-permute-start(f32[8,256]{1,0:T(8,128)S(1)} %pipe_ends.1.refs_0_), channel_id=1, source_target_pairs={{0,1},{1,0},{2,3},{3,2},{4,5},{5,4},{6,7},{7,6},{8,9},{9,8},{10,11... | collective-permute-start | bytes 24584 | tf_op jit(solution)/shard_map/ppermute | solution.py:426
  21.3 10.8 %copy-start = (bf16[1024,256]{1,0:T(8,128)(2,1)S(1)}, bf16[1024,256]{1,0:T(8,128)(2,1)}, u32[]{:S(2)}) copy-start(bf16[1024,256]{1,0:T(8,128)(2,1)} %constant.5.clone.ft_ref) | copy-start | bytes 1572868
  21.3 10.8 %copy-start.2 = (bf16[256,256]{1,0:T(8,128)(2,1)S(1)}, bf16[256,256]{1,0:T(8,128)(2,1)}, u32[]{:S(2)}) copy-start(bf16[256,256]{1,0:T(8,128)(2,1)} %weight_ref.3) | copy-start | bytes 393220
  21.3 10.8 %copy-start.8 = (bf16[1,2048,256]{2,1,0:T(8,128)(2,1)S(1)}, bf16[1,2048,256]{2,1,0:T(8,128)(2,1)}, u32[]{:S(2)}) copy-start(bf16[1,2048,256]{2,1,0:T(8,128)(2,1)} %param.12) | copy-start | bytes 3145732
  21.3 10.8 %copy-start.9 = (bf16[1,2048,256]{2,1,0:T(8,128)(2,1)S(1)}, bf16[1,2048,256]{2,1,0:T(8,128)(2,1)}, u32[]{:S(2)}) copy-start(bf16[1,2048,256]{2,1,0:T(8,128)(2,1)} %param.13) | copy-start | bytes 3145732
  21.3 10.8 %copy-start.11 = (f32[256]{0:T(256)S(1)}, f32[256]{0:T(256)}, u32[]{:S(2)}) copy-start(f32[256]{0:T(256)} %param.15) | copy-start | bytes 3076
  45.4 7.1 %collective-permute-start.4 = (bf16[16,34,256]{2,1,0:T(8,128)(2,1)S(1)}, bf16[16,34,256]{2,1,0:T(8,128)(2,1)S(1)}, u32[]{:S(2)}, u32[]{:S(2)}) collective-permute-start(bf16[16,34,256]{2,1,0:T(8,128)(2,1)S(1)} %pack.1), channel_id=1, source_target_pairs={{0,2},{1,3},{2,0},{3,1},{4,6},{5,7},{6,4},{7,5},{8,10},{9,11},{10,... | collective-permute-start | bytes 835592 | tf_op jit(solution)/shard_map/ppermute | solution.py:426
  48.1 10.7 %all-to-all-start.3 = ((bf16[8,32,256]{2,1,0:T(8,128)(2,1)}), bf16[8,32,256]{2,1,0:T(8,128)(2,1)S(1)}, u32[]{:S(2)}, u32[]{:S(2)}) async-start(bf16[8,32,256]{2,1,0:T(8,128)(2,1)} %get-tuple-element.31), calls=%async_computation.3 | async-start | bytes 262144 | tf_op jit(solution)/shard_map/all_to_all | solution.py:423
  51.5 1.7 %collective-permute-start.3 = (bf16[8,40,256]{2,1,0:T(8,128)(2,1)S(1)}, bf16[8,40,256]{2,1,0:T(8,128)(2,1)S(1)}, u32[]{:S(2)}, u32[]{:S(2)}) collective-permute-start(bf16[8,40,256]{2,1,0:T(8,128)(2,1)S(1)} %all_to_all.20.r_ref.first_ref.refs_0_), channel_id=1, source_target_pairs={{0,1},{1,0},{2,3},{3,2},{4,5},{5,4},{6,7},{7,6},{8,9},{9,8},{10,11... | collective-permute-start | bytes 491528 | tf_op jit(solution)/shard_map/ppermute | solution.py:426
  51.5 1.6 %collective-permute-start.6 = (bf16[8,34,256]{2,1,0:T(8,128)(2,1)S(1)}, bf16[8,34,256]{2,1,0:T(8,128)(2,1)S(1)}, u32[]{:S(2)}, u32[]{:S(2)}) collective-permute-start(bf16[8,34,256]{2,1,0:T(8,128)(2,1)S(1)} %all_to_all.22.r_ref.second_ref.refs_4_), channel_id=1, source_target_pairs={{0,1},{1,0},{2,3},{3,2},{4,5},{5,4},{6,7},{7,6},{8,9},{9,8},{10,11... | collective-permute-start | bytes 417800 | tf_op jit(solution)/shard_map/ppermute | solution.py:426
  52.6 1.5 %collective-permute-start.5 = (bf16[8,34,256]{2,1,0:T(8,128)(2,1)S(1)}, bf16[8,34,256]{2,1,0:T(8,128)(2,1)S(1)}, u32[]{:S(2)}, u32[]{:S(2)}) collective-permute-start(bf16[8,34,256]{2,1,0:T(8,128)(2,1)S(1)} %get-tuple-element.33.refs_2_), channel_id=1, source_target_pairs={{0,1},{1,0},{2,3},{3,2},{4,5},{5,4},{6,7},{7,6},{8,9},{9,8},{10,11... | collective-permute-start | bytes 417800 | tf_op jit(solution)/shard_map/ppermute | solution.py:426
  52.7 1.6 %collective-permute-start.7 = (bf16[8,34,256]{2,1,0:T(8,128)(2,1)S(1)}, bf16[8,34,256]{2,1,0:T(8,128)(2,1)S(1)}, u32[]{:S(2)}, u32[]{:S(2)}) collective-permute-start(bf16[8,34,256]{2,1,0:T(8,128)(2,1)S(1)} %get-tuple-element.35.refs_6_), channel_id=1, source_target_pairs={{0,1},{1,0},{2,3},{3,2},{4,5},{5,4},{6,7},{7,6},{8,9},{9,8},{10,11... | collective-permute-start | bytes 417800 | tf_op jit(solution)/shard_map/ppermute | solution.py:426

commit v14 on v13

--- a/solution.py
+++ b/solution.py
@@ -237,8 +237,8 @@
     modes = (modes.astype(jnp.bfloat16), (modes * signs).astype(jnp.bfloat16))
     weight = weight_ref[...]
     bias = bias_ref[...]
-    for step in range(steps):
-        for side, acc_ref in enumerate((low_ref, high_ref)):
+    for side, acc_ref in enumerate((low_ref, high_ref)):
+        for step in range(steps):
             at = pl.ds(side * half + step * tile, tile)
             pointwise = dot(x_ref[at, :], weight) + bias
             spectral = dot(ft_ref[pl.ds(step * tile, tile), :], modes[side])
@@ -343,8 +343,8 @@
     weight = weight_ref[...]
     row = lax.broadcasted_iota(jnp.int32, (tile, channels), 0)
     going = []
-    for step in range(steps):
-        for side in range(2):
+    for side in range(2):
+        for step in range(steps):
             at = pl.ds(side * half + step * tile, tile)
             grad_cells = dot(ft_ref[pl.ds(step * tile, tile), :], back[side])
             if step == 0 and side == 0:

time: 60.6 us -> 59.8 us (0.987)
  Pallas kernels: 12.2 us -> 11.5 us
    pallas_call x1, Pallas kernels: 3.33 us -> 2.6 us  [body(): call(layer_kernel, [shape(field.shape, bf16)] * 2 + [message], [VMEM] * 8...]
where the time goes in v14:
time: 59.8 us; the launch traced here: 59.5 us
  blocking collectives  32.9 us (55%)
  Pallas kernels  11.5 us (19%)
  starting transfers between devices  8.35 us (14%)
  waiting for transfers between devices  4.62 us (8%)
  local copies, waits for them, and re-layouts  1.29 us (2%)
  between operations  0.85 us (1%)
    all_to_all x3, blocking collectives, exchange(): return lax.all_to_all(value, 'len', split_axis=0, concat_axis=0, tiled=True)  32.9 us
    ppermute x8, starting transfers between devices, swap(): return lax.ppermute(value, 'pipe', [(i, i ^ step) for i in range(pipes)])  4.97 us
    ppermute x8, waiting for transfers between devices, swap(): return lax.ppermute(value, 'pipe', [(i, i ^ step) for i in range(pipes)])  4.16 us
    pallas_call x1, Pallas kernels, body(): call(functools.partial(weight_grad_kernel, pipes, modes, per_copy), [big,...  3.99 us
    all_to_all x1, starting transfers between devices, exchange(): return lax.all_to_all(value, 'len', split_axis=0, concat_axis=0, tiled=True)  3.38 us
    pallas_call x1, Pallas kernels, body(): call(layer_kernel, [shape(field.shape, bf16)] * 2 + [message], [VMEM] * 8...  2.6 us
    pallas_call x1, Pallas kernels, body(): call(mix_grad_kernel, [chunks, early], [VMEM] * 4, [dma] + mix_bufs, out_...  1.93 us
    pallas_call x1, Pallas kernels, body(): call(input_grad_kernel, [shape(field.shape, bf16)], [VMEM] * 5, [pltpu.VM...  1.45 us
  transfers between devices with their start and end apart: 9, of which 6 were waited for; matrix products, arithmetic and copies ran while one was open for 0% of the time, Pallas kernels for 11%

profile of v14, /device:TPU:0, one launch (start us, length us, event | category | flops | bytes accessed | tf_op | source)
XLA Modules:
  0.0 59.5 jit_solution(13676877303783894771)
XLA Ops:
  0.6 0.0 copy-start.7
  0.6 1.2 %copy-done.7 = bf16[1,2048,256]{2,1,0:T(8,128)(2,1)S(1)} copy-done((bf16[1,2048,256]{2,1,0:T(8,128)(2,1)S(1)}, bf16[1,2048,256]{2,1,0:T(8,128)(2,1)}, u32[]{:S(2)}) %copy-start.7) | copy-done | bytes 1048600
  1.9 0.0 copy-start.3
  1.9 0.0 copy-start.6
  1.9 0.0 copy-start.10
  1.9 2.4 %collective-permute-start.2 = (f32[8,256]{1,0:T(8,128)S(1)}, f32[8,256]{1,0:T(8,128)S(1)}, u32[]{:S(2)}, u32[]{:S(2)}) collective-permute-start(f32[8,256]{1,0:T(8,128)S(1)} %pipe_ends.1.refs_0_), channel_id=1, source_target_pairs={{0,3},{1,2},{2,1},{3,0},{4,7},{5,6},{6,5},{7,4},{8,11},{9,10},{10,... | collective-permute-start | bytes 24584 | tf_op jit(solution)/shard_map/ppermute | solution.py:426
  4.4 0.6 %collective-permute-start.1 = (f32[8,256]{1,0:T(8,128)S(1)}, f32[8,256]{1,0:T(8,128)S(1)}, u32[]{:S(2)}, u32[]{:S(2)}) collective-permute-start(f32[8,256]{1,0:T(8,128)S(1)} %pipe_ends.1.refs_0_), channel_id=1, source_target_pairs={{0,2},{1,3},{2,0},{3,1},{4,6},{5,7},{6,4},{7,5},{8,10},{9,11},{10,... | collective-permute-start | bytes 24584 | tf_op jit(solution)/shard_map/ppermute | solution.py:426
  5.0 0.0 collective-permute-start
  5.1 0.4 spectrum.1.spectra_ref
  5.5 0.2 collective-permute-done.2.refs_3_
  5.7 2.3 %collective-permute-done.1.refs_2_ = f32[8,256]{1,0:T(8,128)S(1)} collective-permute-done((f32[8,256]{1,0:T(8,128)S(1)}, f32[8,256]{1,0:T(8,128)S(1)}, u32[]{:S(2)}, u32[]{:S(2)}) %collective-permute-start.1) | collective-permute-done | bytes 8224 | tf_op jit(solution)/shard_map/ppermute | solution.py:426
  8.0 13.2 %all_to_all.20.r_ref.first_ref.refs_0_ = bf16[8,40,256]{2,1,0:T(8,128)(2,1)S(1)} all-to-all(bf16[8,40,256]{2,1,0:T(8,128)(2,1)S(1)} %message.1), channel_id=1, replica_groups=mesh['len'=8,'pipe'=4] {'len'}, dimensions={0} | all-to-all | bytes 327680 | tf_op jit(solution)/shard_map/all_to_all | solution.py:423
  21.3 0.0 copy-start
  21.3 0.0 copy-start.8
  21.3 0.0 copy-start.9
  21.3 1.0 %mix.1 = (bf16[8,32,256]{2,1,0:T(8,128)(2,1)S(1)}, f32[1,256]{1,0:T(1,128)S(1)}, f32[8,256]{1,0:T(8,128)S(1)}) custom-call(bf16[8,40,256]{2,1,0:T(8,128)(2,1)S(1)} %all_to_all.20.r_ref.first_ref.refs_0_, bf16[16,256,256]{2,1,0:T(8,128)(2,1)S(1)} %copy-done.5, bf16[16,256,256]{2,1,0:T(8,128)(2,1)S(1)} %copy-done.6, s32[1,32]{1,0:T(1,128)S(1)} %bitcast.8, ...), custom_call_target="tpu_custom_call" | custom-call | flops 12000000000 | bytes 12582912 | tf_op jit(solution)/shard_map/mix/pallas_call | solution.py:446
  22.3 9.7 %all_to_all.21.modes_ref = bf16[8,32,256]{2,1,0:T(8,128)(2,1)S(1)} all-to-all(bf16[8,32,256]{2,1,0:T(8,128)(2,1)S(1)} %get-tuple-element.23), channel_id=1, replica_groups=mesh['len'=8,'pipe'=4] {'len'}, dimensions={0} | all-to-all | bytes 262144 | tf_op jit(solution)/shard_map/all_to_all | solution.py:423
  32.1 2.6 %layer.1 = (bf16[2048,256]{1,0:T(8,128)(2,1)S(1)}, bf16[2048,256]{1,0:T(8,128)(2,1)S(1)}, bf16[8,34,256]{2,1,0:T(8,128)(2,1)S(1)}) custom-call(bf16[2048,256]{1,0:T(8,128)(2,1)S(1)} %bitcast.14, bf16[2048,256]{1,0:T(8,128)(2,1)S(1)} %bitcast.15, bf16[4,256,256]{2,1,0:T(8,128)(2,1)S(1)} %copy-done.12, bf16[1024,256]{1,0:T(8,128)(2,1)S(1)} %copy-done, ...), custom_call_target="tpu_custom_call" | custom-call | flops 12000000000 | bytes 12582912 | tf_op jit(solution)/shard_map/layer/pallas_call | solution.py:456
  34.7 10.0 %all_to_all.22.r_ref.second_ref.refs_4_ = bf16[8,34,256]{2,1,0:T(8,128)(2,1)S(1)} all-to-all(bf16[8,34,256]{2,1,0:T(8,128)(2,1)S(1)} %get-tuple-element.24), channel_id=1, replica_groups=mesh['len'=8,'pipe'=4] {'len'}, dimensions={0} | all-to-all | bytes 278528 | tf_op jit(solution)/shard_map/all_to_all | solution.py:423
  44.7 0.7 %collective-permute-start.4 = (bf16[16,34,256]{2,1,0:T(8,128)(2,1)S(1)}, bf16[16,34,256]{2,1,0:T(8,128)(2,1)S(1)}, u32[]{:S(2)}, u32[]{:S(2)}) collective-permute-start(bf16[16,34,256]{2,1,0:T(8,128)(2,1)S(1)} %pack.1), channel_id=1, source_target_pairs={{0,2},{1,3},{2,0},{3,1},{4,6},{5,7},{6,4},{7,5},{8,10},{9,11},{10,... | collective-permute-start | bytes 835592 | tf_op jit(solution)/shard_map/ppermute | solution.py:426
  45.4 1.9 %mix_grad.1 = (bf16[8,32,256]{2,1,0:T(8,128)(2,1)}, bf16[2048,256]{1,0:T(8,128)(2,1)}) custom-call(bf16[8,34,256]{2,1,0:T(8,128)(2,1)S(1)} %all_to_all.22.r_ref.second_ref.refs_4_, bf16[16,256,256]{2,1,0:T(8,128)(2,1)S(1)} %copy-done.5, bf16[16,256,256]{2,1,0:T(8,128)(2,1)S(1)} %copy-done.6, bf16[2048,256]{1,0:T(8,128)(2,1)S(1)} %get-tuple-element.26.early_ref), custom_call_target="tpu_custom_call" | custom-call | flops 12000000000 | bytes 12582912 | tf_op jit(solution)/shard_map/mix_grad/pallas_call | solution.py:472
  47.3 3.4 %all-to-all-start.3 = ((bf16[8,32,256]{2,1,0:T(8,128)(2,1)}), bf16[8,32,256]{2,1,0:T(8,128)(2,1)S(1)}, u32[]{:S(2)}, u32[]{:S(2)}) async-start(bf16[8,32,256]{2,1,0:T(8,128)(2,1)} %get-tuple-element.31), calls=%async_computation.3 | async-start | bytes 262144 | tf_op jit(solution)/shard_map/all_to_all | solution.py:423
  50.7 0.1 collective-permute-start.3
  50.8 0.5 collective-permute-start.6
  51.3 0.5 collective-permute-done.4.both_ref
  51.9 0.1 collective-permute-start.5
  51.9 0.5 collective-permute-start.7
  52.4 0.9 %collective-permute-done.5.refs_3_ = bf16[8,34,256]{2,1,0:T(8,128)(2,1)S(1)} collective-permute-done((bf16[8,34,256]{2,1,0:T(8,128)(2,1)S(1)}, bf16[8,34,256]{2,1,0:T(8,128)(2,1)S(1)}, u32[]{:S(2)}, u32[]{:S(2)}) %collective-permute-start.5) | collective-permute-done | bytes 139296 | tf_op jit(solution)/shard_map/ppermute | solution.py:426
  53.3 0.2 collective-permute-done.7.refs_7_
  53.6 4.0 %weight_grad.1 = (f32[16,256,256]{2,1,0:T(8,128)}, f32[16,256,256]{2,1,0:T(8,128)}, f32[8,256]{1,0:T(8,128)S(1)}) custom-call(bf16[8,40,256]{2,1,0:T(8,128)(2,1)S(1)} %all_to_all.20.r_ref.first_ref.refs_0_, bf16[8,40,256]{2,1,0:T(8,128)(2,1)S(1)} %collective-permute-done.3.refs_1_, bf16[8,34,256]{2,1,0:T(8,128)(2,1)S(1)} %get-tuple-element.33.refs_2_, ...), custom_call_target="tpu_custom_call" | custom-call | tf_op jit(solution)/shard_map/weight_grad/pallas_call | solution.py:489
  57.6 0.5 all-to-all-done.3.modes_ref
  58.0 1.4 %input_grad.1 = bf16[2048,256]{1,0:T(8,128)(2,1)} custom-call(bf16[2048,256]{1,0:T(8,128)(2,1)S(1)} %get-tuple-element.28.total_ref, bf16[1024,256]{1,0:T(8,128)(2,1)S(1)} %copy-done, bf16[256,256]{1,0:T(8,128)(2,1)S(1)} %copy-done.2, f32[8,256]{1,0:T(8,128)S(1)} %get-tuple-element.37.rows_ref, bf16[8,32,256]{2,1,0:T(8,128)(2,1)S(1)} %all-to-all-done.3.modes_ref), custom_call_target="tpu_custom_call" | custom-call | tf_op jit(solution)/shard_map/input_grad/pallas_call | solution.py:502
  (25 shorter events, 0.1 us)
Async XLA Ops:
  0.6 1.2 %copy-start.7 = (bf16[1,2048,256]{2,1,0:T(8,128)(2,1)S(1)}, bf16[1,2048,256]{2,1,0:T(8,128)(2,1)}, u32[]{:S(2)}) copy-start(bf16[1,2048,256]{2,1,0:T(8,128)(2,1)} %param.12) | copy-start | bytes 3145732
  1.9 3.2 %copy-start.12 = (bf16[4,256,256]{2,1,0:T(8,128)(2,1)S(1)}, bf16[4,256,256]{2,1,0:T(8,128)(2,1)}, u32[]{:S(2)}) copy-start(bf16[4,256,256]{2,1,0:T(8,128)(2,1)} %constant.4.clone.f_ref) | copy-start | bytes 1572868
  1.9 19.4 %copy-start.1 = (bf16[256,256]{1,0:T(8,128)(2,1)S(1)}, bf16[256,256]{1,0:T(8,128)(2,1)}, u32[]{:S(2)}) copy-start(bf16[256,256]{1,0:T(8,128)(2,1)} %refs_10_.1) | copy-start | bytes 393220
  1.9 19.4 %copy-start.3 = (s32[32]{0:T(128)S(1)}, s32[32]{0:T(128)}, u32[]{:S(2)}) copy-start(s32[32]{0:T(128)} %param.20) | copy-start | bytes 388
  1.9 19.4 %copy-start.4 = (s32[32]{0:T(128)S(1)}, s32[32]{0:T(128)}, u32[]{:S(2)}) copy-start(s32[32]{0:T(128)} %param.21) | copy-start | bytes 388
  1.9 19.4 %copy-start.5 = (bf16[16,256,256]{2,1,0:T(8,128)(2,1)S(1)}, bf16[16,256,256]{2,1,0:T(8,128)(2,1)}, u32[]{:S(2)}) copy-start(bf16[16,256,256]{2,1,0:T(8,128)(2,1)} %real_ref.3) | copy-start | bytes 6291460
  1.9 19.4 %copy-start.6 = (bf16[16,256,256]{2,1,0:T(8,128)(2,1)S(1)}, bf16[16,256,256]{2,1,0:T(8,128)(2,1)}, u32[]{:S(2)}) copy-start(bf16[16,256,256]{2,1,0:T(8,128)(2,1)} %imag_ref.3) | copy-start | bytes 6291460
  1.9 19.4 %copy-start.10 = (f32[256]{0:T(256)S(1)}, f32[256]{0:T(256)}, u32[]{:S(2)}) copy-start(f32[256]{0:T(256)} %param.19) | copy-start | bytes 3076
  1.9 3.8 %collective-permute-start.2 = (f32[8,256]{1,0:T(8,128)S(1)}, f32[8,256]{1,0:T(8,128)S(1)}, u32[]{:S(2)}, u32[]{:S(2)}) collective-permute-start(f32[8,256]{1,0:T(8,128)S(1)} %pipe_ends.1.refs_0_), channel_id=1, source_target_pairs={{0,3},{1,2},{2,1},{3,0},{4,7},{5,6},{6,5},{7,4},{8,11},{9,10},{10,... | collective-permute-start | bytes 24584 | tf_op jit(solution)/shard_map/ppermute | solution.py:426
  4.4 3.7 %collective-permute-start.1 = (f32[8,256]{1,0:T(8,128)S(1)}, f32[8,256]{1,0:T(8,128)S(1)}, u32[]{:S(2)}, u32[]{:S(2)}) collective-permute-start(f32[8,256]{1,0:T(8,128)S(1)} %pipe_ends.1.refs_0_), channel_id=1, source_target_pairs={{0,2},{1,3},{2,0},{3,1},{4,6},{5,7},{6,4},{7,5},{8,10},{9,11},{10,... | collective-permute-start | bytes 24584 | tf_op jit(solution)/shard_map/ppermute | solution.py:426
  5.0 3.0 %collective-permute-start = (f32[8,256]{1,0:T(8,128)S(1)}, f32[8,256]{1,0:T(8,128)S(1)}, u32[]{:S(2)}, u32[]{:S(2)}) collective-permute-start(f32[8,256]{1,0:T(8,128)S(1)} %pipe_ends.1.refs_0_), channel_id=1, source_target_pairs={{0,1},{1,0},{2,3},{3,2},{4,5},{5,4},{6,7},{7,6},{8,9},{9,8},{10,11... | collective-permute-start | bytes 24584 | tf_op jit(solution)/shard_map/ppermute | solution.py:426
  21.3 10.8 %copy-start = (bf16[1024,256]{1,0:T(8,128)(2,1)S(1)}, bf16[1024,256]{1,0:T(8,128)(2,1)}, u32[]{:S(2)}) copy-start(bf16[1024,256]{1,0:T(8,128)(2,1)} %constant.5.clone.ft_ref) | copy-start | bytes 1572868
  21.3 10.8 %copy-start.2 = (bf16[256,256]{1,0:T(8,128)(2,1)S(1)}, bf16[256,256]{1,0:T(8,128)(2,1)}, u32[]{:S(2)}) copy-start(bf16[256,256]{1,0:T(8,128)(2,1)} %weight_ref.3) | copy-start | bytes 393220
  21.3 10.8 %copy-start.8 = (bf16[1,2048,256]{2,1,0:T(8,128)(2,1)S(1)}, bf16[1,2048,256]{2,1,0:T(8,128)(2,1)}, u32[]{:S(2)}) copy-start(bf16[1,2048,256]{2,1,0:T(8,128)(2,1)} %param.12) | copy-start | bytes 3145732
  21.3 10.8 %copy-start.9 = (bf16[1,2048,256]{2,1,0:T(8,128)(2,1)S(1)}, bf16[1,2048,256]{2,1,0:T(8,128)(2,1)}, u32[]{:S(2)}) copy-start(bf16[1,2048,256]{2,1,0:T(8,128)(2,1)} %param.13) | copy-start | bytes 3145732
  21.3 10.8 %copy-start.11 = (f32[256]{0:T(256)S(1)}, f32[256]{0:T(256)}, u32[]{:S(2)}) copy-start(f32[256]{0:T(256)} %param.15) | copy-start | bytes 3076
  44.7 7.1 %collective-permute-start.4 = (bf16[16,34,256]{2,1,0:T(8,128)(2,1)S(1)}, bf16[16,34,256]{2,1,0:T(8,128)(2,1)S(1)}, u32[]{:S(2)}, u32[]{:S(2)}) collective-permute-start(bf16[16,34,256]{2,1,0:T(8,128)(2,1)S(1)} %pack.1), channel_id=1, source_target_pairs={{0,2},{1,3},{2,0},{3,1},{4,6},{5,7},{6,4},{7,5},{8,10},{9,11},{10,... | collective-permute-start | bytes 835592 | tf_op jit(solution)/shard_map/ppermute | solution.py:426
  47.3 10.7 %all-to-all-start.3 = ((bf16[8,32,256]{2,1,0:T(8,128)(2,1)}), bf16[8,32,256]{2,1,0:T(8,128)(2,1)S(1)}, u32[]{:S(2)}, u32[]{:S(2)}) async-start(bf16[8,32,256]{2,1,0:T(8,128)(2,1)} %get-tuple-element.31), calls=%async_computation.3 | async-start | bytes 262144 | tf_op jit(solution)/shard_map/all_to_all | solution.py:423
  50.7 1.7 %collective-permute-start.3 = (bf16[8,40,256]{2,1,0:T(8,128)(2,1)S(1)}, bf16[8,40,256]{2,1,0:T(8,128)(2,1)S(1)}, u32[]{:S(2)}, u32[]{:S(2)}) collective-permute-start(bf16[8,40,256]{2,1,0:T(8,128)(2,1)S(1)} %all_to_all.20.r_ref.first_ref.refs_0_), channel_id=1, source_target_pairs={{0,1},{1,0},{2,3},{3,2},{4,5},{5,4},{6,7},{7,6},{8,9},{9,8},{10,11... | collective-permute-start | bytes 491528 | tf_op jit(solution)/shard_map/ppermute | solution.py:426
  50.8 1.6 %collective-permute-start.6 = (bf16[8,34,256]{2,1,0:T(8,128)(2,1)S(1)}, bf16[8,34,256]{2,1,0:T(8,128)(2,1)S(1)}, u32[]{:S(2)}, u32[]{:S(2)}) collective-permute-start(bf16[8,34,256]{2,1,0:T(8,128)(2,1)S(1)} %all_to_all.22.r_ref.second_ref.refs_4_), channel_id=1, source_target_pairs={{0,1},{1,0},{2,3},{3,2},{4,5},{5,4},{6,7},{7,6},{8,9},{9,8},{10,11... | collective-permute-start | bytes 417800 | tf_op jit(solution)/shard_map/ppermute | solution.py:426
  51.9 1.5 %collective-permute-start.5 = (bf16[8,34,256]{2,1,0:T(8,128)(2,1)S(1)}, bf16[8,34,256]{2,1,0:T(8,128)(2,1)S(1)}, u32[]{:S(2)}, u32[]{:S(2)}) collective-permute-start(bf16[8,34,256]{2,1,0:T(8,128)(2,1)S(1)} %get-tuple-element.33.refs_2_), channel_id=1, source_target_pairs={{0,1},{1,0},{2,3},{3,2},{4,5},{5,4},{6,7},{7,6},{8,9},{9,8},{10,11... | collective-permute-start | bytes 417800 | tf_op jit(solution)/shard_map/ppermute | solution.py:426
  51.9 1.6 %collective-permute-start.7 = (bf16[8,34,256]{2,1,0:T(8,128)(2,1)S(1)}, bf16[8,34,256]{2,1,0:T(8,128)(2,1)S(1)}, u32[]{:S(2)}, u32[]{:S(2)}) collective-permute-start(bf16[8,34,256]{2,1,0:T(8,128)(2,1)S(1)} %get-tuple-element.35.refs_6_), channel_id=1, source_target_pairs={{0,1},{1,0},{2,3},{3,2},{4,5},{5,4},{6,7},{7,6},{8,9},{9,8},{10,11... | collective-permute-start | bytes 417800 | tf_op jit(solution)/shard_map/ppermute | solution.py:426

commit v15 on v14

--- a/solution.py
+++ b/solution.py
@@ -13,6 +13,7 @@
 COUPLING = 0.125
 TILE = 256
 LANES = 128
+PIECE = 64
 GELU_S = math.sqrt(2.0 / math.pi)
 GELU_C = 0.044715
 VMEM = pl.BlockSpec(memory_space=pltpu.VMEM)
@@ -56,10 +57,20 @@
     return jnp.concatenate([ref[lane, at, :] for lane in range(ref.shape[0])], axis=1)
 
 
-def ends_kernel(x_ref, ends_ref):
+def ends_kernel(x_ref, ends_ref, edges_ref, sems):
     cells, channels = x_ref.shape
-    ends = [x_ref[0:1, :], x_ref[cells - 1 : cells, :], jnp.zeros((6, channels), x_ref.dtype)]
-    ends_ref[...] = jnp.concatenate([part.astype(jnp.float32) for part in ends], axis=0)
+    rows = edges_ref.shape[1]
+    copies = [
+        pltpu.make_async_copy(x_ref.at[pl.ds(start, rows)], edges_ref.at[side], sems.at[side])
+        for side, start in enumerate((0, cells - rows))
+    ]
+    for copy in copies:
+        copy.start()
+    for copy in copies:
+        copy.wait()
+    ends = [edges_ref[0, 0:1, :], edges_ref[1, rows - 1 : rows, :]]
+    ends = [part.astype(jnp.float32) for part in ends]
+    ends_ref[...] = jnp.concatenate(ends + [jnp.zeros((6, channels), jnp.float32)], axis=0)
 
 
 def spectrum_kernel(x_ref, f_ref, spectra_ref):
@@ -220,6 +231,7 @@
     msg_ref,
     low_ref,
     high_ref,
+    summed_ref,
 ):
     steps, all_rows, tile = f_ref.shape
     half = steps * tile
@@ -239,20 +251,25 @@
     bias = bias_ref[...]
     for side, acc_ref in enumerate((low_ref, high_ref)):
         for step in range(steps):
-            at = pl.ds(side * half + step * tile, tile)
+            base = side * half + step * tile
+            at = pl.ds(base, tile)
             pointwise = dot(x_ref[at, :], weight) + bias
             spectral = dot(ft_ref[pl.ds(step * tile, tile), :], modes[side])
-            summed = pointwise + (spectral + cond).astype(jnp.bfloat16).astype(jnp.float32)
-            square = summed * summed
-            part = 0.5 + 0.5 * jnp.tanh(summed * (GELU_S + (GELU_S * GELU_C) * square))
-            result = summed * part
-            out_ref[at, :] = result.astype(jnp.bfloat16)
-            slope = part + result * (1.0 - part) * (
-                2.0 * GELU_S + (6.0 * GELU_S * GELU_C) * square
-            )
-            total = (cot_ref[at, :].astype(jnp.float32) * slope).astype(jnp.bfloat16)
-            total_ref[at, :] = total
-            term = dot(f_ref[step], total)
+            pre = (spectral + cond).astype(jnp.bfloat16).astype(jnp.float32)
+            summed_ref[at, :] = pointwise + pre
+            for piece in range(tile // PIECE):
+                here = pl.ds(base + piece * PIECE, PIECE)
+                summed = summed_ref[here, :]
+                square = summed * summed
+                part = 0.5 + 0.5 * jnp.tanh(summed * (GELU_S + (GELU_S * GELU_C) * square))
+                result = summed * part
+                out_ref[here, :] = result.astype(jnp.bfloat16)
+                slope = part + result * (1.0 - part) * (
+                    2.0 * GELU_S + (6.0 * GELU_S * GELU_C) * square
+                )
+                total = cot_ref[here, :].astype(jnp.float32) * slope
+                total_ref[here, :] = total.astype(jnp.bfloat16)
+            term = dot(f_ref[step], total_ref[at, :])
             if step == 0:
                 acc_ref[...] = term
             else:
@@ -430,7 +447,13 @@
     inlet_row = inlet_ids.reshape(1, -1)
     outlet_row = outlet_ids.reshape(1, -1)
     (ends,) = call(
-        ends_kernel, [shape((8, channels), f32)], [VMEM], name="pipe_ends", busy=4
+        ends_kernel,
+        [shape((8, channels), f32)],
+        [HBM],
+        [pltpu.VMEM((2, 16, channels), bf16), dma((2,))],
+        name="pipe_ends",
+        limit=60,
+        busy=4,
     )(field)
     ends = [ends] + [swap(ends, step) for step in range(1, pipes)]
     (spectra,) = call(spectrum_kernel, [chunks], [VMEM] * 2, name="spectrum", busy=12)(
@@ -457,7 +480,7 @@
         layer_kernel,
         [shape(field.shape, bf16)] * 2 + [message],
         [VMEM] * 8,
-        [pltpu.VMEM((all_rows, channels), f32)] * 2,
+        [pltpu.VMEM((all_rows, channels), f32)] * 2 + [pltpu.VMEM(field.shape, f32)],
         name="layer",
         busy=12,
     )(field, cot, f_table, ft_table, point_weight, bias_row, cond, returned)

time: 59.8 us -> 60.5 us (1.012)
  Pallas kernels: 11.5 us -> 13 us
  local copies, waits for them, and re-layouts: 1.29 us -> 0.09 us
    pallas_call x1, Pallas kernels: 0.01 us -> 1.45 us  [body(): call(ends_kernel, [shape((8, channels), f32)], [HBM], [pltpu.VMEM((2, 16,...]
    unnamed x26 -> x28, local copies, waits for them, and re-layouts: 1.29 us -> 0.09 us
where the time goes in v15:
time: 60.5 us; the launch traced here: 60 us
  blocking collectives  32.9 us (54%)
  Pallas kernels  13 us (21%)
  starting transfers between devices  8.35 us (14%)
  waiting for transfers between devices  4.83 us (8%)
  between operations  0.88 us (1%)
    all_to_all x3, blocking collectives, exchange(): return lax.all_to_all(value, 'len', split_axis=0, concat_axis=0, tiled=True)  32.9 us
    ppermute x8, starting transfers between devices, swap(): return lax.ppermute(value, 'pipe', [(i, i ^ step) for i in range(pipes)])  4.96 us
    ppermute x8, waiting for transfers between devices, swap(): return lax.ppermute(value, 'pipe', [(i, i ^ step) for i in range(pipes)])  4.38 us
    pallas_call x1, Pallas kernels, body(): call(functools.partial(weight_grad_kernel, pipes, modes, per_copy), [big,...  3.99 us
    all_to_all x1, starting transfers between devices, exchange(): return lax.all_to_all(value, 'len', split_axis=0, concat_axis=0, tiled=True)  3.38 us
    pallas_call x1, Pallas kernels, body(): call(layer_kernel, [shape(field.shape, bf16)] * 2 + [message], [VMEM] * 8...  2.7 us
    pallas_call x1, Pallas kernels, body(): call(mix_grad_kernel, [chunks, early], [VMEM] * 4, [dma] + mix_bufs, out_...  1.93 us
    pallas_call x1, Pallas kernels, body(): call(input_grad_kernel, [shape(field.shape, bf16)], [VMEM] * 5, [pltpu.VM...  1.46 us
  transfers between devices with their start and end apart: 9, of which 6 were waited for; matrix products, arithmetic and copies ran while one was open for 0% of the time, Pallas kernels for 11%

profile of v15, /device:TPU:0, one launch (start us, length us, event | category | flops | bytes accessed | tf_op | source)
XLA Modules:
  0.0 60.0 jit_solution(6880463257052171479)
XLA Ops:
  0.6 0.0 copy-start.13
  0.7 1.4 %pipe_ends.1.refs_0_ = f32[8,256]{1,0:T(8,128)} custom-call(bf16[2048,256]{1,0:T(8,128)(2,1)} %bitcast.12), custom_call_target="tpu_custom_call" | custom-call | flops 4000000000 | bytes 4194304 | tf_op jit(solution)/shard_map/pipe_ends/pallas_call | solution.py:449
  2.1 0.0 copy-start.1
  2.1 0.0 copy-start.4
  2.2 0.0 copy-start.7
  2.2 0.0 copy-start.11
  2.2 2.4 %collective-permute-start.2 = (f32[8,256]{1,0:T(8,128)}, f32[8,256]{1,0:T(8,128)S(1)}, u32[]{:S(2)}, u32[]{:S(2)}) collective-permute-start(f32[8,256]{1,0:T(8,128)} %pipe_ends.1.refs_0_), channel_id=1, source_target_pairs={{0,3},{1,2},{2,1},{3,0},{4,7},{5,6},{6,5},{7,4},{8,11},{9,10},{10,... | collective-permute-start | bytes 24584 | tf_op jit(solution)/shard_map/ppermute | solution.py:443
  4.6 0.6 %collective-permute-start.1 = (f32[8,256]{1,0:T(8,128)}, f32[8,256]{1,0:T(8,128)S(1)}, u32[]{:S(2)}, u32[]{:S(2)}) collective-permute-start(f32[8,256]{1,0:T(8,128)} %pipe_ends.1.refs_0_), channel_id=1, source_target_pairs={{0,2},{1,3},{2,0},{3,1},{4,6},{5,7},{6,4},{7,5},{8,10},{9,11},{10,... | collective-permute-start | bytes 24584 | tf_op jit(solution)/shard_map/ppermute | solution.py:443
  5.3 0.0 collective-permute-start
  5.3 0.4 spectrum.1.spectra_ref
  5.8 0.4 collective-permute-done.2.refs_3_
  6.2 2.3 %collective-permute-done.1.refs_2_ = f32[8,256]{1,0:T(8,128)S(1)} collective-permute-done((f32[8,256]{1,0:T(8,128)}, f32[8,256]{1,0:T(8,128)S(1)}, u32[]{:S(2)}, u32[]{:S(2)}) %collective-permute-start.1) | collective-permute-done | bytes 8224 | tf_op jit(solution)/shard_map/ppermute | solution.py:443
  8.5 13.2 %all_to_all.20.r_ref.first_ref.refs_0_ = bf16[8,40,256]{2,1,0:T(8,128)(2,1)S(1)} all-to-all(bf16[8,40,256]{2,1,0:T(8,128)(2,1)S(1)} %message.1), channel_id=1, replica_groups=mesh['len'=8,'pipe'=4] {'len'}, dimensions={0} | all-to-all | bytes 327680 | tf_op jit(solution)/shard_map/all_to_all | solution.py:440
  21.8 0.0 copy-start
  21.8 0.0 copy-start.2
  21.8 1.0 %mix.1 = (bf16[8,32,256]{2,1,0:T(8,128)(2,1)S(1)}, f32[1,256]{1,0:T(1,128)S(1)}, f32[8,256]{1,0:T(8,128)S(1)}) custom-call(bf16[8,40,256]{2,1,0:T(8,128)(2,1)S(1)} %all_to_all.20.r_ref.first_ref.refs_0_, bf16[16,256,256]{2,1,0:T(8,128)(2,1)S(1)} %copy-done.6, bf16[16,256,256]{2,1,0:T(8,128)(2,1)S(1)} %copy-done.7, s32[1,32]{1,0:T(1,128)S(1)} %bitcast.8, ...), custom_call_target="tpu_custom_call" | custom-call | flops 12000000000 | bytes 12582912 | tf_op jit(solution)/shard_map/mix/pallas_call | solution.py:469
  22.8 9.7 %all_to_all.21.modes_ref = bf16[8,32,256]{2,1,0:T(8,128)(2,1)S(1)} all-to-all(bf16[8,32,256]{2,1,0:T(8,128)(2,1)S(1)} %get-tuple-element.23), channel_id=1, replica_groups=mesh['len'=8,'pipe'=4] {'len'}, dimensions={0} | all-to-all | bytes 262144 | tf_op jit(solution)/shard_map/all_to_all | solution.py:440
  32.6 2.7 %layer.1 = (bf16[2048,256]{1,0:T(8,128)(2,1)S(1)}, bf16[2048,256]{1,0:T(8,128)(2,1)S(1)}, bf16[8,34,256]{2,1,0:T(8,128)(2,1)S(1)}) custom-call(bf16[2048,256]{1,0:T(8,128)(2,1)S(1)} %bitcast.14, bf16[2048,256]{1,0:T(8,128)(2,1)S(1)} %bitcast.15, bf16[4,256,256]{2,1,0:T(8,128)(2,1)S(1)} %copy-done.13, bf16[1024,256]{1,0:T(8,128)(2,1)S(1)} %copy-done, ...), custom_call_target="tpu_custom_call" | custom-call | flops 12000000000 | bytes 12582912 | tf_op jit(solution)/shard_map/layer/pallas_call | solution.py:479
  35.3 10.0 %all_to_all.22.r_ref.second_ref.refs_4_ = bf16[8,34,256]{2,1,0:T(8,128)(2,1)S(1)} all-to-all(bf16[8,34,256]{2,1,0:T(8,128)(2,1)S(1)} %get-tuple-element.24), channel_id=1, replica_groups=mesh['len'=8,'pipe'=4] {'len'}, dimensions={0} | all-to-all | bytes 278528 | tf_op jit(solution)/shard_map/all_to_all | solution.py:440
  45.3 0.7 %collective-permute-start.4 = (bf16[16,34,256]{2,1,0:T(8,128)(2,1)S(1)}, bf16[16,34,256]{2,1,0:T(8,128)(2,1)S(1)}, u32[]{:S(2)}, u32[]{:S(2)}) collective-permute-start(bf16[16,34,256]{2,1,0:T(8,128)(2,1)S(1)} %pack.1), channel_id=1, source_target_pairs={{0,2},{1,3},{2,0},{3,1},{4,6},{5,7},{6,4},{7,5},{8,10},{9,11},{10,... | collective-permute-start | bytes 835592 | tf_op jit(solution)/shard_map/ppermute | solution.py:443
  46.0 1.9 %mix_grad.1 = (bf16[8,32,256]{2,1,0:T(8,128)(2,1)}, bf16[2048,256]{1,0:T(8,128)(2,1)}) custom-call(bf16[8,34,256]{2,1,0:T(8,128)(2,1)S(1)} %all_to_all.22.r_ref.second_ref.refs_4_, bf16[16,256,256]{2,1,0:T(8,128)(2,1)S(1)} %copy-done.6, bf16[16,256,256]{2,1,0:T(8,128)(2,1)S(1)} %copy-done.7, bf16[2048,256]{1,0:T(8,128)(2,1)S(1)} %get-tuple-element.26.early_ref), custom_call_target="tpu_custom_call" | custom-call | flops 12000000000 | bytes 12582912 | tf_op jit(solution)/shard_map/mix_grad/pallas_call | solution.py:495
  47.9 3.4 %all-to-all-start.3 = ((bf16[8,32,256]{2,1,0:T(8,128)(2,1)}), bf16[8,32,256]{2,1,0:T(8,128)(2,1)S(1)}, u32[]{:S(2)}, u32[]{:S(2)}) async-start(bf16[8,32,256]{2,1,0:T(8,128)(2,1)} %get-tuple-element.31), calls=%async_computation.3 | async-start | bytes 262144 | tf_op jit(solution)/shard_map/all_to_all | solution.py:440
  51.3 0.1 collective-permute-start.3
  51.4 0.5 collective-permute-start.6
  51.9 0.5 collective-permute-done.4.both_ref
  52.4 0.1 collective-permute-start.5
  52.5 0.5 collective-permute-start.7
  53.0 0.9 %collective-permute-done.5.refs_3_ = bf16[8,34,256]{2,1,0:T(8,128)(2,1)S(1)} collective-permute-done((bf16[8,34,256]{2,1,0:T(8,128)(2,1)S(1)}, bf16[8,34,256]{2,1,0:T(8,128)(2,1)S(1)}, u32[]{:S(2)}, u32[]{:S(2)}) %collective-permute-start.5) | collective-permute-done | bytes 139296 | tf_op jit(solution)/shard_map/ppermute | solution.py:443
  53.9 0.2 collective-permute-done.7.refs_7_
  54.1 4.0 %weight_grad.1 = (f32[16,256,256]{2,1,0:T(8,128)}, f32[16,256,256]{2,1,0:T(8,128)}, f32[8,256]{1,0:T(8,128)S(1)}) custom-call(bf16[8,40,256]{2,1,0:T(8,128)(2,1)S(1)} %all_to_all.20.r_ref.first_ref.refs_0_, bf16[8,40,256]{2,1,0:T(8,128)(2,1)S(1)} %collective-permute-done.3.refs_1_, bf16[8,34,256]{2,1,0:T(8,128)(2,1)S(1)} %get-tuple-element.33.refs_2_, ...), custom_call_target="tpu_custom_call" | custom-call | tf_op jit(solution)/shard_map/weight_grad/pallas_call | solution.py:512
  58.1 0.5 all-to-all-done.3.modes_ref
  58.6 1.5 %input_grad.1 = bf16[2048,256]{1,0:T(8,128)(2,1)} custom-call(bf16[2048,256]{1,0:T(8,128)(2,1)S(1)} %get-tuple-element.28.total_ref, bf16[1024,256]{1,0:T(8,128)(2,1)S(1)} %copy-done, bf16[256,256]{1,0:T(8,128)(2,1)S(1)} %copy-done.2, f32[8,256]{1,0:T(8,128)S(1)} %get-tuple-element.37.rows_ref, bf16[8,32,256]{2,1,0:T(8,128)(2,1)S(1)} %all-to-all-done.3.modes_ref), custom_call_target="tpu_custom_call" | custom-call | tf_op jit(solution)/shard_map/input_grad/pallas_call | solution.py:525
  (27 shorter events, 0.1 us)
Async XLA Ops:
  0.6 4.7 %copy-start.8 = (bf16[1,2048,256]{2,1,0:T(8,128)(2,1)S(1)}, bf16[1,2048,256]{2,1,0:T(8,128)(2,1)}, u32[]{:S(2)}) copy-start(bf16[1,2048,256]{2,1,0:T(8,128)(2,1)} %param.12) | copy-start | bytes 3145732
  0.6 4.7 %copy-start.13 = (bf16[4,256,256]{2,1,0:T(8,128)(2,1)S(1)}, bf16[4,256,256]{2,1,0:T(8,128)(2,1)}, u32[]{:S(2)}) copy-start(bf16[4,256,256]{2,1,0:T(8,128)(2,1)} %constant.4.clone.f_ref) | copy-start | bytes 1572868
  2.1 6.4 %copy-start.3 = (f32[8,256]{1,0:T(8,128)S(1)}, f32[8,256]{1,0:T(8,128)}, u32[]{:S(2)}) copy-start(f32[8,256]{1,0:T(8,128)} %pipe_ends.1.refs_0_) | copy-start | bytes 24580
  2.1 19.6 %copy-start.1 = (bf16[256,256]{1,0:T(8,128)(2,1)S(1)}, bf16[256,256]{1,0:T(8,128)(2,1)}, u32[]{:S(2)}) copy-start(bf16[256,256]{1,0:T(8,128)(2,1)} %refs_10_.1) | copy-start | bytes 393220
  2.1 19.6 %copy-start.4 = (s32[32]{0:T(128)S(1)}, s32[32]{0:T(128)}, u32[]{:S(2)}) copy-start(s32[32]{0:T(128)} %param.20) | copy-start | bytes 388
  2.1 19.6 %copy-start.5 = (s32[32]{0:T(128)S(1)}, s32[32]{0:T(128)}, u32[]{:S(2)}) copy-start(s32[32]{0:T(128)} %param.21) | copy-start | bytes 388
  2.2 19.6 %copy-start.6 = (bf16[16,256,256]{2,1,0:T(8,128)(2,1)S(1)}, bf16[16,256,256]{2,1,0:T(8,128)(2,1)}, u32[]{:S(2)}) copy-start(bf16[16,256,256]{2,1,0:T(8,128)(2,1)} %real_ref.3) | copy-start | bytes 6291460
  2.2 19.6 %copy-start.7 = (bf16[16,256,256]{2,1,0:T(8,128)(2,1)S(1)}, bf16[16,256,256]{2,1,0:T(8,128)(2,1)}, u32[]{:S(2)}) copy-start(bf16[16,256,256]{2,1,0:T(8,128)(2,1)} %imag_ref.3) | copy-start | bytes 6291460
  2.2 19.6 %copy-start.11 = (f32[256]{0:T(256)S(1)}, f32[256]{0:T(256)}, u32[]{:S(2)}) copy-start(f32[256]{0:T(256)} %param.19) | copy-start | bytes 3076
  2.2 4.0 %collective-permute-start.2 = (f32[8,256]{1,0:T(8,128)}, f32[8,256]{1,0:T(8,128)S(1)}, u32[]{:S(2)}, u32[]{:S(2)}) collective-permute-start(f32[8,256]{1,0:T(8,128)} %pipe_ends.1.refs_0_), channel_id=1, source_target_pairs={{0,3},{1,2},{2,1},{3,0},{4,7},{5,6},{6,5},{7,4},{8,11},{9,10},{10,... | collective-permute-start | bytes 24584 | tf_op jit(solution)/shard_map/ppermute | solution.py:443
  4.6 3.9 %collective-permute-start.1 = (f32[8,256]{1,0:T(8,128)}, f32[8,256]{1,0:T(8,128)S(1)}, u32[]{:S(2)}, u32[]{:S(2)}) collective-permute-start(f32[8,256]{1,0:T(8,128)} %pipe_ends.1.refs_0_), channel_id=1, source_target_pairs={{0,2},{1,3},{2,0},{3,1},{4,6},{5,7},{6,4},{7,5},{8,10},{9,11},{10,... | collective-permute-start | bytes 24584 | tf_op jit(solution)/shard_map/ppermute | solution.py:443
  5.3 3.2 %collective-permute-start = (f32[8,256]{1,0:T(8,128)}, f32[8,256]{1,0:T(8,128)S(1)}, u32[]{:S(2)}, u32[]{:S(2)}) collective-permute-start(f32[8,256]{1,0:T(8,128)} %pipe_ends.1.refs_0_), channel_id=1, source_target_pairs={{0,1},{1,0},{2,3},{3,2},{4,5},{5,4},{6,7},{7,6},{8,9},{9,8},{10,11... | collective-permute-start | bytes 24584 | tf_op jit(solution)/shard_map/ppermute | solution.py:443
  21.8 10.8 %copy-start = (bf16[1024,256]{1,0:T(8,128)(2,1)S(1)}, bf16[1024,256]{1,0:T(8,128)(2,1)}, u32[]{:S(2)}) copy-start(bf16[1024,256]{1,0:T(8,128)(2,1)} %constant.5.clone.ft_ref) | copy-start | bytes 1572868
  21.8 10.8 %copy-start.2 = (bf16[256,256]{1,0:T(8,128)(2,1)S(1)}, bf16[256,256]{1,0:T(8,128)(2,1)}, u32[]{:S(2)}) copy-start(bf16[256,256]{1,0:T(8,128)(2,1)} %weight_ref.3) | copy-start | bytes 393220
  21.8 10.8 %copy-start.9 = (bf16[1,2048,256]{2,1,0:T(8,128)(2,1)S(1)}, bf16[1,2048,256]{2,1,0:T(8,128)(2,1)}, u32[]{:S(2)}) copy-start(bf16[1,2048,256]{2,1,0:T(8,128)(2,1)} %param.12) | copy-start | bytes 3145732
  21.8 10.8 %copy-start.10 = (bf16[1,2048,256]{2,1,0:T(8,128)(2,1)S(1)}, bf16[1,2048,256]{2,1,0:T(8,128)(2,1)}, u32[]{:S(2)}) copy-start(bf16[1,2048,256]{2,1,0:T(8,128)(2,1)} %param.13) | copy-start | bytes 3145732
  21.8 10.8 %copy-start.12 = (f32[256]{0:T(256)S(1)}, f32[256]{0:T(256)}, u32[]{:S(2)}) copy-start(f32[256]{0:T(256)} %param.15) | copy-start | bytes 3076
  45.3 7.1 %collective-permute-start.4 = (bf16[16,34,256]{2,1,0:T(8,128)(2,1)S(1)}, bf16[16,34,256]{2,1,0:T(8,128)(2,1)S(1)}, u32[]{:S(2)}, u32[]{:S(2)}) collective-permute-start(bf16[16,34,256]{2,1,0:T(8,128)(2,1)S(1)} %pack.1), channel_id=1, source_target_pairs={{0,2},{1,3},{2,0},{3,1},{4,6},{5,7},{6,4},{7,5},{8,10},{9,11},{10,... | collective-permute-start | bytes 835592 | tf_op jit(solution)/shard_map/ppermute | solution.py:443
  47.9 10.7 %all-to-all-start.3 = ((bf16[8,32,256]{2,1,0:T(8,128)(2,1)}), bf16[8,32,256]{2,1,0:T(8,128)(2,1)S(1)}, u32[]{:S(2)}, u32[]{:S(2)}) async-start(bf16[8,32,256]{2,1,0:T(8,128)(2,1)} %get-tuple-element.31), calls=%async_computation.3 | async-start | bytes 262144 | tf_op jit(solution)/shard_map/all_to_all | solution.py:440
  51.3 1.7 %collective-permute-start.3 = (bf16[8,40,256]{2,1,0:T(8,128)(2,1)S(1)}, bf16[8,40,256]{2,1,0:T(8,128)(2,1)S(1)}, u32[]{:S(2)}, u32[]{:S(2)}) collective-permute-start(bf16[8,40,256]{2,1,0:T(8,128)(2,1)S(1)} %all_to_all.20.r_ref.first_ref.refs_0_), channel_id=1, source_target_pairs={{0,1},{1,0},{2,3},{3,2},{4,5},{5,4},{6,7},{7,6},{8,9},{9,8},{10,11... | collective-permute-start | bytes 491528 | tf_op jit(solution)/shard_map/ppermute | solution.py:443
  51.4 1.6 %collective-permute-start.6 = (bf16[8,34,256]{2,1,0:T(8,128)(2,1)S(1)}, bf16[8,34,256]{2,1,0:T(8,128)(2,1)S(1)}, u32[]{:S(2)}, u32[]{:S(2)}) collective-permute-start(bf16[8,34,256]{2,1,0:T(8,128)(2,1)S(1)} %all_to_all.22.r_ref.second_ref.refs_4_), channel_id=1, source_target_pairs={{0,1},{1,0},{2,3},{3,2},{4,5},{5,4},{6,7},{7,6},{8,9},{9,8},{10,11... | collective-permute-start | bytes 417800 | tf_op jit(solution)/shard_map/ppermute | solution.py:443
  52.4 1.5 %collective-permute-start.5 = (bf16[8,34,256]{2,1,0:T(8,128)(2,1)S(1)}, bf16[8,34,256]{2,1,0:T(8,128)(2,1)S(1)}, u32[]{:S(2)}, u32[]{:S(2)}) collective-permute-start(bf16[8,34,256]{2,1,0:T(8,128)(2,1)S(1)} %get-tuple-element.33.refs_2_), channel_id=1, source_target_pairs={{0,1},{1,0},{2,3},{3,2},{4,5},{5,4},{6,7},{7,6},{8,9},{9,8},{10,11... | collective-permute-start | bytes 417800 | tf_op jit(solution)/shard_map/ppermute | solution.py:443
  52.5 1.6 %collective-permute-start.7 = (bf16[8,34,256]{2,1,0:T(8,128)(2,1)S(1)}, bf16[8,34,256]{2,1,0:T(8,128)(2,1)S(1)}, u32[]{:S(2)}, u32[]{:S(2)}) collective-permute-start(bf16[8,34,256]{2,1,0:T(8,128)(2,1)S(1)} %get-tuple-element.35.refs_6_), channel_id=1, source_target_pairs={{0,1},{1,0},{2,3},{3,2},{4,5},{5,4},{6,7},{7,6},{8,9},{9,8},{10,11... | collective-permute-start | bytes 417800 | tf_op jit(solution)/shard_map/ppermute | solution.py:443

commit v16 on v14

--- a/solution.py
+++ b/solution.py
@@ -317,6 +317,19 @@
     wait(going)
 
 
+def pick_kernel(r_ref, out_ref):
+    other = 1 - lax.rem(lax.axis_index("len"), 2)
+    for pair in range(out_ref.shape[0]):
+        out_ref[pair] = r_ref[2 * pair + other]
+
+
+def merge_kernel(r_ref, got_ref, out_ref):
+    mine = lax.rem(lax.axis_index("len"), 2)
+    for pair in range(got_ref.shape[0]):
+        out_ref[2 * pair + mine] = r_ref[2 * pair + mine]
+        out_ref[2 * pair + 1 - mine] = got_ref[pair]
+
+
 def pack_kernel(first_ref, second_ref, out_ref):
     groups, rows = second_ref.shape[0], second_ref.shape[1]
     out_ref[0:groups] = first_ref[:, 0:rows, :]
@@ -419,8 +432,19 @@
     chunks = shape((groups, span, channels), bf16)
     dma = pltpu.SemaphoreType.DMA
 
+    lines = [list(range(first, groups, 2)) for first in range(2)]
+
     def exchange(value):
-        return lax.all_to_all(value, "len", split_axis=0, concat_axis=0, tiled=True)
+        rows = value.shape[1]
+        moved = lax.all_to_all(
+            value, "len", split_axis=0, concat_axis=0, tiled=True, axis_index_groups=lines
+        )
+        half = shape((groups // 2, rows, channels), bf16)
+        (passed,) = call(pick_kernel, [half], [VMEM], name="pick")(moved)
+        got = lax.ppermute(passed, "len", [(i, i ^ 1) for i in range(groups)])
+        return call(merge_kernel, [shape(value.shape, bf16)], [VMEM] * 2, name="merge")(
+            moved, got
+        )[0]
 
     def swap(value, step):
         return lax.ppermute(value, "pipe", [(i, i ^ step) for i in range(pipes)])

time: 59.8 us -> 76.1 us (1.27)
  waiting for transfers between devices: 4.62 us -> 18.6 us
  starting transfers between devices: 8.35 us -> 14.4 us
  blocking collectives: 32.9 us -> 28.9 us
    ppermute x0 -> x4, waiting for transfers between devices: none -> 11.3 us  [exchange(): got = lax.ppermute(passed, 'len', [(i, i ^ 1) for i in range(groups)])]
    ppermute x0 -> x4, starting transfers between devices: none -> 6.08 us  [exchange(): got = lax.ppermute(passed, 'len', [(i, i ^ 1) for i in range(groups)])]
    all_to_all x3, blocking collectives: 32.9 us -> 28.9 us  [exchange(): lax.all_to_all(value, 'len', split_axis=0, concat_axis=0, tiled=True, axi...]
    all_to_all x1, waiting for transfers between devices: 0.46 us -> 4.14 us  [exchange(): lax.all_to_all(value, 'len', split_axis=0, concat_axis=0, tiled=True, axi...]
    ppermute x8, waiting for transfers between devices: 4.16 us -> 3.1 us  [swap(): return lax.ppermute(value, 'pipe', [(i, i ^ step) for i in range(pipes)])]
  transfers between devices with their start and end apart: 9 -> 13, of which waited for: 6 -> 8; matrix products, arithmetic and copies ran while one was open for 0% -> 0% of each run, Pallas kernels for 11% -> 3%
where the time goes in v16:
time: 76.1 us; the launch traced here: 75.7 us
  blocking collectives  28.9 us (38%)
  waiting for transfers between devices  18.6 us (24%)
  starting transfers between devices  14.4 us (19%)
  Pallas kernels  11.6 us (15%)
  local copies, waits for them, and re-layouts  1.29 us (2%)
  between operations  0.95 us (1%)
    all_to_all x3, blocking collectives, exchange(): lax.all_to_all(value, 'len', split_axis=0, concat_axis=0, tiled=True, axi...  28.9 us
    ppermute x4, waiting for transfers between devices, exchange(): got = lax.ppermute(passed, 'len', [(i, i ^ 1) for i in range(groups)])  11.3 us
    ppermute x4, starting transfers between devices, exchange(): got = lax.ppermute(passed, 'len', [(i, i ^ 1) for i in range(groups)])  6.08 us
    ppermute x8, starting transfers between devices, swap(): return lax.ppermute(value, 'pipe', [(i, i ^ step) for i in range(pipes)])  4.97 us
    all_to_all x1, waiting for transfers between devices, exchange(): lax.all_to_all(value, 'len', split_axis=0, concat_axis=0, tiled=True, axi...  4.14 us
    pallas_call x1, Pallas kernels, body(): call(functools.partial(weight_grad_kernel, pipes, modes, per_copy), [big,...  4 us
    all_to_all x1, starting transfers between devices, exchange(): lax.all_to_all(value, 'len', split_axis=0, concat_axis=0, tiled=True, axi...  3.34 us
    ppermute x8, waiting for transfers between devices, swap(): return lax.ppermute(value, 'pipe', [(i, i ^ step) for i in range(pipes)])  3.1 us
  transfers between devices with their start and end apart: 13, of which 8 were waited for; matrix products, arithmetic and copies ran while one was open for 0% of the time, Pallas kernels for 3%

profile of v16, /device:TPU:0, one launch (start us, length us, event | category | flops | bytes accessed | tf_op | source)
XLA Modules:
  0.0 75.7 jit_solution(15119397202272556351)
XLA Ops:
  0.6 1.2 %copy-done.7 = bf16[1,2048,256]{2,1,0:T(8,128)(2,1)S(1)} copy-done((bf16[1,2048,256]{2,1,0:T(8,128)(2,1)S(1)}, bf16[1,2048,256]{2,1,0:T(8,128)(2,1)}, u32[]{:S(2)}) %copy-start.7) | copy-done | bytes 1048600
  1.9 2.4 %collective-permute-start.2 = (f32[8,256]{1,0:T(8,128)S(1)}, f32[8,256]{1,0:T(8,128)S(1)}, u32[]{:S(2)}, u32[]{:S(2)}) collective-permute-start(f32[8,256]{1,0:T(8,128)S(1)} %pipe_ends.1.refs_0_), channel_id=1, source_target_pairs={{0,3},{1,2},{2,1},{3,0},{4,7},{5,6},{6,5},{7,4},{8,11},{9,10},{10,... | collective-permute-start | bytes 24584 | tf_op jit(solution)/shard_map/ppermute | solution.py:450
  4.4 0.6 collective-permute-start.1
  5.0 0.0 collective-permute-start
  5.1 0.4 spectrum.1.spectra_ref
  5.5 0.2 collective-permute-done.2.refs_3_
  5.7 2.3 %collective-permute-done.1.refs_2_ = f32[8,256]{1,0:T(8,128)S(1)} collective-permute-done((f32[8,256]{1,0:T(8,128)S(1)}, f32[8,256]{1,0:T(8,128)S(1)}, u32[]{:S(2)}, u32[]{:S(2)}) %collective-permute-start.1) | collective-permute-done | bytes 8224 | tf_op jit(solution)/shard_map/ppermute | solution.py:450
  8.0 11.4 %all_to_all.20.r_ref = bf16[8,40,256]{2,1,0:T(8,128)(2,1)S(1)} all-to-all(bf16[8,40,256]{2,1,0:T(8,128)(2,1)S(1)} %message.1), channel_id=1, replica_groups={{0,8,16,24},{4,12,20,28},{1,9,17,25},{5,13,21,29},{2,10,18,26},{6,14,22..., dimensions={0} | all-to-all | bytes 327680 | tf_op jit(solution)/shard_map/all_to_all | solution.py:439
  19.5 1.5 %collective-permute-start.3 = (bf16[4,40,256]{2,1,0:T(8,128)(2,1)S(1)}, bf16[4,40,256]{2,1,0:T(8,128)(2,1)S(1)}, u32[]{:S(2)}, u32[]{:S(2)}) collective-permute-start(bf16[4,40,256]{2,1,0:T(8,128)(2,1)S(1)} %pick.4), channel_id=1, source_target_pairs={{0,4},{4,0},{8,12},{12,8},{16,20},{20,16},{24,28},{28,24},{1,5},{5... | collective-permute-start | bytes 245768 | tf_op jit(solution)/shard_map/ppermute | solution.py:444
  21.0 2.9 %collective-permute-done.3.got_ref = bf16[4,40,256]{2,1,0:T(8,128)(2,1)S(1)} collective-permute-done((bf16[4,40,256]{2,1,0:T(8,128)(2,1)S(1)}, bf16[4,40,256]{2,1,0:T(8,128)(2,1)S(1)}, u32[]{:S(2)}, u32[]{:S(2)}) %collective-permute-start.3) | collective-permute-done | bytes 81952 | tf_op jit(solution)/shard_map/ppermute | solution.py:444
  24.0 0.0 copy-start
  24.1 1.0 %mix.1 = (bf16[8,32,256]{2,1,0:T(8,128)(2,1)S(1)}, f32[1,256]{1,0:T(1,128)S(1)}, f32[8,256]{1,0:T(8,128)S(1)}) custom-call(bf16[8,40,256]{2,1,0:T(8,128)(2,1)S(1)} %merge.4.r_ref.first_ref.refs_0_, bf16[16,256,256]{2,1,0:T(8,128)(2,1)S(1)} %copy-done.5, bf16[16,256,256]{2,1,0:T(8,128)(2,1)S(1)} %copy-done.6, s32[1,32]{1,0:T(1,128)S(1)} %bitcast.8, ...), custom_call_target="tpu_custom_call" | custom-call | flops 12000000000 | bytes 12582912 | tf_op jit(solution)/shard_map/mix/pallas_call | solution.py:470
  25.0 8.3 %all_to_all.21.r_ref = bf16[8,32,256]{2,1,0:T(8,128)(2,1)S(1)} all-to-all(bf16[8,32,256]{2,1,0:T(8,128)(2,1)S(1)} %get-tuple-element.23), channel_id=1, replica_groups={{0,8,16,24},{4,12,20,28},{1,9,17,25},{5,13,21,29},{2,10,18,26},{6,14,22..., dimensions={0} | all-to-all | bytes 262144 | tf_op jit(solution)/shard_map/all_to_all | solution.py:439
  33.3 1.5 %collective-permute-start.4 = (bf16[4,32,256]{2,1,0:T(8,128)(2,1)S(1)}, bf16[4,32,256]{2,1,0:T(8,128)(2,1)S(1)}, u32[]{:S(2)}, u32[]{:S(2)}) collective-permute-start(bf16[4,32,256]{2,1,0:T(8,128)(2,1)S(1)} %pick.5), channel_id=1, source_target_pairs={{0,4},{4,0},{8,12},{12,8},{16,20},{20,16},{24,28},{28,24},{1,5},{5... | collective-permute-start | bytes 196616 | tf_op jit(solution)/shard_map/ppermute | solution.py:444
  34.9 2.7 %collective-permute-done.4.got_ref = bf16[4,32,256]{2,1,0:T(8,128)(2,1)S(1)} collective-permute-done((bf16[4,32,256]{2,1,0:T(8,128)(2,1)S(1)}, bf16[4,32,256]{2,1,0:T(8,128)(2,1)S(1)}, u32[]{:S(2)}, u32[]{:S(2)}) %collective-permute-start.4) | collective-permute-done | bytes 65568 | tf_op jit(solution)/shard_map/ppermute | solution.py:444
  37.7 2.6 %layer.1 = (bf16[2048,256]{1,0:T(8,128)(2,1)S(1)}, bf16[2048,256]{1,0:T(8,128)(2,1)S(1)}, bf16[8,34,256]{2,1,0:T(8,128)(2,1)S(1)}) custom-call(bf16[2048,256]{1,0:T(8,128)(2,1)S(1)} %bitcast.14, bf16[2048,256]{1,0:T(8,128)(2,1)S(1)} %bitcast.15, bf16[4,256,256]{2,1,0:T(8,128)(2,1)S(1)} %copy-done.12, bf16[1024,256]{1,0:T(8,128)(2,1)S(1)} %copy-done, ...), custom_call_target="tpu_custom_call" | custom-call | flops 12000000000 | bytes 12582912 | tf_op jit(solution)/shard_map/layer/pallas_call | solution.py:480
  40.3 9.2 %all_to_all.22.r_ref = bf16[8,34,256]{2,1,0:T(8,128)(2,1)S(1)} all-to-all(bf16[8,34,256]{2,1,0:T(8,128)(2,1)S(1)} %get-tuple-element.24), channel_id=1, replica_groups={{0,8,16,24},{4,12,20,28},{1,9,17,25},{5,13,21,29},{2,10,18,26},{6,14,22..., dimensions={0} | all-to-all | bytes 278528 | tf_op jit(solution)/shard_map/all_to_all | solution.py:439
  49.5 1.5 %collective-permute-start.5 = (bf16[4,34,256]{2,1,0:T(8,128)(2,1)S(1)}, bf16[4,34,256]{2,1,0:T(8,128)(2,1)S(1)}, u32[]{:S(2)}, u32[]{:S(2)}) collective-permute-start(bf16[4,34,256]{2,1,0:T(8,128)(2,1)S(1)} %pick.6), channel_id=1, source_target_pairs={{0,4},{4,0},{8,12},{12,8},{16,20},{20,16},{24,28},{28,24},{1,5},{5... | collective-permute-start | bytes 208904 | tf_op jit(solution)/shard_map/ppermute | solution.py:444
  51.0 2.9 %collective-permute-done.5.got_ref = bf16[4,34,256]{2,1,0:T(8,128)(2,1)S(1)} collective-permute-done((bf16[4,34,256]{2,1,0:T(8,128)(2,1)S(1)}, bf16[4,34,256]{2,1,0:T(8,128)(2,1)S(1)}, u32[]{:S(2)}, u32[]{:S(2)}) %collective-permute-start.5) | collective-permute-done | bytes 69664 | tf_op jit(solution)/shard_map/ppermute | solution.py:444
  54.0 0.7 collective-permute-start.7
  54.7 1.9 %mix_grad.1 = (bf16[8,32,256]{2,1,0:T(8,128)(2,1)}, bf16[2048,256]{1,0:T(8,128)(2,1)}) custom-call(bf16[8,34,256]{2,1,0:T(8,128)(2,1)S(1)} %merge.6.r_ref.second_ref.refs_4_, bf16[16,256,256]{2,1,0:T(8,128)(2,1)S(1)} %copy-done.5, bf16[16,256,256]{2,1,0:T(8,128)(2,1)S(1)} %copy-done.6, bf16[2048,256]{1,0:T(8,128)(2,1)S(1)} %get-tuple-element.26.early_ref), custom_call_target="tpu_custom_call" | custom-call | flops 12000000000 | bytes 12582912 | tf_op jit(solution)/shard_map/mix_grad/pallas_call | solution.py:496
  56.7 3.3 %all-to-all-start.3 = ((bf16[8,32,256]{2,1,0:T(8,128)(2,1)}), bf16[8,32,256]{2,1,0:T(8,128)(2,1)S(1)}, u32[]{:S(2)}, u32[]{:S(2)}) async-start(bf16[8,32,256]{2,1,0:T(8,128)(2,1)} %get-tuple-element.31), calls=%async_computation.3 | async-start | bytes 262144 | tf_op jit(solution)/shard_map/all_to_all | solution.py:439
  60.0 0.1 collective-permute-start.6
  60.1 0.5 collective-permute-start.9
  60.6 0.6 collective-permute-done.7.both_ref
  61.2 0.1 collective-permute-start.8
  61.3 0.5 collective-permute-start.10
  61.8 4.1 %all-to-all-done.3.r_ref = bf16[8,32,256]{2,1,0:T(8,128)(2,1)S(1)} async-done(((bf16[8,32,256]{2,1,0:T(8,128)(2,1)}), bf16[8,32,256]{2,1,0:T(8,128)(2,1)S(1)}, u32[]{:S(2)}, u32[]{:S(2)}) %all-to-all-start.3) | async-done | bytes 131104 | tf_op jit(solution)/shard_map/all_to_all | solution.py:439
  65.9 1.5 %collective-permute-start.11 = (bf16[4,32,256]{2,1,0:T(8,128)(2,1)S(1)}, bf16[4,32,256]{2,1,0:T(8,128)(2,1)S(1)}, u32[]{:S(2)}, u32[]{:S(2)}) collective-permute-start(bf16[4,32,256]{2,1,0:T(8,128)(2,1)S(1)} %pick.7), channel_id=1, source_target_pairs={{0,4},{4,0},{8,12},{12,8},{16,20},{20,16},{24,28},{28,24},{1,5},{5... | collective-permute-start | bytes 196616 | tf_op jit(solution)/shard_map/ppermute | solution.py:444
  67.4 2.7 %collective-permute-done.11.got_ref = bf16[4,32,256]{2,1,0:T(8,128)(2,1)S(1)} collective-permute-done((bf16[4,32,256]{2,1,0:T(8,128)(2,1)S(1)}, bf16[4,32,256]{2,1,0:T(8,128)(2,1)S(1)}, u32[]{:S(2)}, u32[]{:S(2)}) %collective-permute-start.11) | collective-permute-done | bytes 65568 | tf_op jit(solution)/shard_map/ppermute | solution.py:444
  70.2 4.0 %weight_grad.1 = (f32[16,256,256]{2,1,0:T(8,128)}, f32[16,256,256]{2,1,0:T(8,128)}, f32[8,256]{1,0:T(8,128)S(1)}) custom-call(bf16[8,40,256]{2,1,0:T(8,128)(2,1)S(1)} %merge.4.r_ref.first_ref.refs_0_, bf16[8,40,256]{2,1,0:T(8,128)(2,1)S(1)} %collective-permute-done.6.refs_1_, bf16[8,34,256]{2,1,0:T(8,128)(2,1)S(1)} %get-tuple-element.33.refs_2_, ...), custom_call_target="tpu_custom_call" | custom-call | tf_op jit(solution)/shard_map/weight_grad/pallas_call | solution.py:513
  74.2 1.5 %input_grad.1 = bf16[2048,256]{1,0:T(8,128)(2,1)} custom-call(bf16[2048,256]{1,0:T(8,128)(2,1)S(1)} %get-tuple-element.28.total_ref, bf16[1024,256]{1,0:T(8,128)(2,1)S(1)} %copy-done, bf16[256,256]{1,0:T(8,128)(2,1)S(1)} %copy-done.2, f32[8,256]{1,0:T(8,128)S(1)} %get-tuple-element.37.rows_ref, bf16[8,32,256]{2,1,0:T(8,128)(2,1)S(1)} %merge.7.modes_ref), custom_call_target="tpu_custom_call" | custom-call | tf_op jit(solution)/shard_map/input_grad/pallas_call | solution.py:526
  (41 shorter events, 0.2 us)
Async XLA Ops:
  0.6 1.2 %copy-start.7 = (bf16[1,2048,256]{2,1,0:T(8,128)(2,1)S(1)}, bf16[1,2048,256]{2,1,0:T(8,128)(2,1)}, u32[]{:S(2)}) copy-start(bf16[1,2048,256]{2,1,0:T(8,128)(2,1)} %param.12) | copy-start | bytes 3145732
  1.9 3.2 %copy-start.12 = (bf16[4,256,256]{2,1,0:T(8,128)(2,1)S(1)}, bf16[4,256,256]{2,1,0:T(8,128)(2,1)}, u32[]{:S(2)}) copy-start(bf16[4,256,256]{2,1,0:T(8,128)(2,1)} %constant.4.clone.f_ref) | copy-start | bytes 1572868
  1.9 22.1 %copy-start.1 = (bf16[256,256]{1,0:T(8,128)(2,1)S(1)}, bf16[256,256]{1,0:T(8,128)(2,1)}, u32[]{:S(2)}) copy-start(bf16[256,256]{1,0:T(8,128)(2,1)} %refs_10_.1) | copy-start | bytes 393220
  1.9 22.1 %copy-start.3 = (s32[32]{0:T(128)S(1)}, s32[32]{0:T(128)}, u32[]{:S(2)}) copy-start(s32[32]{0:T(128)} %param.20) | copy-start | bytes 388
  1.9 22.1 %copy-start.4 = (s32[32]{0:T(128)S(1)}, s32[32]{0:T(128)}, u32[]{:S(2)}) copy-start(s32[32]{0:T(128)} %param.21) | copy-start | bytes 388
  1.9 22.1 %copy-start.5 = (bf16[16,256,256]{2,1,0:T(8,128)(2,1)S(1)}, bf16[16,256,256]{2,1,0:T(8,128)(2,1)}, u32[]{:S(2)}) copy-start(bf16[16,256,256]{2,1,0:T(8,128)(2,1)} %real_ref.3) | copy-start | bytes 6291460
  1.9 22.1 %copy-start.6 = (bf16[16,256,256]{2,1,0:T(8,128)(2,1)S(1)}, bf16[16,256,256]{2,1,0:T(8,128)(2,1)}, u32[]{:S(2)}) copy-start(bf16[16,256,256]{2,1,0:T(8,128)(2,1)} %imag_ref.3) | copy-start | bytes 6291460
  1.9 22.1 %copy-start.10 = (f32[256]{0:T(256)S(1)}, f32[256]{0:T(256)}, u32[]{:S(2)}) copy-start(f32[256]{0:T(256)} %param.19) | copy-start | bytes 3076
  1.9 3.8 %collective-permute-start.2 = (f32[8,256]{1,0:T(8,128)S(1)}, f32[8,256]{1,0:T(8,128)S(1)}, u32[]{:S(2)}, u32[]{:S(2)}) collective-permute-start(f32[8,256]{1,0:T(8,128)S(1)} %pipe_ends.1.refs_0_), channel_id=1, source_target_pairs={{0,3},{1,2},{2,1},{3,0},{4,7},{5,6},{6,5},{7,4},{8,11},{9,10},{10,... | collective-permute-start | bytes 24584 | tf_op jit(solution)/shard_map/ppermute | solution.py:450
  4.4 3.7 %collective-permute-start.1 = (f32[8,256]{1,0:T(8,128)S(1)}, f32[8,256]{1,0:T(8,128)S(1)}, u32[]{:S(2)}, u32[]{:S(2)}) collective-permute-start(f32[8,256]{1,0:T(8,128)S(1)} %pipe_ends.1.refs_0_), channel_id=1, source_target_pairs={{0,2},{1,3},{2,0},{3,1},{4,6},{5,7},{6,4},{7,5},{8,10},{9,11},{10,... | collective-permute-start | bytes 24584 | tf_op jit(solution)/shard_map/ppermute | solution.py:450
  5.0 3.0 %collective-permute-start = (f32[8,256]{1,0:T(8,128)S(1)}, f32[8,256]{1,0:T(8,128)S(1)}, u32[]{:S(2)}, u32[]{:S(2)}) collective-permute-start(f32[8,256]{1,0:T(8,128)S(1)} %pipe_ends.1.refs_0_), channel_id=1, source_target_pairs={{0,1},{1,0},{2,3},{3,2},{4,5},{5,4},{6,7},{7,6},{8,9},{9,8},{10,11... | collective-permute-start | bytes 24584 | tf_op jit(solution)/shard_map/ppermute | solution.py:450
  19.5 4.4 %collective-permute-start.3 = (bf16[4,40,256]{2,1,0:T(8,128)(2,1)S(1)}, bf16[4,40,256]{2,1,0:T(8,128)(2,1)S(1)}, u32[]{:S(2)}, u32[]{:S(2)}) collective-permute-start(bf16[4,40,256]{2,1,0:T(8,128)(2,1)S(1)} %pick.4), channel_id=1, source_target_pairs={{0,4},{4,0},{8,12},{12,8},{16,20},{20,16},{24,28},{28,24},{1,5},{5... | collective-permute-start | bytes 245768 | tf_op jit(solution)/shard_map/ppermute | solution.py:444
  24.0 13.6 %copy-start = (bf16[1024,256]{1,0:T(8,128)(2,1)S(1)}, bf16[1024,256]{1,0:T(8,128)(2,1)}, u32[]{:S(2)}) copy-start(bf16[1024,256]{1,0:T(8,128)(2,1)} %constant.5.clone.ft_ref) | copy-start | bytes 1572868
  24.0 13.6 %copy-start.2 = (bf16[256,256]{1,0:T(8,128)(2,1)S(1)}, bf16[256,256]{1,0:T(8,128)(2,1)}, u32[]{:S(2)}) copy-start(bf16[256,256]{1,0:T(8,128)(2,1)} %weight_ref.3) | copy-start | bytes 393220
  24.0 13.6 %copy-start.8 = (bf16[1,2048,256]{2,1,0:T(8,128)(2,1)S(1)}, bf16[1,2048,256]{2,1,0:T(8,128)(2,1)}, u32[]{:S(2)}) copy-start(bf16[1,2048,256]{2,1,0:T(8,128)(2,1)} %param.12) | copy-start | bytes 3145732
  24.0 13.6 %copy-start.9 = (bf16[1,2048,256]{2,1,0:T(8,128)(2,1)S(1)}, bf16[1,2048,256]{2,1,0:T(8,128)(2,1)}, u32[]{:S(2)}) copy-start(bf16[1,2048,256]{2,1,0:T(8,128)(2,1)} %param.13) | copy-start | bytes 3145732
  24.0 13.6 %copy-start.11 = (f32[256]{0:T(256)S(1)}, f32[256]{0:T(256)}, u32[]{:S(2)}) copy-start(f32[256]{0:T(256)} %param.15) | copy-start | bytes 3076
  33.3 4.3 %collective-permute-start.4 = (bf16[4,32,256]{2,1,0:T(8,128)(2,1)S(1)}, bf16[4,32,256]{2,1,0:T(8,128)(2,1)S(1)}, u32[]{:S(2)}, u32[]{:S(2)}) collective-permute-start(bf16[4,32,256]{2,1,0:T(8,128)(2,1)S(1)} %pick.5), channel_id=1, source_target_pairs={{0,4},{4,0},{8,12},{12,8},{16,20},{20,16},{24,28},{28,24},{1,5},{5... | collective-permute-start | bytes 196616 | tf_op jit(solution)/shard_map/ppermute | solution.py:444
  49.5 4.4 %collective-permute-start.5 = (bf16[4,34,256]{2,1,0:T(8,128)(2,1)S(1)}, bf16[4,34,256]{2,1,0:T(8,128)(2,1)S(1)}, u32[]{:S(2)}, u32[]{:S(2)}) collective-permute-start(bf16[4,34,256]{2,1,0:T(8,128)(2,1)S(1)} %pick.6), channel_id=1, source_target_pairs={{0,4},{4,0},{8,12},{12,8},{16,20},{20,16},{24,28},{28,24},{1,5},{5... | collective-permute-start | bytes 208904 | tf_op jit(solution)/shard_map/ppermute | solution.py:444
  54.0 7.1 %collective-permute-start.7 = (bf16[16,34,256]{2,1,0:T(8,128)(2,1)S(1)}, bf16[16,34,256]{2,1,0:T(8,128)(2,1)S(1)}, u32[]{:S(2)}, u32[]{:S(2)}) collective-permute-start(bf16[16,34,256]{2,1,0:T(8,128)(2,1)S(1)} %pack.1), channel_id=1, source_target_pairs={{0,2},{1,3},{2,0},{3,1},{4,6},{5,7},{6,4},{7,5},{8,10},{9,11},{10,... | collective-permute-start | bytes 835592 | tf_op jit(solution)/shard_map/ppermute | solution.py:450
  56.7 9.2 %all-to-all-start.3 = ((bf16[8,32,256]{2,1,0:T(8,128)(2,1)}), bf16[8,32,256]{2,1,0:T(8,128)(2,1)S(1)}, u32[]{:S(2)}, u32[]{:S(2)}) async-start(bf16[8,32,256]{2,1,0:T(8,128)(2,1)} %get-tuple-element.31), calls=%async_computation.3 | async-start | bytes 262144 | tf_op jit(solution)/shard_map/all_to_all | solution.py:439
  60.0 10.2 %collective-permute-start.6 = (bf16[8,40,256]{2,1,0:T(8,128)(2,1)S(1)}, bf16[8,40,256]{2,1,0:T(8,128)(2,1)S(1)}, u32[]{:S(2)}, u32[]{:S(2)}) collective-permute-start(bf16[8,40,256]{2,1,0:T(8,128)(2,1)S(1)} %merge.4.r_ref.first_ref.refs_0_), channel_id=1, source_target_pairs={{0,1},{1,0},{2,3},{3,2},{4,5},{5,4},{6,7},{7,6},{8,9},{9,8},{10,11... | collective-permute-start | bytes 491528 | tf_op jit(solution)/shard_map/ppermute | solution.py:450
  60.1 10.1 %collective-permute-start.9 = (bf16[8,34,256]{2,1,0:T(8,128)(2,1)S(1)}, bf16[8,34,256]{2,1,0:T(8,128)(2,1)S(1)}, u32[]{:S(2)}, u32[]{:S(2)}) collective-permute-start(bf16[8,34,256]{2,1,0:T(8,128)(2,1)S(1)} %merge.6.r_ref.second_ref.refs_4_), channel_id=1, source_target_pairs={{0,1},{1,0},{2,3},{3,2},{4,5},{5,4},{6,7},{7,6},{8,9},{9,8},{10,11... | collective-permute-start | bytes 417800 | tf_op jit(solution)/shard_map/ppermute | solution.py:450
  61.2 9.0 %collective-permute-start.8 = (bf16[8,34,256]{2,1,0:T(8,128)(2,1)S(1)}, bf16[8,34,256]{2,1,0:T(8,128)(2,1)S(1)}, u32[]{:S(2)}, u32[]{:S(2)}) collective-permute-start(bf16[8,34,256]{2,1,0:T(8,128)(2,1)S(1)} %get-tuple-element.33.refs_2_), channel_id=1, source_target_pairs={{0,1},{1,0},{2,3},{3,2},{4,5},{5,4},{6,7},{7,6},{8,9},{9,8},{10,11... | collective-permute-start | bytes 417800 | tf_op jit(solution)/shard_map/ppermute | solution.py:450
  61.3 9.0 %collective-permute-start.10 = (bf16[8,34,256]{2,1,0:T(8,128)(2,1)S(1)}, bf16[8,34,256]{2,1,0:T(8,128)(2,1)S(1)}, u32[]{:S(2)}, u32[]{:S(2)}) collective-permute-start(bf16[8,34,256]{2,1,0:T(8,128)(2,1)S(1)} %get-tuple-element.35.refs_6_), channel_id=1, source_target_pairs={{0,1},{1,0},{2,3},{3,2},{4,5},{5,4},{6,7},{7,6},{8,9},{9,8},{10,11... | collective-permute-start | bytes 417800 | tf_op jit(solution)/shard_map/ppermute | solution.py:450
  65.9 4.3 %collective-permute-start.11 = (bf16[4,32,256]{2,1,0:T(8,128)(2,1)S(1)}, bf16[4,32,256]{2,1,0:T(8,128)(2,1)S(1)}, u32[]{:S(2)}, u32[]{:S(2)}) collective-permute-start(bf16[4,32,256]{2,1,0:T(8,128)(2,1)S(1)} %pick.7), channel_id=1, source_target_pairs={{0,4},{4,0},{8,12},{12,8},{16,20},{20,16},{24,28},{28,24},{1,5},{5... | collective-permute-start | bytes 196616 | tf_op jit(solution)/shard_map/ppermute | solution.py:444

commit v17 on v14

--- a/solution.py
+++ b/solution.py
@@ -62,7 +62,7 @@
     ends_ref[...] = jnp.concatenate([part.astype(jnp.float32) for part in ends], axis=0)
 
 
-def spectrum_kernel(x_ref, f_ref, spectra_ref):
+def spectrum_kernel(x_ref, f_ref, weight_ref, bias_ref, spectra_ref, pointwise_ref):
     steps, all_rows, tile = f_ref.shape
     half = x_ref.shape[0] // 2
     groups, span, channels = spectra_ref.shape
@@ -78,6 +78,11 @@
     spectra = spectra.astype(jnp.bfloat16)
     for at in range(groups):
         spectra_ref[at] = spectra[at * span : (at + 1) * span]
+    weight = weight_ref[...]
+    bias = bias_ref[...]
+    for step in range(2 * steps):
+        at = pl.ds(step * tile, tile)
+        pointwise_ref[at, :] = dot(x_ref[at, :], weight) + bias
 
 
 def message_kernel(pipes, spectra_ref, *refs):
@@ -207,12 +212,10 @@
 
 
 def layer_kernel(
-    x_ref,
+    pointwise_ref,
     cot_ref,
     f_ref,
     ft_ref,
-    weight_ref,
-    bias_ref,
     cond_ref,
     modes_ref,
     out_ref,
@@ -223,7 +226,7 @@
 ):
     steps, all_rows, tile = f_ref.shape
     half = steps * tile
-    channels = x_ref.shape[1]
+    channels = cot_ref.shape[1]
     groups, rows = msg_ref.shape[0], msg_ref.shape[1]
     span = all_rows // groups
     cond = cond_ref[...]
@@ -235,14 +238,11 @@
     )
     modes = modes * doubled
     modes = (modes.astype(jnp.bfloat16), (modes * signs).astype(jnp.bfloat16))
-    weight = weight_ref[...]
-    bias = bias_ref[...]
     for side, acc_ref in enumerate((low_ref, high_ref)):
         for step in range(steps):
             at = pl.ds(side * half + step * tile, tile)
-            pointwise = dot(x_ref[at, :], weight) + bias
             spectral = dot(ft_ref[pl.ds(step * tile, tile), :], modes[side])
-            summed = pointwise + (spectral + cond).astype(jnp.bfloat16).astype(jnp.float32)
+            summed = pointwise_ref[at, :] + (spectral + cond).astype(jnp.bfloat16).astype(jnp.float32)
             square = summed * summed
             part = 0.5 + 0.5 * jnp.tanh(summed * (GELU_S + (GELU_S * GELU_C) * square))
             result = summed * part
@@ -433,9 +433,13 @@
         ends_kernel, [shape((8, channels), f32)], [VMEM], name="pipe_ends", busy=4
     )(field)
     ends = [ends] + [swap(ends, step) for step in range(1, pipes)]
-    (spectra,) = call(spectrum_kernel, [chunks], [VMEM] * 2, name="spectrum", busy=12)(
-        field, f_table
-    )
+    spectra, pointwise = call(
+        spectrum_kernel,
+        [chunks, shape(field.shape, f32)],
+        [VMEM] * 4,
+        name="spectrum",
+        busy=12,
+    )(field, f_table, point_weight, bias_row)
     (sent,) = call(
         functools.partial(message_kernel, pipes),
         [shape((groups, span + 2 * pipes, channels), bf16)],
@@ -456,11 +460,11 @@
     early, total, sent = call(
         layer_kernel,
         [shape(field.shape, bf16)] * 2 + [message],
-        [VMEM] * 8,
+        [VMEM] * 6,
         [pltpu.VMEM((all_rows, channels), f32)] * 2,
         name="layer",
         busy=12,
-    )(field, cot, f_table, ft_table, point_weight, bias_row, cond, returned)
+    )(pointwise, cot, f_table, ft_table, cond, returned)
     received = exchange(sent)
     received, spectra = lax.optimization_barrier((received, spectra))
     (both,) = call(

time: 59.8 us -> 59.1 us (0.988)
    unnamed x26 -> x24, local copies, waits for them, and re-layouts: 1.29 us -> 1.28 us
where the time goes in v17:
time: 59.1 us; the launch traced here: 58.7 us
  blocking collectives  32.9 us (56%)
  Pallas kernels  11.1 us (19%)
  starting transfers between devices  8.42 us (14%)
  waiting for transfers between devices  4.27 us (7%)
  local copies, waits for them, and re-layouts  1.28 us (2%)
  between operations  0.83 us (1%)
    all_to_all x3, blocking collectives, exchange(): return lax.all_to_all(value, 'len', split_axis=0, concat_axis=0, tiled=True)  32.9 us
    ppermute x8, starting transfers between devices, swap(): return lax.ppermute(value, 'pipe', [(i, i ^ step) for i in range(pipes)])  5.04 us
    pallas_call x1, Pallas kernels, body(): call(functools.partial(weight_grad_kernel, pipes, modes, per_copy), [big,...  3.99 us
    ppermute x8, waiting for transfers between devices, swap(): return lax.ppermute(value, 'pipe', [(i, i ^ step) for i in range(pipes)])  3.74 us
    all_to_all x1, starting transfers between devices, exchange(): return lax.all_to_all(value, 'len', split_axis=0, concat_axis=0, tiled=True)  3.38 us
    pallas_call x1, Pallas kernels, body(): call(mix_grad_kernel, [chunks, early], [VMEM] * 4, [dma] + mix_bufs, out_...  1.93 us
    pallas_call x1, Pallas kernels, body(): call(layer_kernel, [shape(field.shape, bf16)] * 2 + [message], [VMEM] * 6...  1.93 us
    pallas_call x1, Pallas kernels, body(): call(input_grad_kernel, [shape(field.shape, bf16)], [VMEM] * 5, [pltpu.VM...  1.45 us
  transfers between devices with their start and end apart: 9, of which 6 were waited for; matrix products, arithmetic and copies ran while one was open for 0% of the time, Pallas kernels for 11%

profile of v17, /device:TPU:0, one launch (start us, length us, event | category | flops | bytes accessed | tf_op | source)
XLA Modules:
  0.0 58.7 jit_solution(10279890507880916915)
XLA Ops:
  0.6 1.2 %copy-done.7 = bf16[1,2048,256]{2,1,0:T(8,128)(2,1)S(1)} copy-done((bf16[1,2048,256]{2,1,0:T(8,128)(2,1)S(1)}, bf16[1,2048,256]{2,1,0:T(8,128)(2,1)}, u32[]{:S(2)}) %copy-start.7) | copy-done | bytes 1048600
  1.9 2.4 %collective-permute-start.2 = (f32[8,256]{1,0:T(8,128)S(1)}, f32[8,256]{1,0:T(8,128)S(1)}, u32[]{:S(2)}, u32[]{:S(2)}) collective-permute-start(f32[8,256]{1,0:T(8,128)S(1)} %pipe_ends.1.refs_0_), channel_id=1, source_target_pairs={{0,3},{1,2},{2,1},{3,0},{4,7},{5,6},{6,5},{7,4},{8,11},{9,10},{10,... | collective-permute-start | bytes 24584 | tf_op jit(solution)/shard_map/ppermute | solution.py:426
  4.3 0.6 %collective-permute-start.1 = (f32[8,256]{1,0:T(8,128)S(1)}, f32[8,256]{1,0:T(8,128)S(1)}, u32[]{:S(2)}, u32[]{:S(2)}) collective-permute-start(f32[8,256]{1,0:T(8,128)S(1)} %pipe_ends.1.refs_0_), channel_id=1, source_target_pairs={{0,2},{1,3},{2,0},{3,1},{4,6},{5,7},{6,4},{7,5},{8,10},{9,11},{10,... | collective-permute-start | bytes 24584 | tf_op jit(solution)/shard_map/ppermute | solution.py:426
  5.0 0.0 collective-permute-start
  5.0 0.0 copy-start.3
  5.0 0.0 copy-start.4
  5.0 0.0 copy-start.5
  5.0 0.0 copy-start.6
  5.1 0.0 copy-start.10
  5.1 0.7 %spectrum.1 = (bf16[8,32,256]{2,1,0:T(8,128)(2,1)S(1)}, f32[2048,256]{1,0:T(8,128)S(1)}) custom-call(bf16[2048,256]{1,0:T(8,128)(2,1)S(1)} %bitcast.13, bf16[4,256,256]{2,1,0:T(8,128)(2,1)S(1)} %copy-done.11, bf16[256,256]{1,0:T(8,128)(2,1)S(1)} %copy-done.2, f32[1,256]{1,0:T(1,128)S(1)} %bitcast.15), custom_call_target="tpu_custom_call" | custom-call | flops 12000000000 | bytes 12582912 | tf_op jit(solution)/shard_map/spectrum/pallas_call | solution.py:436
  5.8 2.2 %collective-permute-done.1.refs_2_ = f32[8,256]{1,0:T(8,128)S(1)} collective-permute-done((f32[8,256]{1,0:T(8,128)S(1)}, f32[8,256]{1,0:T(8,128)S(1)}, u32[]{:S(2)}, u32[]{:S(2)}) %collective-permute-start.1) | collective-permute-done | bytes 8224 | tf_op jit(solution)/shard_map/ppermute | solution.py:426
  8.0 13.2 %all_to_all.20.r_ref.first_ref.refs_0_ = bf16[8,40,256]{2,1,0:T(8,128)(2,1)S(1)} all-to-all(bf16[8,40,256]{2,1,0:T(8,128)(2,1)S(1)} %message.1), channel_id=1, replica_groups=mesh['len'=8,'pipe'=4] {'len'}, dimensions={0} | all-to-all | bytes 327680 | tf_op jit(solution)/shard_map/all_to_all | solution.py:423
  21.2 0.0 copy-start
  21.2 0.0 copy-start.8
  21.2 1.0 %mix.1 = (bf16[8,32,256]{2,1,0:T(8,128)(2,1)S(1)}, f32[1,256]{1,0:T(1,128)S(1)}, f32[8,256]{1,0:T(8,128)S(1)}) custom-call(bf16[8,40,256]{2,1,0:T(8,128)(2,1)S(1)} %all_to_all.20.r_ref.first_ref.refs_0_, bf16[16,256,256]{2,1,0:T(8,128)(2,1)S(1)} %copy-done.5, bf16[16,256,256]{2,1,0:T(8,128)(2,1)S(1)} %copy-done.6, s32[1,32]{1,0:T(1,128)S(1)} %bitcast.8, ...), custom_call_target="tpu_custom_call" | custom-call | flops 12000000000 | bytes 12582912 | tf_op jit(solution)/shard_map/mix/pallas_call | solution.py:450
  22.2 9.7 %all_to_all.21.modes_ref = bf16[8,32,256]{2,1,0:T(8,128)(2,1)S(1)} all-to-all(bf16[8,32,256]{2,1,0:T(8,128)(2,1)S(1)} %get-tuple-element.27), channel_id=1, replica_groups=mesh['len'=8,'pipe'=4] {'len'}, dimensions={0} | all-to-all | bytes 262144 | tf_op jit(solution)/shard_map/all_to_all | solution.py:423
  32.0 1.9 %layer.1 = (bf16[2048,256]{1,0:T(8,128)(2,1)S(1)}, bf16[2048,256]{1,0:T(8,128)(2,1)S(1)}, bf16[8,34,256]{2,1,0:T(8,128)(2,1)S(1)}) custom-call(f32[2048,256]{1,0:T(8,128)S(1)} %get-tuple-element.24.pointwise_ref, bf16[2048,256]{1,0:T(8,128)(2,1)S(1)} %bitcast.14, bf16[4,256,256]{2,1,0:T(8,128)(2,1)S(1)} %copy-done.11, bf16[1024,256]{1,0:T(8,128)(2,1)S(1)} %copy-done, ...), custom_call_target="tpu_custom_call" | custom-call | flops 12000000000 | bytes 12582912 | tf_op jit(solution)/shard_map/layer/pallas_call | solution.py:460
  33.9 10.0 %all_to_all.22.r_ref.second_ref.refs_4_ = bf16[8,34,256]{2,1,0:T(8,128)(2,1)S(1)} all-to-all(bf16[8,34,256]{2,1,0:T(8,128)(2,1)S(1)} %get-tuple-element.28), channel_id=1, replica_groups=mesh['len'=8,'pipe'=4] {'len'}, dimensions={0} | all-to-all | bytes 278528 | tf_op jit(solution)/shard_map/all_to_all | solution.py:423
  43.9 0.8 %collective-permute-start.4 = (bf16[16,34,256]{2,1,0:T(8,128)(2,1)S(1)}, bf16[16,34,256]{2,1,0:T(8,128)(2,1)S(1)}, u32[]{:S(2)}, u32[]{:S(2)}) collective-permute-start(bf16[16,34,256]{2,1,0:T(8,128)(2,1)S(1)} %pack.1), channel_id=1, source_target_pairs={{0,2},{1,3},{2,0},{3,1},{4,6},{5,7},{6,4},{7,5},{8,10},{9,11},{10,... | collective-permute-start | bytes 835592 | tf_op jit(solution)/shard_map/ppermute | solution.py:426
  44.7 1.9 %mix_grad.1 = (bf16[8,32,256]{2,1,0:T(8,128)(2,1)}, bf16[2048,256]{1,0:T(8,128)(2,1)}) custom-call(bf16[8,34,256]{2,1,0:T(8,128)(2,1)S(1)} %all_to_all.22.r_ref.second_ref.refs_4_, bf16[16,256,256]{2,1,0:T(8,128)(2,1)S(1)} %copy-done.5, bf16[16,256,256]{2,1,0:T(8,128)(2,1)S(1)} %copy-done.6, bf16[2048,256]{1,0:T(8,128)(2,1)S(1)} %get-tuple-element.30.early_ref), custom_call_target="tpu_custom_call" | custom-call | flops 12000000000 | bytes 12582912 | tf_op jit(solution)/shard_map/mix_grad/pallas_call | solution.py:476
  46.6 3.4 %all-to-all-start.3 = ((bf16[8,32,256]{2,1,0:T(8,128)(2,1)}), bf16[8,32,256]{2,1,0:T(8,128)(2,1)S(1)}, u32[]{:S(2)}, u32[]{:S(2)}) async-start(bf16[8,32,256]{2,1,0:T(8,128)(2,1)} %get-tuple-element.35), calls=%async_computation.3 | async-start | bytes 262144 | tf_op jit(solution)/shard_map/all_to_all | solution.py:423
  50.0 0.1 collective-permute-start.3
  50.1 0.5 collective-permute-start.6
  50.6 0.5 collective-permute-done.4.both_ref
  51.1 0.1 collective-permute-start.5
  51.1 0.5 collective-permute-start.7
  51.6 0.1 collective-permute-done.6.refs_5_
  51.7 0.8 %collective-permute-done.5.refs_3_ = bf16[8,34,256]{2,1,0:T(8,128)(2,1)S(1)} collective-permute-done((bf16[8,34,256]{2,1,0:T(8,128)(2,1)S(1)}, bf16[8,34,256]{2,1,0:T(8,128)(2,1)S(1)}, u32[]{:S(2)}, u32[]{:S(2)}) %collective-permute-start.5) | collective-permute-done | bytes 139296 | tf_op jit(solution)/shard_map/ppermute | solution.py:426
  52.5 0.2 collective-permute-done.7.refs_7_
  52.8 4.0 %weight_grad.1 = (f32[16,256,256]{2,1,0:T(8,128)}, f32[16,256,256]{2,1,0:T(8,128)}, f32[8,256]{1,0:T(8,128)S(1)}) custom-call(bf16[8,40,256]{2,1,0:T(8,128)(2,1)S(1)} %all_to_all.20.r_ref.first_ref.refs_0_, bf16[8,40,256]{2,1,0:T(8,128)(2,1)S(1)} %collective-permute-done.3.refs_1_, bf16[8,34,256]{2,1,0:T(8,128)(2,1)S(1)} %get-tuple-element.37.refs_2_, ...), custom_call_target="tpu_custom_call" | custom-call | tf_op jit(solution)/shard_map/weight_grad/pallas_call | solution.py:493
  56.8 0.5 all-to-all-done.3.modes_ref
  57.3 1.4 %input_grad.1 = bf16[2048,256]{1,0:T(8,128)(2,1)} custom-call(bf16[2048,256]{1,0:T(8,128)(2,1)S(1)} %get-tuple-element.32.total_ref, bf16[1024,256]{1,0:T(8,128)(2,1)S(1)} %copy-done, bf16[256,256]{1,0:T(8,128)(2,1)S(1)} %copy-done.2, f32[8,256]{1,0:T(8,128)S(1)} %get-tuple-element.41.rows_ref, bf16[8,32,256]{2,1,0:T(8,128)(2,1)S(1)} %all-to-all-done.3.modes_ref), custom_call_target="tpu_custom_call" | custom-call | tf_op jit(solution)/shard_map/input_grad/pallas_call | solution.py:506
  (23 shorter events, 0.1 us)
Async XLA Ops:
  0.6 1.2 %copy-start.7 = (bf16[1,2048,256]{2,1,0:T(8,128)(2,1)S(1)}, bf16[1,2048,256]{2,1,0:T(8,128)(2,1)}, u32[]{:S(2)}) copy-start(bf16[1,2048,256]{2,1,0:T(8,128)(2,1)} %param.12) | copy-start | bytes 3145732
  1.9 3.1 %copy-start.2 = (bf16[256,256]{1,0:T(8,128)(2,1)S(1)}, bf16[256,256]{1,0:T(8,128)(2,1)}, u32[]{:S(2)}) copy-start(bf16[256,256]{1,0:T(8,128)(2,1)} %weight_ref.3) | copy-start | bytes 393220
  1.9 3.1 %copy-start.9 = (f32[256]{0:T(256)S(1)}, f32[256]{0:T(256)}, u32[]{:S(2)}) copy-start(f32[256]{0:T(256)} %param.15) | copy-start | bytes 3076
  1.9 3.1 %copy-start.11 = (bf16[4,256,256]{2,1,0:T(8,128)(2,1)S(1)}, bf16[4,256,256]{2,1,0:T(8,128)(2,1)}, u32[]{:S(2)}) copy-start(bf16[4,256,256]{2,1,0:T(8,128)(2,1)} %constant.4.clone.f_ref) | copy-start | bytes 1572868
  1.9 3.9 %collective-permute-start.2 = (f32[8,256]{1,0:T(8,128)S(1)}, f32[8,256]{1,0:T(8,128)S(1)}, u32[]{:S(2)}, u32[]{:S(2)}) collective-permute-start(f32[8,256]{1,0:T(8,128)S(1)} %pipe_ends.1.refs_0_), channel_id=1, source_target_pairs={{0,3},{1,2},{2,1},{3,0},{4,7},{5,6},{6,5},{7,4},{8,11},{9,10},{10,... | collective-permute-start | bytes 24584 | tf_op jit(solution)/shard_map/ppermute | solution.py:426
  4.3 3.7 %collective-permute-start.1 = (f32[8,256]{1,0:T(8,128)S(1)}, f32[8,256]{1,0:T(8,128)S(1)}, u32[]{:S(2)}, u32[]{:S(2)}) collective-permute-start(f32[8,256]{1,0:T(8,128)S(1)} %pipe_ends.1.refs_0_), channel_id=1, source_target_pairs={{0,2},{1,3},{2,0},{3,1},{4,6},{5,7},{6,4},{7,5},{8,10},{9,11},{10,... | collective-permute-start | bytes 24584 | tf_op jit(solution)/shard_map/ppermute | solution.py:426
  5.0 3.0 %collective-permute-start = (f32[8,256]{1,0:T(8,128)S(1)}, f32[8,256]{1,0:T(8,128)S(1)}, u32[]{:S(2)}, u32[]{:S(2)}) collective-permute-start(f32[8,256]{1,0:T(8,128)S(1)} %pipe_ends.1.refs_0_), channel_id=1, source_target_pairs={{0,1},{1,0},{2,3},{3,2},{4,5},{5,4},{6,7},{7,6},{8,9},{9,8},{10,11... | collective-permute-start | bytes 24584 | tf_op jit(solution)/shard_map/ppermute | solution.py:426
  5.0 16.2 %copy-start.1 = (bf16[256,256]{1,0:T(8,128)(2,1)S(1)}, bf16[256,256]{1,0:T(8,128)(2,1)}, u32[]{:S(2)}) copy-start(bf16[256,256]{1,0:T(8,128)(2,1)} %refs_10_.1) | copy-start | bytes 393220
  5.0 16.2 %copy-start.3 = (s32[32]{0:T(128)S(1)}, s32[32]{0:T(128)}, u32[]{:S(2)}) copy-start(s32[32]{0:T(128)} %param.20) | copy-start | bytes 388
  5.0 16.2 %copy-start.4 = (s32[32]{0:T(128)S(1)}, s32[32]{0:T(128)}, u32[]{:S(2)}) copy-start(s32[32]{0:T(128)} %param.21) | copy-start | bytes 388
  5.0 16.2 %copy-start.5 = (bf16[16,256,256]{2,1,0:T(8,128)(2,1)S(1)}, bf16[16,256,256]{2,1,0:T(8,128)(2,1)}, u32[]{:S(2)}) copy-start(bf16[16,256,256]{2,1,0:T(8,128)(2,1)} %real_ref.3) | copy-start | bytes 6291460
  5.0 16.2 %copy-start.6 = (bf16[16,256,256]{2,1,0:T(8,128)(2,1)S(1)}, bf16[16,256,256]{2,1,0:T(8,128)(2,1)}, u32[]{:S(2)}) copy-start(bf16[16,256,256]{2,1,0:T(8,128)(2,1)} %imag_ref.3) | copy-start | bytes 6291460
  5.1 16.2 %copy-start.10 = (f32[256]{0:T(256)S(1)}, f32[256]{0:T(256)}, u32[]{:S(2)}) copy-start(f32[256]{0:T(256)} %param.19) | copy-start | bytes 3076
  21.2 10.7 %copy-start = (bf16[1024,256]{1,0:T(8,128)(2,1)S(1)}, bf16[1024,256]{1,0:T(8,128)(2,1)}, u32[]{:S(2)}) copy-start(bf16[1024,256]{1,0:T(8,128)(2,1)} %constant.5.clone.ft_ref) | copy-start | bytes 1572868
  21.2 10.7 %copy-start.8 = (bf16[1,2048,256]{2,1,0:T(8,128)(2,1)S(1)}, bf16[1,2048,256]{2,1,0:T(8,128)(2,1)}, u32[]{:S(2)}) copy-start(bf16[1,2048,256]{2,1,0:T(8,128)(2,1)} %param.13) | copy-start | bytes 3145732
  43.9 7.1 %collective-permute-start.4 = (bf16[16,34,256]{2,1,0:T(8,128)(2,1)S(1)}, bf16[16,34,256]{2,1,0:T(8,128)(2,1)S(1)}, u32[]{:S(2)}, u32[]{:S(2)}) collective-permute-start(bf16[16,34,256]{2,1,0:T(8,128)(2,1)S(1)} %pack.1), channel_id=1, source_target_pairs={{0,2},{1,3},{2,0},{3,1},{4,6},{5,7},{6,4},{7,5},{8,10},{9,11},{10,... | collective-permute-start | bytes 835592 | tf_op jit(solution)/shard_map/ppermute | solution.py:426
  46.6 10.7 %all-to-all-start.3 = ((bf16[8,32,256]{2,1,0:T(8,128)(2,1)}), bf16[8,32,256]{2,1,0:T(8,128)(2,1)S(1)}, u32[]{:S(2)}, u32[]{:S(2)}) async-start(bf16[8,32,256]{2,1,0:T(8,128)(2,1)} %get-tuple-element.35), calls=%async_computation.3 | async-start | bytes 262144 | tf_op jit(solution)/shard_map/all_to_all | solution.py:423
  50.0 1.7 %collective-permute-start.3 = (bf16[8,40,256]{2,1,0:T(8,128)(2,1)S(1)}, bf16[8,40,256]{2,1,0:T(8,128)(2,1)S(1)}, u32[]{:S(2)}, u32[]{:S(2)}) collective-permute-start(bf16[8,40,256]{2,1,0:T(8,128)(2,1)S(1)} %all_to_all.20.r_ref.first_ref.refs_0_), channel_id=1, source_target_pairs={{0,1},{1,0},{2,3},{3,2},{4,5},{5,4},{6,7},{7,6},{8,9},{9,8},{10,11... | collective-permute-start | bytes 491528 | tf_op jit(solution)/shard_map/ppermute | solution.py:426
  50.1 1.6 %collective-permute-start.6 = (bf16[8,34,256]{2,1,0:T(8,128)(2,1)S(1)}, bf16[8,34,256]{2,1,0:T(8,128)(2,1)S(1)}, u32[]{:S(2)}, u32[]{:S(2)}) collective-permute-start(bf16[8,34,256]{2,1,0:T(8,128)(2,1)S(1)} %all_to_all.22.r_ref.second_ref.refs_4_), channel_id=1, source_target_pairs={{0,1},{1,0},{2,3},{3,2},{4,5},{5,4},{6,7},{7,6},{8,9},{9,8},{10,11... | collective-permute-start | bytes 417800 | tf_op jit(solution)/shard_map/ppermute | solution.py:426
  51.1 1.5 %collective-permute-start.5 = (bf16[8,34,256]{2,1,0:T(8,128)(2,1)S(1)}, bf16[8,34,256]{2,1,0:T(8,128)(2,1)S(1)}, u32[]{:S(2)}, u32[]{:S(2)}) collective-permute-start(bf16[8,34,256]{2,1,0:T(8,128)(2,1)S(1)} %get-tuple-element.37.refs_2_), channel_id=1, source_target_pairs={{0,1},{1,0},{2,3},{3,2},{4,5},{5,4},{6,7},{7,6},{8,9},{9,8},{10,11... | collective-permute-start | bytes 417800 | tf_op jit(solution)/shard_map/ppermute | solution.py:426
  51.1 1.6 %collective-permute-start.7 = (bf16[8,34,256]{2,1,0:T(8,128)(2,1)S(1)}, bf16[8,34,256]{2,1,0:T(8,128)(2,1)S(1)}, u32[]{:S(2)}, u32[]{:S(2)}) collective-permute-start(bf16[8,34,256]{2,1,0:T(8,128)(2,1)S(1)} %get-tuple-element.39.refs_6_), channel_id=1, source_target_pairs={{0,1},{1,0},{2,3},{3,2},{4,5},{5,4},{6,7},{7,6},{8,9},{9,8},{10,11... | collective-permute-start | bytes 417800 | tf_op jit(solution)/shard_map/ppermute | solution.py:426

commit v18 on v17

--- a/solution.py
+++ b/solution.py
@@ -221,8 +221,7 @@
     out_ref,
     total_ref,
     msg_ref,
-    low_ref,
-    high_ref,
+    spectral_ref,
 ):
     steps, all_rows, tile = f_ref.shape
     half = steps * tile
@@ -238,11 +237,15 @@
     )
     modes = modes * doubled
     modes = (modes.astype(jnp.bfloat16), (modes * signs).astype(jnp.bfloat16))
-    for side, acc_ref in enumerate((low_ref, high_ref)):
+    for side in range(2):
+        spectral_ref[side * half : (side + 1) * half, :] = dot(ft_ref[...], modes[side])
+    sums = []
+    for side in range(2):
+        terms = None
         for step in range(steps):
             at = pl.ds(side * half + step * tile, tile)
-            spectral = dot(ft_ref[pl.ds(step * tile, tile), :], modes[side])
-            summed = pointwise_ref[at, :] + (spectral + cond).astype(jnp.bfloat16).astype(jnp.float32)
+            pre = (spectral_ref[at, :] + cond).astype(jnp.bfloat16).astype(jnp.float32)
+            summed = pointwise_ref[at, :] + pre
             square = summed * summed
             part = 0.5 + 0.5 * jnp.tanh(summed * (GELU_S + (GELU_S * GELU_C) * square))
             result = summed * part
@@ -252,12 +255,12 @@
             )
             total = (cot_ref[at, :].astype(jnp.float32) * slope).astype(jnp.bfloat16)
             total_ref[at, :] = total
-            term = dot(f_ref[step], total)
-            if step == 0:
-                acc_ref[...] = term
-            else:
-                acc_ref[...] += term
-    acc = low_ref[...] + signs * high_ref[...]
+        for step in range(steps):
+            at = pl.ds(side * half + step * tile, tile)
+            term = dot(f_ref[step], total_ref[at, :])
+            terms = term if terms is None else terms + term
+        sums.append(terms)
+    acc = sums[0] + signs * sums[1]
     grad_cond = acc[0:1, :] * (1.0 / f_ref[0, 0:1, 0:1].astype(jnp.float32))
     upper = grad_cond.astype(jnp.bfloat16).astype(jnp.float32)
     extra = extra_rows(upper, grad_cond - upper, rows - span, channels)
@@ -270,8 +273,9 @@
 def weight_grad_kernel(pipes, modes, per_copy, *refs):
     fields, grads, refs = refs[:pipes], refs[pipes : 2 * pipes], refs[2 * pipes :]
     (inlet_ref, outlet_ref, junc_weight_ref, slope_ref), refs = refs[:4], refs[4:]
-    real_out, imag_out, rows_ref, x_ref, g_ref, real_ref, imag_ref = refs[:7]
-    first_ref, last_ref, upper_ref, lower_ref, sems = refs[7:]
+    total_ref, weight_ref, real_out, imag_out, rows_ref, local_ref = refs[:6]
+    x_ref, g_ref, real_ref, imag_ref = refs[6:10]
+    first_ref, last_ref, upper_ref, lower_ref, sems = refs[10:]
     groups, rows = grads[0].shape[0], grads[0].shape[1]
     span = 2 * modes
     for step in range(pipes):
@@ -314,6 +318,7 @@
     act_grad = (junc_grad * slope_ref[...]).astype(jnp.bfloat16)
     sums_grad = dot(act_grad, junc_weight_ref[...], 1, 1)
     rows_ref[...] = sums_grad.astype(jnp.bfloat16).astype(jnp.float32)
+    local_ref[...] = dot(total_ref[...], weight_ref[...], 1, 1)
     wait(going)
 
 
@@ -330,7 +335,7 @@
 
 
 def input_grad_kernel(
-    total_ref, ft_ref, weight_ref, rows_ref, modes_ref, out_ref, tiles_ref, sems
+    local_ref, ft_ref, rows_ref, modes_ref, out_ref, cells_ref, tiles_ref, sems
 ):
     groups, span, channels = modes_ref.shape
     steps, tile = tiles_ref.shape[0], tiles_ref.shape[2]
@@ -340,20 +345,20 @@
     )
     signs = row_signs(all_rows, span, channels)
     back = (back.astype(jnp.bfloat16), (back * signs).astype(jnp.bfloat16))
-    weight = weight_ref[...]
     row = lax.broadcasted_iota(jnp.int32, (tile, channels), 0)
+    for side in range(2):
+        cells_ref[side * half : (side + 1) * half, :] = dot(ft_ref[...], back[side])
     going = []
     for side in range(2):
         for step in range(steps):
             at = pl.ds(side * half + step * tile, tile)
-            grad_cells = dot(ft_ref[pl.ds(step * tile, tile), :], back[side])
+            grad_cells = cells_ref[at, :]
             if step == 0 and side == 0:
                 grad_cells = grad_cells + jnp.where(row == 0, rows_ref[0:1, :], 0.0)
             if step == steps - 1 and side == 1:
                 grad_cells = grad_cells + jnp.where(row == tile - 1, rows_ref[1:2, :], 0.0)
             spread = grad_cells.astype(jnp.bfloat16).astype(jnp.float32)
-            local = dot(total_ref[at, :], weight, 1, 1)
-            tiles_ref[step, side] = (local + spread).astype(jnp.bfloat16)
+            tiles_ref[step, side] = (local_ref[at, :] + spread).astype(jnp.bfloat16)
             going += started(
                 [
                     pltpu.make_async_copy(
@@ -461,7 +466,7 @@
         layer_kernel,
         [shape(field.shape, bf16)] * 2 + [message],
         [VMEM] * 6,
-        [pltpu.VMEM((all_rows, channels), f32)] * 2,
+        [pltpu.VMEM(field.shape, f32)],
         name="layer",
         busy=12,
     )(pointwise, cot, f_table, ft_table, cond, returned)
@@ -490,27 +495,28 @@
     returned = exchange(mixed)
     big = shape((modes, channels, channels), f32)
     per_copy = math.gcd(modes, 2)
-    grad_real, grad_imag, rows = call(
+    grad_real, grad_imag, rows, local = call(
         functools.partial(weight_grad_kernel, pipes, modes, per_copy),
-        [big, big, shape((8, channels), f32)],
-        [VMEM] * (2 * pipes + 4),
+        [big, big, shape((8, channels), f32), shape(field.shape, f32)],
+        [VMEM] * (2 * pipes + 6),
         [rows_of(pipes * all_rows, channels)] * 2
         + [pltpu.VMEM(big.shape, f32)] * 2
         + pipe_rows
         + [pltpu.VMEM((groups, channels), f32)] * 2
         + [dma((modes // per_copy, 2))],
-        out_specs=[HBM, HBM, VMEM],
+        out_specs=[HBM, HBM, VMEM, VMEM],
         name="weight_grad",
         limit=16,
-    )(*fields, *grads, inlet_row, outlet_row, junc_weight, slope)
+    )(*fields, *grads, inlet_row, outlet_row, junc_weight, slope, total, point_weight)
     (grad_inputs,) = call(
         input_grad_kernel,
         [shape(field.shape, bf16)],
-        [VMEM] * 5,
-        [pltpu.VMEM((steps, 2, TILE, channels), bf16), dma((steps, 2))],
+        [VMEM] * 4,
+        [pltpu.VMEM(field.shape, f32)]
+        + [pltpu.VMEM((steps, 2, TILE, channels), bf16), dma((steps, 2))],
         out_specs=[HBM],
         name="input_grad",
-    )(total, ft_table, point_weight, rows, returned)
+    )(local, ft_table, rows, returned)
     return (
         outputs.reshape(inputs.shape),
         grad_inputs.reshape(inputs.shape),

time: 59.1 us -> 62.5 us (1.058)
  local copies, waits for them, and re-layouts: 1.28 us -> 4.12 us
  waiting for transfers between devices: 4.27 us -> 3.29 us
  Pallas kernels: 11.1 us -> 11.9 us
  starting transfers between devices: 8.42 us -> 9.06 us
    unnamed x24 -> x30, local copies, waits for them, and re-layouts: 1.28 us -> 4.12 us
    pallas_call x1, Pallas kernels: 1.45 us -> 2.25 us  [body(): call(input_grad_kernel, [shape(field.shape, bf16)], [VMEM] * 4, [pltpu.VM...]
    all_to_all x1, starting transfers between devices: 3.38 us -> 4.01 us  [exchange(): return lax.all_to_all(value, 'len', split_axis=0, concat_axis=0, tiled=True)]
  transfers between devices with their start and end apart: 9 -> 9, of which waited for: 6 -> 4; matrix products, arithmetic and copies ran while one was open for 0% -> 0% of each run, Pallas kernels for 11% -> 11%
where the time goes in v18:
time: 62.5 us; the launch traced here: 62.1 us
  blocking collectives  32.9 us (53%)
  Pallas kernels  11.9 us (19%)
  starting transfers between devices  9.06 us (14%)
  local copies, waits for them, and re-layouts  4.12 us (7%)
  waiting for transfers between devices  3.29 us (5%)
  between operations  0.84 us (1%)
    all_to_all x3, blocking collectives, exchange(): return lax.all_to_all(value, 'len', split_axis=0, concat_axis=0, tiled=True)  32.9 us
    ppermute x8, starting transfers between devices, swap(): return lax.ppermute(value, 'pipe', [(i, i ^ step) for i in range(pipes)])  5.04 us
    unnamed x30, local copies, waits for them, and re-layouts  4.12 us
    all_to_all x1, starting transfers between devices, exchange(): return lax.all_to_all(value, 'len', split_axis=0, concat_axis=0, tiled=True)  4.01 us
    pallas_call x1, Pallas kernels, body(): call(functools.partial(weight_grad_kernel, pipes, modes, per_copy), [big,...  3.99 us
    ppermute x8, waiting for transfers between devices, swap(): return lax.ppermute(value, 'pipe', [(i, i ^ step) for i in range(pipes)])  3.29 us
    pallas_call x1, Pallas kernels, body(): call(input_grad_kernel, [shape(field.shape, bf16)], [VMEM] * 4, [pltpu.VM...  2.25 us
    pallas_call x1, Pallas kernels, body(): call(mix_grad_kernel, [chunks, early], [VMEM] * 4, [dma] + mix_bufs, out_...  1.94 us
  transfers between devices with their start and end apart: 9, of which 4 were waited for; matrix products, arithmetic and copies ran while one was open for 0% of the time, Pallas kernels for 11%

profile of v18, /device:TPU:0, one launch (start us, length us, event | category | flops | bytes accessed | tf_op | source)
XLA Modules:
  0.0 62.1 jit_solution(9804978309370730989)
XLA Ops:
  0.6 1.2 %copy-done.10 = bf16[1,2048,256]{2,1,0:T(8,128)(2,1)S(1)} copy-done((bf16[1,2048,256]{2,1,0:T(8,128)(2,1)S(1)}, bf16[1,2048,256]{2,1,0:T(8,128)(2,1)}, u32[]{:S(2)}) %copy-start.10) | copy-done | bytes 1048600
  1.9 2.4 %collective-permute-start.2 = (f32[8,256]{1,0:T(8,128)S(1)}, f32[8,256]{1,0:T(8,128)S(1)}, u32[]{:S(2)}, u32[]{:S(2)}) collective-permute-start(f32[8,256]{1,0:T(8,128)S(1)} %pipe_ends.1.refs_0_), channel_id=1, source_target_pairs={{0,3},{1,2},{2,1},{3,0},{4,7},{5,6},{6,5},{7,4},{8,11},{9,10},{10,... | collective-permute-start | bytes 24584 | tf_op jit(solution)/shard_map/ppermute | solution.py:431
  4.3 0.6 %collective-permute-start.1 = (f32[8,256]{1,0:T(8,128)S(1)}, f32[8,256]{1,0:T(8,128)S(1)}, u32[]{:S(2)}, u32[]{:S(2)}) collective-permute-start(f32[8,256]{1,0:T(8,128)S(1)} %pipe_ends.1.refs_0_), channel_id=1, source_target_pairs={{0,2},{1,3},{2,0},{3,1},{4,6},{5,7},{6,4},{7,5},{8,10},{9,11},{10,... | collective-permute-start | bytes 24584 | tf_op jit(solution)/shard_map/ppermute | solution.py:431
  5.0 0.0 collective-permute-start
  5.0 0.0 copy-start.6
  5.0 0.0 copy-start.7
  5.0 0.0 copy-start.8
  5.1 0.7 %spectrum.1 = (bf16[8,32,256]{2,1,0:T(8,128)(2,1)S(1)}, f32[2048,256]{1,0:T(8,128)S(1)}) custom-call(bf16[2048,256]{1,0:T(8,128)(2,1)S(1)} %bitcast.13, bf16[4,256,256]{2,1,0:T(8,128)(2,1)S(1)} %copy-done.14, bf16[256,256]{1,0:T(8,128)(2,1)S(1)} %copy-done.2, f32[1,256]{1,0:T(1,128)S(1)} %bitcast.15), custom_call_target="tpu_custom_call" | custom-call | flops 12000000000 | bytes 12582912 | tf_op jit(solution)/shard_map/spectrum/pallas_call | solution.py:441
  5.8 2.2 %collective-permute-done.1.refs_2_ = f32[8,256]{1,0:T(8,128)S(1)} collective-permute-done((f32[8,256]{1,0:T(8,128)S(1)}, f32[8,256]{1,0:T(8,128)S(1)}, u32[]{:S(2)}, u32[]{:S(2)}) %collective-permute-start.1) | collective-permute-done | bytes 8224 | tf_op jit(solution)/shard_map/ppermute | solution.py:431
  8.0 13.2 %all_to_all.20.r_ref.first_ref.refs_0_ = bf16[8,40,256]{2,1,0:T(8,128)(2,1)S(1)} all-to-all(bf16[8,40,256]{2,1,0:T(8,128)(2,1)S(1)} %message.1), channel_id=1, replica_groups=mesh['len'=8,'pipe'=4] {'len'}, dimensions={0} | all-to-all | bytes 327680 | tf_op jit(solution)/shard_map/all_to_all | solution.py:428
  21.2 0.0 copy-start
  21.2 0.0 copy-start.11
  21.2 1.0 %mix.1 = (bf16[8,32,256]{2,1,0:T(8,128)(2,1)S(1)}, f32[1,256]{1,0:T(1,128)S(1)}, f32[8,256]{1,0:T(8,128)S(1)}) custom-call(bf16[8,40,256]{2,1,0:T(8,128)(2,1)S(1)} %all_to_all.20.r_ref.first_ref.refs_0_, bf16[16,256,256]{2,1,0:T(8,128)(2,1)S(1)} %copy-done.8, bf16[16,256,256]{2,1,0:T(8,128)(2,1)S(1)} %copy-done.9, s32[1,32]{1,0:T(1,128)S(1)} %bitcast.8, ...), custom_call_target="tpu_custom_call" | custom-call | flops 12000000000 | bytes 12582912 | tf_op jit(solution)/shard_map/mix/pallas_call | solution.py:455
  22.2 9.7 %all_to_all.21.modes_ref = bf16[8,32,256]{2,1,0:T(8,128)(2,1)S(1)} all-to-all(bf16[8,32,256]{2,1,0:T(8,128)(2,1)S(1)} %get-tuple-element.28), channel_id=1, replica_groups=mesh['len'=8,'pipe'=4] {'len'}, dimensions={0} | all-to-all | bytes 262144 | tf_op jit(solution)/shard_map/all_to_all | solution.py:428
  32.0 1.9 %layer.1 = (bf16[2048,256]{1,0:T(8,128)(2,1)S(1)}, bf16[2048,256]{1,0:T(8,128)(2,1)S(1)}, bf16[8,34,256]{2,1,0:T(8,128)(2,1)S(1)}) custom-call(f32[2048,256]{1,0:T(8,128)S(1)} %get-tuple-element.25.pointwise_ref, bf16[2048,256]{1,0:T(8,128)(2,1)S(1)} %bitcast.14, bf16[4,256,256]{2,1,0:T(8,128)(2,1)S(1)} %copy-done.14, bf16[1024,256]{1,0:T(8,128)(2,1)S(1)} %copy-done, ...), custom_call_target="tpu_custom_call" | custom-call | flops 12000000000 | bytes 12582912 | tf_op jit(solution)/shard_map/layer/pallas_call | solution.py:465
  33.9 10.0 %all_to_all.22.r_ref.second_ref.refs_4_ = bf16[8,34,256]{2,1,0:T(8,128)(2,1)S(1)} all-to-all(bf16[8,34,256]{2,1,0:T(8,128)(2,1)S(1)} %get-tuple-element.29), channel_id=1, replica_groups=mesh['len'=8,'pipe'=4] {'len'}, dimensions={0} | all-to-all | bytes 278528 | tf_op jit(solution)/shard_map/all_to_all | solution.py:428
  43.9 0.8 %collective-permute-start.4 = (bf16[16,34,256]{2,1,0:T(8,128)(2,1)S(1)}, bf16[16,34,256]{2,1,0:T(8,128)(2,1)S(1)}, u32[]{:S(2)}, u32[]{:S(2)}) collective-permute-start(bf16[16,34,256]{2,1,0:T(8,128)(2,1)S(1)} %pack.1), channel_id=1, source_target_pairs={{0,2},{1,3},{2,0},{3,1},{4,6},{5,7},{6,4},{7,5},{8,10},{9,11},{10,... | collective-permute-start | bytes 835592 | tf_op jit(solution)/shard_map/ppermute | solution.py:431
  44.7 1.9 %mix_grad.1 = (bf16[8,32,256]{2,1,0:T(8,128)(2,1)}, bf16[2048,256]{1,0:T(8,128)(2,1)}) custom-call(bf16[8,34,256]{2,1,0:T(8,128)(2,1)S(1)} %all_to_all.22.r_ref.second_ref.refs_4_, bf16[16,256,256]{2,1,0:T(8,128)(2,1)S(1)} %copy-done.8, bf16[16,256,256]{2,1,0:T(8,128)(2,1)S(1)} %copy-done.9, bf16[2048,256]{1,0:T(8,128)(2,1)S(1)} %get-tuple-element.31.early_ref), custom_call_target="tpu_custom_call" | custom-call | flops 12000000000 | bytes 12582912 | tf_op jit(solution)/shard_map/mix_grad/pallas_call | solution.py:481
  46.6 4.0 %all-to-all-start.3 = ((bf16[8,32,256]{2,1,0:T(8,128)(2,1)}), bf16[8,32,256]{2,1,0:T(8,128)(2,1)}, u32[]{:S(2)}, u32[]{:S(2)}) async-start(bf16[8,32,256]{2,1,0:T(8,128)(2,1)} %get-tuple-element.35), calls=%async_computation.3 | async-start | bytes 262144 | tf_op jit(solution)/shard_map/all_to_all | solution.py:428
  50.6 0.1 collective-permute-start.3
  50.7 0.5 collective-permute-start.6
  51.2 0.1 collective-permute-start.5
  51.4 0.4 collective-permute-start.7
  51.8 0.5 collective-permute-done.6.refs_5_
  52.3 0.4 collective-permute-done.5.refs_3_
  52.7 0.2 collective-permute-done.7.refs_7_
  52.9 0.9 %copy-done.3 = bf16[256,256]{1,0:T(8,128)(2,1)S(1)} copy-done((bf16[256,256]{1,0:T(8,128)(2,1)S(1)}, bf16[256,256]{1,0:T(8,128)(2,1)}, u32[]{:S(2)}) %copy-start.3) | copy-done | bytes 131096
  53.8 0.9 %copy-done.5 = bf16[256,256]{1,0:T(8,128)(2,1)S(1)} copy-done((bf16[256,256]{1,0:T(8,128)(2,1)S(1)}, bf16[256,256]{1,0:T(8,128)(2,1)}, u32[]{:S(2)}) %copy-start.5) | copy-done | bytes 131096
  54.8 4.0 %weight_grad.1 = (f32[16,256,256]{2,1,0:T(8,128)}, f32[16,256,256]{2,1,0:T(8,128)}, f32[8,256]{1,0:T(8,128)S(1)}, f32[2048,256]{1,0:T(8,128)S(1)}) custom-call(bf16[8,40,256]{2,1,0:T(8,128)(2,1)S(1)} %all_to_all.20.r_ref.first_ref.refs_0_, bf16[8,40,256]{2,1,0:T(8,128)(2,1)S(1)} %collective-permute-done.3.refs_1_, ...), custom_call_target="tpu_custom_call" | custom-call | tf_op jit(solution)/shard_map/weight_grad/pallas_call | solution.py:498
  58.8 0.0 copy-start.1
  58.8 1.0 %copy-done.1 = bf16[1024,256]{1,0:T(8,128)(2,1)S(1)} copy-done((bf16[1024,256]{1,0:T(8,128)(2,1)S(1)}, bf16[1024,256]{1,0:T(8,128)(2,1)}, u32[]{:S(2)}) %copy-start.1) | copy-done | bytes 524312
  59.8 2.2 %input_grad.1 = bf16[2048,256]{1,0:T(8,128)(2,1)} custom-call(f32[2048,256]{1,0:T(8,128)S(1)} %get-tuple-element.42.local_ref, bf16[1024,256]{1,0:T(8,128)(2,1)S(1)} %copy-done.1, f32[8,256]{1,0:T(8,128)S(1)} %get-tuple-element.43.rows_ref, bf16[8,32,256]{2,1,0:T(8,128)(2,1)} %all-to-all-done.3.modes_ref), custom_call_target="tpu_custom_call" | custom-call | tf_op jit(solution)/shard_map/input_grad/pallas_call | solution.py:511
  (29 shorter events, 0.1 us)
Async XLA Ops:
  0.6 1.2 %copy-start.10 = (bf16[1,2048,256]{2,1,0:T(8,128)(2,1)S(1)}, bf16[1,2048,256]{2,1,0:T(8,128)(2,1)}, u32[]{:S(2)}) copy-start(bf16[1,2048,256]{2,1,0:T(8,128)(2,1)} %param.12) | copy-start | bytes 3145732
  1.9 3.1 %copy-start.2 = (bf16[256,256]{1,0:T(8,128)(2,1)S(1)}, bf16[256,256]{1,0:T(8,128)(2,1)}, u32[]{:S(2)}) copy-start(bf16[256,256]{1,0:T(8,128)(2,1)} %refs_13_.1) | copy-start | bytes 393220
  1.9 3.1 %copy-start.12 = (f32[256]{0:T(256)S(1)}, f32[256]{0:T(256)}, u32[]{:S(2)}) copy-start(f32[256]{0:T(256)} %param.15) | copy-start | bytes 3076
  1.9 3.1 %copy-start.14 = (bf16[4,256,256]{2,1,0:T(8,128)(2,1)S(1)}, bf16[4,256,256]{2,1,0:T(8,128)(2,1)}, u32[]{:S(2)}) copy-start(bf16[4,256,256]{2,1,0:T(8,128)(2,1)} %constant.4.clone.f_ref) | copy-start | bytes 1572868
  1.9 3.9 %collective-permute-start.2 = (f32[8,256]{1,0:T(8,128)S(1)}, f32[8,256]{1,0:T(8,128)S(1)}, u32[]{:S(2)}, u32[]{:S(2)}) collective-permute-start(f32[8,256]{1,0:T(8,128)S(1)} %pipe_ends.1.refs_0_), channel_id=1, source_target_pairs={{0,3},{1,2},{2,1},{3,0},{4,7},{5,6},{6,5},{7,4},{8,11},{9,10},{10,... | collective-permute-start | bytes 24584 | tf_op jit(solution)/shard_map/ppermute | solution.py:431
  4.3 3.7 %collective-permute-start.1 = (f32[8,256]{1,0:T(8,128)S(1)}, f32[8,256]{1,0:T(8,128)S(1)}, u32[]{:S(2)}, u32[]{:S(2)}) collective-permute-start(f32[8,256]{1,0:T(8,128)S(1)} %pipe_ends.1.refs_0_), channel_id=1, source_target_pairs={{0,2},{1,3},{2,0},{3,1},{4,6},{5,7},{6,4},{7,5},{8,10},{9,11},{10,... | collective-permute-start | bytes 24584 | tf_op jit(solution)/shard_map/ppermute | solution.py:431
  5.0 3.0 %collective-permute-start = (f32[8,256]{1,0:T(8,128)S(1)}, f32[8,256]{1,0:T(8,128)S(1)}, u32[]{:S(2)}, u32[]{:S(2)}) collective-permute-start(f32[8,256]{1,0:T(8,128)S(1)} %pipe_ends.1.refs_0_), channel_id=1, source_target_pairs={{0,1},{1,0},{2,3},{3,2},{4,5},{5,4},{6,7},{7,6},{8,9},{9,8},{10,11... | collective-permute-start | bytes 24584 | tf_op jit(solution)/shard_map/ppermute | solution.py:431
  5.0 16.2 %copy-start.4 = (bf16[256,256]{1,0:T(8,128)(2,1)S(1)}, bf16[256,256]{1,0:T(8,128)(2,1)}, u32[]{:S(2)}) copy-start(bf16[256,256]{1,0:T(8,128)(2,1)} %refs_10_.1) | copy-start | bytes 393220
  5.0 16.2 %copy-start.6 = (s32[32]{0:T(128)S(1)}, s32[32]{0:T(128)}, u32[]{:S(2)}) copy-start(s32[32]{0:T(128)} %param.20) | copy-start | bytes 388
  5.0 16.2 %copy-start.7 = (s32[32]{0:T(128)S(1)}, s32[32]{0:T(128)}, u32[]{:S(2)}) copy-start(s32[32]{0:T(128)} %param.21) | copy-start | bytes 388
  5.0 16.2 %copy-start.8 = (bf16[16,256,256]{2,1,0:T(8,128)(2,1)S(1)}, bf16[16,256,256]{2,1,0:T(8,128)(2,1)}, u32[]{:S(2)}) copy-start(bf16[16,256,256]{2,1,0:T(8,128)(2,1)} %real_ref.3) | copy-start | bytes 6291460
  5.0 16.2 %copy-start.9 = (bf16[16,256,256]{2,1,0:T(8,128)(2,1)S(1)}, bf16[16,256,256]{2,1,0:T(8,128)(2,1)}, u32[]{:S(2)}) copy-start(bf16[16,256,256]{2,1,0:T(8,128)(2,1)} %imag_ref.3) | copy-start | bytes 6291460
  5.1 16.2 %copy-start.13 = (f32[256]{0:T(256)S(1)}, f32[256]{0:T(256)}, u32[]{:S(2)}) copy-start(f32[256]{0:T(256)} %param.19) | copy-start | bytes 3076
  21.2 10.8 %copy-start = (bf16[1024,256]{1,0:T(8,128)(2,1)S(1)}, bf16[1024,256]{1,0:T(8,128)(2,1)}, u32[]{:S(2)}) copy-start(bf16[1024,256]{1,0:T(8,128)(2,1)} %constant.5.clone.ft_ref) | copy-start | bytes 1572868
  21.2 10.8 %copy-start.11 = (bf16[1,2048,256]{2,1,0:T(8,128)(2,1)S(1)}, bf16[1,2048,256]{2,1,0:T(8,128)(2,1)}, u32[]{:S(2)}) copy-start(bf16[1,2048,256]{2,1,0:T(8,128)(2,1)} %param.13) | copy-start | bytes 3145732
  43.9 7.3 %collective-permute-start.4 = (bf16[16,34,256]{2,1,0:T(8,128)(2,1)S(1)}, bf16[16,34,256]{2,1,0:T(8,128)(2,1)S(1)}, u32[]{:S(2)}, u32[]{:S(2)}) collective-permute-start(bf16[16,34,256]{2,1,0:T(8,128)(2,1)S(1)} %pack.1), channel_id=1, source_target_pairs={{0,2},{1,3},{2,0},{3,1},{4,6},{5,7},{6,4},{7,5},{8,10},{9,11},{10,... | collective-permute-start | bytes 835592 | tf_op jit(solution)/shard_map/ppermute | solution.py:431
  46.6 12.1 %all-to-all-start.3 = ((bf16[8,32,256]{2,1,0:T(8,128)(2,1)}), bf16[8,32,256]{2,1,0:T(8,128)(2,1)}, u32[]{:S(2)}, u32[]{:S(2)}) async-start(bf16[8,32,256]{2,1,0:T(8,128)(2,1)} %get-tuple-element.35), calls=%async_computation.3 | async-start | bytes 262144 | tf_op jit(solution)/shard_map/all_to_all | solution.py:428
  50.6 1.7 %collective-permute-start.3 = (bf16[8,40,256]{2,1,0:T(8,128)(2,1)S(1)}, bf16[8,40,256]{2,1,0:T(8,128)(2,1)S(1)}, u32[]{:S(2)}, u32[]{:S(2)}) collective-permute-start(bf16[8,40,256]{2,1,0:T(8,128)(2,1)S(1)} %all_to_all.20.r_ref.first_ref.refs_0_), channel_id=1, source_target_pairs={{0,1},{1,0},{2,3},{3,2},{4,5},{5,4},{6,7},{7,6},{8,9},{9,8},{10,11... | collective-permute-start | bytes 491528 | tf_op jit(solution)/shard_map/ppermute | solution.py:431
  50.7 1.6 %collective-permute-start.6 = (bf16[8,34,256]{2,1,0:T(8,128)(2,1)S(1)}, bf16[8,34,256]{2,1,0:T(8,128)(2,1)S(1)}, u32[]{:S(2)}, u32[]{:S(2)}) collective-permute-start(bf16[8,34,256]{2,1,0:T(8,128)(2,1)S(1)} %all_to_all.22.r_ref.second_ref.refs_4_), channel_id=1, source_target_pairs={{0,1},{1,0},{2,3},{3,2},{4,5},{5,4},{6,7},{7,6},{8,9},{9,8},{10,11... | collective-permute-start | bytes 417800 | tf_op jit(solution)/shard_map/ppermute | solution.py:431
  51.2 1.5 %collective-permute-start.5 = (bf16[8,34,256]{2,1,0:T(8,128)(2,1)S(1)}, bf16[8,34,256]{2,1,0:T(8,128)(2,1)S(1)}, u32[]{:S(2)}, u32[]{:S(2)}) collective-permute-start(bf16[8,34,256]{2,1,0:T(8,128)(2,1)S(1)} %get-tuple-element.37.refs_2_), channel_id=1, source_target_pairs={{0,1},{1,0},{2,3},{3,2},{4,5},{5,4},{6,7},{7,6},{8,9},{9,8},{10,11... | collective-permute-start | bytes 417800 | tf_op jit(solution)/shard_map/ppermute | solution.py:431
  51.4 1.6 %collective-permute-start.7 = (bf16[8,34,256]{2,1,0:T(8,128)(2,1)S(1)}, bf16[8,34,256]{2,1,0:T(8,128)(2,1)S(1)}, u32[]{:S(2)}, u32[]{:S(2)}) collective-permute-start(bf16[8,34,256]{2,1,0:T(8,128)(2,1)S(1)} %get-tuple-element.39.refs_6_), channel_id=1, source_target_pairs={{0,1},{1,0},{2,3},{3,2},{4,5},{5,4},{6,7},{7,6},{8,9},{9,8},{10,11... | collective-permute-start | bytes 417800 | tf_op jit(solution)/shard_map/ppermute | solution.py:431
  52.9 0.9 %copy-start.3 = (bf16[256,256]{1,0:T(8,128)(2,1)S(1)}, bf16[256,256]{1,0:T(8,128)(2,1)}, u32[]{:S(2)}) copy-start(bf16[256,256]{1,0:T(8,128)(2,1)} %refs_13_.1) | copy-start | bytes 393220
  53.8 0.9 %copy-start.5 = (bf16[256,256]{1,0:T(8,128)(2,1)S(1)}, bf16[256,256]{1,0:T(8,128)(2,1)}, u32[]{:S(2)}) copy-start(bf16[256,256]{1,0:T(8,128)(2,1)} %refs_10_.1) | copy-start | bytes 393220
  58.8 1.0 %copy-start.1 = (bf16[1024,256]{1,0:T(8,128)(2,1)S(1)}, bf16[1024,256]{1,0:T(8,128)(2,1)}, u32[]{:S(2)}) copy-start(bf16[1024,256]{1,0:T(8,128)(2,1)} %constant.5.clone.ft_ref) | copy-start | bytes 1572868

commit v19 on v18

--- a/solution.py
+++ b/solution.py
@@ -318,7 +318,7 @@
     act_grad = (junc_grad * slope_ref[...]).astype(jnp.bfloat16)
     sums_grad = dot(act_grad, junc_weight_ref[...], 1, 1)
     rows_ref[...] = sums_grad.astype(jnp.bfloat16).astype(jnp.float32)
-    local_ref[...] = dot(total_ref[...], weight_ref[...], 1, 1)
+    local_ref[...] = dot(total_ref[...], weight_ref[...], 1, 1).astype(jnp.bfloat16)
     wait(going)
 
 
@@ -358,7 +358,9 @@
             if step == steps - 1 and side == 1:
                 grad_cells = grad_cells + jnp.where(row == tile - 1, rows_ref[1:2, :], 0.0)
             spread = grad_cells.astype(jnp.bfloat16).astype(jnp.float32)
-            tiles_ref[step, side] = (local_ref[at, :] + spread).astype(jnp.bfloat16)
+            tiles_ref[step, side] = (local_ref[at, :].astype(jnp.float32) + spread).astype(
+                jnp.bfloat16
+            )
             going += started(
                 [
                     pltpu.make_async_copy(
@@ -497,7 +499,7 @@
     per_copy = math.gcd(modes, 2)
     grad_real, grad_imag, rows, local = call(
         functools.partial(weight_grad_kernel, pipes, modes, per_copy),
-        [big, big, shape((8, channels), f32), shape(field.shape, f32)],
+        [big, big, shape((8, channels), f32), shape(field.shape, bf16)],
         [VMEM] * (2 * pipes + 6),
         [rows_of(pipes * all_rows, channels)] * 2
         + [pltpu.VMEM(big.shape, f32)] * 2

time: 62.5 us -> 58.9 us (0.942)
  local copies, waits for them, and re-layouts: 4.12 us -> 1.28 us
  Pallas kernels: 11.9 us -> 10.9 us
  waiting for transfers between devices: 3.29 us -> 4.27 us
  starting transfers between devices: 9.06 us -> 8.42 us
    unnamed x30 -> x24, local copies, waits for them, and re-layouts: 4.12 us -> 1.28 us
    pallas_call x1, Pallas kernels: 2.25 us -> 1.34 us  [body(): call(input_grad_kernel, [shape(field.shape, bf16)], [VMEM] * 4, [pltpu.VM...]
    all_to_all x1, starting transfers between devices: 4.01 us -> 3.38 us  [exchange(): return lax.all_to_all(value, 'len', split_axis=0, concat_axis=0, tiled=True)]
  transfers between devices with their start and end apart: 9 -> 9, of which waited for: 4 -> 6; matrix products, arithmetic and copies ran while one was open for 0% -> 0% of each run, Pallas kernels for 11% -> 11%
where the time goes in v19:
time: 58.9 us; the launch traced here: 58.6 us
  blocking collectives  32.9 us (56%)
  Pallas kernels  10.9 us (19%)
  starting transfers between devices  8.42 us (14%)
  waiting for transfers between devices  4.27 us (7%)
  local copies, waits for them, and re-layouts  1.28 us (2%)
  between operations  0.83 us (1%)
    all_to_all x3, blocking collectives, exchange(): return lax.all_to_all(value, 'len', split_axis=0, concat_axis=0, tiled=True)  32.9 us
    ppermute x8, starting transfers between devices, swap(): return lax.ppermute(value, 'pipe', [(i, i ^ step) for i in range(pipes)])  5.03 us
    pallas_call x1, Pallas kernels, body(): call(functools.partial(weight_grad_kernel, pipes, modes, per_copy), [big,...  3.99 us
    ppermute x8, waiting for transfers between devices, swap(): return lax.ppermute(value, 'pipe', [(i, i ^ step) for i in range(pipes)])  3.75 us
    all_to_all x1, starting transfers between devices, exchange(): return lax.all_to_all(value, 'len', split_axis=0, concat_axis=0, tiled=True)  3.38 us
    pallas_call x1, Pallas kernels, body(): call(mix_grad_kernel, [chunks, early], [VMEM] * 4, [dma] + mix_bufs, out_...  1.93 us
    pallas_call x1, Pallas kernels, body(): call(layer_kernel, [shape(field.shape, bf16)] * 2 + [message], [VMEM] * 6...  1.9 us
    pallas_call x1, Pallas kernels, body(): call(input_grad_kernel, [shape(field.shape, bf16)], [VMEM] * 4, [pltpu.VM...  1.34 us
  transfers between devices with their start and end apart: 9, of which 6 were waited for; matrix products, arithmetic and copies ran while one was open for 0% of the time, Pallas kernels for 11%

profile of v19, /device:TPU:0, one launch (start us, length us, event | category | flops | bytes accessed | tf_op | source)
XLA Modules:
  0.0 58.6 jit_solution(14735297753899329839)
XLA Ops:
  0.6 1.2 %copy-done.7 = bf16[1,2048,256]{2,1,0:T(8,128)(2,1)S(1)} copy-done((bf16[1,2048,256]{2,1,0:T(8,128)(2,1)S(1)}, bf16[1,2048,256]{2,1,0:T(8,128)(2,1)}, u32[]{:S(2)}) %copy-start.7) | copy-done | bytes 1048600
  1.9 2.4 %collective-permute-start.2 = (f32[8,256]{1,0:T(8,128)S(1)}, f32[8,256]{1,0:T(8,128)S(1)}, u32[]{:S(2)}, u32[]{:S(2)}) collective-permute-start(f32[8,256]{1,0:T(8,128)S(1)} %pipe_ends.1.refs_0_), channel_id=1, source_target_pairs={{0,3},{1,2},{2,1},{3,0},{4,7},{5,6},{6,5},{7,4},{8,11},{9,10},{10,... | collective-permute-start | bytes 24584 | tf_op jit(solution)/shard_map/ppermute | solution.py:433
  4.3 0.6 %collective-permute-start.1 = (f32[8,256]{1,0:T(8,128)S(1)}, f32[8,256]{1,0:T(8,128)S(1)}, u32[]{:S(2)}, u32[]{:S(2)}) collective-permute-start(f32[8,256]{1,0:T(8,128)S(1)} %pipe_ends.1.refs_0_), channel_id=1, source_target_pairs={{0,2},{1,3},{2,0},{3,1},{4,6},{5,7},{6,4},{7,5},{8,10},{9,11},{10,... | collective-permute-start | bytes 24584 | tf_op jit(solution)/shard_map/ppermute | solution.py:433
  5.0 0.0 collective-permute-start
  5.0 0.0 copy-start.3
  5.0 0.0 copy-start.4
  5.0 0.0 copy-start.5
  5.0 0.0 copy-start.6
  5.1 0.0 copy-start.10
  5.1 0.7 %spectrum.1 = (bf16[8,32,256]{2,1,0:T(8,128)(2,1)S(1)}, f32[2048,256]{1,0:T(8,128)S(1)}) custom-call(bf16[2048,256]{1,0:T(8,128)(2,1)S(1)} %bitcast.13, bf16[4,256,256]{2,1,0:T(8,128)(2,1)S(1)} %copy-done.11, bf16[256,256]{1,0:T(8,128)(2,1)S(1)} %copy-done.1, f32[1,256]{1,0:T(1,128)S(1)} %bitcast.15), custom_call_target="tpu_custom_call" | custom-call | flops 12000000000 | bytes 12582912 | tf_op jit(solution)/shard_map/spectrum/pallas_call | solution.py:443
  5.8 2.2 %collective-permute-done.1.refs_2_ = f32[8,256]{1,0:T(8,128)S(1)} collective-permute-done((f32[8,256]{1,0:T(8,128)S(1)}, f32[8,256]{1,0:T(8,128)S(1)}, u32[]{:S(2)}, u32[]{:S(2)}) %collective-permute-start.1) | collective-permute-done | bytes 8224 | tf_op jit(solution)/shard_map/ppermute | solution.py:433
  8.0 13.2 %all_to_all.20.r_ref.first_ref.refs_0_ = bf16[8,40,256]{2,1,0:T(8,128)(2,1)S(1)} all-to-all(bf16[8,40,256]{2,1,0:T(8,128)(2,1)S(1)} %message.1), channel_id=1, replica_groups=mesh['len'=8,'pipe'=4] {'len'}, dimensions={0} | all-to-all | bytes 327680 | tf_op jit(solution)/shard_map/all_to_all | solution.py:430
  21.2 0.0 copy-start
  21.2 0.0 copy-start.8
  21.2 1.0 %mix.1 = (bf16[8,32,256]{2,1,0:T(8,128)(2,1)S(1)}, f32[1,256]{1,0:T(1,128)S(1)}, f32[8,256]{1,0:T(8,128)S(1)}) custom-call(bf16[8,40,256]{2,1,0:T(8,128)(2,1)S(1)} %all_to_all.20.r_ref.first_ref.refs_0_, bf16[16,256,256]{2,1,0:T(8,128)(2,1)S(1)} %copy-done.5, bf16[16,256,256]{2,1,0:T(8,128)(2,1)S(1)} %copy-done.6, s32[1,32]{1,0:T(1,128)S(1)} %bitcast.8, ...), custom_call_target="tpu_custom_call" | custom-call | flops 12000000000 | bytes 12582912 | tf_op jit(solution)/shard_map/mix/pallas_call | solution.py:457
  22.2 9.7 %all_to_all.21.modes_ref = bf16[8,32,256]{2,1,0:T(8,128)(2,1)S(1)} all-to-all(bf16[8,32,256]{2,1,0:T(8,128)(2,1)S(1)} %get-tuple-element.28), channel_id=1, replica_groups=mesh['len'=8,'pipe'=4] {'len'}, dimensions={0} | all-to-all | bytes 262144 | tf_op jit(solution)/shard_map/all_to_all | solution.py:430
  32.0 1.9 %layer.1 = (bf16[2048,256]{1,0:T(8,128)(2,1)S(1)}, bf16[2048,256]{1,0:T(8,128)(2,1)S(1)}, bf16[8,34,256]{2,1,0:T(8,128)(2,1)S(1)}) custom-call(f32[2048,256]{1,0:T(8,128)S(1)} %get-tuple-element.25.pointwise_ref, bf16[2048,256]{1,0:T(8,128)(2,1)S(1)} %bitcast.14, bf16[4,256,256]{2,1,0:T(8,128)(2,1)S(1)} %copy-done.11, bf16[1024,256]{1,0:T(8,128)(2,1)S(1)} %copy-done, ...), custom_call_target="tpu_custom_call" | custom-call | flops 12000000000 | bytes 12582912 | tf_op jit(solution)/shard_map/layer/pallas_call | solution.py:467
  33.9 10.0 %all_to_all.22.r_ref.second_ref.refs_4_ = bf16[8,34,256]{2,1,0:T(8,128)(2,1)S(1)} all-to-all(bf16[8,34,256]{2,1,0:T(8,128)(2,1)S(1)} %get-tuple-element.29), channel_id=1, replica_groups=mesh['len'=8,'pipe'=4] {'len'}, dimensions={0} | all-to-all | bytes 278528 | tf_op jit(solution)/shard_map/all_to_all | solution.py:430
  43.9 0.8 %collective-permute-start.4 = (bf16[16,34,256]{2,1,0:T(8,128)(2,1)S(1)}, bf16[16,34,256]{2,1,0:T(8,128)(2,1)S(1)}, u32[]{:S(2)}, u32[]{:S(2)}) collective-permute-start(bf16[16,34,256]{2,1,0:T(8,128)(2,1)S(1)} %pack.1), channel_id=1, source_target_pairs={{0,2},{1,3},{2,0},{3,1},{4,6},{5,7},{6,4},{7,5},{8,10},{9,11},{10,... | collective-permute-start | bytes 835592 | tf_op jit(solution)/shard_map/ppermute | solution.py:433
  44.6 1.9 %mix_grad.1 = (bf16[8,32,256]{2,1,0:T(8,128)(2,1)}, bf16[2048,256]{1,0:T(8,128)(2,1)}) custom-call(bf16[8,34,256]{2,1,0:T(8,128)(2,1)S(1)} %all_to_all.22.r_ref.second_ref.refs_4_, bf16[16,256,256]{2,1,0:T(8,128)(2,1)S(1)} %copy-done.5, bf16[16,256,256]{2,1,0:T(8,128)(2,1)S(1)} %copy-done.6, bf16[2048,256]{1,0:T(8,128)(2,1)S(1)} %get-tuple-element.31.early_ref), custom_call_target="tpu_custom_call" | custom-call | flops 12000000000 | bytes 12582912 | tf_op jit(solution)/shard_map/mix_grad/pallas_call | solution.py:483
  46.6 3.4 %all-to-all-start.3 = ((bf16[8,32,256]{2,1,0:T(8,128)(2,1)}), bf16[8,32,256]{2,1,0:T(8,128)(2,1)S(1)}, u32[]{:S(2)}, u32[]{:S(2)}) async-start(bf16[8,32,256]{2,1,0:T(8,128)(2,1)} %get-tuple-element.35), calls=%async_computation.3 | async-start | bytes 262144 | tf_op jit(solution)/shard_map/all_to_all | solution.py:430
  50.0 0.1 collective-permute-start.3
  50.1 0.5 collective-permute-start.6
  50.5 0.5 collective-permute-done.4.both_ref
  51.0 0.1 collective-permute-start.5
  51.1 0.5 collective-permute-start.7
  51.6 0.1 collective-permute-done.6.refs_5_
  51.7 0.8 %collective-permute-done.5.refs_3_ = bf16[8,34,256]{2,1,0:T(8,128)(2,1)S(1)} collective-permute-done((bf16[8,34,256]{2,1,0:T(8,128)(2,1)S(1)}, bf16[8,34,256]{2,1,0:T(8,128)(2,1)S(1)}, u32[]{:S(2)}, u32[]{:S(2)}) %collective-permute-start.5) | collective-permute-done | bytes 139296 | tf_op jit(solution)/shard_map/ppermute | solution.py:433
  52.5 0.2 collective-permute-done.7.refs_7_
  52.7 4.0 %weight_grad.1 = (f32[16,256,256]{2,1,0:T(8,128)}, f32[16,256,256]{2,1,0:T(8,128)}, f32[8,256]{1,0:T(8,128)S(1)}, bf16[2048,256]{1,0:T(8,128)(2,1)S(1)}) custom-call(bf16[8,40,256]{2,1,0:T(8,128)(2,1)S(1)} %all_to_all.20.r_ref.first_ref.refs_0_, bf16[8,40,256]{2,1,0:T(8,128)(2,1)S(1)} %collective-permute-done.3.refs_1_, ...), custom_call_target="tpu_custom_call" | custom-call | tf_op jit(solution)/shard_map/weight_grad/pallas_call | solution.py:500
  56.7 0.5 all-to-all-done.3.modes_ref
  57.3 1.3 %input_grad.1 = bf16[2048,256]{1,0:T(8,128)(2,1)} custom-call(bf16[2048,256]{1,0:T(8,128)(2,1)S(1)} %get-tuple-element.42.local_ref, bf16[1024,256]{1,0:T(8,128)(2,1)S(1)} %copy-done, f32[8,256]{1,0:T(8,128)S(1)} %get-tuple-element.43.rows_ref, bf16[8,32,256]{2,1,0:T(8,128)(2,1)S(1)} %all-to-all-done.3.modes_ref), custom_call_target="tpu_custom_call" | custom-call | tf_op jit(solution)/shard_map/input_grad/pallas_call | solution.py:513
  (23 shorter events, 0.1 us)
Async XLA Ops:
  0.6 1.2 %copy-start.7 = (bf16[1,2048,256]{2,1,0:T(8,128)(2,1)S(1)}, bf16[1,2048,256]{2,1,0:T(8,128)(2,1)}, u32[]{:S(2)}) copy-start(bf16[1,2048,256]{2,1,0:T(8,128)(2,1)} %param.12) | copy-start | bytes 3145732
  1.9 3.1 %copy-start.1 = (bf16[256,256]{1,0:T(8,128)(2,1)S(1)}, bf16[256,256]{1,0:T(8,128)(2,1)}, u32[]{:S(2)}) copy-start(bf16[256,256]{1,0:T(8,128)(2,1)} %refs_13_.1) | copy-start | bytes 393220
  1.9 3.1 %copy-start.9 = (f32[256]{0:T(256)S(1)}, f32[256]{0:T(256)}, u32[]{:S(2)}) copy-start(f32[256]{0:T(256)} %param.15) | copy-start | bytes 3076
  1.9 3.1 %copy-start.11 = (bf16[4,256,256]{2,1,0:T(8,128)(2,1)S(1)}, bf16[4,256,256]{2,1,0:T(8,128)(2,1)}, u32[]{:S(2)}) copy-start(bf16[4,256,256]{2,1,0:T(8,128)(2,1)} %constant.4.clone.f_ref) | copy-start | bytes 1572868
  1.9 3.9 %collective-permute-start.2 = (f32[8,256]{1,0:T(8,128)S(1)}, f32[8,256]{1,0:T(8,128)S(1)}, u32[]{:S(2)}, u32[]{:S(2)}) collective-permute-start(f32[8,256]{1,0:T(8,128)S(1)} %pipe_ends.1.refs_0_), channel_id=1, source_target_pairs={{0,3},{1,2},{2,1},{3,0},{4,7},{5,6},{6,5},{7,4},{8,11},{9,10},{10,... | collective-permute-start | bytes 24584 | tf_op jit(solution)/shard_map/ppermute | solution.py:433
  4.3 3.7 %collective-permute-start.1 = (f32[8,256]{1,0:T(8,128)S(1)}, f32[8,256]{1,0:T(8,128)S(1)}, u32[]{:S(2)}, u32[]{:S(2)}) collective-permute-start(f32[8,256]{1,0:T(8,128)S(1)} %pipe_ends.1.refs_0_), channel_id=1, source_target_pairs={{0,2},{1,3},{2,0},{3,1},{4,6},{5,7},{6,4},{7,5},{8,10},{9,11},{10,... | collective-permute-start | bytes 24584 | tf_op jit(solution)/shard_map/ppermute | solution.py:433
  5.0 3.0 %collective-permute-start = (f32[8,256]{1,0:T(8,128)S(1)}, f32[8,256]{1,0:T(8,128)S(1)}, u32[]{:S(2)}, u32[]{:S(2)}) collective-permute-start(f32[8,256]{1,0:T(8,128)S(1)} %pipe_ends.1.refs_0_), channel_id=1, source_target_pairs={{0,1},{1,0},{2,3},{3,2},{4,5},{5,4},{6,7},{7,6},{8,9},{9,8},{10,11... | collective-permute-start | bytes 24584 | tf_op jit(solution)/shard_map/ppermute | solution.py:433
  5.0 16.2 %copy-start.2 = (bf16[256,256]{1,0:T(8,128)(2,1)S(1)}, bf16[256,256]{1,0:T(8,128)(2,1)}, u32[]{:S(2)}) copy-start(bf16[256,256]{1,0:T(8,128)(2,1)} %refs_10_.1) | copy-start | bytes 393220
  5.0 16.2 %copy-start.3 = (s32[32]{0:T(128)S(1)}, s32[32]{0:T(128)}, u32[]{:S(2)}) copy-start(s32[32]{0:T(128)} %param.20) | copy-start | bytes 388
  5.0 16.2 %copy-start.4 = (s32[32]{0:T(128)S(1)}, s32[32]{0:T(128)}, u32[]{:S(2)}) copy-start(s32[32]{0:T(128)} %param.21) | copy-start | bytes 388
  5.0 16.2 %copy-start.5 = (bf16[16,256,256]{2,1,0:T(8,128)(2,1)S(1)}, bf16[16,256,256]{2,1,0:T(8,128)(2,1)}, u32[]{:S(2)}) copy-start(bf16[16,256,256]{2,1,0:T(8,128)(2,1)} %real_ref.3) | copy-start | bytes 6291460
  5.0 16.2 %copy-start.6 = (bf16[16,256,256]{2,1,0:T(8,128)(2,1)S(1)}, bf16[16,256,256]{2,1,0:T(8,128)(2,1)}, u32[]{:S(2)}) copy-start(bf16[16,256,256]{2,1,0:T(8,128)(2,1)} %imag_ref.3) | copy-start | bytes 6291460
  5.1 16.2 %copy-start.10 = (f32[256]{0:T(256)S(1)}, f32[256]{0:T(256)}, u32[]{:S(2)}) copy-start(f32[256]{0:T(256)} %param.19) | copy-start | bytes 3076
  21.2 10.7 %copy-start = (bf16[1024,256]{1,0:T(8,128)(2,1)S(1)}, bf16[1024,256]{1,0:T(8,128)(2,1)}, u32[]{:S(2)}) copy-start(bf16[1024,256]{1,0:T(8,128)(2,1)} %constant.5.clone.ft_ref) | copy-start | bytes 1572868
  21.2 10.7 %copy-start.8 = (bf16[1,2048,256]{2,1,0:T(8,128)(2,1)S(1)}, bf16[1,2048,256]{2,1,0:T(8,128)(2,1)}, u32[]{:S(2)}) copy-start(bf16[1,2048,256]{2,1,0:T(8,128)(2,1)} %param.13) | copy-start | bytes 3145732
  43.9 7.1 %collective-permute-start.4 = (bf16[16,34,256]{2,1,0:T(8,128)(2,1)S(1)}, bf16[16,34,256]{2,1,0:T(8,128)(2,1)S(1)}, u32[]{:S(2)}, u32[]{:S(2)}) collective-permute-start(bf16[16,34,256]{2,1,0:T(8,128)(2,1)S(1)} %pack.1), channel_id=1, source_target_pairs={{0,2},{1,3},{2,0},{3,1},{4,6},{5,7},{6,4},{7,5},{8,10},{9,11},{10,... | collective-permute-start | bytes 835592 | tf_op jit(solution)/shard_map/ppermute | solution.py:433
  46.6 10.7 %all-to-all-start.3 = ((bf16[8,32,256]{2,1,0:T(8,128)(2,1)}), bf16[8,32,256]{2,1,0:T(8,128)(2,1)S(1)}, u32[]{:S(2)}, u32[]{:S(2)}) async-start(bf16[8,32,256]{2,1,0:T(8,128)(2,1)} %get-tuple-element.35), calls=%async_computation.3 | async-start | bytes 262144 | tf_op jit(solution)/shard_map/all_to_all | solution.py:430
  50.0 1.7 %collective-permute-start.3 = (bf16[8,40,256]{2,1,0:T(8,128)(2,1)S(1)}, bf16[8,40,256]{2,1,0:T(8,128)(2,1)S(1)}, u32[]{:S(2)}, u32[]{:S(2)}) collective-permute-start(bf16[8,40,256]{2,1,0:T(8,128)(2,1)S(1)} %all_to_all.20.r_ref.first_ref.refs_0_), channel_id=1, source_target_pairs={{0,1},{1,0},{2,3},{3,2},{4,5},{5,4},{6,7},{7,6},{8,9},{9,8},{10,11... | collective-permute-start | bytes 491528 | tf_op jit(solution)/shard_map/ppermute | solution.py:433
  50.1 1.6 %collective-permute-start.6 = (bf16[8,34,256]{2,1,0:T(8,128)(2,1)S(1)}, bf16[8,34,256]{2,1,0:T(8,128)(2,1)S(1)}, u32[]{:S(2)}, u32[]{:S(2)}) collective-permute-start(bf16[8,34,256]{2,1,0:T(8,128)(2,1)S(1)} %all_to_all.22.r_ref.second_ref.refs_4_), channel_id=1, source_target_pairs={{0,1},{1,0},{2,3},{3,2},{4,5},{5,4},{6,7},{7,6},{8,9},{9,8},{10,11... | collective-permute-start | bytes 417800 | tf_op jit(solution)/shard_map/ppermute | solution.py:433
  51.0 1.5 %collective-permute-start.5 = (bf16[8,34,256]{2,1,0:T(8,128)(2,1)S(1)}, bf16[8,34,256]{2,1,0:T(8,128)(2,1)S(1)}, u32[]{:S(2)}, u32[]{:S(2)}) collective-permute-start(bf16[8,34,256]{2,1,0:T(8,128)(2,1)S(1)} %get-tuple-element.37.refs_2_), channel_id=1, source_target_pairs={{0,1},{1,0},{2,3},{3,2},{4,5},{5,4},{6,7},{7,6},{8,9},{9,8},{10,11... | collective-permute-start | bytes 417800 | tf_op jit(solution)/shard_map/ppermute | solution.py:433
  51.1 1.6 %collective-permute-start.7 = (bf16[8,34,256]{2,1,0:T(8,128)(2,1)S(1)}, bf16[8,34,256]{2,1,0:T(8,128)(2,1)S(1)}, u32[]{:S(2)}, u32[]{:S(2)}) collective-permute-start(bf16[8,34,256]{2,1,0:T(8,128)(2,1)S(1)} %get-tuple-element.39.refs_6_), channel_id=1, source_target_pairs={{0,1},{1,0},{2,3},{3,2},{4,5},{5,4},{6,7},{7,6},{8,9},{9,8},{10,11... | collective-permute-start | bytes 417800 | tf_op jit(solution)/shard_map/ppermute | solution.py:433

commit v20 on v19

--- a/solution.py
+++ b/solution.py
@@ -85,10 +85,11 @@
         pointwise_ref[at, :] = dot(x_ref[at, :], weight) + bias
 
 
-def message_kernel(pipes, spectra_ref, *refs):
+def message_kernel(order, spectra_ref, *refs):
     groups, span = spectra_ref.shape[0], spectra_ref.shape[1]
+    pipes = len(order)
     msg_ref = refs[pipes]
-    ends = jnp.concatenate([refs[step][0:2, :] for step in range(pipes)], axis=0)
+    ends = jnp.concatenate([refs[order.index(step)][0:2, :] for step in range(pipes)], axis=0)
     ends = ends.astype(jnp.bfloat16)
     for at in range(groups):
         msg_ref[at, 0:span, :] = spectra_ref[at]
@@ -439,7 +440,8 @@
     (ends,) = call(
         ends_kernel, [shape((8, channels), f32)], [VMEM], name="pipe_ends", busy=4
     )(field)
-    ends = [ends] + [swap(ends, step) for step in range(1, pipes)]
+    order = [0, 1, 3, 2]
+    ends = [swap(ends, step) if step else ends for step in order]
     spectra, pointwise = call(
         spectrum_kernel,
         [chunks, shape(field.shape, f32)],
@@ -448,7 +450,7 @@
         busy=12,
     )(field, f_table, point_weight, bias_row)
     (sent,) = call(
-        functools.partial(message_kernel, pipes),
+        functools.partial(message_kernel, order),
         [shape((groups, span + 2 * pipes, channels), bf16)],
         [VMEM] * (1 + pipes),
         name="message",

time: 58.9 us -> 59.4 us (level)
  no operation moved by 1% of the time
where the time goes in v20:
time: 59.4 us; the launch traced here: 59 us
  blocking collectives  32.9 us (55%)
  Pallas kernels  10.9 us (18%)
  starting transfers between devices  8.93 us (15%)
  waiting for transfers between devices  4.19 us (7%)
  local copies, waits for them, and re-layouts  1.28 us (2%)
  between operations  0.81 us (1%)
    all_to_all x3, blocking collectives, exchange(): return lax.all_to_all(value, 'len', split_axis=0, concat_axis=0, tiled=True)  32.9 us
    ppermute x8, starting transfers between devices, swap(): return lax.ppermute(value, 'pipe', [(i, i ^ step) for i in range(pipes)])  5.55 us
    pallas_call x1, Pallas kernels, body(): call(functools.partial(weight_grad_kernel, pipes, modes, per_copy), [big,...  3.99 us
    all_to_all x1, starting transfers between devices, exchange(): return lax.all_to_all(value, 'len', split_axis=0, concat_axis=0, tiled=True)  3.38 us
    ppermute x8, waiting for transfers between devices, swap(): return lax.ppermute(value, 'pipe', [(i, i ^ step) for i in range(pipes)])  3.23 us
    pallas_call x1, Pallas kernels, body(): call(mix_grad_kernel, [chunks, early], [VMEM] * 4, [dma] + mix_bufs, out_...  1.93 us
    pallas_call x1, Pallas kernels, body(): call(layer_kernel, [shape(field.shape, bf16)] * 2 + [message], [VMEM] * 6...  1.9 us
    pallas_call x1, Pallas kernels, body(): call(input_grad_kernel, [shape(field.shape, bf16)], [VMEM] * 4, [pltpu.VM...  1.34 us
  transfers between devices with their start and end apart: 9, of which 6 were waited for; matrix products, arithmetic and copies ran while one was open for 0% of the time, Pallas kernels for 11%

profile of v20, /device:TPU:0, one launch (start us, length us, event | category | flops | bytes accessed | tf_op | source)
XLA Modules:
  0.0 59.0 jit_solution(8979950874195493878)
XLA Ops:
  0.6 1.2 %copy-done.7 = bf16[1,2048,256]{2,1,0:T(8,128)(2,1)S(1)} copy-done((bf16[1,2048,256]{2,1,0:T(8,128)(2,1)S(1)}, bf16[1,2048,256]{2,1,0:T(8,128)(2,1)}, u32[]{:S(2)}) %copy-start.7) | copy-done | bytes 1048600
  1.9 3.0 %collective-permute-start.2 = (f32[8,256]{1,0:T(8,128)S(1)}, f32[8,256]{1,0:T(8,128)S(1)}, u32[]{:S(2)}, u32[]{:S(2)}) collective-permute-start(f32[8,256]{1,0:T(8,128)S(1)} %pipe_ends.1.refs_0_), channel_id=1, source_target_pairs={{0,2},{1,3},{2,0},{3,1},{4,6},{5,7},{6,4},{7,5},{8,10},{9,11},{10,... | collective-permute-start | bytes 24584 | tf_op jit(solution)/shard_map/ppermute | solution.py:434
  4.9 0.2 collective-permute-start
  5.1 0.0 copy-start.3
  5.1 0.0 copy-start.4
  5.1 0.0 copy-start.5
  5.1 0.0 copy-start.6
  5.1 0.0 copy-start.10
  5.1 0.7 %spectrum.1 = (bf16[8,32,256]{2,1,0:T(8,128)(2,1)S(1)}, f32[2048,256]{1,0:T(8,128)S(1)}) custom-call(bf16[2048,256]{1,0:T(8,128)(2,1)S(1)} %bitcast.13, bf16[4,256,256]{2,1,0:T(8,128)(2,1)S(1)} %copy-done.11, bf16[256,256]{1,0:T(8,128)(2,1)S(1)} %copy-done.1, f32[1,256]{1,0:T(1,128)S(1)} %bitcast.15), custom_call_target="tpu_custom_call" | custom-call | flops 12000000000 | bytes 12582912 | tf_op jit(solution)/shard_map/spectrum/pallas_call | solution.py:445
  5.9 0.6 %collective-permute-done.2.refs_3_ = f32[8,256]{1,0:T(8,128)S(1)} collective-permute-done((f32[8,256]{1,0:T(8,128)S(1)}, f32[8,256]{1,0:T(8,128)S(1)}, u32[]{:S(2)}, u32[]{:S(2)}) %collective-permute-start.2) | collective-permute-done | bytes 8224 | tf_op jit(solution)/shard_map/ppermute | solution.py:434
  6.5 1.4 %collective-permute-done.1.refs_2_ = f32[8,256]{1,0:T(8,128)S(1)} collective-permute-done((f32[8,256]{1,0:T(8,128)S(1)}, f32[8,256]{1,0:T(8,128)S(1)}, u32[]{:S(2)}, u32[]{:S(2)}) %collective-permute-start.1) | collective-permute-done | bytes 8224 | tf_op jit(solution)/shard_map/ppermute | solution.py:434
  8.0 13.2 %all_to_all.20.r_ref.first_ref.refs_0_ = bf16[8,40,256]{2,1,0:T(8,128)(2,1)S(1)} all-to-all(bf16[8,40,256]{2,1,0:T(8,128)(2,1)S(1)} %message.1), channel_id=1, replica_groups=mesh['len'=8,'pipe'=4] {'len'}, dimensions={0} | all-to-all | bytes 327680 | tf_op jit(solution)/shard_map/all_to_all | solution.py:431
  21.2 0.0 copy-start
  21.2 0.0 copy-start.8
  21.2 1.0 %mix.1 = (bf16[8,32,256]{2,1,0:T(8,128)(2,1)S(1)}, f32[1,256]{1,0:T(1,128)S(1)}, f32[8,256]{1,0:T(8,128)S(1)}) custom-call(bf16[8,40,256]{2,1,0:T(8,128)(2,1)S(1)} %all_to_all.20.r_ref.first_ref.refs_0_, bf16[16,256,256]{2,1,0:T(8,128)(2,1)S(1)} %copy-done.5, bf16[16,256,256]{2,1,0:T(8,128)(2,1)S(1)} %copy-done.6, s32[1,32]{1,0:T(1,128)S(1)} %bitcast.8, ...), custom_call_target="tpu_custom_call" | custom-call | flops 12000000000 | bytes 12582912 | tf_op jit(solution)/shard_map/mix/pallas_call | solution.py:459
  22.2 9.7 %all_to_all.21.modes_ref = bf16[8,32,256]{2,1,0:T(8,128)(2,1)S(1)} all-to-all(bf16[8,32,256]{2,1,0:T(8,128)(2,1)S(1)} %get-tuple-element.28), channel_id=1, replica_groups=mesh['len'=8,'pipe'=4] {'len'}, dimensions={0} | all-to-all | bytes 262144 | tf_op jit(solution)/shard_map/all_to_all | solution.py:431
  32.0 1.9 %layer.1 = (bf16[2048,256]{1,0:T(8,128)(2,1)S(1)}, bf16[2048,256]{1,0:T(8,128)(2,1)S(1)}, bf16[8,34,256]{2,1,0:T(8,128)(2,1)S(1)}) custom-call(f32[2048,256]{1,0:T(8,128)S(1)} %get-tuple-element.25.pointwise_ref, bf16[2048,256]{1,0:T(8,128)(2,1)S(1)} %bitcast.14, bf16[4,256,256]{2,1,0:T(8,128)(2,1)S(1)} %copy-done.11, bf16[1024,256]{1,0:T(8,128)(2,1)S(1)} %copy-done, ...), custom_call_target="tpu_custom_call" | custom-call | flops 12000000000 | bytes 12582912 | tf_op jit(solution)/shard_map/layer/pallas_call | solution.py:469
  33.9 10.0 %all_to_all.22.r_ref.second_ref.refs_4_ = bf16[8,34,256]{2,1,0:T(8,128)(2,1)S(1)} all-to-all(bf16[8,34,256]{2,1,0:T(8,128)(2,1)S(1)} %get-tuple-element.29), channel_id=1, replica_groups=mesh['len'=8,'pipe'=4] {'len'}, dimensions={0} | all-to-all | bytes 278528 | tf_op jit(solution)/shard_map/all_to_all | solution.py:431
  43.9 1.2 %collective-permute-start.4 = (bf16[16,34,256]{2,1,0:T(8,128)(2,1)S(1)}, bf16[16,34,256]{2,1,0:T(8,128)(2,1)S(1)}, u32[]{:S(2)}, u32[]{:S(2)}) collective-permute-start(bf16[16,34,256]{2,1,0:T(8,128)(2,1)S(1)} %pack.1), channel_id=1, source_target_pairs={{0,2},{1,3},{2,0},{3,1},{4,6},{5,7},{6,4},{7,5},{8,10},{9,11},{10,... | collective-permute-start | bytes 835592 | tf_op jit(solution)/shard_map/ppermute | solution.py:434
  45.1 1.9 %mix_grad.1 = (bf16[8,32,256]{2,1,0:T(8,128)(2,1)}, bf16[2048,256]{1,0:T(8,128)(2,1)}) custom-call(bf16[8,34,256]{2,1,0:T(8,128)(2,1)S(1)} %all_to_all.22.r_ref.second_ref.refs_4_, bf16[16,256,256]{2,1,0:T(8,128)(2,1)S(1)} %copy-done.5, bf16[16,256,256]{2,1,0:T(8,128)(2,1)S(1)} %copy-done.6, bf16[2048,256]{1,0:T(8,128)(2,1)S(1)} %get-tuple-element.31.early_ref), custom_call_target="tpu_custom_call" | custom-call | flops 12000000000 | bytes 12582912 | tf_op jit(solution)/shard_map/mix_grad/pallas_call | solution.py:485
  47.0 3.4 %all-to-all-start.3 = ((bf16[8,32,256]{2,1,0:T(8,128)(2,1)}), bf16[8,32,256]{2,1,0:T(8,128)(2,1)S(1)}, u32[]{:S(2)}, u32[]{:S(2)}) async-start(bf16[8,32,256]{2,1,0:T(8,128)(2,1)} %get-tuple-element.35), calls=%async_computation.3 | async-start | bytes 262144 | tf_op jit(solution)/shard_map/all_to_all | solution.py:431
  50.4 0.1 collective-permute-start.3
  50.5 0.5 collective-permute-start.6
  51.0 0.0 collective-permute-done.4.both_ref
  51.0 0.1 collective-permute-start.5
  51.1 0.5 collective-permute-start.7
  51.6 0.5 collective-permute-done.6.refs_5_
  52.1 0.4 collective-permute-done.5.refs_3_
  52.5 0.2 collective-permute-done.7.refs_7_
  52.7 4.0 %weight_grad.1 = (f32[16,256,256]{2,1,0:T(8,128)}, f32[16,256,256]{2,1,0:T(8,128)}, f32[8,256]{1,0:T(8,128)S(1)}, bf16[2048,256]{1,0:T(8,128)(2,1)S(1)}) custom-call(bf16[8,40,256]{2,1,0:T(8,128)(2,1)S(1)} %all_to_all.20.r_ref.first_ref.refs_0_, bf16[8,40,256]{2,1,0:T(8,128)(2,1)S(1)} %collective-permute-done.3.refs_1_, ...), custom_call_target="tpu_custom_call" | custom-call | tf_op jit(solution)/shard_map/weight_grad/pallas_call | solution.py:502
  56.7 1.0 %all-to-all-done.3.modes_ref = bf16[8,32,256]{2,1,0:T(8,128)(2,1)S(1)} async-done(((bf16[8,32,256]{2,1,0:T(8,128)(2,1)}), bf16[8,32,256]{2,1,0:T(8,128)(2,1)S(1)}, u32[]{:S(2)}, u32[]{:S(2)}) %all-to-all-start.3) | async-done | bytes 131104 | tf_op jit(solution)/shard_map/all_to_all | solution.py:431
  57.7 1.3 %input_grad.1 = bf16[2048,256]{1,0:T(8,128)(2,1)} custom-call(bf16[2048,256]{1,0:T(8,128)(2,1)S(1)} %get-tuple-element.42.local_ref, bf16[1024,256]{1,0:T(8,128)(2,1)S(1)} %copy-done, f32[8,256]{1,0:T(8,128)S(1)} %get-tuple-element.43.rows_ref, bf16[8,32,256]{2,1,0:T(8,128)(2,1)S(1)} %all-to-all-done.3.modes_ref), custom_call_target="tpu_custom_call" | custom-call | tf_op jit(solution)/shard_map/input_grad/pallas_call | solution.py:515
  (23 shorter events, 0.1 us)
Async XLA Ops:
  0.6 1.2 %copy-start.7 = (bf16[1,2048,256]{2,1,0:T(8,128)(2,1)S(1)}, bf16[1,2048,256]{2,1,0:T(8,128)(2,1)}, u32[]{:S(2)}) copy-start(bf16[1,2048,256]{2,1,0:T(8,128)(2,1)} %param.12) | copy-start | bytes 3145732
  1.9 3.2 %copy-start.1 = (bf16[256,256]{1,0:T(8,128)(2,1)S(1)}, bf16[256,256]{1,0:T(8,128)(2,1)}, u32[]{:S(2)}) copy-start(bf16[256,256]{1,0:T(8,128)(2,1)} %refs_13_.1) | copy-start | bytes 393220
  1.9 3.2 %copy-start.9 = (f32[256]{0:T(256)S(1)}, f32[256]{0:T(256)}, u32[]{:S(2)}) copy-start(f32[256]{0:T(256)} %param.15) | copy-start | bytes 3076
  1.9 3.2 %copy-start.11 = (bf16[4,256,256]{2,1,0:T(8,128)(2,1)S(1)}, bf16[4,256,256]{2,1,0:T(8,128)(2,1)}, u32[]{:S(2)}) copy-start(bf16[4,256,256]{2,1,0:T(8,128)(2,1)} %constant.4.clone.f_ref) | copy-start | bytes 1572868
  1.9 4.6 %collective-permute-start.2 = (f32[8,256]{1,0:T(8,128)S(1)}, f32[8,256]{1,0:T(8,128)S(1)}, u32[]{:S(2)}, u32[]{:S(2)}) collective-permute-start(f32[8,256]{1,0:T(8,128)S(1)} %pipe_ends.1.refs_0_), channel_id=1, source_target_pairs={{0,2},{1,3},{2,0},{3,1},{4,6},{5,7},{6,4},{7,5},{8,10},{9,11},{10,... | collective-permute-start | bytes 24584 | tf_op jit(solution)/shard_map/ppermute | solution.py:434
  4.9 3.1 %collective-permute-start.1 = (f32[8,256]{1,0:T(8,128)S(1)}, f32[8,256]{1,0:T(8,128)S(1)}, u32[]{:S(2)}, u32[]{:S(2)}) collective-permute-start(f32[8,256]{1,0:T(8,128)S(1)} %pipe_ends.1.refs_0_), channel_id=1, source_target_pairs={{0,3},{1,2},{2,1},{3,0},{4,7},{5,6},{6,5},{7,4},{8,11},{9,10},{10,... | collective-permute-start | bytes 24584 | tf_op jit(solution)/shard_map/ppermute | solution.py:434
  4.9 3.1 %collective-permute-start = (f32[8,256]{1,0:T(8,128)S(1)}, f32[8,256]{1,0:T(8,128)S(1)}, u32[]{:S(2)}, u32[]{:S(2)}) collective-permute-start(f32[8,256]{1,0:T(8,128)S(1)} %pipe_ends.1.refs_0_), channel_id=1, source_target_pairs={{0,1},{1,0},{2,3},{3,2},{4,5},{5,4},{6,7},{7,6},{8,9},{9,8},{10,11... | collective-permute-start | bytes 24584 | tf_op jit(solution)/shard_map/ppermute | solution.py:434
  5.1 16.1 %copy-start.2 = (bf16[256,256]{1,0:T(8,128)(2,1)S(1)}, bf16[256,256]{1,0:T(8,128)(2,1)}, u32[]{:S(2)}) copy-start(bf16[256,256]{1,0:T(8,128)(2,1)} %refs_10_.1) | copy-start | bytes 393220
  5.1 16.1 %copy-start.3 = (s32[32]{0:T(128)S(1)}, s32[32]{0:T(128)}, u32[]{:S(2)}) copy-start(s32[32]{0:T(128)} %param.20) | copy-start | bytes 388
  5.1 16.1 %copy-start.4 = (s32[32]{0:T(128)S(1)}, s32[32]{0:T(128)}, u32[]{:S(2)}) copy-start(s32[32]{0:T(128)} %param.21) | copy-start | bytes 388
  5.1 16.1 %copy-start.5 = (bf16[16,256,256]{2,1,0:T(8,128)(2,1)S(1)}, bf16[16,256,256]{2,1,0:T(8,128)(2,1)}, u32[]{:S(2)}) copy-start(bf16[16,256,256]{2,1,0:T(8,128)(2,1)} %real_ref.3) | copy-start | bytes 6291460
  5.1 16.1 %copy-start.6 = (bf16[16,256,256]{2,1,0:T(8,128)(2,1)S(1)}, bf16[16,256,256]{2,1,0:T(8,128)(2,1)}, u32[]{:S(2)}) copy-start(bf16[16,256,256]{2,1,0:T(8,128)(2,1)} %imag_ref.3) | copy-start | bytes 6291460
  5.1 16.1 %copy-start.10 = (f32[256]{0:T(256)S(1)}, f32[256]{0:T(256)}, u32[]{:S(2)}) copy-start(f32[256]{0:T(256)} %param.19) | copy-start | bytes 3076
  21.2 10.7 %copy-start = (bf16[1024,256]{1,0:T(8,128)(2,1)S(1)}, bf16[1024,256]{1,0:T(8,128)(2,1)}, u32[]{:S(2)}) copy-start(bf16[1024,256]{1,0:T(8,128)(2,1)} %constant.5.clone.ft_ref) | copy-start | bytes 1572868
  21.2 10.7 %copy-start.8 = (bf16[1,2048,256]{2,1,0:T(8,128)(2,1)S(1)}, bf16[1,2048,256]{2,1,0:T(8,128)(2,1)}, u32[]{:S(2)}) copy-start(bf16[1,2048,256]{2,1,0:T(8,128)(2,1)} %param.13) | copy-start | bytes 3145732
  43.9 7.1 %collective-permute-start.4 = (bf16[16,34,256]{2,1,0:T(8,128)(2,1)S(1)}, bf16[16,34,256]{2,1,0:T(8,128)(2,1)S(1)}, u32[]{:S(2)}, u32[]{:S(2)}) collective-permute-start(bf16[16,34,256]{2,1,0:T(8,128)(2,1)S(1)} %pack.1), channel_id=1, source_target_pairs={{0,2},{1,3},{2,0},{3,1},{4,6},{5,7},{6,4},{7,5},{8,10},{9,11},{10,... | collective-permute-start | bytes 835592 | tf_op jit(solution)/shard_map/ppermute | solution.py:434
  47.0 10.7 %all-to-all-start.3 = ((bf16[8,32,256]{2,1,0:T(8,128)(2,1)}), bf16[8,32,256]{2,1,0:T(8,128)(2,1)S(1)}, u32[]{:S(2)}, u32[]{:S(2)}) async-start(bf16[8,32,256]{2,1,0:T(8,128)(2,1)} %get-tuple-element.35), calls=%async_computation.3 | async-start | bytes 262144 | tf_op jit(solution)/shard_map/all_to_all | solution.py:431
  50.4 1.7 %collective-permute-start.3 = (bf16[8,40,256]{2,1,0:T(8,128)(2,1)S(1)}, bf16[8,40,256]{2,1,0:T(8,128)(2,1)S(1)}, u32[]{:S(2)}, u32[]{:S(2)}) collective-permute-start(bf16[8,40,256]{2,1,0:T(8,128)(2,1)S(1)} %all_to_all.20.r_ref.first_ref.refs_0_), channel_id=1, source_target_pairs={{0,1},{1,0},{2,3},{3,2},{4,5},{5,4},{6,7},{7,6},{8,9},{9,8},{10,11... | collective-permute-start | bytes 491528 | tf_op jit(solution)/shard_map/ppermute | solution.py:434
  50.5 1.6 %collective-permute-start.6 = (bf16[8,34,256]{2,1,0:T(8,128)(2,1)S(1)}, bf16[8,34,256]{2,1,0:T(8,128)(2,1)S(1)}, u32[]{:S(2)}, u32[]{:S(2)}) collective-permute-start(bf16[8,34,256]{2,1,0:T(8,128)(2,1)S(1)} %all_to_all.22.r_ref.second_ref.refs_4_), channel_id=1, source_target_pairs={{0,1},{1,0},{2,3},{3,2},{4,5},{5,4},{6,7},{7,6},{8,9},{9,8},{10,11... | collective-permute-start | bytes 417800 | tf_op jit(solution)/shard_map/ppermute | solution.py:434
  51.0 1.5 %collective-permute-start.5 = (bf16[8,34,256]{2,1,0:T(8,128)(2,1)S(1)}, bf16[8,34,256]{2,1,0:T(8,128)(2,1)S(1)}, u32[]{:S(2)}, u32[]{:S(2)}) collective-permute-start(bf16[8,34,256]{2,1,0:T(8,128)(2,1)S(1)} %get-tuple-element.37.refs_2_), channel_id=1, source_target_pairs={{0,1},{1,0},{2,3},{3,2},{4,5},{5,4},{6,7},{7,6},{8,9},{9,8},{10,11... | collective-permute-start | bytes 417800 | tf_op jit(solution)/shard_map/ppermute | solution.py:434
  51.1 1.6 %collective-permute-start.7 = (bf16[8,34,256]{2,1,0:T(8,128)(2,1)S(1)}, bf16[8,34,256]{2,1,0:T(8,128)(2,1)S(1)}, u32[]{:S(2)}, u32[]{:S(2)}) collective-permute-start(bf16[8,34,256]{2,1,0:T(8,128)(2,1)S(1)} %get-tuple-element.39.refs_6_), channel_id=1, source_target_pairs={{0,1},{1,0},{2,3},{3,2},{4,5},{5,4},{6,7},{7,6},{8,9},{9,8},{10,11... | collective-permute-start | bytes 417800 | tf_op jit(solution)/shard_map/ppermute | solution.py:434

commit v21 on v19

--- a/solution.py
+++ b/solution.py
@@ -144,6 +144,7 @@
     first_ref,
     last_ref,
 ):
+    mix_rows(False, r_ref, real_ref, imag_ref, out_ref, x_ref, y_ref)
     groups, rows = r_ref.shape[0], r_ref.shape[1]
     span = rows - 2 * pipes
     column = lax.axis_index("pipe")
@@ -160,7 +161,6 @@
     junc_rows = (act * sigmoid_part).astype(jnp.bfloat16).astype(jnp.float32)
     cond_ref[...] = COUPLING * (junc_rows[0:1] + junc_rows[1:2])
     slope_ref[...] = sigmoid_part * (1.0 + act * (1.0 - sigmoid_part))
-    mix_rows(False, r_ref, real_ref, imag_ref, out_ref, x_ref, y_ref)
 
 
 def mix_grad_kernel(

time: 58.9 us -> 58.8 us (level)
  no operation moved by 1% of the time
where the time goes in v21:
time: 58.8 us; the launch traced here: 58.5 us
  blocking collectives  32.9 us (56%)
  Pallas kernels  10.8 us (18%)
  starting transfers between devices  8.42 us (14%)
  waiting for transfers between devices  4.27 us (7%)
  local copies, waits for them, and re-layouts  1.28 us (2%)
  between operations  0.83 us (1%)
    all_to_all x3, blocking collectives, exchange(): return lax.all_to_all(value, 'len', split_axis=0, concat_axis=0, tiled=True)  32.9 us
    ppermute x8, starting transfers between devices, swap(): return lax.ppermute(value, 'pipe', [(i, i ^ step) for i in range(pipes)])  5.04 us
    pallas_call x1, Pallas kernels, body(): call(functools.partial(weight_grad_kernel, pipes, modes, per_copy), [big,...  3.99 us
    ppermute x8, waiting for transfers between devices, swap(): return lax.ppermute(value, 'pipe', [(i, i ^ step) for i in range(pipes)])  3.74 us
    all_to_all x1, starting transfers between devices, exchange(): return lax.all_to_all(value, 'len', split_axis=0, concat_axis=0, tiled=True)  3.38 us
    pallas_call x1, Pallas kernels, body(): call(mix_grad_kernel, [chunks, early], [VMEM] * 4, [dma] + mix_bufs, out_...  1.93 us
    pallas_call x1, Pallas kernels, body(): call(layer_kernel, [shape(field.shape, bf16)] * 2 + [message], [VMEM] * 6...  1.9 us
    pallas_call x1, Pallas kernels, body(): call(input_grad_kernel, [shape(field.shape, bf16)], [VMEM] * 4, [pltpu.VM...  1.34 us
  transfers between devices with their start and end apart: 9, of which 6 were waited for; matrix products, arithmetic and copies ran while one was open for 0% of the time, Pallas kernels for 11%

profile of v21, /device:TPU:0, one launch (start us, length us, event | category | flops | bytes accessed | tf_op | source)
XLA Modules:
  0.0 58.5 jit_solution(787851045470592797)
XLA Ops:
  0.6 1.2 %copy-done.7 = bf16[1,2048,256]{2,1,0:T(8,128)(2,1)S(1)} copy-done((bf16[1,2048,256]{2,1,0:T(8,128)(2,1)S(1)}, bf16[1,2048,256]{2,1,0:T(8,128)(2,1)}, u32[]{:S(2)}) %copy-start.7) | copy-done | bytes 1048600
  1.9 2.4 %collective-permute-start.2 = (f32[8,256]{1,0:T(8,128)S(1)}, f32[8,256]{1,0:T(8,128)S(1)}, u32[]{:S(2)}, u32[]{:S(2)}) collective-permute-start(f32[8,256]{1,0:T(8,128)S(1)} %pipe_ends.1.refs_0_), channel_id=1, source_target_pairs={{0,3},{1,2},{2,1},{3,0},{4,7},{5,6},{6,5},{7,4},{8,11},{9,10},{10,... | collective-permute-start | bytes 24584 | tf_op jit(solution)/shard_map/ppermute | solution.py:433
  4.3 0.6 %collective-permute-start.1 = (f32[8,256]{1,0:T(8,128)S(1)}, f32[8,256]{1,0:T(8,128)S(1)}, u32[]{:S(2)}, u32[]{:S(2)}) collective-permute-start(f32[8,256]{1,0:T(8,128)S(1)} %pipe_ends.1.refs_0_), channel_id=1, source_target_pairs={{0,2},{1,3},{2,0},{3,1},{4,6},{5,7},{6,4},{7,5},{8,10},{9,11},{10,... | collective-permute-start | bytes 24584 | tf_op jit(solution)/shard_map/ppermute | solution.py:433
  5.0 0.0 collective-permute-start
  5.0 0.0 copy-start.3
  5.0 0.0 copy-start.4
  5.0 0.0 copy-start.5
  5.0 0.0 copy-start.6
  5.1 0.0 copy-start.10
  5.1 0.7 %spectrum.1 = (bf16[8,32,256]{2,1,0:T(8,128)(2,1)S(1)}, f32[2048,256]{1,0:T(8,128)S(1)}) custom-call(bf16[2048,256]{1,0:T(8,128)(2,1)S(1)} %bitcast.13, bf16[4,256,256]{2,1,0:T(8,128)(2,1)S(1)} %copy-done.11, bf16[256,256]{1,0:T(8,128)(2,1)S(1)} %copy-done.1, f32[1,256]{1,0:T(1,128)S(1)} %bitcast.15), custom_call_target="tpu_custom_call" | custom-call | flops 12000000000 | bytes 12582912 | tf_op jit(solution)/shard_map/spectrum/pallas_call | solution.py:443
  5.8 2.2 %collective-permute-done.1.refs_2_ = f32[8,256]{1,0:T(8,128)S(1)} collective-permute-done((f32[8,256]{1,0:T(8,128)S(1)}, f32[8,256]{1,0:T(8,128)S(1)}, u32[]{:S(2)}, u32[]{:S(2)}) %collective-permute-start.1) | collective-permute-done | bytes 8224 | tf_op jit(solution)/shard_map/ppermute | solution.py:433
  8.0 13.2 %all_to_all.20.r_ref.first_ref.refs_0_ = bf16[8,40,256]{2,1,0:T(8,128)(2,1)S(1)} all-to-all(bf16[8,40,256]{2,1,0:T(8,128)(2,1)S(1)} %message.1), channel_id=1, replica_groups=mesh['len'=8,'pipe'=4] {'len'}, dimensions={0} | all-to-all | bytes 327680 | tf_op jit(solution)/shard_map/all_to_all | solution.py:430
  21.2 0.0 copy-start
  21.2 0.0 copy-start.8
  21.2 0.8 %mix.1 = (bf16[8,32,256]{2,1,0:T(8,128)(2,1)S(1)}, f32[1,256]{1,0:T(1,128)S(1)}, f32[8,256]{1,0:T(8,128)S(1)}) custom-call(bf16[8,40,256]{2,1,0:T(8,128)(2,1)S(1)} %all_to_all.20.r_ref.first_ref.refs_0_, bf16[16,256,256]{2,1,0:T(8,128)(2,1)S(1)} %copy-done.5, bf16[16,256,256]{2,1,0:T(8,128)(2,1)S(1)} %copy-done.6, s32[1,32]{1,0:T(1,128)S(1)} %bitcast.8, ...), custom_call_target="tpu_custom_call" | custom-call | flops 12000000000 | bytes 12582912 | tf_op jit(solution)/shard_map/mix/pallas_call | solution.py:457
  22.1 9.7 %all_to_all.21.modes_ref = bf16[8,32,256]{2,1,0:T(8,128)(2,1)S(1)} all-to-all(bf16[8,32,256]{2,1,0:T(8,128)(2,1)S(1)} %get-tuple-element.28), channel_id=1, replica_groups=mesh['len'=8,'pipe'=4] {'len'}, dimensions={0} | all-to-all | bytes 262144 | tf_op jit(solution)/shard_map/all_to_all | solution.py:430
  31.8 1.9 %layer.1 = (bf16[2048,256]{1,0:T(8,128)(2,1)S(1)}, bf16[2048,256]{1,0:T(8,128)(2,1)S(1)}, bf16[8,34,256]{2,1,0:T(8,128)(2,1)S(1)}) custom-call(f32[2048,256]{1,0:T(8,128)S(1)} %get-tuple-element.25.pointwise_ref, bf16[2048,256]{1,0:T(8,128)(2,1)S(1)} %bitcast.14, bf16[4,256,256]{2,1,0:T(8,128)(2,1)S(1)} %copy-done.11, bf16[1024,256]{1,0:T(8,128)(2,1)S(1)} %copy-done, ...), custom_call_target="tpu_custom_call" | custom-call | flops 12000000000 | bytes 12582912 | tf_op jit(solution)/shard_map/layer/pallas_call | solution.py:467
  33.7 10.0 %all_to_all.22.r_ref.second_ref.refs_4_ = bf16[8,34,256]{2,1,0:T(8,128)(2,1)S(1)} all-to-all(bf16[8,34,256]{2,1,0:T(8,128)(2,1)S(1)} %get-tuple-element.29), channel_id=1, replica_groups=mesh['len'=8,'pipe'=4] {'len'}, dimensions={0} | all-to-all | bytes 278528 | tf_op jit(solution)/shard_map/all_to_all | solution.py:430
  43.7 0.8 %collective-permute-start.4 = (bf16[16,34,256]{2,1,0:T(8,128)(2,1)S(1)}, bf16[16,34,256]{2,1,0:T(8,128)(2,1)S(1)}, u32[]{:S(2)}, u32[]{:S(2)}) collective-permute-start(bf16[16,34,256]{2,1,0:T(8,128)(2,1)S(1)} %pack.1), channel_id=1, source_target_pairs={{0,2},{1,3},{2,0},{3,1},{4,6},{5,7},{6,4},{7,5},{8,10},{9,11},{10,... | collective-permute-start | bytes 835592 | tf_op jit(solution)/shard_map/ppermute | solution.py:433
  44.5 1.9 %mix_grad.1 = (bf16[8,32,256]{2,1,0:T(8,128)(2,1)}, bf16[2048,256]{1,0:T(8,128)(2,1)}) custom-call(bf16[8,34,256]{2,1,0:T(8,128)(2,1)S(1)} %all_to_all.22.r_ref.second_ref.refs_4_, bf16[16,256,256]{2,1,0:T(8,128)(2,1)S(1)} %copy-done.5, bf16[16,256,256]{2,1,0:T(8,128)(2,1)S(1)} %copy-done.6, bf16[2048,256]{1,0:T(8,128)(2,1)S(1)} %get-tuple-element.31.early_ref), custom_call_target="tpu_custom_call" | custom-call | flops 12000000000 | bytes 12582912 | tf_op jit(solution)/shard_map/mix_grad/pallas_call | solution.py:483
  46.5 3.4 %all-to-all-start.3 = ((bf16[8,32,256]{2,1,0:T(8,128)(2,1)}), bf16[8,32,256]{2,1,0:T(8,128)(2,1)S(1)}, u32[]{:S(2)}, u32[]{:S(2)}) async-start(bf16[8,32,256]{2,1,0:T(8,128)(2,1)} %get-tuple-element.35), calls=%async_computation.3 | async-start | bytes 262144 | tf_op jit(solution)/shard_map/all_to_all | solution.py:430
  49.8 0.1 collective-permute-start.3
  49.9 0.5 collective-permute-start.6
  50.4 0.5 collective-permute-done.4.both_ref
  50.9 0.1 collective-permute-start.5
  51.0 0.5 collective-permute-start.7
  51.5 0.1 collective-permute-done.6.refs_5_
  51.5 0.8 %collective-permute-done.5.refs_3_ = bf16[8,34,256]{2,1,0:T(8,128)(2,1)S(1)} collective-permute-done((bf16[8,34,256]{2,1,0:T(8,128)(2,1)S(1)}, bf16[8,34,256]{2,1,0:T(8,128)(2,1)S(1)}, u32[]{:S(2)}, u32[]{:S(2)}) %collective-permute-start.5) | collective-permute-done | bytes 139296 | tf_op jit(solution)/shard_map/ppermute | solution.py:433
  52.4 0.2 collective-permute-done.7.refs_7_
  52.6 4.0 %weight_grad.1 = (f32[16,256,256]{2,1,0:T(8,128)}, f32[16,256,256]{2,1,0:T(8,128)}, f32[8,256]{1,0:T(8,128)S(1)}, bf16[2048,256]{1,0:T(8,128)(2,1)S(1)}) custom-call(bf16[8,40,256]{2,1,0:T(8,128)(2,1)S(1)} %all_to_all.20.r_ref.first_ref.refs_0_, bf16[8,40,256]{2,1,0:T(8,128)(2,1)S(1)} %collective-permute-done.3.refs_1_, ...), custom_call_target="tpu_custom_call" | custom-call | tf_op jit(solution)/shard_map/weight_grad/pallas_call | solution.py:500
  56.6 0.5 all-to-all-done.3.modes_ref
  57.1 1.3 %input_grad.1 = bf16[2048,256]{1,0:T(8,128)(2,1)} custom-call(bf16[2048,256]{1,0:T(8,128)(2,1)S(1)} %get-tuple-element.42.local_ref, bf16[1024,256]{1,0:T(8,128)(2,1)S(1)} %copy-done, f32[8,256]{1,0:T(8,128)S(1)} %get-tuple-element.43.rows_ref, bf16[8,32,256]{2,1,0:T(8,128)(2,1)S(1)} %all-to-all-done.3.modes_ref), custom_call_target="tpu_custom_call" | custom-call | tf_op jit(solution)/shard_map/input_grad/pallas_call | solution.py:513
  (23 shorter events, 0.1 us)
Async XLA Ops:
  0.6 1.2 %copy-start.7 = (bf16[1,2048,256]{2,1,0:T(8,128)(2,1)S(1)}, bf16[1,2048,256]{2,1,0:T(8,128)(2,1)}, u32[]{:S(2)}) copy-start(bf16[1,2048,256]{2,1,0:T(8,128)(2,1)} %param.12) | copy-start | bytes 3145732
  1.9 3.1 %copy-start.1 = (bf16[256,256]{1,0:T(8,128)(2,1)S(1)}, bf16[256,256]{1,0:T(8,128)(2,1)}, u32[]{:S(2)}) copy-start(bf16[256,256]{1,0:T(8,128)(2,1)} %refs_13_.1) | copy-start | bytes 393220
  1.9 3.1 %copy-start.9 = (f32[256]{0:T(256)S(1)}, f32[256]{0:T(256)}, u32[]{:S(2)}) copy-start(f32[256]{0:T(256)} %param.15) | copy-start | bytes 3076
  1.9 3.1 %copy-start.11 = (bf16[4,256,256]{2,1,0:T(8,128)(2,1)S(1)}, bf16[4,256,256]{2,1,0:T(8,128)(2,1)}, u32[]{:S(2)}) copy-start(bf16[4,256,256]{2,1,0:T(8,128)(2,1)} %constant.4.clone.f_ref) | copy-start | bytes 1572868
  1.9 3.9 %collective-permute-start.2 = (f32[8,256]{1,0:T(8,128)S(1)}, f32[8,256]{1,0:T(8,128)S(1)}, u32[]{:S(2)}, u32[]{:S(2)}) collective-permute-start(f32[8,256]{1,0:T(8,128)S(1)} %pipe_ends.1.refs_0_), channel_id=1, source_target_pairs={{0,3},{1,2},{2,1},{3,0},{4,7},{5,6},{6,5},{7,4},{8,11},{9,10},{10,... | collective-permute-start | bytes 24584 | tf_op jit(solution)/shard_map/ppermute | solution.py:433
  4.3 3.7 %collective-permute-start.1 = (f32[8,256]{1,0:T(8,128)S(1)}, f32[8,256]{1,0:T(8,128)S(1)}, u32[]{:S(2)}, u32[]{:S(2)}) collective-permute-start(f32[8,256]{1,0:T(8,128)S(1)} %pipe_ends.1.refs_0_), channel_id=1, source_target_pairs={{0,2},{1,3},{2,0},{3,1},{4,6},{5,7},{6,4},{7,5},{8,10},{9,11},{10,... | collective-permute-start | bytes 24584 | tf_op jit(solution)/shard_map/ppermute | solution.py:433
  5.0 3.0 %collective-permute-start = (f32[8,256]{1,0:T(8,128)S(1)}, f32[8,256]{1,0:T(8,128)S(1)}, u32[]{:S(2)}, u32[]{:S(2)}) collective-permute-start(f32[8,256]{1,0:T(8,128)S(1)} %pipe_ends.1.refs_0_), channel_id=1, source_target_pairs={{0,1},{1,0},{2,3},{3,2},{4,5},{5,4},{6,7},{7,6},{8,9},{9,8},{10,11... | collective-permute-start | bytes 24584 | tf_op jit(solution)/shard_map/ppermute | solution.py:433
  5.0 16.2 %copy-start.2 = (bf16[256,256]{1,0:T(8,128)(2,1)S(1)}, bf16[256,256]{1,0:T(8,128)(2,1)}, u32[]{:S(2)}) copy-start(bf16[256,256]{1,0:T(8,128)(2,1)} %refs_10_.1) | copy-start | bytes 393220
  5.0 16.2 %copy-start.3 = (s32[32]{0:T(128)S(1)}, s32[32]{0:T(128)}, u32[]{:S(2)}) copy-start(s32[32]{0:T(128)} %param.20) | copy-start | bytes 388
  5.0 16.2 %copy-start.4 = (s32[32]{0:T(128)S(1)}, s32[32]{0:T(128)}, u32[]{:S(2)}) copy-start(s32[32]{0:T(128)} %param.21) | copy-start | bytes 388
  5.0 16.2 %copy-start.5 = (bf16[16,256,256]{2,1,0:T(8,128)(2,1)S(1)}, bf16[16,256,256]{2,1,0:T(8,128)(2,1)}, u32[]{:S(2)}) copy-start(bf16[16,256,256]{2,1,0:T(8,128)(2,1)} %real_ref.3) | copy-start | bytes 6291460
  5.0 16.2 %copy-start.6 = (bf16[16,256,256]{2,1,0:T(8,128)(2,1)S(1)}, bf16[16,256,256]{2,1,0:T(8,128)(2,1)}, u32[]{:S(2)}) copy-start(bf16[16,256,256]{2,1,0:T(8,128)(2,1)} %imag_ref.3) | copy-start | bytes 6291460
  5.1 16.2 %copy-start.10 = (f32[256]{0:T(256)S(1)}, f32[256]{0:T(256)}, u32[]{:S(2)}) copy-start(f32[256]{0:T(256)} %param.19) | copy-start | bytes 3076
  21.2 10.6 %copy-start = (bf16[1024,256]{1,0:T(8,128)(2,1)S(1)}, bf16[1024,256]{1,0:T(8,128)(2,1)}, u32[]{:S(2)}) copy-start(bf16[1024,256]{1,0:T(8,128)(2,1)} %constant.5.clone.ft_ref) | copy-start | bytes 1572868
  21.2 10.6 %copy-start.8 = (bf16[1,2048,256]{2,1,0:T(8,128)(2,1)S(1)}, bf16[1,2048,256]{2,1,0:T(8,128)(2,1)}, u32[]{:S(2)}) copy-start(bf16[1,2048,256]{2,1,0:T(8,128)(2,1)} %param.13) | copy-start | bytes 3145732
  43.7 7.1 %collective-permute-start.4 = (bf16[16,34,256]{2,1,0:T(8,128)(2,1)S(1)}, bf16[16,34,256]{2,1,0:T(8,128)(2,1)S(1)}, u32[]{:S(2)}, u32[]{:S(2)}) collective-permute-start(bf16[16,34,256]{2,1,0:T(8,128)(2,1)S(1)} %pack.1), channel_id=1, source_target_pairs={{0,2},{1,3},{2,0},{3,1},{4,6},{5,7},{6,4},{7,5},{8,10},{9,11},{10,... | collective-permute-start | bytes 835592 | tf_op jit(solution)/shard_map/ppermute | solution.py:433
  46.5 10.7 %all-to-all-start.3 = ((bf16[8,32,256]{2,1,0:T(8,128)(2,1)}), bf16[8,32,256]{2,1,0:T(8,128)(2,1)S(1)}, u32[]{:S(2)}, u32[]{:S(2)}) async-start(bf16[8,32,256]{2,1,0:T(8,128)(2,1)} %get-tuple-element.35), calls=%async_computation.3 | async-start | bytes 262144 | tf_op jit(solution)/shard_map/all_to_all | solution.py:430
  49.8 1.7 %collective-permute-start.3 = (bf16[8,40,256]{2,1,0:T(8,128)(2,1)S(1)}, bf16[8,40,256]{2,1,0:T(8,128)(2,1)S(1)}, u32[]{:S(2)}, u32[]{:S(2)}) collective-permute-start(bf16[8,40,256]{2,1,0:T(8,128)(2,1)S(1)} %all_to_all.20.r_ref.first_ref.refs_0_), channel_id=1, source_target_pairs={{0,1},{1,0},{2,3},{3,2},{4,5},{5,4},{6,7},{7,6},{8,9},{9,8},{10,11... | collective-permute-start | bytes 491528 | tf_op jit(solution)/shard_map/ppermute | solution.py:433
  49.9 1.6 %collective-permute-start.6 = (bf16[8,34,256]{2,1,0:T(8,128)(2,1)S(1)}, bf16[8,34,256]{2,1,0:T(8,128)(2,1)S(1)}, u32[]{:S(2)}, u32[]{:S(2)}) collective-permute-start(bf16[8,34,256]{2,1,0:T(8,128)(2,1)S(1)} %all_to_all.22.r_ref.second_ref.refs_4_), channel_id=1, source_target_pairs={{0,1},{1,0},{2,3},{3,2},{4,5},{5,4},{6,7},{7,6},{8,9},{9,8},{10,11... | collective-permute-start | bytes 417800 | tf_op jit(solution)/shard_map/ppermute | solution.py:433
  50.9 1.5 %collective-permute-start.5 = (bf16[8,34,256]{2,1,0:T(8,128)(2,1)S(1)}, bf16[8,34,256]{2,1,0:T(8,128)(2,1)S(1)}, u32[]{:S(2)}, u32[]{:S(2)}) collective-permute-start(bf16[8,34,256]{2,1,0:T(8,128)(2,1)S(1)} %get-tuple-element.37.refs_2_), channel_id=1, source_target_pairs={{0,1},{1,0},{2,3},{3,2},{4,5},{5,4},{6,7},{7,6},{8,9},{9,8},{10,11... | collective-permute-start | bytes 417800 | tf_op jit(solution)/shard_map/ppermute | solution.py:433
  51.0 1.6 %collective-permute-start.7 = (bf16[8,34,256]{2,1,0:T(8,128)(2,1)S(1)}, bf16[8,34,256]{2,1,0:T(8,128)(2,1)S(1)}, u32[]{:S(2)}, u32[]{:S(2)}) collective-permute-start(bf16[8,34,256]{2,1,0:T(8,128)(2,1)S(1)} %get-tuple-element.39.refs_6_), channel_id=1, source_target_pairs={{0,1},{1,0},{2,3},{3,2},{4,5},{5,4},{6,7},{7,6},{8,9},{9,8},{10,11... | collective-permute-start | bytes 417800 | tf_op jit(solution)/shard_map/ppermute | solution.py:433

commit v22 on v21

--- a/solution.py
+++ b/solution.py
@@ -155,7 +155,8 @@
             row = 2 * step + side
             put(ref, at, jnp.concatenate([part[row : row + 1] for part in ends], axis=0))
     picked_in, picked_out = selection(inlet_ref, outlet_ref, pipes)
-    sums = dot(picked_in, whole(first_ref)) + dot(picked_out, whole(last_ref))
+    count = pipes * groups
+    sums = dot(picked_in, whole(first_ref, count)) + dot(picked_out, whole(last_ref, count))
     act = dot(sums.astype(jnp.bfloat16), junc_weight_ref[...]) + junc_bias_ref[...]
     sigmoid_part = jax.nn.sigmoid(act)
     junc_rows = (act * sigmoid_part).astype(jnp.bfloat16).astype(jnp.float32)
@@ -187,8 +188,8 @@
     return (inlets == own).astype(jnp.bfloat16), (outlets == own).astype(jnp.bfloat16)
 
 
-def whole(ref):
-    return take(ref, pl.ds(0, ref.shape[1])).astype(jnp.bfloat16)
+def whole(ref, count):
+    return take(ref, pl.ds(0, count)).astype(jnp.bfloat16)
 
 
 def started(copies):
@@ -314,7 +315,8 @@
         put(last_ref, at, lower_ref[...])
     picked_in, picked_out = selection(inlet_ref, outlet_ref, pipes)
     picked = picked_in + picked_out
-    junc_grad = COUPLING * (dot(picked, whole(first_ref)) + dot(picked, whole(last_ref)))
+    sums = dot(picked, whole(first_ref, count)) + dot(picked, whole(last_ref, count))
+    junc_grad = COUPLING * sums
     act_grad = (junc_grad * slope_ref[...]).astype(jnp.bfloat16)
     sums_grad = dot(act_grad, junc_weight_ref[...], 1, 1)
     rows_ref[...] = sums_grad.astype(jnp.bfloat16).astype(jnp.float32)
@@ -371,8 +373,9 @@
     wait(going)
 
 
-def rows_of(count, channels):
-    return pltpu.VMEM((channels // LANES, count, LANES), jnp.float32)
+def rows_of(count, stride, channels):
+    rows = -(-(count + stride) // 8) * 8
+    return pltpu.VMEM((channels // LANES, rows, LANES), jnp.float32)
 
 
 def call(kernel, outs, specs, scratch=(), out_specs=None, name=None, limit=8, busy=0):
@@ -432,8 +435,8 @@
     def swap(value, step):
         return lax.ppermute(value, "pipe", [(i, i ^ step) for i in range(pipes)])
 
-    mix_bufs = [rows_of(all_rows, channels)] * 2
-    pipe_rows = [rows_of(pipes * groups, channels)] * 2
+    mix_bufs = [rows_of(all_rows, span, channels)] * 2
+    pipe_rows = [rows_of(pipes * groups, pipes, channels)] * 2
     inlet_row = inlet_ids.reshape(1, -1)
     outlet_row = outlet_ids.reshape(1, -1)
     (ends,) = call(
@@ -501,7 +504,7 @@
         functools.partial(weight_grad_kernel, pipes, modes, per_copy),
         [big, big, shape((8, channels), f32), shape(field.shape, bf16)],
         [VMEM] * (2 * pipes + 6),
-        [rows_of(pipes * all_rows, channels)] * 2
+        [rows_of(pipes * all_rows, span, channels)] * 2
         + [pltpu.VMEM(big.shape, f32)] * 2
         + pipe_rows
         + [pltpu.VMEM((groups, channels), f32)] * 2

time: 58.8 us -> 58.8 us (level)
  no operation moved by 1% of the time
where the time goes in v22:
time: 58.8 us; the launch traced here: 58.5 us
  blocking collectives  32.9 us (56%)
  Pallas kernels  10.8 us (18%)
  starting transfers between devices  8.42 us (14%)
  waiting for transfers between devices  4.27 us (7%)
  local copies, waits for them, and re-layouts  1.28 us (2%)
  between operations  0.83 us (1%)
    all_to_all x3, blocking collectives, exchange(): return lax.all_to_all(value, 'len', split_axis=0, concat_axis=0, tiled=True)  32.9 us
    ppermute x8, starting transfers between devices, swap(): return lax.ppermute(value, 'pipe', [(i, i ^ step) for i in range(pipes)])  5.04 us
    pallas_call x1, Pallas kernels, body(): call(functools.partial(weight_grad_kernel, pipes, modes, per_copy), [big,...  3.99 us
    ppermute x8, waiting for transfers between devices, swap(): return lax.ppermute(value, 'pipe', [(i, i ^ step) for i in range(pipes)])  3.74 us
    all_to_all x1, starting transfers between devices, exchange(): return lax.all_to_all(value, 'len', split_axis=0, concat_axis=0, tiled=True)  3.38 us
    pallas_call x1, Pallas kernels, body(): call(mix_grad_kernel, [chunks, early], [VMEM] * 4, [dma] + mix_bufs, out_...  1.93 us
    pallas_call x1, Pallas kernels, body(): call(layer_kernel, [shape(field.shape, bf16)] * 2 + [message], [VMEM] * 6...  1.9 us
    pallas_call x1, Pallas kernels, body(): call(input_grad_kernel, [shape(field.shape, bf16)], [VMEM] * 4, [pltpu.VM...  1.34 us
  transfers between devices with their start and end apart: 9, of which 6 were waited for; matrix products, arithmetic and copies ran while one was open for 0% of the time, Pallas kernels for 11%

profile of v22, /device:TPU:0, one launch (start us, length us, event | category | flops | bytes accessed | tf_op | source)
XLA Modules:
  0.0 58.5 jit_solution(1787182283406072508)
XLA Ops:
  0.6 1.2 %copy-done.7 = bf16[1,2048,256]{2,1,0:T(8,128)(2,1)S(1)} copy-done((bf16[1,2048,256]{2,1,0:T(8,128)(2,1)S(1)}, bf16[1,2048,256]{2,1,0:T(8,128)(2,1)}, u32[]{:S(2)}) %copy-start.7) | copy-done | bytes 1048600
  1.9 2.4 %collective-permute-start.2 = (f32[8,256]{1,0:T(8,128)S(1)}, f32[8,256]{1,0:T(8,128)S(1)}, u32[]{:S(2)}, u32[]{:S(2)}) collective-permute-start(f32[8,256]{1,0:T(8,128)S(1)} %pipe_ends.1.refs_0_), channel_id=1, source_target_pairs={{0,3},{1,2},{2,1},{3,0},{4,7},{5,6},{6,5},{7,4},{8,11},{9,10},{10,... | collective-permute-start | bytes 24584 | tf_op jit(solution)/shard_map/ppermute | solution.py:436
  4.3 0.6 %collective-permute-start.1 = (f32[8,256]{1,0:T(8,128)S(1)}, f32[8,256]{1,0:T(8,128)S(1)}, u32[]{:S(2)}, u32[]{:S(2)}) collective-permute-start(f32[8,256]{1,0:T(8,128)S(1)} %pipe_ends.1.refs_0_), channel_id=1, source_target_pairs={{0,2},{1,3},{2,0},{3,1},{4,6},{5,7},{6,4},{7,5},{8,10},{9,11},{10,... | collective-permute-start | bytes 24584 | tf_op jit(solution)/shard_map/ppermute | solution.py:436
  5.0 0.0 collective-permute-start
  5.0 0.0 copy-start.3
  5.0 0.0 copy-start.4
  5.0 0.0 copy-start.5
  5.0 0.0 copy-start.6
  5.1 0.0 copy-start.10
  5.1 0.7 %spectrum.1 = (bf16[8,32,256]{2,1,0:T(8,128)(2,1)S(1)}, f32[2048,256]{1,0:T(8,128)S(1)}) custom-call(bf16[2048,256]{1,0:T(8,128)(2,1)S(1)} %bitcast.13, bf16[4,256,256]{2,1,0:T(8,128)(2,1)S(1)} %copy-done.11, bf16[256,256]{1,0:T(8,128)(2,1)S(1)} %copy-done.1, f32[1,256]{1,0:T(1,128)S(1)} %bitcast.15), custom_call_target="tpu_custom_call" | custom-call | flops 12000000000 | bytes 12582912 | tf_op jit(solution)/shard_map/spectrum/pallas_call | solution.py:446
  5.8 2.2 %collective-permute-done.1.refs_2_ = f32[8,256]{1,0:T(8,128)S(1)} collective-permute-done((f32[8,256]{1,0:T(8,128)S(1)}, f32[8,256]{1,0:T(8,128)S(1)}, u32[]{:S(2)}, u32[]{:S(2)}) %collective-permute-start.1) | collective-permute-done | bytes 8224 | tf_op jit(solution)/shard_map/ppermute | solution.py:436
  8.0 13.2 %all_to_all.20.r_ref.first_ref.refs_0_ = bf16[8,40,256]{2,1,0:T(8,128)(2,1)S(1)} all-to-all(bf16[8,40,256]{2,1,0:T(8,128)(2,1)S(1)} %message.1), channel_id=1, replica_groups=mesh['len'=8,'pipe'=4] {'len'}, dimensions={0} | all-to-all | bytes 327680 | tf_op jit(solution)/shard_map/all_to_all | solution.py:433
  21.2 0.0 copy-start
  21.2 0.0 copy-start.8
  21.2 0.8 %mix.1 = (bf16[8,32,256]{2,1,0:T(8,128)(2,1)S(1)}, f32[1,256]{1,0:T(1,128)S(1)}, f32[8,256]{1,0:T(8,128)S(1)}) custom-call(bf16[8,40,256]{2,1,0:T(8,128)(2,1)S(1)} %all_to_all.20.r_ref.first_ref.refs_0_, bf16[16,256,256]{2,1,0:T(8,128)(2,1)S(1)} %copy-done.5, bf16[16,256,256]{2,1,0:T(8,128)(2,1)S(1)} %copy-done.6, s32[1,32]{1,0:T(1,128)S(1)} %bitcast.8, ...), custom_call_target="tpu_custom_call" | custom-call | flops 12000000000 | bytes 12582912 | tf_op jit(solution)/shard_map/mix/pallas_call | solution.py:460
  22.1 9.7 %all_to_all.21.modes_ref = bf16[8,32,256]{2,1,0:T(8,128)(2,1)S(1)} all-to-all(bf16[8,32,256]{2,1,0:T(8,128)(2,1)S(1)} %get-tuple-element.28), channel_id=1, replica_groups=mesh['len'=8,'pipe'=4] {'len'}, dimensions={0} | all-to-all | bytes 262144 | tf_op jit(solution)/shard_map/all_to_all | solution.py:433
  31.8 1.9 %layer.1 = (bf16[2048,256]{1,0:T(8,128)(2,1)S(1)}, bf16[2048,256]{1,0:T(8,128)(2,1)S(1)}, bf16[8,34,256]{2,1,0:T(8,128)(2,1)S(1)}) custom-call(f32[2048,256]{1,0:T(8,128)S(1)} %get-tuple-element.25.pointwise_ref, bf16[2048,256]{1,0:T(8,128)(2,1)S(1)} %bitcast.14, bf16[4,256,256]{2,1,0:T(8,128)(2,1)S(1)} %copy-done.11, bf16[1024,256]{1,0:T(8,128)(2,1)S(1)} %copy-done, ...), custom_call_target="tpu_custom_call" | custom-call | flops 12000000000 | bytes 12582912 | tf_op jit(solution)/shard_map/layer/pallas_call | solution.py:470
  33.7 10.0 %all_to_all.22.r_ref.second_ref.refs_4_ = bf16[8,34,256]{2,1,0:T(8,128)(2,1)S(1)} all-to-all(bf16[8,34,256]{2,1,0:T(8,128)(2,1)S(1)} %get-tuple-element.29), channel_id=1, replica_groups=mesh['len'=8,'pipe'=4] {'len'}, dimensions={0} | all-to-all | bytes 278528 | tf_op jit(solution)/shard_map/all_to_all | solution.py:433
  43.7 0.8 %collective-permute-start.4 = (bf16[16,34,256]{2,1,0:T(8,128)(2,1)S(1)}, bf16[16,34,256]{2,1,0:T(8,128)(2,1)S(1)}, u32[]{:S(2)}, u32[]{:S(2)}) collective-permute-start(bf16[16,34,256]{2,1,0:T(8,128)(2,1)S(1)} %pack.1), channel_id=1, source_target_pairs={{0,2},{1,3},{2,0},{3,1},{4,6},{5,7},{6,4},{7,5},{8,10},{9,11},{10,... | collective-permute-start | bytes 835592 | tf_op jit(solution)/shard_map/ppermute | solution.py:436
  44.5 1.9 %mix_grad.1 = (bf16[8,32,256]{2,1,0:T(8,128)(2,1)}, bf16[2048,256]{1,0:T(8,128)(2,1)}) custom-call(bf16[8,34,256]{2,1,0:T(8,128)(2,1)S(1)} %all_to_all.22.r_ref.second_ref.refs_4_, bf16[16,256,256]{2,1,0:T(8,128)(2,1)S(1)} %copy-done.5, bf16[16,256,256]{2,1,0:T(8,128)(2,1)S(1)} %copy-done.6, bf16[2048,256]{1,0:T(8,128)(2,1)S(1)} %get-tuple-element.31.early_ref), custom_call_target="tpu_custom_call" | custom-call | flops 12000000000 | bytes 12582912 | tf_op jit(solution)/shard_map/mix_grad/pallas_call | solution.py:486
  46.5 3.4 %all-to-all-start.3 = ((bf16[8,32,256]{2,1,0:T(8,128)(2,1)}), bf16[8,32,256]{2,1,0:T(8,128)(2,1)S(1)}, u32[]{:S(2)}, u32[]{:S(2)}) async-start(bf16[8,32,256]{2,1,0:T(8,128)(2,1)} %get-tuple-element.35), calls=%async_computation.3 | async-start | bytes 262144 | tf_op jit(solution)/shard_map/all_to_all | solution.py:433
  49.8 0.1 collective-permute-start.3
  49.9 0.5 collective-permute-start.6
  50.4 0.5 collective-permute-done.4.both_ref
  50.9 0.1 collective-permute-start.5
  51.0 0.5 collective-permute-start.7
  51.5 0.1 collective-permute-done.6.refs_5_
  51.5 0.8 %collective-permute-done.5.refs_3_ = bf16[8,34,256]{2,1,0:T(8,128)(2,1)S(1)} collective-permute-done((bf16[8,34,256]{2,1,0:T(8,128)(2,1)S(1)}, bf16[8,34,256]{2,1,0:T(8,128)(2,1)S(1)}, u32[]{:S(2)}, u32[]{:S(2)}) %collective-permute-start.5) | collective-permute-done | bytes 139296 | tf_op jit(solution)/shard_map/ppermute | solution.py:436
  52.4 0.2 collective-permute-done.7.refs_7_
  52.6 4.0 %weight_grad.1 = (f32[16,256,256]{2,1,0:T(8,128)}, f32[16,256,256]{2,1,0:T(8,128)}, f32[8,256]{1,0:T(8,128)S(1)}, bf16[2048,256]{1,0:T(8,128)(2,1)S(1)}) custom-call(bf16[8,40,256]{2,1,0:T(8,128)(2,1)S(1)} %all_to_all.20.r_ref.first_ref.refs_0_, bf16[8,40,256]{2,1,0:T(8,128)(2,1)S(1)} %collective-permute-done.3.refs_1_, ...), custom_call_target="tpu_custom_call" | custom-call | tf_op jit(solution)/shard_map/weight_grad/pallas_call | solution.py:503
  56.6 0.5 all-to-all-done.3.modes_ref
  57.1 1.3 %input_grad.1 = bf16[2048,256]{1,0:T(8,128)(2,1)} custom-call(bf16[2048,256]{1,0:T(8,128)(2,1)S(1)} %get-tuple-element.42.local_ref, bf16[1024,256]{1,0:T(8,128)(2,1)S(1)} %copy-done, f32[8,256]{1,0:T(8,128)S(1)} %get-tuple-element.43.rows_ref, bf16[8,32,256]{2,1,0:T(8,128)(2,1)S(1)} %all-to-all-done.3.modes_ref), custom_call_target="tpu_custom_call" | custom-call | tf_op jit(solution)/shard_map/input_grad/pallas_call | solution.py:516
  (23 shorter events, 0.1 us)
Async XLA Ops:
  0.6 1.2 %copy-start.7 = (bf16[1,2048,256]{2,1,0:T(8,128)(2,1)S(1)}, bf16[1,2048,256]{2,1,0:T(8,128)(2,1)}, u32[]{:S(2)}) copy-start(bf16[1,2048,256]{2,1,0:T(8,128)(2,1)} %param.12) | copy-start | bytes 3145732
  1.9 3.1 %copy-start.1 = (bf16[256,256]{1,0:T(8,128)(2,1)S(1)}, bf16[256,256]{1,0:T(8,128)(2,1)}, u32[]{:S(2)}) copy-start(bf16[256,256]{1,0:T(8,128)(2,1)} %refs_13_.1) | copy-start | bytes 393220
  1.9 3.1 %copy-start.9 = (f32[256]{0:T(256)S(1)}, f32[256]{0:T(256)}, u32[]{:S(2)}) copy-start(f32[256]{0:T(256)} %param.15) | copy-start | bytes 3076
  1.9 3.1 %copy-start.11 = (bf16[4,256,256]{2,1,0:T(8,128)(2,1)S(1)}, bf16[4,256,256]{2,1,0:T(8,128)(2,1)}, u32[]{:S(2)}) copy-start(bf16[4,256,256]{2,1,0:T(8,128)(2,1)} %constant.4.clone.f_ref) | copy-start | bytes 1572868
  1.9 3.9 %collective-permute-start.2 = (f32[8,256]{1,0:T(8,128)S(1)}, f32[8,256]{1,0:T(8,128)S(1)}, u32[]{:S(2)}, u32[]{:S(2)}) collective-permute-start(f32[8,256]{1,0:T(8,128)S(1)} %pipe_ends.1.refs_0_), channel_id=1, source_target_pairs={{0,3},{1,2},{2,1},{3,0},{4,7},{5,6},{6,5},{7,4},{8,11},{9,10},{10,... | collective-permute-start | bytes 24584 | tf_op jit(solution)/shard_map/ppermute | solution.py:436
  4.3 3.7 %collective-permute-start.1 = (f32[8,256]{1,0:T(8,128)S(1)}, f32[8,256]{1,0:T(8,128)S(1)}, u32[]{:S(2)}, u32[]{:S(2)}) collective-permute-start(f32[8,256]{1,0:T(8,128)S(1)} %pipe_ends.1.refs_0_), channel_id=1, source_target_pairs={{0,2},{1,3},{2,0},{3,1},{4,6},{5,7},{6,4},{7,5},{8,10},{9,11},{10,... | collective-permute-start | bytes 24584 | tf_op jit(solution)/shard_map/ppermute | solution.py:436
  5.0 3.0 %collective-permute-start = (f32[8,256]{1,0:T(8,128)S(1)}, f32[8,256]{1,0:T(8,128)S(1)}, u32[]{:S(2)}, u32[]{:S(2)}) collective-permute-start(f32[8,256]{1,0:T(8,128)S(1)} %pipe_ends.1.refs_0_), channel_id=1, source_target_pairs={{0,1},{1,0},{2,3},{3,2},{4,5},{5,4},{6,7},{7,6},{8,9},{9,8},{10,11... | collective-permute-start | bytes 24584 | tf_op jit(solution)/shard_map/ppermute | solution.py:436
  5.0 16.2 %copy-start.2 = (bf16[256,256]{1,0:T(8,128)(2,1)S(1)}, bf16[256,256]{1,0:T(8,128)(2,1)}, u32[]{:S(2)}) copy-start(bf16[256,256]{1,0:T(8,128)(2,1)} %refs_10_.1) | copy-start | bytes 393220
  5.0 16.2 %copy-start.3 = (s32[32]{0:T(128)S(1)}, s32[32]{0:T(128)}, u32[]{:S(2)}) copy-start(s32[32]{0:T(128)} %param.20) | copy-start | bytes 388
  5.0 16.2 %copy-start.4 = (s32[32]{0:T(128)S(1)}, s32[32]{0:T(128)}, u32[]{:S(2)}) copy-start(s32[32]{0:T(128)} %param.21) | copy-start | bytes 388
  5.0 16.2 %copy-start.5 = (bf16[16,256,256]{2,1,0:T(8,128)(2,1)S(1)}, bf16[16,256,256]{2,1,0:T(8,128)(2,1)}, u32[]{:S(2)}) copy-start(bf16[16,256,256]{2,1,0:T(8,128)(2,1)} %real_ref.3) | copy-start | bytes 6291460
  5.0 16.2 %copy-start.6 = (bf16[16,256,256]{2,1,0:T(8,128)(2,1)S(1)}, bf16[16,256,256]{2,1,0:T(8,128)(2,1)}, u32[]{:S(2)}) copy-start(bf16[16,256,256]{2,1,0:T(8,128)(2,1)} %imag_ref.3) | copy-start | bytes 6291460
  5.1 16.2 %copy-start.10 = (f32[256]{0:T(256)S(1)}, f32[256]{0:T(256)}, u32[]{:S(2)}) copy-start(f32[256]{0:T(256)} %param.19) | copy-start | bytes 3076
  21.2 10.6 %copy-start = (bf16[1024,256]{1,0:T(8,128)(2,1)S(1)}, bf16[1024,256]{1,0:T(8,128)(2,1)}, u32[]{:S(2)}) copy-start(bf16[1024,256]{1,0:T(8,128)(2,1)} %constant.5.clone.ft_ref) | copy-start | bytes 1572868
  21.2 10.6 %copy-start.8 = (bf16[1,2048,256]{2,1,0:T(8,128)(2,1)S(1)}, bf16[1,2048,256]{2,1,0:T(8,128)(2,1)}, u32[]{:S(2)}) copy-start(bf16[1,2048,256]{2,1,0:T(8,128)(2,1)} %param.13) | copy-start | bytes 3145732
  43.7 7.1 %collective-permute-start.4 = (bf16[16,34,256]{2,1,0:T(8,128)(2,1)S(1)}, bf16[16,34,256]{2,1,0:T(8,128)(2,1)S(1)}, u32[]{:S(2)}, u32[]{:S(2)}) collective-permute-start(bf16[16,34,256]{2,1,0:T(8,128)(2,1)S(1)} %pack.1), channel_id=1, source_target_pairs={{0,2},{1,3},{2,0},{3,1},{4,6},{5,7},{6,4},{7,5},{8,10},{9,11},{10,... | collective-permute-start | bytes 835592 | tf_op jit(solution)/shard_map/ppermute | solution.py:436
  46.5 10.7 %all-to-all-start.3 = ((bf16[8,32,256]{2,1,0:T(8,128)(2,1)}), bf16[8,32,256]{2,1,0:T(8,128)(2,1)S(1)}, u32[]{:S(2)}, u32[]{:S(2)}) async-start(bf16[8,32,256]{2,1,0:T(8,128)(2,1)} %get-tuple-element.35), calls=%async_computation.3 | async-start | bytes 262144 | tf_op jit(solution)/shard_map/all_to_all | solution.py:433
  49.8 1.7 %collective-permute-start.3 = (bf16[8,40,256]{2,1,0:T(8,128)(2,1)S(1)}, bf16[8,40,256]{2,1,0:T(8,128)(2,1)S(1)}, u32[]{:S(2)}, u32[]{:S(2)}) collective-permute-start(bf16[8,40,256]{2,1,0:T(8,128)(2,1)S(1)} %all_to_all.20.r_ref.first_ref.refs_0_), channel_id=1, source_target_pairs={{0,1},{1,0},{2,3},{3,2},{4,5},{5,4},{6,7},{7,6},{8,9},{9,8},{10,11... | collective-permute-start | bytes 491528 | tf_op jit(solution)/shard_map/ppermute | solution.py:436
  49.9 1.6 %collective-permute-start.6 = (bf16[8,34,256]{2,1,0:T(8,128)(2,1)S(1)}, bf16[8,34,256]{2,1,0:T(8,128)(2,1)S(1)}, u32[]{:S(2)}, u32[]{:S(2)}) collective-permute-start(bf16[8,34,256]{2,1,0:T(8,128)(2,1)S(1)} %all_to_all.22.r_ref.second_ref.refs_4_), channel_id=1, source_target_pairs={{0,1},{1,0},{2,3},{3,2},{4,5},{5,4},{6,7},{7,6},{8,9},{9,8},{10,11... | collective-permute-start | bytes 417800 | tf_op jit(solution)/shard_map/ppermute | solution.py:436
  50.9 1.5 %collective-permute-start.5 = (bf16[8,34,256]{2,1,0:T(8,128)(2,1)S(1)}, bf16[8,34,256]{2,1,0:T(8,128)(2,1)S(1)}, u32[]{:S(2)}, u32[]{:S(2)}) collective-permute-start(bf16[8,34,256]{2,1,0:T(8,128)(2,1)S(1)} %get-tuple-element.37.refs_2_), channel_id=1, source_target_pairs={{0,1},{1,0},{2,3},{3,2},{4,5},{5,4},{6,7},{7,6},{8,9},{9,8},{10,11... | collective-permute-start | bytes 417800 | tf_op jit(solution)/shard_map/ppermute | solution.py:436
  51.0 1.6 %collective-permute-start.7 = (bf16[8,34,256]{2,1,0:T(8,128)(2,1)S(1)}, bf16[8,34,256]{2,1,0:T(8,128)(2,1)S(1)}, u32[]{:S(2)}, u32[]{:S(2)}) collective-permute-start(bf16[8,34,256]{2,1,0:T(8,128)(2,1)S(1)} %get-tuple-element.39.refs_6_), channel_id=1, source_target_pairs={{0,1},{1,0},{2,3},{3,2},{4,5},{5,4},{6,7},{7,6},{8,9},{9,8},{10,11... | collective-permute-start | bytes 417800 | tf_op jit(solution)/shard_map/ppermute | solution.py:436
